TPU v7x, 32 devices: a whole 2x2x4 slice. The times are simulated.
32 devices in a mesh: grp: 2 (over y), row: 4 (over z), col: 4 (over x, core).
Axes of the slice: x: 2, y: 2, z: 4, core: 2. Of those that a mesh axis runs over, the one named last changes fastest.
Arguments:
- x_state: float32 [4096, 256], P(('col', 'row'), 'grp'), parts along dimension 1, may hold values from -6 to 6
- q_lin: float32 [4096, 256], P(('col', 'row'), 'grp'), parts along dimension 1, may hold values from -6 to 6
- p_diag: float32 [4096], P(('col', 'row')), may hold values from 0.5 to 2
- z_state: float32 [3072, 256], P('row', 'grp'), parts along dimension 1, may hold values from -3 to 3
- y_state: float32 [3072, 256], P('row', 'grp'), parts along dimension 1, may hold values from -3 to 3
- lower_bound: float32 [3072, 256], P('row', 'grp'), parts along dimension 1, may hold values from -1.5 to -0.3
- upper_bound: float32 [3072, 256], P('row', 'grp'), parts along dimension 1, may hold values from 0.3 to 1.5
- a_blocks: float32 [24, 16, 128, 128], P('row', 'col'), may hold values from -0.125 to 0.125
- a_cols: int32 [24, 16], P('row', 'col'), may hold values from 0 to 7, as said below
- p_blocks: float32 [4, 16, 128, 128], P('col', 'row'), as said below
- p_pairs: int32 [4, 4, 2], P('col', 'row'), may hold values from 0 to 7, as said below
Outputs:
- x_next: float32 [4096, 256], P(('col', 'row'), 'grp'), parts along dimension 1
- z_next: float32 [3072, 256], P('row', 'grp'), parts along dimension 1
- y_next: float32 [3072, 256], P('row', 'grp'), parts along dimension 1
There are 2 independent parts, one for each index of `grp`. A program takes and returns all parts, laid end to end along the dimension named above; an argument that names none is the same for every part. Nothing has to cross between parts.
Inputs may be any that keep to these rules, and one draw needn't show every extreme that they name: `a_cols`: in each block row, the 4 entries of one variable range are distinct local block columns of that range. `p_pairs`: each entry holds local block rows i and j of one pair term within its variable range, with i different from j. `p_blocks`: for pair k the slots 4k, 4k+1, 4k+2, 4k+3 hold F F^T, F H^T, H F^T, H H^T of one positive semidefinite term, so that P is symmetric positive definite.
All inputs are finite; a program needn't handle non-finite values.
Results may differ from a plain program's by a relative error of at most 0.00026.
Values sent between devices are 32-bit elements; how exact they have to be, the bound alone decides.
No kernel may reach another device: no remote copies, remote signals or barrier semaphores. Data moves between devices by JAX's collectives and lax.ppermute only.
A program may use at most 64 MiB of HBM per device.

v0:
```python
import jax
import jax.numpy as jnp
from jax import lax
from jax.sharding import PartitionSpec as P

ADMM_ITERS = 2
CG_STEPS = 2


rho_penalty = 0.5
sigma_shift = 1e-06
relaxation = 1.6
highest = lax.Precision.HIGHEST


def local(
    x_state,
    q_lin,
    p_diag,
    z_state,
    y_state,
    lower_bound,
    upper_bound,
    a_blocks,
    a_cols,
    p_blocks,
    p_pairs,
):
    block = a_blocks.shape[-1]
    slab_blocks, per_range = a_cols.shape
    n_rows = lax.axis_size("row")
    own_count = x_state.shape[0]
    range_rows = own_count * n_rows
    n_range = range_rows // block
    qp_count = x_state.shape[1]
    a_flat = a_blocks.reshape(slab_blocks * per_range, block, block)
    col_flat = a_cols.reshape(-1)
    range_ids = jnp.arange(n_range, dtype=jnp.int32)
    place_cols = (col_flat[:, None] == range_ids[None, :]).astype(jnp.float32)
    pair_first = p_pairs[0, 0, 0]
    pair_second = p_pairs[0, 0, 1]
    pair_rows = jnp.stack([pair_first, pair_first, pair_second, pair_second])
    pair_cols = jnp.stack([pair_first, pair_second, pair_first, pair_second])
    place_rows = (pair_rows[:, None] == range_ids[None, :]).astype(jnp.float32)
    pair_blocks = p_blocks.reshape(4, block, block)
    col_squares = jnp.sum(a_flat * a_flat, axis=1)
    col_total = jnp.einsum("kt,kj->tj", place_cols, col_squares, precision=highest)
    diag_first = jnp.diagonal(pair_blocks[0])
    diag_second = jnp.diagonal(pair_blocks[3])
    pair_total = (
        place_rows[0][:, None] * diag_first[None, :] + place_rows[3][:, None] * diag_second[None, :]
    )
    local_diag = (pair_total + rho_penalty * col_total).reshape(range_rows)

    def products(whole, offset):
        range_grid = whole.reshape(n_range, block, qp_count)
        picked = range_grid[col_flat]
        slab_part = jnp.einsum("kij,kjq->kiq", a_flat, picked, precision=highest)
        slab_part = slab_part.reshape(slab_blocks, per_range, block, qp_count).sum(axis=1)
        slab_sum = lax.psum(slab_part.reshape(slab_blocks * block, qp_count), "col")
        back_in = (rho_penalty * slab_sum - offset).reshape(slab_blocks, block, qp_count)
        back_parts = jnp.einsum("rkij,riq->rkjq", a_blocks, back_in, precision=highest)
        back_parts = back_parts.reshape(slab_blocks * per_range, block, qp_count)
        pair_part = jnp.einsum(
            "kij,kjq->kiq", pair_blocks, range_grid[pair_cols], precision=highest
        )
        var_term = jnp.einsum("kt,kjq->tjq", place_cols, back_parts, precision=highest)
        var_term = var_term + jnp.einsum("kt,kiq->tiq", place_rows, pair_part, precision=highest)
        return (slab_sum, var_term.reshape(range_rows, qp_count))

    primal, q_range, diag_range = (x_state, q_lin, p_diag)
    diag_sum = lax.psum_scatter(local_diag, "row", scatter_dimension=0, tiled=True)

    def reach_range(vector):
        return lax.all_gather(vector, "row", axis=0, tiled=True)

    def settle_rows(var_term):
        return lax.psum_scatter(var_term, "row", scatter_dimension=0, tiled=True)

    def column_sums(pieces):
        return lax.psum((pieces[0],), ("row", "col"))

    diag_k = (diag_range + sigma_shift + diag_sum)[:, None]
    shift_k = (diag_range + sigma_shift)[:, None]
    slack, duals = (z_state, y_state)
    zero_slab = jnp.zeros_like(z_state)
    for outer_step in range(ADMM_ITERS):
        slab_now, var_term = products(reach_range(primal), rho_penalty * slack - duals)
        residual = -q_range - diag_range[:, None] * primal - settle_rows(var_term)
        precond = residual / diag_k
        (rz_now,) = column_sums((jnp.sum(residual * precond, axis=0),))
        direction = precond
        x_hat, ax_hat = (primal, slab_now)
        for inner_step in range(CG_STEPS):
            final_step = inner_step + 1 == CG_STEPS
            a_dir, dir_term = products(reach_range(direction), zero_slab)
            k_dir = shift_k * direction + settle_rows(dir_term)
            (curvature,) = column_sums((jnp.sum(direction * k_dir, axis=0),))
            step_size = rz_now / curvature
            if not final_step:
                residual = residual - step_size * k_dir
                precond = residual / diag_k
                (rz_next,) = column_sums((jnp.sum(residual * precond, axis=0),))
            x_hat = x_hat + step_size * direction
            ax_hat = ax_hat + step_size * a_dir
            if not final_step:
                direction = precond + rz_next / rz_now * direction
                rz_now = rz_next
        relaxed = relaxation * ax_hat + (1.0 - relaxation) * slack
        z_new = jnp.clip(relaxed + duals / rho_penalty, lower_bound, upper_bound)
        duals = duals + rho_penalty * (relaxed - z_new)
        primal = relaxation * x_hat + (1.0 - relaxation) * primal
        slack = z_new
    return (primal, slack, duals)


def solution(mesh):
    placed = (
        P(("col", "row"), "grp"),
        P(("col", "row"), "grp"),
        P(("col", "row")),
        P("row", "grp"),
        P("row", "grp"),
        P("row", "grp"),
        P("row", "grp"),
        P("row", "col", None, None),
        P("row", "col"),
        P("col", "row", None, None),
        P("col", "row", None),
    )
    return jax.shard_map(
        local,
        mesh=mesh,
        in_specs=placed,
        out_specs=(P(("col", "row"), "grp"), P("row", "grp"), P("row", "grp")),
        check_vma=False,
    )
```

profile of v0, /device:TPU:0, one launch (start us, length us, event | category | flops | bytes accessed | tf_op | source)
XLA Modules:
  0.0 729.0 jit_solution(13160724611083791855)
XLA Ops:
  8.1 17.6 %all_gather.18 = f32[1024,128]{1,0:T(8,128)S(1)} all-gather(f32[256,128]{1,0:T(8,128)} %param.11), channel_id=1, replica_groups=mesh['grp'=2,'row'=4,'col'=4] {'row'}, dimensions={0}, use_global_device_ids=true | all-gather | bytes 655360 | tf_op jit(solution)/shard_map/all_gather | solution.py:75
  25.7 1.8 gather_fusion
  27.5 5.2 fusion.39
  32.7 1.6 reduce_sum.137
  40.6 29.2 %all-reduce.10.cloned.1.call-done = f32[768,128]{1,0:T(8,128)} async-done(((f32[768,128]{1,0:T(8,128)}), f32[768,128]{1,0:T(8,128)}) %all-reduce.10.cloned.1.call-update) | async-done | bytes 393232 | tf_op jit(solution)/shard_map/psum | solution.py:60
  72.3 1.6 copy.93
  73.9 2.1 fusion.19
  81.7 11.7 %all-reduce = f32[1024]{0:T(1024)S(1)} all-reduce(f32[1024]{0:T(1024)S(1)} %fusion.1), channel_id=3, replica_groups=mesh['grp'=2,'row'=4,'col'=4] {'row'}, use_global_device_ids=true, to_apply=%region_4.5.clone | all-reduce | flops 1024 | bytes 8192
  93.4 5.8 reduce-scatter.7.cloned.1.call-done
  100.3 16.0 %all_gather.19 = f32[1024,128]{1,0:T(8,128)S(1)} all-gather(f32[256,128]{1,0:T(8,128)S(1)} %get-tuple-element.18), channel_id=1, replica_groups=mesh['grp'=2,'row'=4,'col'=4] {'row'}, dimensions={0}, use_global_device_ids=true | all-gather | bytes 655360 | tf_op jit(solution)/shard_map/all_gather | solution.py:75
  117.7 1.9 gather_fusion.4
  119.7 4.1 fusion.41
  124.6 1.9 copy.98
  126.6 1.5 convolution_bitcast_fusion.4
  129.0 28.9 %all-reduce.12.cloned.1.call-done = f32[768,128]{1,0:T(8,128)} async-done(((f32[768,128]{1,0:T(8,128)}), f32[768,128]{1,0:T(8,128)}) %all-reduce.12.cloned.1.call-update) | async-done | bytes 393232 | tf_op jit(solution)/shard_map/psum | solution.py:60
  158.9 1.5 fusion.42
  160.4 1.6 copy.100
  162.0 2.1 fusion.17
  165.6 21.8 %reduce-scatter.9.cloned.1.call-done = f32[256,128]{1,0:T(8,128)} async-done(((f32[1024,128]{1,0:T(8,128)}), f32[256,128]{1,0:T(8,128)}) %reduce-scatter.9.cloned.1.call-update) | async-done | bytes 131088 | tf_op jit(solution)/shard_map/reduce_scatter | solution.py:78
  188.4 29.5 %all-reduce.2 = (f32[128]{0:T(128)S(1)}, f32[128]{0:T(128)S(1)}) all-reduce(f32[128]{0:T(128)S(1)} %get-tuple-element.6, f32[128]{0:T(128)S(1)} %get-tuple-element.5), channel_id=1, replica_groups=mesh['grp'=2,'row'=4,'col'=4] {'row','col'}, use_global_device_ids=true, to_apply=%region_6.7 | all-reduce | flops 256 | bytes 2048 | tf_op jit(solution)/shard_map/psum | solution.py:81
  219.0 29.5 %psum.102 = f32[128]{0:T(128)S(1)} all-reduce(f32[128]{0:T(128)S(1)} %multiply_reduce_fusion.6), channel_id=1, replica_groups=mesh['grp'=2,'row'=4,'col'=4] {'row','col'}, use_global_device_ids=true, to_apply=%region_13.14 | all-reduce | flops 128 | bytes 1024 | tf_op jit(solution)/shard_map/psum | solution.py:81
  250.1 16.3 %all_gather.20 = f32[1024,128]{1,0:T(8,128)S(1)} all-gather(f32[256,128]{1,0:T(8,128)S(1)} %multiply_add_fusion.8), channel_id=1, replica_groups=mesh['grp'=2,'row'=4,'col'=4] {'row'}, dimensions={0}, use_global_device_ids=true | all-gather | bytes 655360 | tf_op jit(solution)/shard_map/all_gather | solution.py:75
  267.7 1.9 gather_fusion.6
  269.7 4.1 fusion.43
  274.6 1.9 copy.105
  276.7 1.5 convolution_bitcast_fusion.3
  279.1 27.6 %all-reduce.14.cloned.1.call-done = f32[768,128]{1,0:T(8,128)} async-done(((f32[768,128]{1,0:T(8,128)}), f32[768,128]{1,0:T(8,128)}) %all-reduce.14.cloned.1.call-update) | async-done | bytes 393232 | tf_op jit(solution)/shard_map/psum | solution.py:60
  307.8 1.5 fusion.44
  309.3 1.6 copy.107
  311.0 2.1 fusion.15
  314.6 21.7 %reduce-scatter.11.cloned.1.call-done = f32[256,128]{1,0:T(8,128)} async-done(((f32[1024,128]{1,0:T(8,128)}), f32[256,128]{1,0:T(8,128)}) %reduce-scatter.11.cloned.1.call-update) | async-done | bytes 131088 | tf_op jit(solution)/shard_map/reduce_scatter | solution.py:78
  337.3 29.5 %psum.104 = f32[128]{0:T(128)S(1)} all-reduce(f32[128]{0:T(128)S(1)} %multiply_reduce_fusion.5), channel_id=1, replica_groups=mesh['grp'=2,'row'=4,'col'=4] {'row','col'}, use_global_device_ids=true, to_apply=%region_18.19 | all-reduce | flops 128 | bytes 1024 | tf_op jit(solution)/shard_map/psum | solution.py:81
  367.6 16.3 %all_gather.21 = f32[1024,128]{1,0:T(8,128)S(1)} all-gather(f32[256,128]{1,0:T(8,128)S(1)} %multiply_add_fusion.7), channel_id=1, replica_groups=mesh['grp'=2,'row'=4,'col'=4] {'row'}, dimensions={0}, use_global_device_ids=true | all-gather | bytes 655360 | tf_op jit(solution)/shard_map/all_gather | solution.py:75
  385.3 1.9 gather_fusion.8
  387.2 4.1 fusion.45
  392.1 2.0 copy.112
  394.2 2.3 convolution_bitcast_fusion.2
  396.5 1.8 copy.116
  398.3 25.7 %all-reduce.16.cloned.1.call-done = f32[768,128]{1,0:T(8,128)} async-done(((f32[768,128]{1,0:T(8,128)}), f32[768,128]{1,0:T(8,128)}) %all-reduce.16.cloned.1.call-update) | async-done | bytes 393232 | tf_op jit(solution)/shard_map/psum | solution.py:60
  424.0 2.5 subtract_subtract_fusion
  426.5 1.6 fusion.46
  428.1 1.6 copy.114
  429.7 2.1 fusion.13
  433.5 21.5 %reduce-scatter.13.cloned.1.call-done = f32[256,128]{1,0:T(8,128)} async-done(((f32[1024,128]{1,0:T(8,128)}), f32[256,128]{1,0:T(8,128)}) %reduce-scatter.13.cloned.1.call-update) | async-done | bytes 131088 | tf_op jit(solution)/shard_map/reduce_scatter | solution.py:78
  456.1 15.9 %all_gather.22 = f32[1024,128]{1,0:T(8,128)S(1)} all-gather(f32[256,128]{1,0:T(8,128)S(1)} %get-tuple-element.13), channel_id=1, replica_groups=mesh['grp'=2,'row'=4,'col'=4] {'row'}, dimensions={0}, use_global_device_ids=true | all-gather | bytes 655360 | tf_op jit(solution)/shard_map/all_gather | solution.py:75
  473.4 1.9 gather_fusion.10
  475.3 4.1 fusion.47
  480.3 1.9 copy.119
  482.2 1.5 convolution_bitcast_fusion.1
  484.6 28.6 %all-reduce.18.cloned.1.call-done = f32[768,128]{1,0:T(8,128)} async-done(((f32[768,128]{1,0:T(8,128)}), f32[768,128]{1,0:T(8,128)}) %all-reduce.18.cloned.1.call-update) | async-done | bytes 393232 | tf_op jit(solution)/shard_map/psum | solution.py:60
  515.8 1.6 copy.121
  517.5 2.1 fusion.11
  521.0 21.7 %reduce-scatter.15.cloned.1.call-done = f32[256,128]{1,0:T(8,128)} async-done(((f32[1024,128]{1,0:T(8,128)}), f32[256,128]{1,0:T(8,128)}) %reduce-scatter.15.cloned.1.call-update) | async-done | bytes 131088 | tf_op jit(solution)/shard_map/reduce_scatter | solution.py:78
  543.8 29.5 %all-reduce.1 = (f32[128]{0:T(128)S(1)}, f32[128]{0:T(128)S(1)}) all-reduce(f32[128]{0:T(128)S(1)} %get-tuple-element.4, f32[128]{0:T(128)S(1)} %get-tuple-element.3), channel_id=1, replica_groups=mesh['grp'=2,'row'=4,'col'=4] {'row','col'}, use_global_device_ids=true, to_apply=%region_23.24 | all-reduce | flops 256 | bytes 2048 | tf_op jit(solution)/shard_map/psum | solution.py:81
  574.4 29.5 %psum.109 = f32[128]{0:T(128)S(1)} all-reduce(f32[128]{0:T(128)S(1)} %multiply_reduce_fusion.2), channel_id=1, replica_groups=mesh['grp'=2,'row'=4,'col'=4] {'row','col'}, use_global_device_ids=true, to_apply=%region_30.31 | all-reduce | flops 128 | bytes 1024 | tf_op jit(solution)/shard_map/psum | solution.py:81
  605.5 16.3 %all_gather.23 = f32[1024,128]{1,0:T(8,128)S(1)} all-gather(f32[256,128]{1,0:T(8,128)S(1)} %multiply_add_fusion.5), channel_id=1, replica_groups=mesh['grp'=2,'row'=4,'col'=4] {'row'}, dimensions={0}, use_global_device_ids=true | all-gather | bytes 655360 | tf_op jit(solution)/shard_map/all_gather | solution.py:75
  623.2 1.9 gather_fusion.12
  625.1 4.1 fusion.49
  630.0 1.9 copy.126
  632.2 1.5 convolution_bitcast_fusion
  633.9 28.2 %all-reduce.20.cloned.1.call-done = f32[768,128]{1,0:T(8,128)} async-done(((f32[768,128]{1,0:T(8,128)}), f32[768,128]{1,0:T(8,128)}) %all-reduce.20.cloned.1.call-update) | async-done | bytes 393232 | tf_op jit(solution)/shard_map/psum | solution.py:60
  663.1 1.5 fusion.50
  667.4 21.8 %reduce-scatter.17.cloned.1.call-done = f32[256,128]{1,0:T(8,128)} async-done(((f32[1024,128]{1,0:T(8,128)}), f32[256,128]{1,0:T(8,128)}) %reduce-scatter.17.cloned.1.call-update) | async-done | bytes 131088 | tf_op jit(solution)/shard_map/reduce_scatter | solution.py:78
  690.2 29.6 %psum.111 = f32[128]{0:T(128)S(1)} all-reduce(f32[128]{0:T(128)S(1)} %multiply_reduce_fusion.1), channel_id=1, replica_groups=mesh['grp'=2,'row'=4,'col'=4] {'row','col'}, use_global_device_ids=true, to_apply=%region_35.36 | all-reduce | flops 128 | bytes 1024 | tf_op jit(solution)/shard_map/psum | solution.py:81
  (197 shorter events, 57.7 us)
Async XLA Ops:
  7.2 62.6 %all-reduce.10.cloned.1.call-start = ((), (), s32[]{:S(2)}) async-start(), calls=%async_computation.6 | async-start | bytes 786432 | tf_op jit(solution)/shard_map/psum | solution.py:60
  8.1 19.4 %copy-start.32 = (s32[1024]{0:T(1024)}, s32[1024]{0:T(1024)S(1)}, u32[]{:S(2)}) copy-start(s32[1024]{0:T(1024)S(1)} %pad_clamp_fusion.1) | copy-start | bytes 12292
  25.7 1.8 copy-start
  32.7 2.7 copy-start.40
  32.7 5.1 copy-start.1
  34.3 35.5 %copy-start.9 = (f32[768,128]{1,0:T(8,128)S(1)}, f32[768,128]{1,0:T(8,128)}, u32[]{:S(2)}) copy-start(f32[768,128]{1,0:T(8,128)} %param.15) | copy-start | bytes 1179652
  34.3 35.5 %copy-start.11 = (f32[768,128]{1,0:T(8,128)S(1)}, f32[768,128]{1,0:T(8,128)}, u32[]{:S(2)}) copy-start(f32[768,128]{1,0:T(8,128)} %param.14) | copy-start | bytes 1179652
  35.2 64.1 %reduce-scatter.7.cloned.1.call-start = ((), (), s32[]{:S(2)}) async-start(), calls=%async_computation.7 | async-start | bytes 655360 | tf_op jit(solution)/shard_map/reduce_scatter | solution.py:78
  37.2 2.0 copy-start.31
  73.9 2.1 copy-start.25
  76.6 3.5 copy-start.43
  77.5 15.9 %copy-start.33 = (f32[256]{0:T(256)S(1)}, f32[256]{0:T(256)}, u32[]{:S(2)}) copy-start(f32[256]{0:T(256)} %param.13) | copy-start | bytes 3076
  77.5 21.8 %copy-start.22 = (f32[256,128]{1,0:T(8,128)S(1)}, f32[256,128]{1,0:T(8,128)}, u32[]{:S(2)}) copy-start(f32[256,128]{1,0:T(8,128)} %param.11) | copy-start | bytes 393220
  77.5 21.8 %copy-start.29 = (f32[256,128]{1,0:T(8,128)S(1)}, f32[256,128]{1,0:T(8,128)}, u32[]{:S(2)}) copy-start(f32[256,128]{1,0:T(8,128)} %param.12) | copy-start | bytes 393220
  77.5 80.3 %all-reduce.12.cloned.1.call-start = ((), (), s32[]{:S(2)}) async-start(), calls=%async_computation.8 | async-start | bytes 786432 | tf_op jit(solution)/shard_map/psum | solution.py:60
  126.5 60.8 %reduce-scatter.9.cloned.1.call-start = ((), (), s32[]{:S(2)}) async-start(), calls=%async_computation.9 | async-start | bytes 655360 | tf_op jit(solution)/shard_map/reduce_scatter | solution.py:78
  162.0 2.1 copy-start.26
  165.5 141.2 %all-reduce.14.cloned.1.call-start = ((), (), s32[]{:S(2)}) async-start(), calls=%async_computation.10 | async-start | bytes 786432 | tf_op jit(solution)/shard_map/psum | solution.py:60
  217.9 30.6 %copy-start.35 = (f32[128]{0:T(128)}, f32[128]{0:T(128)S(1)}, u32[]{:S(2)}) copy-start(f32[128]{0:T(128)S(1)} %div.52) | copy-start | bytes 1540
  248.5 0.5 copy-start.46
  250.1 17.7 %copy-start.4 = (f32[256,128]{1,0:T(8,128)}, f32[256,128]{1,0:T(8,128)S(1)}, u32[]{:S(2)}) copy-start(f32[256,128]{1,0:T(8,128)S(1)} %multiply_add_fusion.8) | copy-start | bytes 393220
  276.5 59.8 %reduce-scatter.11.cloned.1.call-start = ((), (), s32[]{:S(2)}) async-start(), calls=%async_computation.11 | async-start | bytes 655360 | tf_op jit(solution)/shard_map/reduce_scatter | solution.py:78
  311.0 2.1 copy-start.27
  313.1 23.3 %copy-start.5 = (f32[256,128]{1,0:T(8,128)S(1)}, f32[256,128]{1,0:T(8,128)}, u32[]{:S(2)}) copy-start(f32[256,128]{1,0:T(8,128)} %copy-done.4) | copy-start | bytes 393220
  313.1 53.8 %copy-start.47 = (f32[128]{0:T(128)S(1)}, f32[128]{0:T(128)}, u32[]{:S(2)}) copy-start(f32[128]{0:T(128)} %copy-done.46) | copy-start | bytes 1540
  313.1 54.4 %copy-start.23 = (f32[256,128]{1,0:T(8,128)S(1)}, f32[256,128]{1,0:T(8,128)}, u32[]{:S(2)}) copy-start(f32[256,128]{1,0:T(8,128)} %param.11) | copy-start | bytes 393220
  313.1 54.4 %copy-start.36 = (f32[128]{0:T(128)S(1)}, f32[128]{0:T(128)}, u32[]{:S(2)}) copy-start(f32[128]{0:T(128)} %copy-done.35) | copy-start | bytes 1540
  314.5 109.5 %all-reduce.16.cloned.1.call-start = ((), (), s32[]{:S(2)}) async-start(), calls=%async_computation.12 | async-start | bytes 786432 | tf_op jit(solution)/shard_map/psum | solution.py:60
  366.9 0.6 copy-start.41
  367.6 17.7 %copy-start.6 = (f32[256,128]{1,0:T(8,128)}, f32[256,128]{1,0:T(8,128)S(1)}, u32[]{:S(2)}) copy-start(f32[256,128]{1,0:T(8,128)S(1)} %multiply_add_fusion.7) | copy-start | bytes 393220
  392.1 31.9 %copy-start.10 = (f32[768,128]{1,0:T(8,128)S(1)}, f32[768,128]{1,0:T(8,128)}, u32[]{:S(2)}) copy-start(f32[768,128]{1,0:T(8,128)} %param.15) | copy-start | bytes 1179652
  392.1 31.9 %copy-start.12 = (f32[768,128]{1,0:T(8,128)S(1)}, f32[768,128]{1,0:T(8,128)}, u32[]{:S(2)}) copy-start(f32[768,128]{1,0:T(8,128)} %param.14) | copy-start | bytes 1179652
  392.1 31.9 %copy-start.13 = (f32[768,128]{1,0:T(8,128)S(1)}, f32[768,128]{1,0:T(8,128)}, u32[]{:S(2)}) copy-start(f32[768,128]{1,0:T(8,128)} %all-reduce.10.cloned.1.call-done) | copy-start | bytes 1179652
  392.1 31.9 %copy-start.14 = (f32[768,128]{1,0:T(8,128)S(1)}, f32[768,128]{1,0:T(8,128)}, u32[]{:S(2)}) copy-start(f32[768,128]{1,0:T(8,128)} %all-reduce.12.cloned.1.call-done) | copy-start | bytes 1179652
  392.1 31.9 %copy-start.37 = (f32[128]{0:T(128)S(1)}, f32[128]{0:T(128)}, u32[]{:S(2)}) copy-start(f32[128]{0:T(128)} %copy-done.35) | copy-start | bytes 1540
  392.1 31.9 %copy-start.42 = (f32[128]{0:T(128)S(1)}, f32[128]{0:T(128)}, u32[]{:S(2)}) copy-start(f32[128]{0:T(128)} %copy-done.41) | copy-start | bytes 1540
  394.2 60.9 %reduce-scatter.13.cloned.1.call-start = ((), (), s32[]{:S(2)}) async-start(), calls=%async_computation.13 | async-start | bytes 655360 | tf_op jit(solution)/shard_map/reduce_scatter | solution.py:78
  429.7 2.1 copy-start.24
  431.8 23.3 %copy-start.7 = (f32[256,128]{1,0:T(8,128)S(1)}, f32[256,128]{1,0:T(8,128)}, u32[]{:S(2)}) copy-start(f32[256,128]{1,0:T(8,128)} %copy-done.6) | copy-start | bytes 393220
  431.8 23.3 %copy-start.30 = (f32[256,128]{1,0:T(8,128)S(1)}, f32[256,128]{1,0:T(8,128)}, u32[]{:S(2)}) copy-start(f32[256,128]{1,0:T(8,128)} %param.12) | copy-start | bytes 393220
  431.8 23.2 %copy-start.34 = (f32[256]{0:T(256)S(1)}, f32[256]{0:T(256)}, u32[]{:S(2)}) copy-start(f32[256]{0:T(256)} %param.13) | copy-start | bytes 3076
  433.3 80.0 %all-reduce.18.cloned.1.call-start = ((), (), s32[]{:S(2)}) async-start(), calls=%async_computation.14 | async-start | bytes 786432 | tf_op jit(solution)/shard_map/psum | solution.py:60
  482.2 60.6 %reduce-scatter.15.cloned.1.call-start = ((), (), s32[]{:S(2)}) async-start(), calls=%async_computation.15 | async-start | bytes 655360 | tf_op jit(solution)/shard_map/reduce_scatter | solution.py:78
  517.5 2.1 copy-start.28
  521.0 141.1 %all-reduce.20.cloned.1.call-start = ((), (), s32[]{:S(2)}) async-start(), calls=%async_computation.16 | async-start | bytes 786432 | tf_op jit(solution)/shard_map/psum | solution.py:60
  573.4 30.6 %copy-start.38 = (f32[128]{0:T(128)}, f32[128]{0:T(128)S(1)}, u32[]{:S(2)}) copy-start(f32[128]{0:T(128)S(1)} %div.58) | copy-start | bytes 1540
  603.9 0.5 copy-start.44
  605.5 17.7 %copy-start.2 = (f32[256,128]{1,0:T(8,128)}, f32[256,128]{1,0:T(8,128)S(1)}, u32[]{:S(2)}) copy-start(f32[256,128]{1,0:T(8,128)S(1)} %multiply_add_fusion.5) | copy-start | bytes 393220
  631.9 57.2 %reduce-scatter.17.cloned.1.call-start = ((), (), s32[]{:S(2)}) async-start(), calls=%async_computation.17 | async-start | bytes 655360 | tf_op jit(solution)/shard_map/reduce_scatter | solution.py:78
  665.8 23.4 %copy-start.3 = (f32[256,128]{1,0:T(8,128)S(1)}, f32[256,128]{1,0:T(8,128)}, u32[]{:S(2)}) copy-start(f32[256,128]{1,0:T(8,128)} %copy-done.2) | copy-start | bytes 393220
  665.8 53.9 %copy-start.45 = (f32[128]{0:T(128)S(1)}, f32[128]{0:T(128)}, u32[]{:S(2)}) copy-start(f32[128]{0:T(128)} %copy-done.44) | copy-start | bytes 1540
  665.9 53.9 %copy-start.8 = (f32[256,128]{1,0:T(8,128)S(1)}, f32[256,128]{1,0:T(8,128)}, u32[]{:S(2)}) copy-start(f32[256,128]{1,0:T(8,128)} %copy-done.6) | copy-start | bytes 393220
  665.9 53.9 %copy-start.39 = (f32[128]{0:T(128)S(1)}, f32[128]{0:T(128)}, u32[]{:S(2)}) copy-start(f32[128]{0:T(128)} %copy-done.38) | copy-start | bytes 1540
  665.9 54.7 %copy-start.15 = (f32[768,128]{1,0:T(8,128)S(1)}, f32[768,128]{1,0:T(8,128)}, u32[]{:S(2)}) copy-start(f32[768,128]{1,0:T(8,128)} %param.17) | copy-start | bytes 1179652
  665.9 54.7 %copy-start.16 = (f32[768,128]{1,0:T(8,128)S(1)}, f32[768,128]{1,0:T(8,128)}, u32[]{:S(2)}) copy-start(f32[768,128]{1,0:T(8,128)} %param.16) | copy-start | bytes 1179652
  665.9 54.7 %copy-start.17 = (f32[768,128]{1,0:T(8,128)S(1)}, f32[768,128]{1,0:T(8,128)}, u32[]{:S(2)}) copy-start(f32[768,128]{1,0:T(8,128)} %all-reduce.16.cloned.1.call-done) | copy-start | bytes 1179652
  665.9 54.7 %copy-start.18 = (f32[768,128]{1,0:T(8,128)S(1)}, f32[768,128]{1,0:T(8,128)}, u32[]{:S(2)}) copy-start(f32[768,128]{1,0:T(8,128)} %get-tuple-element.16) | copy-start | bytes 1179652
  665.9 54.6 %copy-start.19 = (f32[768,128]{1,0:T(8,128)S(1)}, f32[768,128]{1,0:T(8,128)}, u32[]{:S(2)}) copy-start(f32[768,128]{1,0:T(8,128)} %get-tuple-element.17) | copy-start | bytes 1179652
  665.9 54.6 %copy-start.20 = (f32[768,128]{1,0:T(8,128)S(1)}, f32[768,128]{1,0:T(8,128)}, u32[]{:S(2)}) copy-start(f32[768,128]{1,0:T(8,128)} %all-reduce.18.cloned.1.call-done) | copy-start | bytes 1179652
  665.9 54.6 %copy-start.21 = (f32[768,128]{1,0:T(8,128)S(1)}, f32[768,128]{1,0:T(8,128)}, u32[]{:S(2)}) copy-start(f32[768,128]{1,0:T(8,128)} %all-reduce.20.cloned.1.call-done) | copy-start | bytes 1179652
Sparse Core Ops, SparseCore 0:
  35.3 34.3 all-reduce.9
  77.6 21.6 reduce-scatter.6
  126.6 31.1 all-reduce.11
  165.7 21.6 reduce-scatter.8
  276.6 30.0 all-reduce.13
  314.6 21.6 reduce-scatter.10
  394.3 29.6 all-reduce.15
  433.4 21.6 reduce-scatter.12
  482.3 30.9 all-reduce.17
  521.1 21.6 reduce-scatter.14
  632.1 29.9 all-reduce.19
  667.5 21.6 reduce-scatter.16
where the time goes:
time: 737 us; the launch traced here: 729 us
  blocking collectives  287 us (39%)
  waiting for transfers between devices  283 us (38%)
  matrix products  57.9 us (8%)
  local copies, waits for them, and re-layouts  55.2 us (7%)
  other arithmetic  28.7 us (4%)
  between operations  16 us (2%)
    psum x6, blocking collectives, column_sums(): return lax.psum((pieces[0],), ('row', 'col'))  177 us
    psum x6, waiting for transfers between devices, products(): slab_sum = lax.psum(slab_part.reshape(slab_blocks * block, qp_count), 'col')  168 us
    reduce_scatter x6, waiting for transfers between devices, settle_rows(): return lax.psum_scatter(var_term, 'row', scatter_dimension=0, tiled=True)  114 us
    all_gather x6, blocking collectives, reach_range(): return lax.all_gather(vector, 'row', axis=0, tiled=True)  98.3 us
    dot_general x6, matrix products, products(): slab_part = jnp.einsum('kij,kjq->kiq', a_flat, picked, precision=highest)  25.5 us
  transfers between devices with their start and end apart: 12, of which 12 were waited for; matrix products, arithmetic and copies ran while one was open for 3% of the time, Pallas kernels for 0%

commit v1 on v0

v1 whole, which is shorter than its diff:
```python
import functools

import jax
import jax.numpy as jnp
from jax import lax
from jax.experimental import pallas as pl
from jax.experimental.pallas import tpu as pltpu
from jax.sharding import PartitionSpec as P

ADMM_ITERS = 2
RHO = 0.5
SIGMA = 1e-06
RELAX = 1.6
BLK = 128
LANES = 128
HALF = 64
SC = 8
F32 = jnp.float32
BF16 = jnp.bfloat16

VMEM = pl.BlockSpec(memory_space=pltpu.VMEM)
SMEM = pl.BlockSpec(memory_space=pltpu.SMEM)


def call(body, outs, ins, smem=(), scratch=(), flops=0):
    n_bytes = sum(v.size * v.dtype.itemsize for v in ins)
    return pl.pallas_call(
        body,
        out_shape=[jax.ShapeDtypeStruct(s, d) for s, d in outs],
        in_specs=[SMEM] * len(smem) + [VMEM] * len(ins),
        out_specs=[VMEM] * len(outs),
        scratch_shapes=list(scratch),
        compiler_params=pltpu.CompilerParams(vmem_limit_bytes=30 * 1024 * 1024),
        cost_estimate=pl.CostEstimate(flops=flops, bytes_accessed=n_bytes, transcendentals=0),
    )(*smem, *ins)


def low_half(shape):
    return lax.broadcasted_iota(jnp.int32, shape, 1) < HALF


def turn(v):
    return pltpu.roll(v, HALF, 1)


def fold(v):
    return v + turn(v)


def col_sum(v):
    return fold(jnp.sum(v, axis=0, keepdims=True))


def split_bf16(v):
    hi = v.astype(BF16).astype(F32)
    return hi, v - hi


def pair_up(v):
    hi, lo = split_bf16(v)
    low = low_half(v.shape)
    first = jnp.where(low, hi, turn(lo)).astype(BF16)
    second = jnp.where(low, turn(hi), lo).astype(BF16)
    return first, second


def dot(a, b):
    return jnp.dot(a, b, preferred_element_type=F32)


def pack_rows(*rows):
    at = lax.broadcasted_iota(jnp.int32, (SC, LANES), 0)
    tile = jnp.zeros((SC, LANES), F32)
    for k, row in enumerate(rows):
        tile = jnp.where(at == k, row, tile)
    return tile


def send_kernel(place, x, q, msg):
    core = place[1]
    low = low_half(x.shape)
    xv = jnp.where(core == 0, turn(x[...]), x[...])
    qv = jnp.where(core == 0, q[...], turn(q[...]))
    msg[...] = jnp.where(low, xv, qv)


def recv_kernel(place, x, q, got, x_own, q_own):
    core = place[1]
    low = low_half(x.shape)
    xv = jnp.where(core == 0, x[...], turn(x[...]))
    qv = jnp.where(core == 0, q[...], turn(q[...]))
    x_own[...] = jnp.where(low, xv, turn(got[...]))
    q_own[...] = jnp.where(low, qv, got[...])


def slab_kernel(place, *refs):
    core = place[1]
    count = len(refs) // 2
    for src, dst in zip(refs[:count], refs[count:]):
        rows = dst.shape[0]
        v = jnp.where(core == 0, src[...], turn(src[...]))
        dst[...] = jnp.where(low_half(dst.shape), v[:rows], turn(v[rows:]))


def prep_kernel(slab, per, cols, pairs, a_mine, a_other, p_mine, p_other, a_hi, a_lo, t_hi, t_lo, p_hi, p_lo, diag):
    span = a_hi.shape[1] // 2
    n_range = span // BLK
    for ref in (a_hi, a_lo, t_hi, t_lo):
        ref[...] = jnp.zeros(ref.shape, BF16)
    diag[...] = jnp.zeros(diag.shape, F32)
    for t, src in enumerate((a_mine, a_other)):
        for m in range(slab):
            rows = slice(m * BLK, (m + 1) * BLK)
            for s in range(per):
                k = m * per + s
                col = cols[t * slab * per + k]
                at = pl.multiple_of(t * span + col * BLK, BLK)
                block = src[k]
                hi, lo = split_bf16(block)
                a_hi[rows, pl.ds(at, BLK)] = hi.astype(BF16)
                a_lo[rows, pl.ds(at, BLK)] = lo.astype(BF16)
                hi, lo = split_bf16(block.T)
                t_hi[pl.ds(at, BLK), rows] = hi.astype(BF16)
                t_lo[pl.ds(at, BLK), rows] = lo.astype(BF16)
                here = pl.ds(t * n_range + col, 1)
                diag[here, :] += RHO * jnp.sum(block * block, axis=0, keepdims=True)
    shape = (BLK, BLK)
    eye = lax.broadcasted_iota(jnp.int32, shape, 0) == lax.broadcasted_iota(jnp.int32, shape, 1)
    for t, src in enumerate((p_mine, p_other)):
        for e in range(4):
            hi, lo = split_bf16(src[e])
            rows = slice((e // 2) * BLK, (e // 2 + 1) * BLK)
            lanes = slice((e % 2) * BLK, (e % 2 + 1) * BLK)
            p_hi[t, rows, lanes] = hi.astype(BF16)
            p_lo[t, rows, lanes] = lo.astype(BF16)
        for e in range(2):
            here = pl.ds(t * n_range + pairs[2 * t + e], 1)
            diag[here, :] += jnp.sum(jnp.where(eye, src[3 * e], 0.0), axis=0, keepdims=True)


def forward_kernel(n, own, scalars, place, pairs, *refs):
    msgs, rest = refs[:n], refs[n:]
    a_hi, a_lo, p_hi, p_lo = rest[:4]
    rest = rest[4:]
    if scalars == 2:
        pp_first, rest = rest[0], rest[1:]
    msg, pp, whole, wide = rest
    row = place[0]
    span = whole.shape[0]
    for k in range(n):
        at = lax.rem(row + n - k, n) * own
        at = pl.multiple_of(at, own)
        v = msgs[k][0:own, :]
        whole[pl.ds(at, own), :] = v
        first, second = pair_up(v)
        wide[pl.ds(at, own), :] = first
        wide[pl.ds(pl.multiple_of(span + at, own), own), :] = second
    x = wide[...]
    total = fold(dot(a_hi[...], x) + dot(a_lo[...], x))
    rows = total.shape[0] // 2
    msg[0:rows, :] = jnp.where(low_half((rows, LANES)), total[:rows], total[rows:])
    parts = []
    for t in range(2):
        at_i = pl.multiple_of(t * span + pairs[2 * t] * BLK, BLK)
        at_j = pl.multiple_of(t * span + pairs[2 * t + 1] * BLK, BLK)
        v = jnp.concatenate([wide[pl.ds(at_i, BLK), :], wide[pl.ds(at_j, BLK), :]], axis=0)
        parts.append(fold(dot(p_hi[t], v) + dot(p_lo[t], v)))
    low2 = low_half((2 * BLK, LANES))
    pp_now = jnp.where(low2, parts[0], parts[1])
    pp[...] = pp_now
    if scalars:
        picked = []
        for t in range(2):
            at_i = pl.multiple_of(pairs[2 * t] * BLK, BLK)
            at_j = pl.multiple_of(pairs[2 * t + 1] * BLK, BLK)
            picked.append(jnp.concatenate([whole[pl.ds(at_i, BLK), :], whole[pl.ds(at_j, BLK), :]], axis=0))
        vec = jnp.where(low2, picked[0], picked[1])
        tile = msgs[0][own : own + SC, :]
        for k in range(1, n):
            tile = tile + msgs[k][own : own + SC, :]
        tile = fold(tile)
        at = lax.broadcasted_iota(jnp.int32, (SC, LANES), 0)
        tile = jnp.where(at == 3, col_sum(vec * pp_now), tile)
        if scalars == 2:
            tile = jnp.where(at == 4, col_sum(vec * pp_first[...]), tile)
        msg[rows : rows + SC, :] = tile


def back_product(n, own, place, pairs, w, pp_now, t_hi, t_lo, total, outs, extra):
    row = place[0]
    span = total.shape[0]
    first, second = pair_up(w)
    wide = jnp.concatenate([first, second], axis=0)
    part = fold(dot(t_hi[...], wide) + dot(t_lo[...], wide))
    low = low_half((span, LANES))
    total[...] = jnp.where(low, part[:span], part[span:])
    low1 = low_half((BLK, LANES))
    for t in range(2):
        side = low1 if t == 0 else jnp.logical_not(low1)
        for e in range(2):
            at = pl.ds(pl.multiple_of(pairs[2 * t + e] * BLK, BLK), BLK)
            total[at, :] += jnp.where(side, pp_now[e * BLK : (e + 1) * BLK], 0.0)
    for k in range(n):
        at = pl.multiple_of(lax.rem(row + k, n) * own, own)
        outs[k][0:own, :] = total[pl.ds(at, own), :]
        if extra is not None:
            outs[k][own : own + extra.shape[0], :] = extra


def start_back_kernel(n, nx, own, place, pairs, *refs):
    msgs, rest = refs[:nx], refs[nx:]
    z, y, pp, diag, t_hi, t_lo = rest[:6]
    outs, (ax, total) = rest[6 : 6 + n], rest[6 + n :]
    ax_now = msgs[0][...]
    for k in range(1, nx):
        ax_now = ax_now + msgs[k][...]
    ax[...] = ax_now
    w = RHO * ax_now - (RHO * z[...] - y[...])
    back_product(n, own, place, pairs, w, pp[...], t_hi, t_lo, total, outs, diag[...])


def step_back_kernel(n, nx, own, place, pairs, *refs):
    msgs, rest = refs[:nx], refs[nx:]
    pp, t_hi, t_lo = rest[:3]
    outs, (ad, scal, total) = rest[3 : 3 + n], rest[3 + n :]
    rows = ad.shape[0]
    v = msgs[0][...]
    for k in range(1, nx):
        v = v + msgs[k][...]
    ad_now = v[:rows]
    tile = v[rows:]
    ad[...] = ad_now
    scal[...] = tile
    curve = RHO * col_sum(ad_now * ad_now) + tile[3:4]
    back_product(
        n, own, place, pairs, RHO * ad_now, pp[...], t_hi, t_lo, total, outs, pack_rows(curve)
    )


def residual_kernel(n, own, first, place, *refs):
    msgs, rest = refs[:n], refs[n:]
    if first:
        x, q, pd, msg, res, dk, full = rest
        rows = msgs[0].shape[0] - own
        tile = msgs[0][own:, :]
        for k in range(1, n):
            tile = tile + msgs[k][own:, :]
        n_range = rows // 2
        low1 = low_half((BLK, LANES))
        for b in range(n_range):
            mine = jnp.broadcast_to(tile[b : b + 1], (BLK, LANES)).T
            other = jnp.broadcast_to(tile[n_range + b : n_range + b + 1], (BLK, LANES)).T
            full[b * BLK : (b + 1) * BLK, :] = jnp.where(low1, mine, other)
        at = pl.multiple_of(place[0] * own, own)
        diag = pd[...] + SIGMA + full[pl.ds(at, own), :]
        dk[...] = diag
    else:
        x, q, pd, dk, msg, res = rest
        diag = dk[...]
    total = msgs[0][0:own, :]
    for k in range(1, n):
        total = total + msgs[k][0:own, :]
    r = -q[...] - pd[...] * x[...] - total
    s = r / diag
    res[...] = r
    msg[0:own, :] = s
    shift = pd[...] + SIGMA
    rz = jnp.sum(r * s, axis=0, keepdims=True)
    dd = jnp.sum(shift * s * s, axis=0, keepdims=True)
    msg[own : own + SC, :] = pack_rows(rz, dd)


def step_kernel(n, own, *refs):
    msgs, rest = refs[:n], refs[n:]
    scal, prev, r, pd, dk, msg, step_out = rest
    total = msgs[0][...]
    for k in range(1, n):
        total = total + msgs[k][...]
    shift = pd[...] + SIGMA
    d = prev[0:own, :]
    kd = shift * d + total[:own]
    curve = total[own : own + 1] + scal[1:2, :]
    step = scal[0:1, :] / curve
    r_new = r[...] - step * kd
    s = r_new / dk[...]
    msg[0:own, :] = s
    rz = jnp.sum(r_new * s, axis=0, keepdims=True)
    ss = jnp.sum(shift * s * s, axis=0, keepdims=True)
    sd = jnp.sum(shift * s * d, axis=0, keepdims=True)
    msg[own : own + SC, :] = pack_rows(rz, ss, sd)
    step_out[...] = jnp.broadcast_to(step, step_out.shape)


def curve_kernel(nx, *refs):
    msgs, rest = refs[:nx], refs[nx:]
    scal, ad, ad2, share, keep = rest
    rows = ad.shape[0]
    v = msgs[0][...]
    for k in range(1, nx):
        v = v + msgs[k][...]
    tile = v[rows:]
    beta = tile[0:1] / scal[0:1, :]
    ad_now = v[:rows] + beta * ad[...]
    ad2[...] = ad_now
    flat = tile[1:2] + 2.0 * beta * tile[2:3] + beta * beta * scal[1:2, :]
    pair = tile[3:4] + 2.0 * beta * tile[4:5] + beta * beta * scal[3:4, :]
    share[...] = pack_rows(RHO * col_sum(ad_now * ad_now) + pair)
    keep[...] = pack_rows(tile[0:1], beta, flat)


def admm_update(n, own, refs):
    shares, rest = refs[:n], refs[n:]
    keep, step_in, ax, ad, ad2, z, y, lower, upper, x, msg1, msg2 = rest[:12]
    tile = shares[0][...]
    for k in range(1, n):
        tile = tile + shares[k][...]
    beta = keep[1:2, :]
    step1 = step_in[0:1, :]
    step2 = keep[0:1, :] / (tile[0:1] + keep[2:3, :])
    d1 = msg1[0:own, :]
    d2 = msg2[0:own, :] + beta * d1
    x_hat = x[...] + step1 * d1 + step2 * d2
    x_new = RELAX * x_hat + (1.0 - RELAX) * x[...]
    ax_hat = ax[...] + step1 * ad[...] + step2 * ad2[...]
    relaxed = RELAX * ax_hat + (1.0 - RELAX) * z[...]
    z_new = jnp.clip(relaxed + y[...] / RHO, lower[...], upper[...])
    y_new = y[...] + RHO * (relaxed - z_new)
    return beta, step1, step2, x_new, ax_hat, z_new, y_new, rest[12:]


def update_kernel(n, own, place, pairs, *refs):
    beta, step1, step2, x_new, ax_hat, z_new, y_new, rest = admm_update(n, own, refs)
    ax = refs[n + 2]
    ppx, pp1, pp2, t_hi, t_lo = rest[:5]
    outs, (x_out, z_out, y_out, ax_out, ppx_out, total) = rest[5 : 5 + n], rest[5 + n :]
    x_out[...] = x_new
    z_out[...] = z_new
    y_out[...] = y_new
    ax_new = RELAX * ax_hat + (1.0 - RELAX) * ax[...]
    ax_out[...] = ax_new
    pp_hat = ppx[...] + step1 * pp1[...] + step2 * (pp2[...] + beta * pp1[...])
    pp_new = RELAX * pp_hat + (1.0 - RELAX) * ppx[...]
    ppx_out[...] = pp_new
    w = RHO * ax_new - (RHO * z_new - y_new)
    back_product(n, own, place, pairs, w, pp_new, t_hi, t_lo, total, outs, None)


def last_kernel(n, own, *refs):
    _, _, _, x_new, _, z_new, y_new, rest = admm_update(n, own, refs)
    (out,) = rest
    rows = z_new.shape[0]
    out[0:rows, :] = z_new
    out[rows : 2 * rows, :] = y_new
    out[2 * rows :, :] = x_new


def finish_kernel(place, mine, got, x, z, y):
    core = place[1]
    rows = z.shape[0] // 2
    for k, dst in enumerate((z, y)):
        a = mine[k * rows : (k + 1) * rows, :]
        b = got[k * rows : (k + 1) * rows, :]
        low = low_half(a.shape)
        left = jnp.where(core == 0, a, b)
        right = jnp.where(core == 0, b, a)
        dst[0:rows, :] = jnp.where(low, left, turn(right))
        dst[rows : 2 * rows, :] = jnp.where(low, turn(left), right)
    a = mine[2 * rows :, :]
    b = got[2 * rows :, :]
    low = low_half(a.shape)
    x[...] = jnp.where(core == 0, jnp.where(low, a, b), jnp.where(low, turn(b), turn(a)))


def local(x_state, q_lin, p_diag, z_state, y_state, lower_bound, upper_bound, a_blocks, a_cols, p_blocks, p_pairs):
    slab, per = a_cols.shape
    n = lax.axis_size("row")
    n_col = lax.axis_size("col")
    nx = n_col // 2
    own = x_state.shape[0]
    span = own * n
    n_range = span // BLK
    slab_rows = slab * BLK
    half_rows = slab_rows // 2
    row_at = lax.axis_index("row")
    core_at = lax.axis_index("col") % 2
    place = jnp.stack([row_at, core_at]).astype(jnp.int32)

    def to_core(v):
        return lax.ppermute(v, "col", [(c, c ^ 1) for c in range(n_col)])

    def to_x(v):
        got = [lax.ppermute(v, "col", [(c, (c + 2 * k) % n_col) for c in range(n_col)]) for k in range(1, nx)]
        return [v] + got

    def to_row(pieces):
        got = [lax.ppermute(pieces[k], "row", [(i, (i + k) % n) for i in range(n)]) for k in range(1, n)]
        return [pieces[0]] + got

    a_mine = a_blocks.reshape(slab * per, BLK, BLK)
    p_mine = p_blocks.reshape(4, BLK, BLK)
    ints = jnp.concatenate([a_cols.reshape(-1), p_pairs.reshape(-1)])
    (send,) = call(send_kernel, [((own, LANES), F32)], [x_state, q_lin], [place])
    got_xq = to_core(send)
    a_other = to_core(a_mine)
    ints_other = to_core(ints)
    p_other = to_core(p_mine)
    pd_other = to_core(p_diag)
    count = slab * per
    cols = jnp.concatenate([ints[:count], ints_other[:count]])
    pairs = jnp.concatenate([ints[count:], ints_other[count:]])
    pd = jnp.concatenate(
        [jnp.broadcast_to(p_diag[:, None], (own, HALF)), jnp.broadcast_to(pd_other[:, None], (own, HALF))], axis=1
    )
    x, q = call(recv_kernel, [((own, LANES), F32)] * 2, [x_state, q_lin, got_xq], [place])
    x_parts = to_row([x] * n)
    z, y, lower, upper = call(
        slab_kernel, [((half_rows, LANES), F32)] * 4, [z_state, y_state, lower_bound, upper_bound], [place]
    )
    wide = 2 * span
    a_hi, a_lo, t_hi, t_lo, p_hi, p_lo, diag = call(
        functools.partial(prep_kernel, slab, per),
        [((slab_rows, wide), BF16)] * 2
        + [((wide, slab_rows), BF16)] * 2
        + [((2, 2 * BLK, 2 * BLK), BF16)] * 2
        + [((2 * n_range, LANES), F32)],
        [a_mine, a_other, p_mine, p_other],
        [cols, pairs],
        flops=10**8,
    )
    prod_flops = 4 * slab_rows * wide * LANES
    total_scratch = [pltpu.VMEM((span, LANES), F32)]

    def forward(msgs, scalars, pp_first=()):
        extra = SC if scalars else 0
        return call(
            functools.partial(forward_kernel, n, own, scalars),
            [((half_rows + extra, LANES), F32), ((2 * BLK, LANES), F32)],
            [*msgs, a_hi, a_lo, p_hi, p_lo, *pp_first],
            [place, pairs],
            total_scratch + [pltpu.VMEM((wide, LANES), BF16)],
            flops=prod_flops,
        )

    msg, ppx = forward(x_parts, 0)
    *pieces, ax = call(
        functools.partial(start_back_kernel, n, nx, own),
        [((own + 2 * n_range, LANES), F32)] * n + [((half_rows, LANES), F32)],
        [*to_x(msg), z, y, ppx, diag, t_hi, t_lo],
        [place, pairs],
        total_scratch,
        flops=prod_flops,
    )
    own_shape = ((own, LANES), F32)
    msg_shape = ((own + SC, LANES), F32)
    tile_shape = ((SC, LANES), F32)
    slab_shape = ((half_rows, LANES), F32)
    for outer in range(ADMM_ITERS):
        if outer == 0:
            msg1, r, dk = call(
                functools.partial(residual_kernel, n, own, True),
                [msg_shape, own_shape, own_shape],
                [*to_row(pieces), x, q, pd],
                [place],
                total_scratch,
            )
        else:
            msg1, r = call(
                functools.partial(residual_kernel, n, own, False),
                [msg_shape, own_shape],
                [*to_row(pieces), x, q, pd, dk],
                [place],
            )
        msg, pp1 = forward(to_row([msg1] * n), 1)
        *pieces, ad, scal = call(
            functools.partial(step_back_kernel, n, nx, own),
            [msg_shape] * n + [slab_shape, tile_shape],
            [*to_x(msg), pp1, t_hi, t_lo],
            [place, pairs],
            total_scratch,
            flops=prod_flops,
        )
        msg2, step = call(
            functools.partial(step_kernel, n, own),
            [msg_shape, tile_shape],
            [*to_row(pieces), scal, msg1, r, pd, dk],
        )
        msg, pp2 = forward(to_row([msg2] * n), 2, (pp1,))
        ad2, share, keep = call(
            functools.partial(curve_kernel, nx),
            [slab_shape, tile_shape, tile_shape],
            [*to_x(msg), scal, ad],
        )
        shares = to_row([share] * n)
        state = [*shares, keep, step, ax, ad, ad2, z, y, lower, upper, x, msg1, msg2]
        if outer + 1 < ADMM_ITERS:
            *pieces, x, z, y, ax, ppx = call(
                functools.partial(update_kernel, n, own),
                [own_shape] * n + [own_shape, slab_shape, slab_shape, slab_shape, ((2 * BLK, LANES), F32)],
                [*state, ppx, pp1, pp2, t_hi, t_lo],
                [place, pairs],
                total_scratch,
                flops=prod_flops,
            )
        else:
            (out,) = call(
                functools.partial(last_kernel, n, own), [((2 * half_rows + own, LANES), F32)], state
            )
    return call(
        finish_kernel,
        [own_shape, ((slab_rows, LANES), F32), ((slab_rows, LANES), F32)],
        [out, to_core(out)],
        [place],
    )


def solution(mesh):
    placed = (
        P(("col", "row"), "grp"),
        P(("col", "row"), "grp"),
        P(("col", "row")),
        P("row", "grp"),
        P("row", "grp"),
        P("row", "grp"),
        P("row", "grp"),
        P("row", "col", None, None),
        P("row", "col"),
        P("col", "row", None, None),
        P("col", "row", None),
    )

    def run(*args):
        return tuple(local(*args))

    return jax.shard_map(
        run,
        mesh=mesh,
        in_specs=placed,
        out_specs=(P(("col", "row"), "grp"), P("row", "grp"), P("row", "grp")),
        check_vma=False,
    )
```

time: 737 us -> 206 us (0.28)
  blocking collectives: 287 us -> 0 us
  waiting for transfers between devices: 283 us -> 103 us
  matrix products: 57.9 us -> 0 us
  starting transfers between devices: 1.14 us -> 57.3 us
  local copies, waits for them, and re-layouts: 55.2 us -> 7.09 us
  Pallas kernels: 0 us -> 35.8 us
  other arithmetic: 28.7 us -> 1.71 us
  between operations: 16 us -> 0.83 us
    psum x6 -> x0, blocking collectives: 177 us -> none  [column_sums(): return lax.psum((pieces[0],), ('row', 'col'))]
    psum x6 -> x0, waiting for transfers between devices: 168 us -> none  [products(): slab_sum = lax.psum(slab_part.reshape(slab_blocks * block, qp_count), 'col')]
    reduce_scatter x6 -> x0, waiting for transfers between devices: 114 us -> none  [settle_rows(): return lax.psum_scatter(var_term, 'row', scatter_dimension=0, tiled=True)]
    ppermute x0 -> x44, waiting for transfers between devices: none -> 103 us  [the longest x33 79.2 us: to_row(): lax.ppermute(pieces[k], 'row', [(i, (i + k) % n) for i in range(n)])]
    all_gather x6 -> x0, blocking collectives: 98.3 us -> none  [reach_range(): return lax.all_gather(vector, 'row', axis=0, tiled=True)]
    dot_general x31 -> x0, matrix products: 57.9 us -> none  [the longest x6 25.5 us: products(): slab_part = jnp.einsum('kij,kjq->kiq', a_flat, picked, precision=highest)]
    ppermute x0 -> x44, starting transfers between devices: none -> 57.3 us  [the longest x33 48.1 us: to_row(): lax.ppermute(pieces[k], 'row', [(i, (i + k) % n) for i in range(n)])]
    pallas_call x0 -> x21, Pallas kernels: none -> 35.8 us  [call(): pl.pallas_call(body, out_shape=[jax.ShapeDtypeStruct(s, d) for s, d in ou...]
  transfers between devices with their start and end apart: 12 -> 44, of which waited for: 12 -> 29; matrix products, arithmetic and copies ran while one was open for 3% -> 1% of each run, Pallas kernels for 0% -> 3%
where the time goes in v1:
time: 206 us; the launch traced here: 205 us
  waiting for transfers between devices  103 us (50%)
  starting transfers between devices  57.3 us (28%)
  Pallas kernels  35.8 us (17%)
  local copies, waits for them, and re-layouts  7.09 us (3%)
    ppermute x33, waiting for transfers between devices, to_row(): lax.ppermute(pieces[k], 'row', [(i, (i + k) % n) for i in range(n)])  79.2 us
    ppermute x33, starting transfers between devices, to_row(): lax.ppermute(pieces[k], 'row', [(i, (i + k) % n) for i in range(n)])  48.1 us
    pallas_call x21, Pallas kernels, call(): pl.pallas_call(body, out_shape=[jax.ShapeDtypeStruct(s, d) for s, d in ou...  35.8 us
    ppermute x5, waiting for transfers between devices, to_x(): lax.ppermute(v, 'col', [(c, (c + 2 * k) % n_col) for c in range(n_col)])  20.2 us
    ppermute x5, starting transfers between devices, to_x(): lax.ppermute(v, 'col', [(c, (c + 2 * k) % n_col) for c in range(n_col)])  8.02 us
    unnamed x23, local copies, waits for them, and re-layouts  6.76 us
  transfers between devices with their start and end apart: 44, of which 29 were waited for; matrix products, arithmetic and copies ran while one was open for 1% of the time, Pallas kernels for 3%

profile of v1, /device:TPU:0, one launch (start us, length us, event | category | flops | bytes accessed | tf_op | source)
XLA Modules:
  0.0 205.3 jit_solution(1645346222507288949)
XLA Ops:
  8.5 5.1 %collective-permute-start.4 = (f32[256,128]{1,0:T(8,128)S(1)}, f32[256,128]{1,0:T(8,128)S(1)}, u32[]{:S(2)}, u32[]{:S(2)}) collective-permute-start(f32[256,128]{1,0:T(8,128)S(1)} %get-tuple-element.65.refs_0_.refs_4_.refs_13_), channel_id=1, source_target_pairs={{0,12},{4,0},{8,4},{12,8},{1,13},{5,1},{9,5},{13,9},{2,14},{6,2},{... | collective-permute-start | bytes 393224 | tf_op jit(solution)/shard_map/ppermute | solution.py:396
  13.6 1.0 collective-permute-start.2
  15.5 1.4 copy-done
  17.8 3.0 %shard_map.132 = (bf16[768,2048]{1,0:T(8,128)(2,1)S(1)}, bf16[768,2048]{1,0:T(8,128)(2,1)S(1)}, bf16[2048,768]{1,0:T(8,128)(2,1)S(1)}, bf16[2048,768]{1,0:T(8,12...) custom-call(s32[48]{0:T(128)S(1)} %pad_add_fusion.3.cols, ...), custom_call_target="tpu_custom_call" | custom-call | flops 100000000 | bytes 3670016 | tf_op jit(solution)/shard_map/pallas_call | solution.py:27
  20.8 4.3 %collective-permute-done.3.refs_2_ = f32[256,128]{1,0:T(8,128)S(1)} collective-permute-done((f32[256,128]{1,0:T(8,128)S(1)}, f32[256,128]{1,0:T(8,128)S(1)}, u32[]{:S(2)}, u32[]{:S(2)}) %collective-permute-start.3) | collective-permute-done | bytes 131104 | tf_op jit(solution)/shard_map/ppermute | solution.py:396
  25.2 2.8 %shard_map.133 = (f32[384,128]{1,0:T(8,128)S(1)}, f32[256,128]{1,0:T(8,128)S(1)}) custom-call(s32[2]{0:T(128)S(1)} %pad_add_fusion.place, s32[4]{0:T(128)S(1)} %pad_add_fusion.2.pairs, f32[256,128]{1,0:T(8,128)S(1)} %get-tuple-element.65.refs_0_.refs_4_.refs_13_, f32[256,128]{1,0:T(8,128)S(1)} %collective-permute-done.2.refs_1_, ...), custom_call_target="tpu_custom_call" | custom-call | flops 805306368 | bytes 7340032 | tf_op jit(solution)/shard_map/pallas_call | solution.py:27
  28.0 1.5 collective-permute-start.7
  29.5 1.3 shard_map.134
  30.8 3.5 %collective-permute-done.7.refs_1_ = f32[384,128]{1,0:T(8,128)S(1)} collective-permute-done((f32[384,128]{1,0:T(8,128)S(1)}, f32[384,128]{1,0:T(8,128)S(1)}, u32[]{:S(2)}, u32[]{:S(2)}) %collective-permute-start.7) | collective-permute-done | bytes 196640 | tf_op jit(solution)/shard_map/ppermute | solution.py:392
  34.4 2.6 %shard_map.135 = (f32[272,128]{1,0:T(8,128)S(1)}, f32[272,128]{1,0:T(8,128)S(1)}, f32[272,128]{1,0:T(8,128)S(1)}, f32[272,128]{1,0:T(8,128)S(1)}, f32[384,128]{1,0:T(8,128)S(1)}) custom-call(s32[2]{0:T(128)S(1)} %pad_add_fusion.place, s32[4]{0:T(128)S(1)} %pad_add_fusion.2.pairs, f32[384,128]{1,0:T(8,128)S(1)} %get-tuple-element.70.refs_0_, ...), custom_call_target="tpu_custom_call" | custom-call | flops 805306368 | bytes 7217152 | tf_op jit(solution)/shard_map/pallas_call | solution.py:27
  37.4 2.0 collective-permute-start.9
  39.4 2.8 %collective-permute-start.10 = (f32[272,128]{1,0:T(8,128)S(1)}, f32[272,128]{1,0:T(8,128)S(1)}, u32[]{:S(2)}, u32[]{:S(2)}) collective-permute-start(f32[272,128]{1,0:T(8,128)S(1)} %get-tuple-element.80), channel_id=1, source_target_pairs={{0,12},{4,0},{8,4},{12,8},{1,13},{5,1},{9,5},{13,9},{2,14},{6,2},{... | collective-permute-start | bytes 417800 | tf_op jit(solution)/shard_map/ppermute | solution.py:396
  42.2 1.1 collective-permute-done.11
  43.7 1.8 collective-permute-done.8.refs_1_
  45.5 3.7 %collective-permute-done.9.refs_2_ = f32[272,128]{1,0:T(8,128)S(1)} collective-permute-done((f32[272,128]{1,0:T(8,128)S(1)}, f32[272,128]{1,0:T(8,128)S(1)}, u32[]{:S(2)}, u32[]{:S(2)}) %collective-permute-start.9) | collective-permute-done | bytes 139296 | tf_op jit(solution)/shard_map/ppermute | solution.py:396
  49.2 1.0 shard_map.136
  50.2 4.0 %collective-permute-start.14 = (f32[264,128]{1,0:T(8,128)S(1)}, f32[264,128]{1,0:T(8,128)S(1)}, u32[]{:S(2)}, u32[]{:S(2)}) collective-permute-start(f32[264,128]{1,0:T(8,128)S(1)} %get-tuple-element.82.refs_0_.refs_5_.refs_14_), channel_id=1, source_target_pairs={{0,12},{4,0},{8,4},{12,8},{1,13},{5,1},{9,5},{13,9},{2,14},{6,2},{... | collective-permute-start | bytes 405512 | tf_op jit(solution)/shard_map/ppermute | solution.py:396
  54.8 3.4 %collective-permute-done.14.refs_3_ = f32[264,128]{1,0:T(8,128)S(1)} collective-permute-done((f32[264,128]{1,0:T(8,128)S(1)}, f32[264,128]{1,0:T(8,128)S(1)}, u32[]{:S(2)}, u32[]{:S(2)}) %collective-permute-start.14) | collective-permute-done | bytes 135200 | tf_op jit(solution)/shard_map/ppermute | solution.py:396
  58.2 7.4 %collective-permute-done.13.refs_2_ = f32[264,128]{1,0:T(8,128)S(1)} collective-permute-done((f32[264,128]{1,0:T(8,128)S(1)}, f32[264,128]{1,0:T(8,128)S(1)}, u32[]{:S(2)}, u32[]{:S(2)}) %collective-permute-start.13) | collective-permute-done | bytes 135200 | tf_op jit(solution)/shard_map/ppermute | solution.py:396
  65.5 2.9 %shard_map.137 = (f32[392,128]{1,0:T(8,128)S(1)}, f32[256,128]{1,0:T(8,128)S(1)}) custom-call(s32[2]{0:T(128)S(1)} %pad_add_fusion.place, s32[4]{0:T(128)S(1)} %pad_add_fusion.2.pairs, f32[264,128]{1,0:T(8,128)S(1)} %get-tuple-element.82.refs_0_.refs_5_.refs_14_, f32[264,128]{1,0:T(8,128)S(1)} %collective-permute-done.12.refs_1_, ...), custom_call_target="tpu_custom_call" | custom-call | flops 805306368 | bytes 7356416 | tf_op jit(solution)/shard_map/pallas_call | solution.py:27
  68.4 1.5 collective-permute-start.15
  69.9 4.4 %collective-permute-done.15.refs_1_ = f32[392,128]{1,0:T(8,128)S(1)} collective-permute-done((f32[392,128]{1,0:T(8,128)S(1)}, f32[392,128]{1,0:T(8,128)S(1)}, u32[]{:S(2)}, u32[]{:S(2)}) %collective-permute-start.15) | collective-permute-done | bytes 200736 | tf_op jit(solution)/shard_map/ppermute | solution.py:392
  74.3 2.6 %shard_map.138 = (f32[264,128]{1,0:T(8,128)S(1)}, f32[264,128]{1,0:T(8,128)S(1)}, f32[264,128]{1,0:T(8,128)S(1)}, f32[264,128]{1,0:T(8,128)S(1)}, f32[384,128]{1,0:T(8,128)S(1)}, /*index=5*/f32[8,128]{1,0:T(8,128)S(1)}) custom-call(s32[2]{0:T(128)S(1)} %pad_add_fusion.place, s32[4]{0:T(128)S(1)} %pad_add_fusion.2.pairs, ...), custom_call_target="tpu_custom_call" | custom-call | flops 805306368 | bytes 6823936 | tf_op jit(solution)/shard_map/pallas_call | solution.py:27
  76.9 1.4 collective-permute-start.17
  78.3 2.8 %collective-permute-start.18 = (f32[264,128]{1,0:T(8,128)S(1)}, f32[264,128]{1,0:T(8,128)S(1)}, u32[]{:S(2)}, u32[]{:S(2)}) collective-permute-start(f32[264,128]{1,0:T(8,128)S(1)} %get-tuple-element.88), channel_id=1, source_target_pairs={{0,12},{4,0},{8,4},{12,8},{1,13},{5,1},{9,5},{13,9},{2,14},{6,2},{... | collective-permute-start | bytes 405512 | tf_op jit(solution)/shard_map/ppermute | solution.py:396
  81.1 4.1 %collective-permute-done.16.refs_1_ = f32[264,128]{1,0:T(8,128)S(1)} collective-permute-done((f32[264,128]{1,0:T(8,128)S(1)}, f32[264,128]{1,0:T(8,128)S(1)}, u32[]{:S(2)}, u32[]{:S(2)}) %collective-permute-start.16) | collective-permute-done | bytes 135200 | tf_op jit(solution)/shard_map/ppermute | solution.py:396
  85.2 3.0 %collective-permute-done.17.refs_2_ = f32[264,128]{1,0:T(8,128)S(1)} collective-permute-done((f32[264,128]{1,0:T(8,128)S(1)}, f32[264,128]{1,0:T(8,128)S(1)}, u32[]{:S(2)}, u32[]{:S(2)}) %collective-permute-start.17) | collective-permute-done | bytes 135200 | tf_op jit(solution)/shard_map/ppermute | solution.py:396
  88.3 3.3 %collective-permute-start.21 = (f32[264,128]{1,0:T(8,128)S(1)}, f32[264,128]{1,0:T(8,128)S(1)}, u32[]{:S(2)}, u32[]{:S(2)}) collective-permute-start(f32[264,128]{1,0:T(8,128)S(1)} %get-tuple-element.92.refs_0_.refs_15_), channel_id=1, source_target_pairs={{0,12},{4,0},{8,4},{12,8},{1,13},{5,1},{9,5},{13,9},{2,14},{6,2},{... | collective-permute-start | bytes 405512 | tf_op jit(solution)/shard_map/ppermute | solution.py:396
  92.3 3.4 %collective-permute-done.21.refs_3_ = f32[264,128]{1,0:T(8,128)S(1)} collective-permute-done((f32[264,128]{1,0:T(8,128)S(1)}, f32[264,128]{1,0:T(8,128)S(1)}, u32[]{:S(2)}, u32[]{:S(2)}) %collective-permute-start.21) | collective-permute-done | bytes 135200 | tf_op jit(solution)/shard_map/ppermute | solution.py:396
  95.7 7.9 %collective-permute-done.20.refs_2_ = f32[264,128]{1,0:T(8,128)S(1)} collective-permute-done((f32[264,128]{1,0:T(8,128)S(1)}, f32[264,128]{1,0:T(8,128)S(1)}, u32[]{:S(2)}, u32[]{:S(2)}) %collective-permute-start.20) | collective-permute-done | bytes 135200 | tf_op jit(solution)/shard_map/ppermute | solution.py:396
  103.6 2.9 %shard_map.140 = (f32[392,128]{1,0:T(8,128)S(1)}, f32[256,128]{1,0:T(8,128)S(1)}) custom-call(s32[2]{0:T(128)S(1)} %pad_add_fusion.place, s32[4]{0:T(128)S(1)} %pad_add_fusion.2.pairs, f32[264,128]{1,0:T(8,128)S(1)} %get-tuple-element.92.refs_0_.refs_15_, f32[264,128]{1,0:T(8,128)S(1)} %collective-permute-done.19.refs_1_, ...), custom_call_target="tpu_custom_call" | custom-call | flops 805306368 | bytes 7487488 | tf_op jit(solution)/shard_map/pallas_call | solution.py:27
  106.5 1.5 collective-permute-start.22
  108.0 4.2 %collective-permute-done.22.refs_1_ = f32[392,128]{1,0:T(8,128)S(1)} collective-permute-done((f32[392,128]{1,0:T(8,128)S(1)}, f32[392,128]{1,0:T(8,128)S(1)}, u32[]{:S(2)}, u32[]{:S(2)}) %collective-permute-start.22) | collective-permute-done | bytes 200736 | tf_op jit(solution)/shard_map/ppermute | solution.py:392
  112.4 1.2 collective-permute-start.24
  113.6 2.0 collective-permute-start.23
  117.0 2.0 collective-permute-done.23.refs_1_
  119.0 3.3 %shard_map.142 = (f32[256,128]{1,0:T(8,128)S(1)}, f32[256,128]{1,0:T(8,128)S(1)}, f32[256,128]{1,0:T(8,128)S(1)}, f32[256,128]{1,0:T(8,128)S(1)}, f32[256,128]{1...) custom-call(s32[2]{0:T(128)S(1)} %pad_add_fusion.place, ...), custom_call_target="tpu_custom_call" | custom-call | flops 805306368 | bytes 8486912 | tf_op jit(solution)/shard_map/pallas_call | solution.py:27
  122.5 1.8 collective-permute-start.27
  124.3 1.8 collective-permute-start.28
  126.1 3.2 %collective-permute-done.26.refs_1_ = f32[256,128]{1,0:T(8,128)S(1)} collective-permute-done((f32[256,128]{1,0:T(8,128)S(1)}, f32[256,128]{1,0:T(8,128)S(1)}, u32[]{:S(2)}, u32[]{:S(2)}) %collective-permute-start.26) | collective-permute-done | bytes 131104 | tf_op jit(solution)/shard_map/ppermute | solution.py:396
  129.4 3.1 %collective-permute-done.27.refs_2_ = f32[256,128]{1,0:T(8,128)S(1)} collective-permute-done((f32[256,128]{1,0:T(8,128)S(1)}, f32[256,128]{1,0:T(8,128)S(1)}, u32[]{:S(2)}, u32[]{:S(2)}) %collective-permute-start.27) | collective-permute-done | bytes 131104 | tf_op jit(solution)/shard_map/ppermute | solution.py:396
  133.1 2.6 %collective-permute-start.31 = (f32[264,128]{1,0:T(8,128)S(1)}, f32[264,128]{1,0:T(8,128)S(1)}, u32[]{:S(2)}, u32[]{:S(2)}) collective-permute-start(f32[264,128]{1,0:T(8,128)S(1)} %get-tuple-element.108.refs_0_.refs_5_.refs_14_), channel_id=1, source_target_pairs={{0,12},{4,0},{8,4},{12,8},{1,13},{5,1},{9,5},{13,9},{2,14},{6,2},{... | collective-permute-start | bytes 405512 | tf_op jit(solution)/shard_map/ppermute | solution.py:396
  136.6 3.2 %collective-permute-done.31.refs_3_ = f32[264,128]{1,0:T(8,128)S(1)} collective-permute-done((f32[264,128]{1,0:T(8,128)S(1)}, f32[264,128]{1,0:T(8,128)S(1)}, u32[]{:S(2)}, u32[]{:S(2)}) %collective-permute-start.31) | collective-permute-done | bytes 135200 | tf_op jit(solution)/shard_map/ppermute | solution.py:396
  139.8 7.2 %collective-permute-done.30.refs_2_ = f32[264,128]{1,0:T(8,128)S(1)} collective-permute-done((f32[264,128]{1,0:T(8,128)S(1)}, f32[264,128]{1,0:T(8,128)S(1)}, u32[]{:S(2)}, u32[]{:S(2)}) %collective-permute-start.30) | collective-permute-done | bytes 135200 | tf_op jit(solution)/shard_map/ppermute | solution.py:396
  147.0 2.9 %shard_map.144 = (f32[392,128]{1,0:T(8,128)S(1)}, f32[256,128]{1,0:T(8,128)S(1)}) custom-call(s32[2]{0:T(128)S(1)} %pad_add_fusion.place, s32[4]{0:T(128)S(1)} %pad_add_fusion.2.pairs, f32[264,128]{1,0:T(8,128)S(1)} %get-tuple-element.108.refs_0_.refs_5_.refs_14_, f32[264,128]{1,0:T(8,128)S(1)} %collective-permute-done.29.refs_1_, ...), custom_call_target="tpu_custom_call" | custom-call | flops 805306368 | bytes 7356416 | tf_op jit(solution)/shard_map/pallas_call | solution.py:27
  149.8 1.7 collective-permute-start.32
  151.5 4.1 %collective-permute-done.32.refs_1_ = f32[392,128]{1,0:T(8,128)S(1)} collective-permute-done((f32[392,128]{1,0:T(8,128)S(1)}, f32[392,128]{1,0:T(8,128)S(1)}, u32[]{:S(2)}, u32[]{:S(2)}) %collective-permute-start.32) | collective-permute-done | bytes 200736 | tf_op jit(solution)/shard_map/ppermute | solution.py:392
  155.6 2.6 %shard_map.145 = (f32[264,128]{1,0:T(8,128)S(1)}, f32[264,128]{1,0:T(8,128)S(1)}, f32[264,128]{1,0:T(8,128)S(1)}, f32[264,128]{1,0:T(8,128)S(1)}, f32[384,128]{1,0:T(8,128)S(1)}, /*index=5*/f32[8,128]{1,0:T(8,128)S(1)}) custom-call(s32[2]{0:T(128)S(1)} %pad_add_fusion.place, s32[4]{0:T(128)S(1)} %pad_add_fusion.2.pairs, ...), custom_call_target="tpu_custom_call" | custom-call | flops 805306368 | bytes 6823936 | tf_op jit(solution)/shard_map/pallas_call | solution.py:27
  158.2 1.7 collective-permute-start.34
  159.9 2.8 %collective-permute-start.35 = (f32[264,128]{1,0:T(8,128)S(1)}, f32[264,128]{1,0:T(8,128)S(1)}, u32[]{:S(2)}, u32[]{:S(2)}) collective-permute-start(f32[264,128]{1,0:T(8,128)S(1)} %get-tuple-element.114), channel_id=1, source_target_pairs={{0,12},{4,0},{8,4},{12,8},{1,13},{5,1},{9,5},{13,9},{2,14},{6,2},{... | collective-permute-start | bytes 405512 | tf_op jit(solution)/shard_map/ppermute | solution.py:396
  162.8 3.1 %collective-permute-done.33.refs_1_ = f32[264,128]{1,0:T(8,128)S(1)} collective-permute-done((f32[264,128]{1,0:T(8,128)S(1)}, f32[264,128]{1,0:T(8,128)S(1)}, u32[]{:S(2)}, u32[]{:S(2)}) %collective-permute-start.33) | collective-permute-done | bytes 135200 | tf_op jit(solution)/shard_map/ppermute | solution.py:396
  165.9 2.8 %collective-permute-done.34.refs_2_ = f32[264,128]{1,0:T(8,128)S(1)} collective-permute-done((f32[264,128]{1,0:T(8,128)S(1)}, f32[264,128]{1,0:T(8,128)S(1)}, u32[]{:S(2)}, u32[]{:S(2)}) %collective-permute-start.34) | collective-permute-done | bytes 135200 | tf_op jit(solution)/shard_map/ppermute | solution.py:396
  168.8 4.5 %collective-permute-start.38 = (f32[264,128]{1,0:T(8,128)S(1)}, f32[264,128]{1,0:T(8,128)S(1)}, u32[]{:S(2)}, u32[]{:S(2)}) collective-permute-start(f32[264,128]{1,0:T(8,128)S(1)} %get-tuple-element.117.refs_0_.refs_15_), channel_id=1, source_target_pairs={{0,12},{4,0},{8,4},{12,8},{1,13},{5,1},{9,5},{13,9},{2,14},{6,2},{... | collective-permute-start | bytes 405512 | tf_op jit(solution)/shard_map/ppermute | solution.py:396
  173.9 3.4 %collective-permute-done.38.refs_3_ = f32[264,128]{1,0:T(8,128)S(1)} collective-permute-done((f32[264,128]{1,0:T(8,128)S(1)}, f32[264,128]{1,0:T(8,128)S(1)}, u32[]{:S(2)}, u32[]{:S(2)}) %collective-permute-start.38) | collective-permute-done | bytes 135200 | tf_op jit(solution)/shard_map/ppermute | solution.py:396
  177.3 7.4 %collective-permute-done.37.refs_2_ = f32[264,128]{1,0:T(8,128)S(1)} collective-permute-done((f32[264,128]{1,0:T(8,128)S(1)}, f32[264,128]{1,0:T(8,128)S(1)}, u32[]{:S(2)}, u32[]{:S(2)}) %collective-permute-start.37) | collective-permute-done | bytes 135200 | tf_op jit(solution)/shard_map/ppermute | solution.py:396
  184.8 3.4 %shard_map.147 = (f32[392,128]{1,0:T(8,128)S(1)}, f32[256,128]{1,0:T(8,128)}) custom-call(s32[2]{0:T(128)S(1)} %pad_add_fusion.place, s32[4]{0:T(128)S(1)} %pad_add_fusion.2.pairs, f32[264,128]{1,0:T(8,128)S(1)} %get-tuple-element.117.refs_0_.refs_15_, f32[264,128]{1,0:T(8,128)S(1)} %collective-permute-done.36.refs_1_, ...), custom_call_target="tpu_custom_call" | custom-call | flops 805306368 | bytes 7487488 | tf_op jit(solution)/shard_map/pallas_call | solution.py:27
  188.2 1.7 collective-permute-start.39
  189.9 4.1 %collective-permute-done.39.refs_1_ = f32[392,128]{1,0:T(8,128)S(1)} collective-permute-done((f32[392,128]{1,0:T(8,128)S(1)}, f32[392,128]{1,0:T(8,128)S(1)}, u32[]{:S(2)}, u32[]{:S(2)}) %collective-permute-start.39) | collective-permute-done | bytes 200736 | tf_op jit(solution)/shard_map/ppermute | solution.py:392
  194.6 1.4 collective-permute-start.41
  196.0 2.0 collective-permute-start.40
  197.9 1.2 collective-permute-done.41.refs_2_
  199.1 2.3 %collective-permute-done.40.refs_1_ = f32[8,128]{1,0:T(8,128)S(1)} collective-permute-done((f32[8,128]{1,0:T(8,128)S(1)}, f32[8,128]{1,0:T(8,128)S(1)}, u32[]{:S(2)}, u32[]{:S(2)}) %collective-permute-start.40) | collective-permute-done | bytes 4128 | tf_op jit(solution)/shard_map/ppermute | solution.py:396
  201.7 1.9 collective-permute-done.43.got
  203.5 1.7 shard_map.150
  (77 shorter events, 16.8 us)
Async XLA Ops:
  0.6 14.8 %collective-permute-start.5 = (f32[24,128,128]{2,1,0:T(8,128)}, f32[24,128,128]{2,1,0:T(8,128)S(1)}, u32[]{:S(2)}, u32[]{:S(2)}) collective-permute-start(f32[24,128,128]{2,1,0:T(8,128)} %bitcast.6), channel_id=1, source_target_pairs={{0,1},{1,0},{2,3},{3,2},{4,5},{5,4},{6,7},{7,6},{8,9},{9,8},{10,11... | collective-permute-start | bytes 4718600 | tf_op jit(solution)/shard_map/ppermute | solution.py:389
  1.2 0.9 copy-start.1
  2.1 0.9 copy-start.3
  3.7 2.2 %collective-permute-start.1 = (f32[256,128]{1,0:T(8,128)S(1)}, f32[256,128]{1,0:T(8,128)S(1)}, u32[]{:S(2)}, u32[]{:S(2)}) collective-permute-start(f32[256,128]{1,0:T(8,128)S(1)} %shard_map.130), channel_id=1, source_target_pairs={{0,1},{1,0},{2,3},{3,2},{4,5},{5,4},{6,7},{7,6},{8,9},{9,8},{10,11... | collective-permute-start | bytes 393224 | tf_op jit(solution)/shard_map/ppermute | solution.py:389
  3.8 11.6 %collective-permute-start.6 = (f32[4,128,128]{2,1,0:T(8,128)}, f32[4,128,128]{2,1,0:T(8,128)S(1)}, u32[]{:S(2)}, u32[]{:S(2)}) collective-permute-start(f32[4,128,128]{2,1,0:T(8,128)} %bitcast.8), channel_id=1, source_target_pairs={{0,1},{1,0},{2,3},{3,2},{4,5},{5,4},{6,7},{7,6},{8,9},{9,8},{10,11... | collective-permute-start | bytes 786440 | tf_op jit(solution)/shard_map/ppermute | solution.py:389
  5.9 7.7 %collective-permute-start = (s32[26]{0:T(128)S(1)}, s32[26]{0:T(128)S(1)}, u32[]{:S(2)}, u32[]{:S(2)}) collective-permute-start(s32[26]{0:T(128)S(1)} %pad_add_fusion.1), channel_id=1, source_target_pairs={{0,1},{1,0},{2,3},{3,2},{4,5},{5,4},{6,7},{7,6},{8,9},{9,8},{10,11... | collective-permute-start | bytes 320 | tf_op jit(solution)/shard_map/ppermute | solution.py:389
  5.9 0.9 copy-start.2
  6.9 0.9 copy-start.4
  8.5 12.4 %collective-permute-start.4 = (f32[256,128]{1,0:T(8,128)S(1)}, f32[256,128]{1,0:T(8,128)S(1)}, u32[]{:S(2)}, u32[]{:S(2)}) collective-permute-start(f32[256,128]{1,0:T(8,128)S(1)} %get-tuple-element.65.refs_0_.refs_4_.refs_13_), channel_id=1, source_target_pairs={{0,12},{4,0},{8,4},{12,8},{1,13},{5,1},{9,5},{13,9},{2,14},{6,2},{... | collective-permute-start | bytes 393224 | tf_op jit(solution)/shard_map/ppermute | solution.py:396
  13.5 11.6 %collective-permute-start.3 = (f32[256,128]{1,0:T(8,128)S(1)}, f32[256,128]{1,0:T(8,128)S(1)}, u32[]{:S(2)}, u32[]{:S(2)}) collective-permute-start(f32[256,128]{1,0:T(8,128)S(1)} %get-tuple-element.65.refs_0_.refs_4_.refs_13_), channel_id=1, source_target_pairs={{0,8},{4,12},{8,0},{12,4},{1,9},{5,13},{9,1},{13,5},{2,10},{6,14},... | collective-permute-start | bytes 393224 | tf_op jit(solution)/shard_map/ppermute | solution.py:396
  13.6 11.6 %collective-permute-start.2 = (f32[256,128]{1,0:T(8,128)S(1)}, f32[256,128]{1,0:T(8,128)S(1)}, u32[]{:S(2)}, u32[]{:S(2)}) collective-permute-start(f32[256,128]{1,0:T(8,128)S(1)} %get-tuple-element.65.refs_0_.refs_4_.refs_13_), channel_id=1, source_target_pairs={{0,4},{4,8},{8,12},{12,0},{1,5},{5,9},{9,13},{13,1},{2,6},{6,10},{... | collective-permute-start | bytes 393224 | tf_op jit(solution)/shard_map/ppermute | solution.py:396
  15.4 1.4 copy-start
  16.9 0.9 copy-start.9
  25.1 4.4 %copy-start.5 = (f32[768,128]{1,0:T(8,128)S(1)}, f32[768,128]{1,0:T(8,128)}, u32[]{:S(2)}) copy-start(f32[768,128]{1,0:T(8,128)} %refs_0_.1) | copy-start | bytes 1179652
  25.1 4.4 %copy-start.6 = (f32[768,128]{1,0:T(8,128)S(1)}, f32[768,128]{1,0:T(8,128)}, u32[]{:S(2)}) copy-start(f32[768,128]{1,0:T(8,128)} %refs_1_.1) | copy-start | bytes 1179652
  25.1 4.4 %copy-start.7 = (f32[768,128]{1,0:T(8,128)S(1)}, f32[768,128]{1,0:T(8,128)}, u32[]{:S(2)}) copy-start(f32[768,128]{1,0:T(8,128)} %refs_2_.1) | copy-start | bytes 1179652
  25.1 4.4 %copy-start.8 = (f32[768,128]{1,0:T(8,128)S(1)}, f32[768,128]{1,0:T(8,128)}, u32[]{:S(2)}) copy-start(f32[768,128]{1,0:T(8,128)} %refs_3_.1) | copy-start | bytes 1179652
  28.0 6.4 %collective-permute-start.7 = (f32[384,128]{1,0:T(8,128)S(1)}, f32[384,128]{1,0:T(8,128)S(1)}, u32[]{:S(2)}, u32[]{:S(2)}) collective-permute-start(f32[384,128]{1,0:T(8,128)S(1)} %get-tuple-element.70.refs_0_), channel_id=1, source_target_pairs={{0,2},{1,3},{2,0},{3,1},{4,6},{5,7},{6,4},{7,5},{8,10},{9,11},{10,... | collective-permute-start | bytes 589832 | tf_op jit(solution)/shard_map/ppermute | solution.py:392
  34.4 7.9 %copy-start.10 = (f32[256]{0:T(256)S(1)}, f32[256]{0:T(256)}, u32[]{:S(2)}) copy-start(f32[256]{0:T(256)} %param.13) | copy-start | bytes 3076
  37.0 8.5 %collective-permute-start.8 = (f32[272,128]{1,0:T(8,128)S(1)}, f32[272,128]{1,0:T(8,128)S(1)}, u32[]{:S(2)}, u32[]{:S(2)}) collective-permute-start(f32[272,128]{1,0:T(8,128)S(1)} %get-tuple-element.78), channel_id=1, source_target_pairs={{0,4},{4,8},{8,12},{12,0},{1,5},{5,9},{9,13},{13,1},{2,6},{6,10},{... | collective-permute-start | bytes 417800 | tf_op jit(solution)/shard_map/ppermute | solution.py:396
  37.4 11.8 %collective-permute-start.9 = (f32[272,128]{1,0:T(8,128)S(1)}, f32[272,128]{1,0:T(8,128)S(1)}, u32[]{:S(2)}, u32[]{:S(2)}) collective-permute-start(f32[272,128]{1,0:T(8,128)S(1)} %get-tuple-element.79), channel_id=1, source_target_pairs={{0,8},{4,12},{8,0},{12,4},{1,9},{5,13},{9,1},{13,5},{2,10},{6,14},... | collective-permute-start | bytes 417800 | tf_op jit(solution)/shard_map/ppermute | solution.py:396
  39.4 9.8 %collective-permute-start.10 = (f32[272,128]{1,0:T(8,128)S(1)}, f32[272,128]{1,0:T(8,128)S(1)}, u32[]{:S(2)}, u32[]{:S(2)}) collective-permute-start(f32[272,128]{1,0:T(8,128)S(1)} %get-tuple-element.80), channel_id=1, source_target_pairs={{0,12},{4,0},{8,4},{12,8},{1,13},{5,1},{9,5},{13,9},{2,14},{6,2},{... | collective-permute-start | bytes 417800 | tf_op jit(solution)/shard_map/ppermute | solution.py:396
  42.2 1.1 collective-permute-start.11
  50.2 8.0 %collective-permute-start.14 = (f32[264,128]{1,0:T(8,128)S(1)}, f32[264,128]{1,0:T(8,128)S(1)}, u32[]{:S(2)}, u32[]{:S(2)}) collective-permute-start(f32[264,128]{1,0:T(8,128)S(1)} %get-tuple-element.82.refs_0_.refs_5_.refs_14_), channel_id=1, source_target_pairs={{0,12},{4,0},{8,4},{12,8},{1,13},{5,1},{9,5},{13,9},{2,14},{6,2},{... | collective-permute-start | bytes 405512 | tf_op jit(solution)/shard_map/ppermute | solution.py:396
  54.1 11.4 %collective-permute-start.13 = (f32[264,128]{1,0:T(8,128)S(1)}, f32[264,128]{1,0:T(8,128)S(1)}, u32[]{:S(2)}, u32[]{:S(2)}) collective-permute-start(f32[264,128]{1,0:T(8,128)S(1)} %get-tuple-element.82.refs_0_.refs_5_.refs_14_), channel_id=1, source_target_pairs={{0,8},{4,12},{8,0},{12,4},{1,9},{5,13},{9,1},{13,5},{2,10},{6,14},... | collective-permute-start | bytes 405512 | tf_op jit(solution)/shard_map/ppermute | solution.py:396
  54.2 11.3 %collective-permute-start.12 = (f32[264,128]{1,0:T(8,128)S(1)}, f32[264,128]{1,0:T(8,128)S(1)}, u32[]{:S(2)}, u32[]{:S(2)}) collective-permute-start(f32[264,128]{1,0:T(8,128)S(1)} %get-tuple-element.82.refs_0_.refs_5_.refs_14_), channel_id=1, source_target_pairs={{0,4},{4,8},{8,12},{12,0},{1,5},{5,9},{9,13},{13,1},{2,6},{6,10},{... | collective-permute-start | bytes 405512 | tf_op jit(solution)/shard_map/ppermute | solution.py:396
  68.4 5.9 %collective-permute-start.15 = (f32[392,128]{1,0:T(8,128)S(1)}, f32[392,128]{1,0:T(8,128)S(1)}, u32[]{:S(2)}, u32[]{:S(2)}) collective-permute-start(f32[392,128]{1,0:T(8,128)S(1)} %get-tuple-element.83.refs_0_), channel_id=1, source_target_pairs={{0,2},{1,3},{2,0},{3,1},{4,6},{5,7},{6,4},{7,5},{8,10},{9,11},{10,... | collective-permute-start | bytes 602120 | tf_op jit(solution)/shard_map/ppermute | solution.py:392
  76.9 8.3 %collective-permute-start.16 = (f32[264,128]{1,0:T(8,128)S(1)}, f32[264,128]{1,0:T(8,128)S(1)}, u32[]{:S(2)}, u32[]{:S(2)}) collective-permute-start(f32[264,128]{1,0:T(8,128)S(1)} %get-tuple-element.86), channel_id=1, source_target_pairs={{0,4},{4,8},{8,12},{12,0},{1,5},{5,9},{9,13},{13,1},{2,6},{6,10},{... | collective-permute-start | bytes 405512 | tf_op jit(solution)/shard_map/ppermute | solution.py:396
  76.9 11.3 %collective-permute-start.17 = (f32[264,128]{1,0:T(8,128)S(1)}, f32[264,128]{1,0:T(8,128)S(1)}, u32[]{:S(2)}, u32[]{:S(2)}) collective-permute-start(f32[264,128]{1,0:T(8,128)S(1)} %get-tuple-element.87), channel_id=1, source_target_pairs={{0,8},{4,12},{8,0},{12,4},{1,9},{5,13},{9,1},{13,5},{2,10},{6,14},... | collective-permute-start | bytes 405512 | tf_op jit(solution)/shard_map/ppermute | solution.py:396
  78.3 9.9 %collective-permute-start.18 = (f32[264,128]{1,0:T(8,128)S(1)}, f32[264,128]{1,0:T(8,128)S(1)}, u32[]{:S(2)}, u32[]{:S(2)}) collective-permute-start(f32[264,128]{1,0:T(8,128)S(1)} %get-tuple-element.88), channel_id=1, source_target_pairs={{0,12},{4,0},{8,4},{12,8},{1,13},{5,1},{9,5},{13,9},{2,14},{6,2},{... | collective-permute-start | bytes 405512 | tf_op jit(solution)/shard_map/ppermute | solution.py:396
  88.3 7.4 %collective-permute-start.21 = (f32[264,128]{1,0:T(8,128)S(1)}, f32[264,128]{1,0:T(8,128)S(1)}, u32[]{:S(2)}, u32[]{:S(2)}) collective-permute-start(f32[264,128]{1,0:T(8,128)S(1)} %get-tuple-element.92.refs_0_.refs_15_), channel_id=1, source_target_pairs={{0,12},{4,0},{8,4},{12,8},{1,13},{5,1},{9,5},{13,9},{2,14},{6,2},{... | collective-permute-start | bytes 405512 | tf_op jit(solution)/shard_map/ppermute | solution.py:396
  91.7 11.9 %collective-permute-start.20 = (f32[264,128]{1,0:T(8,128)S(1)}, f32[264,128]{1,0:T(8,128)S(1)}, u32[]{:S(2)}, u32[]{:S(2)}) collective-permute-start(f32[264,128]{1,0:T(8,128)S(1)} %get-tuple-element.92.refs_0_.refs_15_), channel_id=1, source_target_pairs={{0,8},{4,12},{8,0},{12,4},{1,9},{5,13},{9,1},{13,5},{2,10},{6,14},... | collective-permute-start | bytes 405512 | tf_op jit(solution)/shard_map/ppermute | solution.py:396
  92.3 11.3 %collective-permute-start.19 = (f32[264,128]{1,0:T(8,128)S(1)}, f32[264,128]{1,0:T(8,128)S(1)}, u32[]{:S(2)}, u32[]{:S(2)}) collective-permute-start(f32[264,128]{1,0:T(8,128)S(1)} %get-tuple-element.92.refs_0_.refs_15_), channel_id=1, source_target_pairs={{0,4},{4,8},{8,12},{12,0},{1,5},{5,9},{9,13},{13,1},{2,6},{6,10},{... | collective-permute-start | bytes 405512 | tf_op jit(solution)/shard_map/ppermute | solution.py:396
  106.5 5.8 %collective-permute-start.22 = (f32[392,128]{1,0:T(8,128)S(1)}, f32[392,128]{1,0:T(8,128)S(1)}, u32[]{:S(2)}, u32[]{:S(2)}) collective-permute-start(f32[392,128]{1,0:T(8,128)S(1)} %get-tuple-element.93.refs_0_), channel_id=1, source_target_pairs={{0,2},{1,3},{2,0},{3,1},{4,6},{5,7},{6,4},{7,5},{8,10},{9,11},{10,... | collective-permute-start | bytes 602120 | tf_op jit(solution)/shard_map/ppermute | solution.py:392
  112.4 3.6 %collective-permute-start.25 = (f32[8,128]{1,0:T(8,128)S(1)}, f32[8,128]{1,0:T(8,128)S(1)}, u32[]{:S(2)}, u32[]{:S(2)}) collective-permute-start(f32[8,128]{1,0:T(8,128)S(1)} %get-tuple-element.95.refs_0_), channel_id=1, source_target_pairs={{0,12},{4,0},{8,4},{12,8},{1,13},{5,1},{9,5},{13,9},{2,14},{6,2},{... | collective-permute-start | bytes 12296 | tf_op jit(solution)/shard_map/ppermute | solution.py:396
  112.4 4.6 %collective-permute-start.24 = (f32[8,128]{1,0:T(8,128)S(1)}, f32[8,128]{1,0:T(8,128)S(1)}, u32[]{:S(2)}, u32[]{:S(2)}) collective-permute-start(f32[8,128]{1,0:T(8,128)S(1)} %get-tuple-element.95.refs_0_), channel_id=1, source_target_pairs={{0,8},{4,12},{8,0},{12,4},{1,9},{5,13},{9,1},{13,5},{2,10},{6,14},... | collective-permute-start | bytes 12296 | tf_op jit(solution)/shard_map/ppermute | solution.py:396
  113.6 5.4 %collective-permute-start.23 = (f32[8,128]{1,0:T(8,128)S(1)}, f32[8,128]{1,0:T(8,128)S(1)}, u32[]{:S(2)}, u32[]{:S(2)}) collective-permute-start(f32[8,128]{1,0:T(8,128)S(1)} %get-tuple-element.95.refs_0_), channel_id=1, source_target_pairs={{0,4},{4,8},{8,12},{12,0},{1,5},{5,9},{9,13},{13,1},{2,6},{6,10},{... | collective-permute-start | bytes 12296 | tf_op jit(solution)/shard_map/ppermute | solution.py:396
  122.3 7.1 %collective-permute-start.26 = (f32[256,128]{1,0:T(8,128)S(1)}, f32[256,128]{1,0:T(8,128)S(1)}, u32[]{:S(2)}, u32[]{:S(2)}) collective-permute-start(f32[256,128]{1,0:T(8,128)S(1)} %get-tuple-element.104), channel_id=1, source_target_pairs={{0,4},{4,8},{8,12},{12,0},{1,5},{5,9},{9,13},{13,1},{2,6},{6,10},{... | collective-permute-start | bytes 393224 | tf_op jit(solution)/shard_map/ppermute | solution.py:396
  122.5 10.0 %collective-permute-start.27 = (f32[256,128]{1,0:T(8,128)S(1)}, f32[256,128]{1,0:T(8,128)S(1)}, u32[]{:S(2)}, u32[]{:S(2)}) collective-permute-start(f32[256,128]{1,0:T(8,128)S(1)} %get-tuple-element.105), channel_id=1, source_target_pairs={{0,8},{4,12},{8,0},{12,4},{1,9},{5,13},{9,1},{13,5},{2,10},{6,14},... | collective-permute-start | bytes 393224 | tf_op jit(solution)/shard_map/ppermute | solution.py:396
  124.3 8.1 %collective-permute-start.28 = (f32[256,128]{1,0:T(8,128)S(1)}, f32[256,128]{1,0:T(8,128)S(1)}, u32[]{:S(2)}, u32[]{:S(2)}) collective-permute-start(f32[256,128]{1,0:T(8,128)S(1)} %get-tuple-element.106), channel_id=1, source_target_pairs={{0,12},{4,0},{8,4},{12,8},{1,13},{5,1},{9,5},{13,9},{2,14},{6,2},{... | collective-permute-start | bytes 393224 | tf_op jit(solution)/shard_map/ppermute | solution.py:396
  133.1 6.7 %collective-permute-start.31 = (f32[264,128]{1,0:T(8,128)S(1)}, f32[264,128]{1,0:T(8,128)S(1)}, u32[]{:S(2)}, u32[]{:S(2)}) collective-permute-start(f32[264,128]{1,0:T(8,128)S(1)} %get-tuple-element.108.refs_0_.refs_5_.refs_14_), channel_id=1, source_target_pairs={{0,12},{4,0},{8,4},{12,8},{1,13},{5,1},{9,5},{13,9},{2,14},{6,2},{... | collective-permute-start | bytes 405512 | tf_op jit(solution)/shard_map/ppermute | solution.py:396
  135.7 11.2 %collective-permute-start.30 = (f32[264,128]{1,0:T(8,128)S(1)}, f32[264,128]{1,0:T(8,128)S(1)}, u32[]{:S(2)}, u32[]{:S(2)}) collective-permute-start(f32[264,128]{1,0:T(8,128)S(1)} %get-tuple-element.108.refs_0_.refs_5_.refs_14_), channel_id=1, source_target_pairs={{0,8},{4,12},{8,0},{12,4},{1,9},{5,13},{9,1},{13,5},{2,10},{6,14},... | collective-permute-start | bytes 405512 | tf_op jit(solution)/shard_map/ppermute | solution.py:396
  136.6 10.4 %collective-permute-start.29 = (f32[264,128]{1,0:T(8,128)S(1)}, f32[264,128]{1,0:T(8,128)S(1)}, u32[]{:S(2)}, u32[]{:S(2)}) collective-permute-start(f32[264,128]{1,0:T(8,128)S(1)} %get-tuple-element.108.refs_0_.refs_5_.refs_14_), channel_id=1, source_target_pairs={{0,4},{4,8},{8,12},{12,0},{1,5},{5,9},{9,13},{13,1},{2,6},{6,10},{... | collective-permute-start | bytes 405512 | tf_op jit(solution)/shard_map/ppermute | solution.py:396
  149.8 5.8 %collective-permute-start.32 = (f32[392,128]{1,0:T(8,128)S(1)}, f32[392,128]{1,0:T(8,128)S(1)}, u32[]{:S(2)}, u32[]{:S(2)}) collective-permute-start(f32[392,128]{1,0:T(8,128)S(1)} %get-tuple-element.109.refs_0_), channel_id=1, source_target_pairs={{0,2},{1,3},{2,0},{3,1},{4,6},{5,7},{6,4},{7,5},{8,10},{9,11},{10,... | collective-permute-start | bytes 602120 | tf_op jit(solution)/shard_map/ppermute | solution.py:392
  158.2 7.7 %collective-permute-start.33 = (f32[264,128]{1,0:T(8,128)S(1)}, f32[264,128]{1,0:T(8,128)S(1)}, u32[]{:S(2)}, u32[]{:S(2)}) collective-permute-start(f32[264,128]{1,0:T(8,128)S(1)} %get-tuple-element.112), channel_id=1, source_target_pairs={{0,4},{4,8},{8,12},{12,0},{1,5},{5,9},{9,13},{13,1},{2,6},{6,10},{... | collective-permute-start | bytes 405512 | tf_op jit(solution)/shard_map/ppermute | solution.py:396
  158.2 10.5 %collective-permute-start.34 = (f32[264,128]{1,0:T(8,128)S(1)}, f32[264,128]{1,0:T(8,128)S(1)}, u32[]{:S(2)}, u32[]{:S(2)}) collective-permute-start(f32[264,128]{1,0:T(8,128)S(1)} %get-tuple-element.113), channel_id=1, source_target_pairs={{0,8},{4,12},{8,0},{12,4},{1,9},{5,13},{9,1},{13,5},{2,10},{6,14},... | collective-permute-start | bytes 405512 | tf_op jit(solution)/shard_map/ppermute | solution.py:396
  159.9 8.8 %collective-permute-start.35 = (f32[264,128]{1,0:T(8,128)S(1)}, f32[264,128]{1,0:T(8,128)S(1)}, u32[]{:S(2)}, u32[]{:S(2)}) collective-permute-start(f32[264,128]{1,0:T(8,128)S(1)} %get-tuple-element.114), channel_id=1, source_target_pairs={{0,12},{4,0},{8,4},{12,8},{1,13},{5,1},{9,5},{13,9},{2,14},{6,2},{... | collective-permute-start | bytes 405512 | tf_op jit(solution)/shard_map/ppermute | solution.py:396
  168.8 8.5 %collective-permute-start.38 = (f32[264,128]{1,0:T(8,128)S(1)}, f32[264,128]{1,0:T(8,128)S(1)}, u32[]{:S(2)}, u32[]{:S(2)}) collective-permute-start(f32[264,128]{1,0:T(8,128)S(1)} %get-tuple-element.117.refs_0_.refs_15_), channel_id=1, source_target_pairs={{0,12},{4,0},{8,4},{12,8},{1,13},{5,1},{9,5},{13,9},{2,14},{6,2},{... | collective-permute-start | bytes 405512 | tf_op jit(solution)/shard_map/ppermute | solution.py:396
  173.3 11.5 %collective-permute-start.37 = (f32[264,128]{1,0:T(8,128)S(1)}, f32[264,128]{1,0:T(8,128)S(1)}, u32[]{:S(2)}, u32[]{:S(2)}) collective-permute-start(f32[264,128]{1,0:T(8,128)S(1)} %get-tuple-element.117.refs_0_.refs_15_), channel_id=1, source_target_pairs={{0,8},{4,12},{8,0},{12,4},{1,9},{5,13},{9,1},{13,5},{2,10},{6,14},... | collective-permute-start | bytes 405512 | tf_op jit(solution)/shard_map/ppermute | solution.py:396
  173.3 11.5 %collective-permute-start.36 = (f32[264,128]{1,0:T(8,128)S(1)}, f32[264,128]{1,0:T(8,128)S(1)}, u32[]{:S(2)}, u32[]{:S(2)}) collective-permute-start(f32[264,128]{1,0:T(8,128)S(1)} %get-tuple-element.117.refs_0_.refs_15_), channel_id=1, source_target_pairs={{0,4},{4,8},{8,12},{12,0},{1,5},{5,9},{9,13},{13,1},{2,6},{6,10},{... | collective-permute-start | bytes 405512 | tf_op jit(solution)/shard_map/ppermute | solution.py:396
  188.2 5.8 %collective-permute-start.39 = (f32[392,128]{1,0:T(8,128)S(1)}, f32[392,128]{1,0:T(8,128)S(1)}, u32[]{:S(2)}, u32[]{:S(2)}) collective-permute-start(f32[392,128]{1,0:T(8,128)S(1)} %get-tuple-element.118.refs_0_), channel_id=1, source_target_pairs={{0,2},{1,3},{2,0},{3,1},{4,6},{5,7},{6,4},{7,5},{8,10},{9,11},{10,... | collective-permute-start | bytes 602120 | tf_op jit(solution)/shard_map/ppermute | solution.py:392
  194.2 3.8 %collective-permute-start.42 = (f32[8,128]{1,0:T(8,128)S(1)}, f32[8,128]{1,0:T(8,128)S(1)}, u32[]{:S(2)}, u32[]{:S(2)}) collective-permute-start(f32[8,128]{1,0:T(8,128)S(1)} %get-tuple-element.120.refs_0_), channel_id=1, source_target_pairs={{0,12},{4,0},{8,4},{12,8},{1,13},{5,1},{9,5},{13,9},{2,14},{6,2},{... | collective-permute-start | bytes 12296 | tf_op jit(solution)/shard_map/ppermute | solution.py:396
  194.6 4.5 %collective-permute-start.41 = (f32[8,128]{1,0:T(8,128)S(1)}, f32[8,128]{1,0:T(8,128)S(1)}, u32[]{:S(2)}, u32[]{:S(2)}) collective-permute-start(f32[8,128]{1,0:T(8,128)S(1)} %get-tuple-element.120.refs_0_), channel_id=1, source_target_pairs={{0,8},{4,12},{8,0},{12,4},{1,9},{5,13},{9,1},{13,5},{2,10},{6,14},... | collective-permute-start | bytes 12296 | tf_op jit(solution)/shard_map/ppermute | solution.py:396
  196.0 5.4 %collective-permute-start.40 = (f32[8,128]{1,0:T(8,128)S(1)}, f32[8,128]{1,0:T(8,128)S(1)}, u32[]{:S(2)}, u32[]{:S(2)}) collective-permute-start(f32[8,128]{1,0:T(8,128)S(1)} %get-tuple-element.120.refs_0_), channel_id=1, source_target_pairs={{0,4},{4,8},{8,12},{12,0},{1,5},{5,9},{9,13},{13,1},{2,6},{6,10},{... | collective-permute-start | bytes 12296 | tf_op jit(solution)/shard_map/ppermute | solution.py:396
  201.6 2.0 collective-permute-start.43

commit v2 on v1

--- a/solution.py
+++ b/solution.py
@@ -76,21 +76,17 @@
     return tile
 
 
-def send_kernel(place, x, q, msg):
+def mix_cores(core, mine, other):
+    low = low_half(mine.shape)
+    a = jnp.where(core == 0, mine, turn(mine))
+    b = jnp.where(core == 0, turn(other), other)
+    return jnp.where(low, a, b)
+
+
+def own_kernel(place, x, x_other, q, q_other, x_own, q_own):
     core = place[1]
-    low = low_half(x.shape)
-    xv = jnp.where(core == 0, turn(x[...]), x[...])
-    qv = jnp.where(core == 0, q[...], turn(q[...]))
-    msg[...] = jnp.where(low, xv, qv)
-
-
-def recv_kernel(place, x, q, got, x_own, q_own):
-    core = place[1]
-    low = low_half(x.shape)
-    xv = jnp.where(core == 0, x[...], turn(x[...]))
-    qv = jnp.where(core == 0, q[...], turn(q[...]))
-    x_own[...] = jnp.where(low, xv, turn(got[...]))
-    q_own[...] = jnp.where(low, qv, got[...])
+    x_own[...] = mix_cores(core, x[...], x_other[...])
+    q_own[...] = mix_cores(core, q[...], q_other[...])
 
 
 def slab_kernel(place, *refs):
@@ -140,6 +136,8 @@
 
 def forward_kernel(n, own, scalars, place, pairs, *refs):
     msgs, rest = refs[:n], refs[n:]
+    if scalars == 0:
+        others, rest = rest[:n], rest[n:]
     a_hi, a_lo, p_hi, p_lo = rest[:4]
     rest = rest[4:]
     if scalars == 2:
@@ -148,9 +146,10 @@
     row = place[0]
     span = whole.shape[0]
     for k in range(n):
-        at = lax.rem(row + n - k, n) * own
-        at = pl.multiple_of(at, own)
+        at = pl.multiple_of(lax.bitwise_xor(row, k) * own, own)
         v = msgs[k][0:own, :]
+        if scalars == 0:
+            v = mix_cores(place[1], v, others[k][...])
         whole[pl.ds(at, own), :] = v
         first, second = pair_up(v)
         wide[pl.ds(at, own), :] = first
@@ -201,7 +200,7 @@
             at = pl.ds(pl.multiple_of(pairs[2 * t + e] * BLK, BLK), BLK)
             total[at, :] += jnp.where(side, pp_now[e * BLK : (e + 1) * BLK], 0.0)
     for k in range(n):
-        at = pl.multiple_of(lax.rem(row + k, n) * own, own)
+        at = pl.multiple_of(lax.bitwise_xor(row, k) * own, own)
         outs[k][0:own, :] = total[pl.ds(at, own), :]
         if extra is not None:
             outs[k][own : own + extra.shape[0], :] = extra
@@ -389,18 +388,23 @@
         return lax.ppermute(v, "col", [(c, c ^ 1) for c in range(n_col)])
 
     def to_x(v):
-        got = [lax.ppermute(v, "col", [(c, (c + 2 * k) % n_col) for c in range(n_col)]) for k in range(1, nx)]
-        return [v] + got
-
-    def to_row(pieces):
-        got = [lax.ppermute(pieces[k], "row", [(i, (i + k) % n) for i in range(n)]) for k in range(1, n)]
-        return [pieces[0]] + got
+        return [v] + [lax.ppermute(v, "col", [(c, c ^ (2 * k)) for c in range(n_col)]) for k in range(1, nx)]
+
+    swaps = [2, 3, 1] if n == 4 else list(range(1, n))
+
+    def to_row(pieces, order=None):
+        got = {0: pieces[0]}
+        for k in order or swaps:
+            got[k] = lax.ppermute(pieces[k], "row", [(i, i ^ k) for i in range(n)])
+        return [got[k] for k in range(n)]
+
+    def to_all_rows(v):
+        return to_row([v] * n, swaps[::-1])
 
     a_mine = a_blocks.reshape(slab * per, BLK, BLK)
     p_mine = p_blocks.reshape(4, BLK, BLK)
     ints = jnp.concatenate([a_cols.reshape(-1), p_pairs.reshape(-1)])
-    (send,) = call(send_kernel, [((own, LANES), F32)], [x_state, q_lin], [place])
-    got_xq = to_core(send)
+    x_rows = to_all_rows(x_state)
     a_other = to_core(a_mine)
     ints_other = to_core(ints)
     p_other = to_core(p_mine)
@@ -411,8 +415,8 @@
     pd = jnp.concatenate(
         [jnp.broadcast_to(p_diag[:, None], (own, HALF)), jnp.broadcast_to(pd_other[:, None], (own, HALF))], axis=1
     )
-    x, q = call(recv_kernel, [((own, LANES), F32)] * 2, [x_state, q_lin, got_xq], [place])
-    x_parts = to_row([x] * n)
+    x_others = [to_core(v) for v in x_rows]
+    x, q = call(own_kernel, [((own, LANES), F32)] * 2, [x_state, x_others[0], q_lin, to_core(q_lin)], [place])
     z, y, lower, upper = call(
         slab_kernel, [((half_rows, LANES), F32)] * 4, [z_state, y_state, lower_bound, upper_bound], [place]
     )
@@ -441,7 +445,7 @@
             flops=prod_flops,
         )
 
-    msg, ppx = forward(x_parts, 0)
+    msg, ppx = forward(x_rows + x_others, 0)
     *pieces, ax = call(
         functools.partial(start_back_kernel, n, nx, own),
         [((own + 2 * n_range, LANES), F32)] * n + [((half_rows, LANES), F32)],
@@ -470,7 +474,7 @@
                 [*to_row(pieces), x, q, pd, dk],
                 [place],
             )
-        msg, pp1 = forward(to_row([msg1] * n), 1)
+        msg, pp1 = forward(to_all_rows(msg1), 1)
         *pieces, ad, scal = call(
             functools.partial(step_back_kernel, n, nx, own),
             [msg_shape] * n + [slab_shape, tile_shape],
@@ -484,13 +488,13 @@
             [msg_shape, tile_shape],
             [*to_row(pieces), scal, msg1, r, pd, dk],
         )
-        msg, pp2 = forward(to_row([msg2] * n), 2, (pp1,))
+        msg, pp2 = forward(to_all_rows(msg2), 2, (pp1,))
         ad2, share, keep = call(
             functools.partial(curve_kernel, nx),
             [slab_shape, tile_shape, tile_shape],
             [*to_x(msg), scal, ad],
         )
-        shares = to_row([share] * n)
+        shares = to_all_rows(share)
         state = [*shares, keep, step, ax, ad, ad2, z, y, lower, upper, x, msg1, msg2]
         if outer + 1 < ADMM_ITERS:
             *pieces, x, z, y, ax, ppx = call(

time: 206 us -> 203 us (0.985)
  starting transfers between devices: 57.3 us -> 61 us
  local copies, waits for them, and re-layouts: 7.09 us -> 3.49 us
  waiting for transfers between devices: 103 us -> 99.6 us
    ppermute x38, waiting for transfers between devices: 99.5 us -> 95.8 us  [the longest x33 74.6 us: to_row(): got[k] = lax.ppermute(pieces[k], 'row', [(i, i ^ k) for i in range(n)])]
    unnamed x23 -> x19, local copies, waits for them, and re-layouts: 6.76 us -> 3.16 us
    ppermute x38, starting transfers between devices: 56.1 us -> 59.2 us  [the longest x33 51.5 us: to_row(): got[k] = lax.ppermute(pieces[k], 'row', [(i, i ^ k) for i in range(n)])]
    pallas_call x21 -> x20, Pallas kernels: 35.8 us -> 35.6 us  [call(): pl.pallas_call(body, out_shape=[jax.ShapeDtypeStruct(s, d) for s, d in ou...]
  transfers between devices with their start and end apart: 44 -> 48, of which waited for: 29 -> 30; matrix products, arithmetic and copies ran while one was open for 1% -> 1% of each run, Pallas kernels for 3% -> 2%
where the time goes in v2:
time: 203 us; the launch traced here: 202 us
  waiting for transfers between devices  99.6 us (49%)
  starting transfers between devices  61 us (30%)
  Pallas kernels  35.6 us (18%)
  local copies, waits for them, and re-layouts  3.49 us (2%)
    ppermute x33, waiting for transfers between devices, to_row(): got[k] = lax.ppermute(pieces[k], 'row', [(i, i ^ k) for i in range(n)])  74.6 us
    ppermute x33, starting transfers between devices, to_row(): got[k] = lax.ppermute(pieces[k], 'row', [(i, i ^ k) for i in range(n)])  51.5 us
    pallas_call x20, Pallas kernels, call(): pl.pallas_call(body, out_shape=[jax.ShapeDtypeStruct(s, d) for s, d in ou...  35.6 us
    ppermute x5, waiting for transfers between devices, to_x(): lax.ppermute(v, 'col', [(c, c ^ 2 * k) for c in range(n_col)])  21.2 us
    ppermute x5, starting transfers between devices, to_x(): lax.ppermute(v, 'col', [(c, c ^ 2 * k) for c in range(n_col)])  7.76 us
  transfers between devices with their start and end apart: 48, of which 30 were waited for; matrix products, arithmetic and copies ran while one was open for 1% of the time, Pallas kernels for 2%

profile of v2, /device:TPU:0, one launch (start us, length us, event | category | flops | bytes accessed | tf_op | source)
XLA Modules:
  0.0 202.3 jit_solution(6856361422756778646)
XLA Ops:
  1.2 5.0 %collective-permute-start.3 = (f32[256,128]{1,0:T(8,128)}, f32[256,128]{1,0:T(8,128)S(1)}, u32[]{:S(2)}, u32[]{:S(2)}) collective-permute-start(f32[256,128]{1,0:T(8,128)} %x.1), channel_id=1, source_target_pairs={{0,12},{4,8},{8,4},{12,0},{1,13},{5,9},{9,5},{13,1},{2,14},{6,10},... | collective-permute-start | bytes 393224 | tf_op jit(solution)/shard_map/ppermute | solution.py:398
  7.9 1.1 collective-permute-done
  9.0 1.3 collective-permute-done.3.refs_3_
  10.3 7.5 %collective-permute-done.2.refs_2_ = f32[256,128]{1,0:T(8,128)S(1)} collective-permute-done((f32[256,128]{1,0:T(8,128)}, f32[256,128]{1,0:T(8,128)S(1)}, u32[]{:S(2)}, u32[]{:S(2)}) %collective-permute-start.2) | collective-permute-done | bytes 131104 | tf_op jit(solution)/shard_map/ppermute | solution.py:398
  19.3 1.4 copy-done
  21.6 3.0 %shard_map.130 = (bf16[768,2048]{1,0:T(8,128)(2,1)S(1)}, bf16[768,2048]{1,0:T(8,128)(2,1)S(1)}, bf16[2048,768]{1,0:T(8,128)(2,1)S(1)}, bf16[2048,768]{1,0:T(8,12...) custom-call(s32[48]{0:T(128)S(1)} %pad_add_fusion.3.cols, ...), custom_call_target="tpu_custom_call" | custom-call | flops 100000000 | bytes 3670016 | tf_op jit(solution)/shard_map/pallas_call | solution.py:27
  24.7 3.0 %shard_map.131 = (f32[384,128]{1,0:T(8,128)S(1)}, f32[256,128]{1,0:T(8,128)S(1)}) custom-call(s32[2]{0:T(128)S(1)} %pad_add_fusion.place, s32[4]{0:T(128)S(1)} %pad_add_fusion.2.pairs, f32[256,128]{1,0:T(8,128)S(1)} %copy-done.1, f32[256,128]{1,0:T(8,128)S(1)} %collective-permute-done.1.refs_1_, f32[256,128]{1,0:T(8,128)S(1)} %collective-permute-done.2.refs_2_, ...), custom_call_target="tpu_custom_call" | custom-call | flops 805306368 | bytes 7864320 | tf_op jit(solution)/shard_map/pallas_call | solution.py:27
  27.8 1.6 collective-permute-start.10
  29.4 1.3 shard_map.132
  30.7 4.4 %collective-permute-done.10.refs_1_ = f32[384,128]{1,0:T(8,128)S(1)} collective-permute-done((f32[384,128]{1,0:T(8,128)S(1)}, f32[384,128]{1,0:T(8,128)S(1)}, u32[]{:S(2)}, u32[]{:S(2)}) %collective-permute-start.10) | collective-permute-done | bytes 196640 | tf_op jit(solution)/shard_map/ppermute | solution.py:391
  35.1 2.6 %shard_map.133 = (f32[272,128]{1,0:T(8,128)S(1)}, f32[272,128]{1,0:T(8,128)S(1)}, f32[272,128]{1,0:T(8,128)S(1)}, f32[272,128]{1,0:T(8,128)S(1)}, f32[384,128]{1,0:T(8,128)S(1)}) custom-call(s32[2]{0:T(128)S(1)} %pad_add_fusion.place, s32[4]{0:T(128)S(1)} %pad_add_fusion.2.pairs, f32[384,128]{1,0:T(8,128)S(1)} %get-tuple-element.69.refs_0_, ...), custom_call_target="tpu_custom_call" | custom-call | flops 805306368 | bytes 7217152 | tf_op jit(solution)/shard_map/pallas_call | solution.py:27
  37.8 3.0 %collective-permute-start.12 = (f32[272,128]{1,0:T(8,128)S(1)}, f32[272,128]{1,0:T(8,128)S(1)}, u32[]{:S(2)}, u32[]{:S(2)}) collective-permute-start(f32[272,128]{1,0:T(8,128)S(1)} %get-tuple-element.78), channel_id=1, source_target_pairs={{0,8},{4,12},{8,0},{12,4},{1,9},{5,13},{9,1},{13,5},{2,10},{6,14},... | collective-permute-start | bytes 417800 | tf_op jit(solution)/shard_map/ppermute | solution.py:398
  40.8 1.4 collective-permute-start.13
  45.2 6.1 %collective-permute-done.12.refs_2_ = f32[272,128]{1,0:T(8,128)S(1)} collective-permute-done((f32[272,128]{1,0:T(8,128)S(1)}, f32[272,128]{1,0:T(8,128)S(1)}, u32[]{:S(2)}, u32[]{:S(2)}) %collective-permute-start.12) | collective-permute-done | bytes 139296 | tf_op jit(solution)/shard_map/ppermute | solution.py:398
  52.3 2.4 %collective-permute-start.18 = (f32[264,128]{1,0:T(8,128)S(1)}, f32[264,128]{1,0:T(8,128)S(1)}, u32[]{:S(2)}, u32[]{:S(2)}) collective-permute-start(f32[264,128]{1,0:T(8,128)S(1)} %get-tuple-element.82.refs_0_.refs_5_.refs_14_), channel_id=1, source_target_pairs={{0,12},{4,8},{8,4},{12,0},{1,13},{5,9},{9,5},{13,1},{2,14},{6,10},... | collective-permute-start | bytes 405512 | tf_op jit(solution)/shard_map/ppermute | solution.py:398
  54.8 1.3 collective-permute-start.17
  56.8 3.9 %collective-permute-done.18.refs_3_ = f32[264,128]{1,0:T(8,128)S(1)} collective-permute-done((f32[264,128]{1,0:T(8,128)S(1)}, f32[264,128]{1,0:T(8,128)S(1)}, u32[]{:S(2)}, u32[]{:S(2)}) %collective-permute-start.18) | collective-permute-done | bytes 135200 | tf_op jit(solution)/shard_map/ppermute | solution.py:398
  60.7 5.2 %collective-permute-done.17.refs_2_ = f32[264,128]{1,0:T(8,128)S(1)} collective-permute-done((f32[264,128]{1,0:T(8,128)S(1)}, f32[264,128]{1,0:T(8,128)S(1)}, u32[]{:S(2)}, u32[]{:S(2)}) %collective-permute-start.17) | collective-permute-done | bytes 135200 | tf_op jit(solution)/shard_map/ppermute | solution.py:398
  65.9 2.9 %shard_map.136 = (f32[392,128]{1,0:T(8,128)S(1)}, f32[256,128]{1,0:T(8,128)S(1)}) custom-call(s32[2]{0:T(128)S(1)} %pad_add_fusion.place, s32[4]{0:T(128)S(1)} %pad_add_fusion.2.pairs, f32[264,128]{1,0:T(8,128)S(1)} %get-tuple-element.82.refs_0_.refs_5_.refs_14_, f32[264,128]{1,0:T(8,128)S(1)} %collective-permute-done.16.refs_1_, ...), custom_call_target="tpu_custom_call" | custom-call | flops 805306368 | bytes 7356416 | tf_op jit(solution)/shard_map/pallas_call | solution.py:27
  68.7 1.5 collective-permute-start.19
  70.3 4.2 %collective-permute-done.19.refs_1_ = f32[392,128]{1,0:T(8,128)S(1)} collective-permute-done((f32[392,128]{1,0:T(8,128)S(1)}, f32[392,128]{1,0:T(8,128)S(1)}, u32[]{:S(2)}, u32[]{:S(2)}) %collective-permute-start.19) | collective-permute-done | bytes 200736 | tf_op jit(solution)/shard_map/ppermute | solution.py:391
  74.5 2.8 %shard_map.137 = (f32[264,128]{1,0:T(8,128)S(1)}, f32[264,128]{1,0:T(8,128)S(1)}, f32[264,128]{1,0:T(8,128)S(1)}, f32[264,128]{1,0:T(8,128)S(1)}, f32[384,128]{1,0:T(8,128)S(1)}, /*index=5*/f32[8,128]{1,0:T(8,128)S(1)}) custom-call(s32[2]{0:T(128)S(1)} %pad_add_fusion.place, s32[4]{0:T(128)S(1)} %pad_add_fusion.2.pairs, ...), custom_call_target="tpu_custom_call" | custom-call | flops 805306368 | bytes 6823936 | tf_op jit(solution)/shard_map/pallas_call | solution.py:27
  77.4 3.4 %collective-permute-start.21 = (f32[264,128]{1,0:T(8,128)S(1)}, f32[264,128]{1,0:T(8,128)S(1)}, u32[]{:S(2)}, u32[]{:S(2)}) collective-permute-start(f32[264,128]{1,0:T(8,128)S(1)} %get-tuple-element.87), channel_id=1, source_target_pairs={{0,8},{4,12},{8,0},{12,4},{1,9},{5,13},{9,1},{13,5},{2,10},{6,14},... | collective-permute-start | bytes 405512 | tf_op jit(solution)/shard_map/ppermute | solution.py:398
  82.6 7.2 %collective-permute-done.21.refs_2_ = f32[264,128]{1,0:T(8,128)S(1)} collective-permute-done((f32[264,128]{1,0:T(8,128)S(1)}, f32[264,128]{1,0:T(8,128)S(1)}, u32[]{:S(2)}, u32[]{:S(2)}) %collective-permute-start.21) | collective-permute-done | bytes 135200 | tf_op jit(solution)/shard_map/ppermute | solution.py:398
  89.9 2.5 %collective-permute-start.25 = (f32[264,128]{1,0:T(8,128)S(1)}, f32[264,128]{1,0:T(8,128)S(1)}, u32[]{:S(2)}, u32[]{:S(2)}) collective-permute-start(f32[264,128]{1,0:T(8,128)S(1)} %get-tuple-element.92.refs_0_.refs_15_), channel_id=1, source_target_pairs={{0,12},{4,8},{8,4},{12,0},{1,13},{5,9},{9,5},{13,1},{2,14},{6,10},... | collective-permute-start | bytes 405512 | tf_op jit(solution)/shard_map/ppermute | solution.py:398
  92.4 2.7 %collective-permute-start.24 = (f32[264,128]{1,0:T(8,128)S(1)}, f32[264,128]{1,0:T(8,128)S(1)}, u32[]{:S(2)}, u32[]{:S(2)}) collective-permute-start(f32[264,128]{1,0:T(8,128)S(1)} %get-tuple-element.92.refs_0_.refs_15_), channel_id=1, source_target_pairs={{0,8},{4,12},{8,0},{12,4},{1,9},{5,13},{9,1},{13,5},{2,10},{6,14},... | collective-permute-start | bytes 405512 | tf_op jit(solution)/shard_map/ppermute | solution.py:398
  95.6 2.6 %collective-permute-done.25.refs_3_ = f32[264,128]{1,0:T(8,128)S(1)} collective-permute-done((f32[264,128]{1,0:T(8,128)S(1)}, f32[264,128]{1,0:T(8,128)S(1)}, u32[]{:S(2)}, u32[]{:S(2)}) %collective-permute-start.25) | collective-permute-done | bytes 135200 | tf_op jit(solution)/shard_map/ppermute | solution.py:398
  98.2 4.6 %collective-permute-done.24.refs_2_ = f32[264,128]{1,0:T(8,128)S(1)} collective-permute-done((f32[264,128]{1,0:T(8,128)S(1)}, f32[264,128]{1,0:T(8,128)S(1)}, u32[]{:S(2)}, u32[]{:S(2)}) %collective-permute-start.24) | collective-permute-done | bytes 135200 | tf_op jit(solution)/shard_map/ppermute | solution.py:398
  102.8 2.9 %shard_map.139 = (f32[392,128]{1,0:T(8,128)S(1)}, f32[256,128]{1,0:T(8,128)S(1)}) custom-call(s32[2]{0:T(128)S(1)} %pad_add_fusion.place, s32[4]{0:T(128)S(1)} %pad_add_fusion.2.pairs, f32[264,128]{1,0:T(8,128)S(1)} %get-tuple-element.92.refs_0_.refs_15_, f32[264,128]{1,0:T(8,128)S(1)} %collective-permute-done.23.refs_1_, ...), custom_call_target="tpu_custom_call" | custom-call | flops 805306368 | bytes 7487488 | tf_op jit(solution)/shard_map/pallas_call | solution.py:27
  105.6 1.6 collective-permute-start.26
  107.2 4.2 %collective-permute-done.26.refs_1_ = f32[392,128]{1,0:T(8,128)S(1)} collective-permute-done((f32[392,128]{1,0:T(8,128)S(1)}, f32[392,128]{1,0:T(8,128)S(1)}, u32[]{:S(2)}, u32[]{:S(2)}) %collective-permute-start.26) | collective-permute-done | bytes 200736 | tf_op jit(solution)/shard_map/ppermute | solution.py:391
  111.6 2.5 %collective-permute-start.29 = (f32[8,128]{1,0:T(8,128)S(1)}, f32[8,128]{1,0:T(8,128)S(1)}, u32[]{:S(2)}, u32[]{:S(2)}) collective-permute-start(f32[8,128]{1,0:T(8,128)S(1)} %get-tuple-element.95.refs_0_), channel_id=1, source_target_pairs={{0,12},{4,8},{8,4},{12,0},{1,13},{5,9},{9,5},{13,1},{2,14},{6,10},... | collective-permute-start | bytes 12296 | tf_op jit(solution)/shard_map/ppermute | solution.py:398
  114.1 1.9 collective-permute-start.27
  116.0 1.0 collective-permute-done.29.refs_3_
  117.0 1.6 collective-permute-done.28.refs_2_
  118.6 3.3 %shard_map.141 = (f32[256,128]{1,0:T(8,128)S(1)}, f32[256,128]{1,0:T(8,128)S(1)}, f32[256,128]{1,0:T(8,128)S(1)}, f32[256,128]{1,0:T(8,128)S(1)}, f32[256,128]{1...) custom-call(s32[2]{0:T(128)S(1)} %pad_add_fusion.place, ...), custom_call_target="tpu_custom_call" | custom-call | flops 805306368 | bytes 8486912 | tf_op jit(solution)/shard_map/pallas_call | solution.py:27
  121.9 1.0 collective-permute-start.30
  122.9 1.0 collective-permute-start.31
  123.9 2.4 %collective-permute-start.32 = (f32[256,128]{1,0:T(8,128)S(1)}, f32[256,128]{1,0:T(8,128)S(1)}, u32[]{:S(2)}, u32[]{:S(2)}) collective-permute-start(f32[256,128]{1,0:T(8,128)S(1)} %get-tuple-element.106), channel_id=1, source_target_pairs={{0,12},{4,8},{8,4},{12,0},{1,13},{5,9},{9,5},{13,1},{2,14},{6,10},... | collective-permute-start | bytes 393224 | tf_op jit(solution)/shard_map/ppermute | solution.py:398
  126.9 7.9 %collective-permute-done.31.refs_2_ = f32[256,128]{1,0:T(8,128)S(1)} collective-permute-done((f32[256,128]{1,0:T(8,128)S(1)}, f32[256,128]{1,0:T(8,128)S(1)}, u32[]{:S(2)}, u32[]{:S(2)}) %collective-permute-start.31) | collective-permute-done | bytes 131104 | tf_op jit(solution)/shard_map/ppermute | solution.py:398
  135.4 2.8 %collective-permute-start.35 = (f32[264,128]{1,0:T(8,128)S(1)}, f32[264,128]{1,0:T(8,128)S(1)}, u32[]{:S(2)}, u32[]{:S(2)}) collective-permute-start(f32[264,128]{1,0:T(8,128)S(1)} %get-tuple-element.108.refs_0_.refs_5_.refs_14_), channel_id=1, source_target_pairs={{0,12},{4,8},{8,4},{12,0},{1,13},{5,9},{9,5},{13,1},{2,14},{6,10},... | collective-permute-start | bytes 405512 | tf_op jit(solution)/shard_map/ppermute | solution.py:398
  138.2 2.1 %collective-permute-start.34 = (f32[264,128]{1,0:T(8,128)S(1)}, f32[264,128]{1,0:T(8,128)S(1)}, u32[]{:S(2)}, u32[]{:S(2)}) collective-permute-start(f32[264,128]{1,0:T(8,128)S(1)} %get-tuple-element.108.refs_0_.refs_5_.refs_14_), channel_id=1, source_target_pairs={{0,8},{4,12},{8,0},{12,4},{1,9},{5,13},{9,1},{13,5},{2,10},{6,14},... | collective-permute-start | bytes 405512 | tf_op jit(solution)/shard_map/ppermute | solution.py:398
  140.6 1.7 collective-permute-done.35.refs_3_
  142.3 4.3 %collective-permute-done.34.refs_2_ = f32[264,128]{1,0:T(8,128)S(1)} collective-permute-done((f32[264,128]{1,0:T(8,128)S(1)}, f32[264,128]{1,0:T(8,128)S(1)}, u32[]{:S(2)}, u32[]{:S(2)}) %collective-permute-start.34) | collective-permute-done | bytes 135200 | tf_op jit(solution)/shard_map/ppermute | solution.py:398
  146.6 2.9 %shard_map.143 = (f32[392,128]{1,0:T(8,128)S(1)}, f32[256,128]{1,0:T(8,128)S(1)}) custom-call(s32[2]{0:T(128)S(1)} %pad_add_fusion.place, s32[4]{0:T(128)S(1)} %pad_add_fusion.2.pairs, f32[264,128]{1,0:T(8,128)S(1)} %get-tuple-element.108.refs_0_.refs_5_.refs_14_, f32[264,128]{1,0:T(8,128)S(1)} %collective-permute-done.33.refs_1_, ...), custom_call_target="tpu_custom_call" | custom-call | flops 805306368 | bytes 7356416 | tf_op jit(solution)/shard_map/pallas_call | solution.py:27
  149.5 1.6 collective-permute-start.36
  151.1 4.2 %collective-permute-done.36.refs_1_ = f32[392,128]{1,0:T(8,128)S(1)} collective-permute-done((f32[392,128]{1,0:T(8,128)S(1)}, f32[392,128]{1,0:T(8,128)S(1)}, u32[]{:S(2)}, u32[]{:S(2)}) %collective-permute-start.36) | collective-permute-done | bytes 200736 | tf_op jit(solution)/shard_map/ppermute | solution.py:391
  155.2 2.6 %shard_map.144 = (f32[264,128]{1,0:T(8,128)S(1)}, f32[264,128]{1,0:T(8,128)S(1)}, f32[264,128]{1,0:T(8,128)S(1)}, f32[264,128]{1,0:T(8,128)S(1)}, f32[384,128]{1,0:T(8,128)S(1)}, /*index=5*/f32[8,128]{1,0:T(8,128)S(1)}) custom-call(s32[2]{0:T(128)S(1)} %pad_add_fusion.place, s32[4]{0:T(128)S(1)} %pad_add_fusion.2.pairs, ...), custom_call_target="tpu_custom_call" | custom-call | flops 805306368 | bytes 6823936 | tf_op jit(solution)/shard_map/pallas_call | solution.py:27
  158.1 3.2 %collective-permute-start.38 = (f32[264,128]{1,0:T(8,128)S(1)}, f32[264,128]{1,0:T(8,128)S(1)}, u32[]{:S(2)}, u32[]{:S(2)}) collective-permute-start(f32[264,128]{1,0:T(8,128)S(1)} %get-tuple-element.113), channel_id=1, source_target_pairs={{0,8},{4,12},{8,0},{12,4},{1,9},{5,13},{9,1},{13,5},{2,10},{6,14},... | collective-permute-start | bytes 405512 | tf_op jit(solution)/shard_map/ppermute | solution.py:398
  162.3 3.8 %collective-permute-done.37.refs_1_ = f32[264,128]{1,0:T(8,128)S(1)} collective-permute-done((f32[264,128]{1,0:T(8,128)S(1)}, f32[264,128]{1,0:T(8,128)S(1)}, u32[]{:S(2)}, u32[]{:S(2)}) %collective-permute-start.37) | collective-permute-done | bytes 135200 | tf_op jit(solution)/shard_map/ppermute | solution.py:398
  166.1 4.6 %collective-permute-done.38.refs_2_ = f32[264,128]{1,0:T(8,128)S(1)} collective-permute-done((f32[264,128]{1,0:T(8,128)S(1)}, f32[264,128]{1,0:T(8,128)S(1)}, u32[]{:S(2)}, u32[]{:S(2)}) %collective-permute-start.38) | collective-permute-done | bytes 135200 | tf_op jit(solution)/shard_map/ppermute | solution.py:398
  170.9 2.6 %collective-permute-start.42 = (f32[264,128]{1,0:T(8,128)S(1)}, f32[264,128]{1,0:T(8,128)S(1)}, u32[]{:S(2)}, u32[]{:S(2)}) collective-permute-start(f32[264,128]{1,0:T(8,128)S(1)} %get-tuple-element.117.refs_0_.refs_15_), channel_id=1, source_target_pairs={{0,12},{4,8},{8,4},{12,0},{1,13},{5,9},{9,5},{13,1},{2,14},{6,10},... | collective-permute-start | bytes 405512 | tf_op jit(solution)/shard_map/ppermute | solution.py:398
  173.4 1.4 collective-permute-start.41
  175.3 2.5 %collective-permute-done.42.refs_3_ = f32[264,128]{1,0:T(8,128)S(1)} collective-permute-done((f32[264,128]{1,0:T(8,128)S(1)}, f32[264,128]{1,0:T(8,128)S(1)}, u32[]{:S(2)}, u32[]{:S(2)}) %collective-permute-start.42) | collective-permute-done | bytes 135200 | tf_op jit(solution)/shard_map/ppermute | solution.py:398
  177.8 4.3 %collective-permute-done.41.refs_2_ = f32[264,128]{1,0:T(8,128)S(1)} collective-permute-done((f32[264,128]{1,0:T(8,128)S(1)}, f32[264,128]{1,0:T(8,128)S(1)}, u32[]{:S(2)}, u32[]{:S(2)}) %collective-permute-start.41) | collective-permute-done | bytes 135200 | tf_op jit(solution)/shard_map/ppermute | solution.py:398
  182.1 3.5 %shard_map.146 = (f32[392,128]{1,0:T(8,128)S(1)}, f32[256,128]{1,0:T(8,128)}) custom-call(s32[2]{0:T(128)S(1)} %pad_add_fusion.place, s32[4]{0:T(128)S(1)} %pad_add_fusion.2.pairs, f32[264,128]{1,0:T(8,128)S(1)} %get-tuple-element.117.refs_0_.refs_15_, f32[264,128]{1,0:T(8,128)S(1)} %collective-permute-done.40.refs_1_, ...), custom_call_target="tpu_custom_call" | custom-call | flops 805306368 | bytes 7487488 | tf_op jit(solution)/shard_map/pallas_call | solution.py:27
  185.6 1.5 collective-permute-start.43
  187.1 4.2 %collective-permute-done.43.refs_1_ = f32[392,128]{1,0:T(8,128)S(1)} collective-permute-done((f32[392,128]{1,0:T(8,128)S(1)}, f32[392,128]{1,0:T(8,128)S(1)}, u32[]{:S(2)}, u32[]{:S(2)}) %collective-permute-start.43) | collective-permute-done | bytes 200736 | tf_op jit(solution)/shard_map/ppermute | solution.py:391
  191.5 2.4 %collective-permute-start.46 = (f32[8,128]{1,0:T(8,128)S(1)}, f32[8,128]{1,0:T(8,128)S(1)}, u32[]{:S(2)}, u32[]{:S(2)}) collective-permute-start(f32[8,128]{1,0:T(8,128)S(1)} %get-tuple-element.120.refs_0_), channel_id=1, source_target_pairs={{0,12},{4,8},{8,4},{12,0},{1,13},{5,9},{9,5},{13,1},{2,14},{6,10},... | collective-permute-start | bytes 12296 | tf_op jit(solution)/shard_map/ppermute | solution.py:398
  193.9 2.0 collective-permute-start.44
  195.9 1.0 collective-permute-done.46.refs_3_
  196.9 1.5 collective-permute-done.45.refs_2_
  198.7 1.9 collective-permute-done.47.got
  200.6 1.7 shard_map.149
  (80 shorter events, 16.0 us)
Async XLA Ops:
  0.6 18.6 %collective-permute-start.8 = (f32[24,128,128]{2,1,0:T(8,128)}, f32[24,128,128]{2,1,0:T(8,128)S(1)}, u32[]{:S(2)}, u32[]{:S(2)}) collective-permute-start(f32[24,128,128]{2,1,0:T(8,128)} %bitcast.6), channel_id=1, source_target_pairs={{0,1},{1,0},{2,3},{3,2},{4,5},{5,4},{6,7},{7,6},{8,9},{9,8},{10,11... | collective-permute-start | bytes 4718600 | tf_op jit(solution)/shard_map/ppermute | solution.py:388
  1.1 17.2 %collective-permute-start.9 = (f32[4,128,128]{2,1,0:T(8,128)}, f32[4,128,128]{2,1,0:T(8,128)S(1)}, u32[]{:S(2)}, u32[]{:S(2)}) collective-permute-start(f32[4,128,128]{2,1,0:T(8,128)} %bitcast.8), channel_id=1, source_target_pairs={{0,1},{1,0},{2,3},{3,2},{4,5},{5,4},{6,7},{7,6},{8,9},{9,8},{10,11... | collective-permute-start | bytes 786440 | tf_op jit(solution)/shard_map/ppermute | solution.py:388
  1.2 9.1 %collective-permute-start.3 = (f32[256,128]{1,0:T(8,128)}, f32[256,128]{1,0:T(8,128)S(1)}, u32[]{:S(2)}, u32[]{:S(2)}) collective-permute-start(f32[256,128]{1,0:T(8,128)} %x.1), channel_id=1, source_target_pairs={{0,12},{4,8},{8,4},{12,0},{1,13},{5,9},{9,5},{13,1},{2,14},{6,10},... | collective-permute-start | bytes 393224 | tf_op jit(solution)/shard_map/ppermute | solution.py:398
  7.8 1.1 collective-permute-start
  7.8 9.9 %collective-permute-start.2 = (f32[256,128]{1,0:T(8,128)}, f32[256,128]{1,0:T(8,128)S(1)}, u32[]{:S(2)}, u32[]{:S(2)}) collective-permute-start(f32[256,128]{1,0:T(8,128)} %x.1), channel_id=1, source_target_pairs={{0,8},{4,12},{8,0},{12,4},{1,9},{5,13},{9,1},{13,5},{2,10},{6,14},... | collective-permute-start | bytes 393224 | tf_op jit(solution)/shard_map/ppermute | solution.py:398
  9.0 8.8 %collective-permute-start.1 = (f32[256,128]{1,0:T(8,128)}, f32[256,128]{1,0:T(8,128)S(1)}, u32[]{:S(2)}, u32[]{:S(2)}) collective-permute-start(f32[256,128]{1,0:T(8,128)} %x.1), channel_id=1, source_target_pairs={{0,4},{4,0},{8,12},{12,8},{1,5},{5,1},{9,13},{13,9},{2,6},{6,2},{1... | collective-permute-start | bytes 393224 | tf_op jit(solution)/shard_map/ppermute | solution.py:398
  10.3 14.3 %collective-permute-start.4 = (f32[256,128]{1,0:T(8,128)}, f32[256,128]{1,0:T(8,128)S(1)}, u32[]{:S(2)}, u32[]{:S(2)}) collective-permute-start(f32[256,128]{1,0:T(8,128)} %x.1), channel_id=1, source_target_pairs={{0,1},{1,0},{2,3},{3,2},{4,5},{5,4},{6,7},{7,6},{8,9},{9,8},{10,11... | collective-permute-start | bytes 393224 | tf_op jit(solution)/shard_map/ppermute | solution.py:388
  17.8 6.9 %collective-permute-start.7 = (f32[256,128]{1,0:T(8,128)S(1)}, f32[256,128]{1,0:T(8,128)S(1)}, u32[]{:S(2)}, u32[]{:S(2)}) collective-permute-start(f32[256,128]{1,0:T(8,128)S(1)} %collective-permute-done.3.refs_3_), channel_id=1, source_target_pairs={{0,1},{1,0},{2,3},{3,2},{4,5},{5,4},{6,7},{7,6},{8,9},{9,8},{10,11... | collective-permute-start | bytes 393224 | tf_op jit(solution)/shard_map/ppermute | solution.py:388
  17.8 6.9 %collective-permute-start.6 = (f32[256,128]{1,0:T(8,128)S(1)}, f32[256,128]{1,0:T(8,128)S(1)}, u32[]{:S(2)}, u32[]{:S(2)}) collective-permute-start(f32[256,128]{1,0:T(8,128)S(1)} %collective-permute-done.2.refs_2_), channel_id=1, source_target_pairs={{0,1},{1,0},{2,3},{3,2},{4,5},{5,4},{6,7},{7,6},{8,9},{9,8},{10,11... | collective-permute-start | bytes 393224 | tf_op jit(solution)/shard_map/ppermute | solution.py:388
  18.3 6.4 %collective-permute-start.5 = (f32[256,128]{1,0:T(8,128)S(1)}, f32[256,128]{1,0:T(8,128)S(1)}, u32[]{:S(2)}, u32[]{:S(2)}) collective-permute-start(f32[256,128]{1,0:T(8,128)S(1)} %collective-permute-done.1.refs_1_), channel_id=1, source_target_pairs={{0,1},{1,0},{2,3},{3,2},{4,5},{5,4},{6,7},{7,6},{8,9},{9,8},{10,11... | collective-permute-start | bytes 393224 | tf_op jit(solution)/shard_map/ppermute | solution.py:388
  19.3 1.4 copy-start
  20.7 0.9 copy-start.6
  21.6 3.1 %copy-start.1 = (f32[256,128]{1,0:T(8,128)S(1)}, f32[256,128]{1,0:T(8,128)}, u32[]{:S(2)}) copy-start(f32[256,128]{1,0:T(8,128)} %x.1) | copy-start | bytes 393220
  24.7 4.7 %copy-start.2 = (f32[768,128]{1,0:T(8,128)S(1)}, f32[768,128]{1,0:T(8,128)}, u32[]{:S(2)}) copy-start(f32[768,128]{1,0:T(8,128)} %refs_0_.3) | copy-start | bytes 1179652
  24.7 4.6 %copy-start.3 = (f32[768,128]{1,0:T(8,128)S(1)}, f32[768,128]{1,0:T(8,128)}, u32[]{:S(2)}) copy-start(f32[768,128]{1,0:T(8,128)} %refs_1_.1) | copy-start | bytes 1179652
  24.7 4.6 %copy-start.4 = (f32[768,128]{1,0:T(8,128)S(1)}, f32[768,128]{1,0:T(8,128)}, u32[]{:S(2)}) copy-start(f32[768,128]{1,0:T(8,128)} %refs_2_.1) | copy-start | bytes 1179652
  24.7 4.6 %copy-start.5 = (f32[768,128]{1,0:T(8,128)S(1)}, f32[768,128]{1,0:T(8,128)}, u32[]{:S(2)}) copy-start(f32[768,128]{1,0:T(8,128)} %refs_3_.1) | copy-start | bytes 1179652
  27.8 7.3 %collective-permute-start.10 = (f32[384,128]{1,0:T(8,128)S(1)}, f32[384,128]{1,0:T(8,128)S(1)}, u32[]{:S(2)}, u32[]{:S(2)}) collective-permute-start(f32[384,128]{1,0:T(8,128)S(1)} %get-tuple-element.69.refs_0_), channel_id=1, source_target_pairs={{0,2},{1,3},{2,0},{3,1},{4,6},{5,7},{6,4},{7,5},{8,10},{9,11},{10,... | collective-permute-start | bytes 589832 | tf_op jit(solution)/shard_map/ppermute | solution.py:391
  35.1 7.1 %copy-start.7 = (f32[256,128]{1,0:T(8,128)S(1)}, f32[256,128]{1,0:T(8,128)}, u32[]{:S(2)}) copy-start(f32[256,128]{1,0:T(8,128)} %q.1) | copy-start | bytes 393220
  35.1 7.1 %copy-start.8 = (f32[256]{0:T(256)S(1)}, f32[256]{0:T(256)}, u32[]{:S(2)}) copy-start(f32[256]{0:T(256)} %param.13) | copy-start | bytes 3076
  37.7 7.5 %collective-permute-start.11 = (f32[272,128]{1,0:T(8,128)S(1)}, f32[272,128]{1,0:T(8,128)S(1)}, u32[]{:S(2)}, u32[]{:S(2)}) collective-permute-start(f32[272,128]{1,0:T(8,128)S(1)} %get-tuple-element.77), channel_id=1, source_target_pairs={{0,4},{4,0},{8,12},{12,8},{1,5},{5,1},{9,13},{13,9},{2,6},{6,2},{1... | collective-permute-start | bytes 417800 | tf_op jit(solution)/shard_map/ppermute | solution.py:398
  37.8 13.5 %collective-permute-start.12 = (f32[272,128]{1,0:T(8,128)S(1)}, f32[272,128]{1,0:T(8,128)S(1)}, u32[]{:S(2)}, u32[]{:S(2)}) collective-permute-start(f32[272,128]{1,0:T(8,128)S(1)} %get-tuple-element.78), channel_id=1, source_target_pairs={{0,8},{4,12},{8,0},{12,4},{1,9},{5,13},{9,1},{13,5},{2,10},{6,14},... | collective-permute-start | bytes 417800 | tf_op jit(solution)/shard_map/ppermute | solution.py:398
  40.8 10.5 %collective-permute-start.13 = (f32[272,128]{1,0:T(8,128)S(1)}, f32[272,128]{1,0:T(8,128)S(1)}, u32[]{:S(2)}, u32[]{:S(2)}) collective-permute-start(f32[272,128]{1,0:T(8,128)S(1)} %get-tuple-element.79), channel_id=1, source_target_pairs={{0,12},{4,8},{8,4},{12,0},{1,13},{5,9},{9,5},{13,1},{2,14},{6,10},... | collective-permute-start | bytes 417800 | tf_op jit(solution)/shard_map/ppermute | solution.py:398
  42.2 1.7 collective-permute-start.14
  42.2 1.3 collective-permute-start.15
  52.3 8.4 %collective-permute-start.18 = (f32[264,128]{1,0:T(8,128)S(1)}, f32[264,128]{1,0:T(8,128)S(1)}, u32[]{:S(2)}, u32[]{:S(2)}) collective-permute-start(f32[264,128]{1,0:T(8,128)S(1)} %get-tuple-element.82.refs_0_.refs_5_.refs_14_), channel_id=1, source_target_pairs={{0,12},{4,8},{8,4},{12,0},{1,13},{5,9},{9,5},{13,1},{2,14},{6,10},... | collective-permute-start | bytes 405512 | tf_op jit(solution)/shard_map/ppermute | solution.py:398
  54.8 11.1 %collective-permute-start.17 = (f32[264,128]{1,0:T(8,128)S(1)}, f32[264,128]{1,0:T(8,128)S(1)}, u32[]{:S(2)}, u32[]{:S(2)}) collective-permute-start(f32[264,128]{1,0:T(8,128)S(1)} %get-tuple-element.82.refs_0_.refs_5_.refs_14_), channel_id=1, source_target_pairs={{0,8},{4,12},{8,0},{12,4},{1,9},{5,13},{9,1},{13,5},{2,10},{6,14},... | collective-permute-start | bytes 405512 | tf_op jit(solution)/shard_map/ppermute | solution.py:398
  56.1 9.8 %collective-permute-start.16 = (f32[264,128]{1,0:T(8,128)S(1)}, f32[264,128]{1,0:T(8,128)S(1)}, u32[]{:S(2)}, u32[]{:S(2)}) collective-permute-start(f32[264,128]{1,0:T(8,128)S(1)} %get-tuple-element.82.refs_0_.refs_5_.refs_14_), channel_id=1, source_target_pairs={{0,4},{4,0},{8,12},{12,8},{1,5},{5,1},{9,13},{13,9},{2,6},{6,2},{1... | collective-permute-start | bytes 405512 | tf_op jit(solution)/shard_map/ppermute | solution.py:398
  68.7 5.8 %collective-permute-start.19 = (f32[392,128]{1,0:T(8,128)S(1)}, f32[392,128]{1,0:T(8,128)S(1)}, u32[]{:S(2)}, u32[]{:S(2)}) collective-permute-start(f32[392,128]{1,0:T(8,128)S(1)} %get-tuple-element.83.refs_0_), channel_id=1, source_target_pairs={{0,2},{1,3},{2,0},{3,1},{4,6},{5,7},{6,4},{7,5},{8,10},{9,11},{10,... | collective-permute-start | bytes 602120 | tf_op jit(solution)/shard_map/ppermute | solution.py:391
  77.3 5.3 %collective-permute-start.20 = (f32[264,128]{1,0:T(8,128)S(1)}, f32[264,128]{1,0:T(8,128)S(1)}, u32[]{:S(2)}, u32[]{:S(2)}) collective-permute-start(f32[264,128]{1,0:T(8,128)S(1)} %get-tuple-element.86), channel_id=1, source_target_pairs={{0,4},{4,0},{8,12},{12,8},{1,5},{5,1},{9,13},{13,9},{2,6},{6,2},{1... | collective-permute-start | bytes 405512 | tf_op jit(solution)/shard_map/ppermute | solution.py:398
  77.4 12.3 %collective-permute-start.21 = (f32[264,128]{1,0:T(8,128)S(1)}, f32[264,128]{1,0:T(8,128)S(1)}, u32[]{:S(2)}, u32[]{:S(2)}) collective-permute-start(f32[264,128]{1,0:T(8,128)S(1)} %get-tuple-element.87), channel_id=1, source_target_pairs={{0,8},{4,12},{8,0},{12,4},{1,9},{5,13},{9,1},{13,5},{2,10},{6,14},... | collective-permute-start | bytes 405512 | tf_op jit(solution)/shard_map/ppermute | solution.py:398
  80.8 9.0 %collective-permute-start.22 = (f32[264,128]{1,0:T(8,128)S(1)}, f32[264,128]{1,0:T(8,128)S(1)}, u32[]{:S(2)}, u32[]{:S(2)}) collective-permute-start(f32[264,128]{1,0:T(8,128)S(1)} %get-tuple-element.88), channel_id=1, source_target_pairs={{0,12},{4,8},{8,4},{12,0},{1,13},{5,9},{9,5},{13,1},{2,14},{6,10},... | collective-permute-start | bytes 405512 | tf_op jit(solution)/shard_map/ppermute | solution.py:398
  89.9 8.3 %collective-permute-start.25 = (f32[264,128]{1,0:T(8,128)S(1)}, f32[264,128]{1,0:T(8,128)S(1)}, u32[]{:S(2)}, u32[]{:S(2)}) collective-permute-start(f32[264,128]{1,0:T(8,128)S(1)} %get-tuple-element.92.refs_0_.refs_15_), channel_id=1, source_target_pairs={{0,12},{4,8},{8,4},{12,0},{1,13},{5,9},{9,5},{13,1},{2,14},{6,10},... | collective-permute-start | bytes 405512 | tf_op jit(solution)/shard_map/ppermute | solution.py:398
  92.4 10.4 %collective-permute-start.24 = (f32[264,128]{1,0:T(8,128)S(1)}, f32[264,128]{1,0:T(8,128)S(1)}, u32[]{:S(2)}, u32[]{:S(2)}) collective-permute-start(f32[264,128]{1,0:T(8,128)S(1)} %get-tuple-element.92.refs_0_.refs_15_), channel_id=1, source_target_pairs={{0,8},{4,12},{8,0},{12,4},{1,9},{5,13},{9,1},{13,5},{2,10},{6,14},... | collective-permute-start | bytes 405512 | tf_op jit(solution)/shard_map/ppermute | solution.py:398
  95.2 7.6 %collective-permute-start.23 = (f32[264,128]{1,0:T(8,128)S(1)}, f32[264,128]{1,0:T(8,128)S(1)}, u32[]{:S(2)}, u32[]{:S(2)}) collective-permute-start(f32[264,128]{1,0:T(8,128)S(1)} %get-tuple-element.92.refs_0_.refs_15_), channel_id=1, source_target_pairs={{0,4},{4,0},{8,12},{12,8},{1,5},{5,1},{9,13},{13,9},{2,6},{6,2},{1... | collective-permute-start | bytes 405512 | tf_op jit(solution)/shard_map/ppermute | solution.py:398
  105.6 5.8 %collective-permute-start.26 = (f32[392,128]{1,0:T(8,128)S(1)}, f32[392,128]{1,0:T(8,128)S(1)}, u32[]{:S(2)}, u32[]{:S(2)}) collective-permute-start(f32[392,128]{1,0:T(8,128)S(1)} %get-tuple-element.93.refs_0_), channel_id=1, source_target_pairs={{0,2},{1,3},{2,0},{3,1},{4,6},{5,7},{6,4},{7,5},{8,10},{9,11},{10,... | collective-permute-start | bytes 602120 | tf_op jit(solution)/shard_map/ppermute | solution.py:391
  111.6 5.4 %collective-permute-start.29 = (f32[8,128]{1,0:T(8,128)S(1)}, f32[8,128]{1,0:T(8,128)S(1)}, u32[]{:S(2)}, u32[]{:S(2)}) collective-permute-start(f32[8,128]{1,0:T(8,128)S(1)} %get-tuple-element.95.refs_0_), channel_id=1, source_target_pairs={{0,12},{4,8},{8,4},{12,0},{1,13},{5,9},{9,5},{13,1},{2,14},{6,10},... | collective-permute-start | bytes 12296 | tf_op jit(solution)/shard_map/ppermute | solution.py:398
  114.1 4.5 %collective-permute-start.28 = (f32[8,128]{1,0:T(8,128)S(1)}, f32[8,128]{1,0:T(8,128)S(1)}, u32[]{:S(2)}, u32[]{:S(2)}) collective-permute-start(f32[8,128]{1,0:T(8,128)S(1)} %get-tuple-element.95.refs_0_), channel_id=1, source_target_pairs={{0,8},{4,12},{8,0},{12,4},{1,9},{5,13},{9,1},{13,5},{2,10},{6,14},... | collective-permute-start | bytes 12296 | tf_op jit(solution)/shard_map/ppermute | solution.py:398
  114.1 4.5 %collective-permute-start.27 = (f32[8,128]{1,0:T(8,128)S(1)}, f32[8,128]{1,0:T(8,128)S(1)}, u32[]{:S(2)}, u32[]{:S(2)}) collective-permute-start(f32[8,128]{1,0:T(8,128)S(1)} %get-tuple-element.95.refs_0_), channel_id=1, source_target_pairs={{0,4},{4,0},{8,12},{12,8},{1,5},{5,1},{9,13},{13,9},{2,6},{6,2},{1... | collective-permute-start | bytes 12296 | tf_op jit(solution)/shard_map/ppermute | solution.py:398
  121.9 5.0 %collective-permute-start.30 = (f32[256,128]{1,0:T(8,128)S(1)}, f32[256,128]{1,0:T(8,128)S(1)}, u32[]{:S(2)}, u32[]{:S(2)}) collective-permute-start(f32[256,128]{1,0:T(8,128)S(1)} %get-tuple-element.104), channel_id=1, source_target_pairs={{0,4},{4,0},{8,12},{12,8},{1,5},{5,1},{9,13},{13,9},{2,6},{6,2},{1... | collective-permute-start | bytes 393224 | tf_op jit(solution)/shard_map/ppermute | solution.py:398
  122.9 11.8 %collective-permute-start.31 = (f32[256,128]{1,0:T(8,128)S(1)}, f32[256,128]{1,0:T(8,128)S(1)}, u32[]{:S(2)}, u32[]{:S(2)}) collective-permute-start(f32[256,128]{1,0:T(8,128)S(1)} %get-tuple-element.105), channel_id=1, source_target_pairs={{0,8},{4,12},{8,0},{12,4},{1,9},{5,13},{9,1},{13,5},{2,10},{6,14},... | collective-permute-start | bytes 393224 | tf_op jit(solution)/shard_map/ppermute | solution.py:398
  123.9 10.8 %collective-permute-start.32 = (f32[256,128]{1,0:T(8,128)S(1)}, f32[256,128]{1,0:T(8,128)S(1)}, u32[]{:S(2)}, u32[]{:S(2)}) collective-permute-start(f32[256,128]{1,0:T(8,128)S(1)} %get-tuple-element.106), channel_id=1, source_target_pairs={{0,12},{4,8},{8,4},{12,0},{1,13},{5,9},{9,5},{13,1},{2,14},{6,10},... | collective-permute-start | bytes 393224 | tf_op jit(solution)/shard_map/ppermute | solution.py:398
  135.4 6.9 %collective-permute-start.35 = (f32[264,128]{1,0:T(8,128)S(1)}, f32[264,128]{1,0:T(8,128)S(1)}, u32[]{:S(2)}, u32[]{:S(2)}) collective-permute-start(f32[264,128]{1,0:T(8,128)S(1)} %get-tuple-element.108.refs_0_.refs_5_.refs_14_), channel_id=1, source_target_pairs={{0,12},{4,8},{8,4},{12,0},{1,13},{5,9},{9,5},{13,1},{2,14},{6,10},... | collective-permute-start | bytes 405512 | tf_op jit(solution)/shard_map/ppermute | solution.py:398
  138.2 8.5 %collective-permute-start.34 = (f32[264,128]{1,0:T(8,128)S(1)}, f32[264,128]{1,0:T(8,128)S(1)}, u32[]{:S(2)}, u32[]{:S(2)}) collective-permute-start(f32[264,128]{1,0:T(8,128)S(1)} %get-tuple-element.108.refs_0_.refs_5_.refs_14_), channel_id=1, source_target_pairs={{0,8},{4,12},{8,0},{12,4},{1,9},{5,13},{9,1},{13,5},{2,10},{6,14},... | collective-permute-start | bytes 405512 | tf_op jit(solution)/shard_map/ppermute | solution.py:398
  140.3 6.3 %collective-permute-start.33 = (f32[264,128]{1,0:T(8,128)S(1)}, f32[264,128]{1,0:T(8,128)S(1)}, u32[]{:S(2)}, u32[]{:S(2)}) collective-permute-start(f32[264,128]{1,0:T(8,128)S(1)} %get-tuple-element.108.refs_0_.refs_5_.refs_14_), channel_id=1, source_target_pairs={{0,4},{4,0},{8,12},{12,8},{1,5},{5,1},{9,13},{13,9},{2,6},{6,2},{1... | collective-permute-start | bytes 405512 | tf_op jit(solution)/shard_map/ppermute | solution.py:398
  149.5 5.8 %collective-permute-start.36 = (f32[392,128]{1,0:T(8,128)S(1)}, f32[392,128]{1,0:T(8,128)S(1)}, u32[]{:S(2)}, u32[]{:S(2)}) collective-permute-start(f32[392,128]{1,0:T(8,128)S(1)} %get-tuple-element.109.refs_0_), channel_id=1, source_target_pairs={{0,2},{1,3},{2,0},{3,1},{4,6},{5,7},{6,4},{7,5},{8,10},{9,11},{10,... | collective-permute-start | bytes 602120 | tf_op jit(solution)/shard_map/ppermute | solution.py:391
  157.9 8.3 %collective-permute-start.37 = (f32[264,128]{1,0:T(8,128)S(1)}, f32[264,128]{1,0:T(8,128)S(1)}, u32[]{:S(2)}, u32[]{:S(2)}) collective-permute-start(f32[264,128]{1,0:T(8,128)S(1)} %get-tuple-element.112), channel_id=1, source_target_pairs={{0,4},{4,0},{8,12},{12,8},{1,5},{5,1},{9,13},{13,9},{2,6},{6,2},{1... | collective-permute-start | bytes 405512 | tf_op jit(solution)/shard_map/ppermute | solution.py:398
  158.1 12.6 %collective-permute-start.38 = (f32[264,128]{1,0:T(8,128)S(1)}, f32[264,128]{1,0:T(8,128)S(1)}, u32[]{:S(2)}, u32[]{:S(2)}) collective-permute-start(f32[264,128]{1,0:T(8,128)S(1)} %get-tuple-element.113), channel_id=1, source_target_pairs={{0,8},{4,12},{8,0},{12,4},{1,9},{5,13},{9,1},{13,5},{2,10},{6,14},... | collective-permute-start | bytes 405512 | tf_op jit(solution)/shard_map/ppermute | solution.py:398
  161.3 9.4 %collective-permute-start.39 = (f32[264,128]{1,0:T(8,128)S(1)}, f32[264,128]{1,0:T(8,128)S(1)}, u32[]{:S(2)}, u32[]{:S(2)}) collective-permute-start(f32[264,128]{1,0:T(8,128)S(1)} %get-tuple-element.114), channel_id=1, source_target_pairs={{0,12},{4,8},{8,4},{12,0},{1,13},{5,9},{9,5},{13,1},{2,14},{6,10},... | collective-permute-start | bytes 405512 | tf_op jit(solution)/shard_map/ppermute | solution.py:398
  170.9 7.0 %collective-permute-start.42 = (f32[264,128]{1,0:T(8,128)S(1)}, f32[264,128]{1,0:T(8,128)S(1)}, u32[]{:S(2)}, u32[]{:S(2)}) collective-permute-start(f32[264,128]{1,0:T(8,128)S(1)} %get-tuple-element.117.refs_0_.refs_15_), channel_id=1, source_target_pairs={{0,12},{4,8},{8,4},{12,0},{1,13},{5,9},{9,5},{13,1},{2,14},{6,10},... | collective-permute-start | bytes 405512 | tf_op jit(solution)/shard_map/ppermute | solution.py:398
  173.4 8.7 %collective-permute-start.41 = (f32[264,128]{1,0:T(8,128)S(1)}, f32[264,128]{1,0:T(8,128)S(1)}, u32[]{:S(2)}, u32[]{:S(2)}) collective-permute-start(f32[264,128]{1,0:T(8,128)S(1)} %get-tuple-element.117.refs_0_.refs_15_), channel_id=1, source_target_pairs={{0,8},{4,12},{8,0},{12,4},{1,9},{5,13},{9,1},{13,5},{2,10},{6,14},... | collective-permute-start | bytes 405512 | tf_op jit(solution)/shard_map/ppermute | solution.py:398
  174.8 7.3 %collective-permute-start.40 = (f32[264,128]{1,0:T(8,128)S(1)}, f32[264,128]{1,0:T(8,128)S(1)}, u32[]{:S(2)}, u32[]{:S(2)}) collective-permute-start(f32[264,128]{1,0:T(8,128)S(1)} %get-tuple-element.117.refs_0_.refs_15_), channel_id=1, source_target_pairs={{0,4},{4,0},{8,12},{12,8},{1,5},{5,1},{9,13},{13,9},{2,6},{6,2},{1... | collective-permute-start | bytes 405512 | tf_op jit(solution)/shard_map/ppermute | solution.py:398
  185.6 5.7 %collective-permute-start.43 = (f32[392,128]{1,0:T(8,128)S(1)}, f32[392,128]{1,0:T(8,128)S(1)}, u32[]{:S(2)}, u32[]{:S(2)}) collective-permute-start(f32[392,128]{1,0:T(8,128)S(1)} %get-tuple-element.118.refs_0_), channel_id=1, source_target_pairs={{0,2},{1,3},{2,0},{3,1},{4,6},{5,7},{6,4},{7,5},{8,10},{9,11},{10,... | collective-permute-start | bytes 602120 | tf_op jit(solution)/shard_map/ppermute | solution.py:391
  191.5 5.4 %collective-permute-start.46 = (f32[8,128]{1,0:T(8,128)S(1)}, f32[8,128]{1,0:T(8,128)S(1)}, u32[]{:S(2)}, u32[]{:S(2)}) collective-permute-start(f32[8,128]{1,0:T(8,128)S(1)} %get-tuple-element.120.refs_0_), channel_id=1, source_target_pairs={{0,12},{4,8},{8,4},{12,0},{1,13},{5,9},{9,5},{13,1},{2,14},{6,10},... | collective-permute-start | bytes 12296 | tf_op jit(solution)/shard_map/ppermute | solution.py:398
  193.9 4.5 %collective-permute-start.45 = (f32[8,128]{1,0:T(8,128)S(1)}, f32[8,128]{1,0:T(8,128)S(1)}, u32[]{:S(2)}, u32[]{:S(2)}) collective-permute-start(f32[8,128]{1,0:T(8,128)S(1)} %get-tuple-element.120.refs_0_), channel_id=1, source_target_pairs={{0,8},{4,12},{8,0},{12,4},{1,9},{5,13},{9,1},{13,5},{2,10},{6,14},... | collective-permute-start | bytes 12296 | tf_op jit(solution)/shard_map/ppermute | solution.py:398
  193.9 4.5 %collective-permute-start.44 = (f32[8,128]{1,0:T(8,128)S(1)}, f32[8,128]{1,0:T(8,128)S(1)}, u32[]{:S(2)}, u32[]{:S(2)}) collective-permute-start(f32[8,128]{1,0:T(8,128)S(1)} %get-tuple-element.120.refs_0_), channel_id=1, source_target_pairs={{0,4},{4,0},{8,12},{12,8},{1,5},{5,1},{9,13},{13,9},{2,6},{6,2},{1... | collective-permute-start | bytes 12296 | tf_op jit(solution)/shard_map/ppermute | solution.py:398
  198.6 2.0 collective-permute-start.47

commit v3 on v0

v3 whole, which is shorter than its diff:
```python
import functools

import jax
import jax.numpy as jnp
from jax import lax
from jax.experimental import pallas as pl
from jax.experimental.pallas import tpu as pltpu
from jax.sharding import PartitionSpec as P

ADMM_ITERS = 2
RHO = 0.5
SIGMA = 1e-06
RELAX = 1.6
BLK = 128
LANES = 128
HALF = 64
SC = 8
F32 = jnp.float32
BF16 = jnp.bfloat16

VMEM = pl.BlockSpec(memory_space=pltpu.VMEM)
SMEM = pl.BlockSpec(memory_space=pltpu.SMEM)


def call(body, outs, ins, smem=(), scratch=(), flops=0):
    n_bytes = sum(v.size * v.dtype.itemsize for v in ins)
    return pl.pallas_call(
        body,
        out_shape=[jax.ShapeDtypeStruct(s, d) for s, d in outs],
        in_specs=[SMEM] * len(smem) + [VMEM] * len(ins),
        out_specs=[VMEM] * len(outs),
        scratch_shapes=list(scratch),
        compiler_params=pltpu.CompilerParams(vmem_limit_bytes=30 * 1024 * 1024),
        cost_estimate=pl.CostEstimate(flops=flops, bytes_accessed=n_bytes, transcendentals=0),
    )(*smem, *ins)


def low_half(shape):
    return lax.broadcasted_iota(jnp.int32, shape, 1) < HALF


def turn(v):
    return pltpu.roll(v, HALF, 1)


def fold(v):
    return v + turn(v)


def col_sum(v):
    return fold(jnp.sum(v, axis=0, keepdims=True))


def split_bf16(v):
    hi = v.astype(BF16).astype(F32)
    return hi, v - hi


def pair_up(v):
    hi, lo = split_bf16(v)
    low = low_half(v.shape)
    first = jnp.where(low, hi, turn(lo)).astype(BF16)
    second = jnp.where(low, turn(hi), lo).astype(BF16)
    return first, second


def dot(a, b):
    return jnp.dot(a, b, preferred_element_type=F32)


def pack_rows(*rows):
    at = lax.broadcasted_iota(jnp.int32, (SC, LANES), 0)
    tile = jnp.zeros((SC, LANES), F32)
    for k, row in enumerate(rows):
        tile = jnp.where(at == k, row, tile)
    return tile


def pick(near, a, b):
    low = low_half(a.shape)
    return jnp.where(low, jnp.where(near == 0, a, turn(a)), jnp.where(near == 0, turn(b), b))


def pack_kernel(place, x, q, z, y, lower, upper, same, diff, zy, bounds):
    mine = place[1]
    theirs = 1 - mine
    same[...] = pick(mine, x[...], q[...])
    diff[...] = pick(theirs, x[...], q[...])
    zy[...] = pick(theirs, z[...], y[...])
    bounds[...] = pick(theirs, lower[...], upper[...])


def gather_kernel(n, own, place, *refs):
    msgs, (x, q, full) = refs[:n], refs[n:]
    half = x.shape[0]
    for k in range(n):
        at = pl.multiple_of(lax.bitwise_xor(place[0], k) * own, own)
        full[pl.ds(at, own), :] = msgs[k][...]
    first, second = full[0:half, :], full[half:, :]
    low = low_half(first.shape)
    x[...] = jnp.where(low, first, turn(second))
    q[...] = jnp.where(low, turn(first), second)


def slab_kernel(place, a, b, got, a_out, b_out):
    mine = place[1]
    low = low_half(a.shape)
    av = jnp.where(mine == 0, a[...], turn(a[...]))
    bv = jnp.where(mine == 0, b[...], turn(b[...]))
    a_out[...] = jnp.where(low, av, turn(got[...]))
    b_out[...] = jnp.where(low, bv, got[...])


def prep_kernel(slab, per, cols, pairs, a_mine, a_other, p_mine, p_other, a_hi, a_lo, t_hi, t_lo, p_hi, p_lo, diag):
    for ref in (a_hi, a_lo, t_hi, t_lo):
        ref[...] = jnp.zeros(ref.shape, BF16)
    diag[...] = jnp.zeros(diag.shape, F32)
    for t, src in enumerate((a_mine, a_other)):
        for m in range(slab):
            rows = slice((t * slab + m) * BLK, (t * slab + m + 1) * BLK)
            for s in range(per):
                k = m * per + s
                col = cols[t * slab * per + k]
                at = pl.multiple_of(col * BLK, BLK)
                block = src[k]
                hi, lo = split_bf16(block)
                a_hi[rows, pl.ds(at, BLK)] = hi.astype(BF16)
                a_lo[rows, pl.ds(at, BLK)] = lo.astype(BF16)
                hi, lo = split_bf16(block.T)
                t_hi[pl.ds(at, BLK), rows] = hi.astype(BF16)
                t_lo[pl.ds(at, BLK), rows] = lo.astype(BF16)
                diag[pl.ds(col, 1), :] += RHO * jnp.sum(block * block, axis=0, keepdims=True)
    shape = (BLK, BLK)
    eye = lax.broadcasted_iota(jnp.int32, shape, 0) == lax.broadcasted_iota(jnp.int32, shape, 1)
    for t, src in enumerate((p_mine, p_other)):
        for e in range(4):
            hi, lo = split_bf16(src[e])
            rows = slice((e // 2) * BLK, (e // 2 + 1) * BLK)
            lanes = slice((e % 2) * BLK, (e % 2 + 1) * BLK)
            p_hi[t, rows, lanes] = hi.astype(BF16)
            p_lo[t, rows, lanes] = lo.astype(BF16)
        for e in range(2):
            here = pl.ds(pairs[2 * t + e], 1)
            diag[here, :] += jnp.sum(jnp.where(eye, src[3 * e], 0.0), axis=0, keepdims=True)


def forward(pairs, vec, mats, wide, msg, pp, tile=None, pp_first=None):
    a_hi, a_lo, p_hi, p_lo = mats
    half = vec.shape[0]
    first, second = pair_up(vec)
    wide[0:half, :] = first
    wide[half:, :] = second
    x = wide[...]
    total = fold(dot(a_hi[...], x) + dot(a_lo[...], x))
    rows = total.shape[0] // 2
    msg[0:rows, :] = jnp.where(low_half((rows, LANES)), total[:rows], total[rows:])
    parts, picked = [], []
    for t in range(2):
        at_i = pl.multiple_of(pairs[2 * t] * BLK, BLK)
        at_j = pl.multiple_of(pairs[2 * t + 1] * BLK, BLK)
        v = jnp.concatenate([wide[pl.ds(at_i, BLK), :], wide[pl.ds(at_j, BLK), :]], axis=0)
        parts.append(fold(dot(p_hi[t], v) + dot(p_lo[t], v)))
        picked.append(fold(v.astype(F32)))
    low2 = low_half((2 * BLK, LANES))
    pp_now = jnp.where(low2, parts[0], parts[1])
    pp[...] = pp_now
    if tile is not None:
        at = lax.broadcasted_iota(jnp.int32, (SC, LANES), 0)
        here = jnp.where(low2, picked[0], picked[1])
        tile = jnp.where(at == 3, col_sum(here * pp_now), tile)
        if pp_first is not None:
            tile = jnp.where(at == 4, col_sum(here * pp_first), tile)
        msg[rows : rows + SC, :] = tile


def backward(pairs, w, pp_now, t_hi, t_lo, full, out, extra=()):
    half = full.shape[0] // 2
    wide = jnp.concatenate(pair_up(w), axis=0)
    full[...] = fold(dot(t_hi[...], wide) + dot(t_lo[...], wide))
    turned = turn(pp_now)
    low2 = low_half(pp_now.shape)
    for t in range(2):
        both = jnp.where(low2, pp_now, turned) if t == 0 else jnp.where(low2, turned, pp_now)
        for e in range(2):
            at = pl.ds(pl.multiple_of(pairs[2 * t + e] * BLK, BLK), BLK)
            full[at, :] += both[e * BLK : (e + 1) * BLK]
    out[0:half, :] = jnp.where(low_half((half, LANES)), full[0:half, :], full[half:, :])
    at = half
    for rows in extra:
        out[at : at + rows.shape[0], :] = rows
        at += rows.shape[0]


def add_kernel(a, b, out):
    out[...] = a[...] + b[...]


def first_kernel(pairs, x, a_hi, a_lo, p_hi, p_lo, msg, pp, wide):
    forward(pairs, x[...], (a_hi, a_lo, p_hi, p_lo), wide, msg, pp)


def start_back_kernel(pairs, m1, m2, z, y, pp, diag, pd, t_hi, t_lo, out, ax, full):
    ax_now = m1[...] + m2[...]
    ax[...] = ax_now
    w = RHO * ax_now - (RHO * z[...] - y[...])
    backward(pairs, w, pp[...], t_hi, t_lo, full, out, (diag[...], pd[...]))


def step_back_kernel(pairs, m1, m2, pp, t_hi, t_lo, out, ad, scal, full):
    rows = ad.shape[0]
    ad_now = m1[0:rows, :] + m2[0:rows, :]
    tile = m1[rows:, :] + m2[rows:, :]
    ad[...] = ad_now
    scal[...] = tile
    curve = RHO * col_sum(ad_now * ad_now) + tile[3:4]
    backward(pairs, RHO * ad_now, pp[...], t_hi, t_lo, full, out, (pack_rows(curve),))


def to_columns(tile):
    half = tile.shape[0] // 2
    low = low_half((BLK, LANES))
    blocks = []
    for b in range(half):
        first = jnp.broadcast_to(tile[b : b + 1], (BLK, LANES)).T
        second = jnp.broadcast_to(tile[half + b : half + b + 1], (BLK, LANES)).T
        blocks.append(jnp.where(low, first, second))
    return jnp.concatenate(blocks, axis=0)


def residual_kernel(fresh, pairs, m1, m2, x, q, *refs):
    half = x.shape[0]
    if fresh:
        mats, (msg, pp, s_out, res, pd_out, dk_out, wide) = refs[:4], refs[4:]
        n_range = (m1.shape[0] - half) // 2
        pd = to_columns(m1[half + n_range :, :] + m2[half + n_range :, :])
        dk = pd + SIGMA + to_columns(m1[half : half + n_range, :] + m2[half : half + n_range, :])
        pd_out[...] = pd
        dk_out[...] = dk
    else:
        pd, dk = refs[0][...], refs[1][...]
        mats, (msg, pp, s_out, res, wide) = refs[2:6], refs[6:]
    total = m1[0:half, :] + m2[0:half, :]
    r = -q[...] - pd * x[...] - total
    s = r / dk
    res[...] = r
    s_out[...] = s
    tile = pack_rows(col_sum(r * s), col_sum((pd + SIGMA) * s * s))
    forward(pairs, s, mats, wide, msg, pp, tile)


def step_kernel(pairs, m1, m2, scal, d_in, r, pd, dk, pp_first, a_hi, a_lo, p_hi, p_lo, msg, pp, s_out, step_out, wide):
    half = d_in.shape[0]
    shift = pd[...] + SIGMA
    d = d_in[...]
    kd = shift * d + (m1[0:half, :] + m2[0:half, :])
    curve = m1[half : half + 1, :] + m2[half : half + 1, :] + scal[1:2, :]
    step = scal[0:1, :] / curve
    r_new = r[...] - step * kd
    s = r_new / dk[...]
    s_out[...] = s
    step_out[...] = jnp.broadcast_to(step, step_out.shape)
    tile = pack_rows(col_sum(r_new * s), col_sum(shift * s * s), col_sum(shift * s * d))
    forward(pairs, s, (a_hi, a_lo, p_hi, p_lo), wide, msg, pp, tile, pp_first[...])


def curve_kernel(m1, m2, scal, ad, ad2, share, keep):
    rows = ad.shape[0]
    tile = m1[rows:, :] + m2[rows:, :]
    beta = tile[0:1] / scal[0:1, :]
    ad_now = m1[0:rows, :] + m2[0:rows, :] + beta * ad[...]
    ad2[...] = ad_now
    flat = tile[1:2] + 2.0 * beta * tile[2:3] + beta * beta * scal[1:2, :]
    pair = tile[3:4] + 2.0 * beta * tile[4:5] + beta * beta * scal[3:4, :]
    share[...] = pack_rows(RHO * col_sum(ad_now * ad_now) + pair)
    keep[...] = pack_rows(tile[0:1], beta, flat)


def admm_update(s1, s2, keep, step_in, ax, ad, ad2, z, y, lower, upper, x, d1_in, s2_in):
    beta = keep[1:2, :]
    step1 = step_in[0:1, :]
    step2 = keep[0:1, :] / (s1[0:1, :] + s2[0:1, :] + keep[2:3, :])
    d1 = d1_in[...]
    d2 = s2_in[...] + beta * d1
    x_hat = x[...] + step1 * d1 + step2 * d2
    x_new = RELAX * x_hat + (1.0 - RELAX) * x[...]
    ax_hat = ax[...] + step1 * ad[...] + step2 * ad2[...]
    relaxed = RELAX * ax_hat + (1.0 - RELAX) * z[...]
    z_new = jnp.clip(relaxed + y[...] / RHO, lower[...], upper[...])
    y_new = y[...] + RHO * (relaxed - z_new)
    return beta, step1, step2, x_new, ax_hat, z_new, y_new


def update_kernel(pairs, *refs):
    state, rest = refs[:14], refs[14:]
    ppx, pp1, pp2, t_hi, t_lo, out, x_out, z_out, y_out, ax_out, ppx_out, full = rest
    beta, step1, step2, x_new, ax_hat, z_new, y_new = admm_update(*state)
    ax = state[4]
    x_out[...] = x_new
    z_out[...] = z_new
    y_out[...] = y_new
    ax_new = RELAX * ax_hat + (1.0 - RELAX) * ax[...]
    ax_out[...] = ax_new
    pp_hat = ppx[...] + step1 * pp1[...] + step2 * (pp2[...] + beta * pp1[...])
    pp_new = RELAX * pp_hat + (1.0 - RELAX) * ppx[...]
    ppx_out[...] = pp_new
    w = RHO * ax_new - (RHO * z_new - y_new)
    backward(pairs, w, pp_new, t_hi, t_lo, full, out)


def last_kernel(own, place, *refs):
    state, (send, z_out, y_out, x_out, full) = refs[:14], refs[14:]
    _, _, _, x_new, _, z_new, y_new = admm_update(*state)
    rows, half = z_new.shape[0], x_new.shape[0]
    low = low_half(x_new.shape)
    full[0:half, :] = jnp.where(low, x_new, turn(x_new))
    full[half:, :] = jnp.where(low, turn(x_new), x_new)
    z_out[...] = z_new
    y_out[...] = y_new
    x_out[...] = full[pl.ds(pl.multiple_of(place[0] * own, own), own), :]
    low = low_half(z_new.shape)
    send[0:rows, :] = jnp.where(low, turn(z_new), y_new)
    at = pl.multiple_of(lax.bitwise_xor(place[0], 1) * own, own)
    part = full[pl.ds(at, own), :]
    send[rows:, :] = jnp.where(low_half((own // 2, LANES)), part[: own // 2], part[own // 2 :])


def finish_kernel(place, z_in, y_in, x_in, got, x, z, y):
    mine = place[1]
    rows = z.shape[0]
    low = low_half(z.shape)
    zy = got[0:rows, :]
    z_other = jnp.where(low, zy, turn(zy))
    y_other = jnp.where(low, turn(zy), zy)
    side = jnp.where(low, 0, 1) == mine
    z_mine = jnp.where(low, z_in[...], turn(z_in[...]))
    y_mine = jnp.where(low, y_in[...], turn(y_in[...]))
    z[...] = jnp.where(side, z_mine, z_other)
    y[...] = jnp.where(side, y_mine, y_other)
    part = got[rows:, :]
    low = low_half(part.shape)
    n_half = part.shape[0]
    side = jnp.where(low, 0, 1) == mine
    x[0:n_half, :] = jnp.where(side, x_in[0:n_half, :], jnp.where(low, part, turn(part)))
    x[n_half:, :] = jnp.where(side, x_in[n_half:, :], jnp.where(low, turn(part), part))


def local(x_state, q_lin, p_diag, z_state, y_state, lower_bound, upper_bound, a_blocks, a_cols, p_blocks, p_pairs):
    slab, per = a_cols.shape
    n = lax.axis_size("row")
    n_col = lax.axis_size("col")
    own = x_state.shape[0]
    span = own * n
    half = span // 2
    n_range = span // BLK
    slab_rows = slab * BLK
    wide_rows = 2 * slab_rows
    row_at = lax.axis_index("row").astype(jnp.int32)
    place = jnp.stack([row_at, row_at % 2])

    def swap(v, axis, size, mask):
        return lax.ppermute(v, axis, [(i, i ^ mask) for i in range(size)])

    def to_partner(v):
        return swap(v, "row", n, 1)

    def reduce_over(v, axis, size, mask):
        while mask * 2 < size:
            (v,) = call(add_kernel, [(v.shape, F32)], [v, swap(v, axis, size, mask)])
            mask *= 2
        return [v, swap(v, axis, size, mask)]

    def over_col(v):
        return reduce_over(v, "col", n_col, 1)

    def over_row(v):
        return reduce_over(v, "row", n, 2)

    a_mine = a_blocks.reshape(slab * per, BLK, BLK)
    p_mine = p_blocks.reshape(4, BLK, BLK)
    a_other = to_partner(a_mine)
    p_other = to_partner(p_mine)
    ints = jnp.concatenate([a_cols.reshape(-1), p_pairs.reshape(-1)])
    ints_other = to_partner(ints)
    pd_other = to_partner(p_diag)
    count = slab * per
    cols = jnp.concatenate([ints[:count], ints_other[:count]])
    pairs = jnp.concatenate([ints[count:], ints_other[count:]])
    pd_rows = jnp.zeros((span,), F32)
    pd_rows = lax.dynamic_update_slice(pd_rows, p_diag, (row_at * own,))
    pd_rows = lax.dynamic_update_slice(pd_rows, pd_other, ((row_at ^ 1) * own,))
    pd_rows = pd_rows.reshape(n_range, BLK)
    own_shape = ((own, LANES), F32)
    vec_shape = ((half, LANES), F32)
    slab_shape = ((slab_rows, LANES), F32)
    tile_shape = ((SC, LANES), F32)
    pp_shape = ((2 * BLK, LANES), F32)
    same, diff, zy, bounds = call(
        pack_kernel,
        [own_shape, own_shape, slab_shape, slab_shape],
        [x_state, q_lin, z_state, y_state, lower_bound, upper_bound],
        [place],
    )
    swaps = [2, 3, 1] if n == 4 else list(range(1, n))
    got = {k: swap(diff if k % 2 else same, "row", n, k) for k in swaps}
    x, q = call(
        functools.partial(gather_kernel, n, own),
        [vec_shape, vec_shape],
        [same] + [got[k] for k in range(1, n)],
        [place],
        [pltpu.VMEM((span, LANES), F32)],
    )
    z, y = call(slab_kernel, [slab_shape] * 2, [z_state, y_state, to_partner(zy)], [place])
    lower, upper = call(slab_kernel, [slab_shape] * 2, [lower_bound, upper_bound, to_partner(bounds)], [place])
    *mats, t_hi, t_lo, p_hi, p_lo, diag = call(
        functools.partial(prep_kernel, slab, per),
        [((wide_rows, span), BF16)] * 2
        + [((span, wide_rows), BF16)] * 2
        + [((2, 2 * BLK, 2 * BLK), BF16)] * 2
        + [((n_range, LANES), F32)],
        [a_mine, a_other, p_mine, p_other],
        [cols, pairs],
        flops=10**8,
    )
    mats = [*mats, p_hi, p_lo]
    backs = [t_hi, t_lo]
    flops = 4 * span * wide_rows * LANES
    wide = [pltpu.VMEM((span, LANES), BF16)]
    full = [pltpu.VMEM((span, LANES), F32)]
    msg_shape = ((slab_rows + SC, LANES), F32)

    msg, ppx = call(first_kernel, [slab_shape, pp_shape], [x, *mats], [pairs], wide, flops)
    part, ax = call(
        start_back_kernel,
        [((half + 2 * n_range, LANES), F32), slab_shape],
        [*over_col(msg), z, y, ppx, diag, pd_rows, *backs],
        [pairs],
        full,
        flops,
    )
    for outer in range(ADMM_ITERS):
        if outer == 0:
            msg, pp1, d1, r, pd, dk = call(
                functools.partial(residual_kernel, True),
                [msg_shape, pp_shape] + [vec_shape] * 4,
                [*over_row(part), x, q, *mats],
                [pairs],
                wide,
                flops,
            )
        else:
            msg, pp1, d1, r = call(
                functools.partial(residual_kernel, False),
                [msg_shape, pp_shape, vec_shape, vec_shape],
                [*over_row(part), x, q, pd, dk, *mats],
                [pairs],
                wide,
                flops,
            )
        part, ad, scal = call(
            step_back_kernel,
            [((half + SC, LANES), F32), slab_shape, tile_shape],
            [*over_col(msg), pp1, *backs],
            [pairs],
            full,
            flops,
        )
        msg, pp2, s2, step = call(
            step_kernel,
            [msg_shape, pp_shape, vec_shape, tile_shape],
            [*over_row(part), scal, d1, r, pd, dk, pp1, *mats],
            [pairs],
            wide,
            flops,
        )
        ad2, share, keep = call(
            curve_kernel, [slab_shape, tile_shape, tile_shape], [*over_col(msg), scal, ad]
        )
        state = [*over_row(share), keep, step, ax, ad, ad2, z, y, lower, upper, x, d1, s2]
        if outer + 1 < ADMM_ITERS:
            part, x, z, y, ax, ppx = call(
                update_kernel,
                [vec_shape, vec_shape, slab_shape, slab_shape, slab_shape, pp_shape],
                [*state, ppx, pp1, pp2, *backs],
                [pairs],
                full,
                flops,
            )
        else:
            send, z, y, x = call(
                functools.partial(last_kernel, own),
                [((slab_rows + own // 2, LANES), F32), slab_shape, slab_shape, own_shape],
                state,
                [place],
                full,
            )
    return call(finish_kernel, [own_shape, slab_shape, slab_shape], [z, y, x, to_partner(send)], [place])


def solution(mesh):
    placed = (
        P(("col", "row"), "grp"),
        P(("col", "row"), "grp"),
        P(("col", "row")),
        P("row", "grp"),
        P("row", "grp"),
        P("row", "grp"),
        P("row", "grp"),
        P("row", "col", None, None),
        P("row", "col"),
        P("col", "row", None, None),
        P("col", "row", None),
    )

    def run(*args):
        return tuple(local(*args))

    return jax.shard_map(
        run,
        mesh=mesh,
        in_specs=placed,
        out_specs=(P(("col", "row"), "grp"), P("row", "grp"), P("row", "grp")),
        check_vma=False,
    )
```

time: 737 us -> 244 us (0.33); the launches traced: 729 us -> 244 us
  blocking collectives: 287 us -> 0 us
  waiting for transfers between devices: 283 us -> 153 us
  matrix products: 57.9 us -> 0 us
  Pallas kernels: 0 us -> 39.1 us
  local copies, waits for them, and re-layouts: 55.2 us -> 23.7 us
  other arithmetic: 28.7 us -> 1.61 us
  starting transfers between devices: 1.14 us -> 25.6 us
  between operations: 16 us -> 0.92 us
    psum x6 -> x0, blocking collectives: 177 us -> none  [column_sums(): return lax.psum((pieces[0],), ('row', 'col'))]
    psum x6 -> x0, waiting for transfers between devices: 168 us -> none  [products(): slab_sum = lax.psum(slab_part.reshape(slab_blocks * block, qp_count), 'col')]
    ppermute x0 -> x26, waiting for transfers between devices: none -> 153 us  [swap(): return lax.ppermute(v, axis, [(i, i ^ mask) for i in range(size)])]
    reduce_scatter x6 -> x0, waiting for transfers between devices: 114 us -> none  [settle_rows(): return lax.psum_scatter(var_term, 'row', scatter_dimension=0, tiled=True)]
    all_gather x6 -> x0, blocking collectives: 98.3 us -> none  [reach_range(): return lax.all_gather(vector, 'row', axis=0, tiled=True)]
    dot_general x31 -> x0, matrix products: 57.9 us -> none  [the longest x6 25.5 us: products(): slab_part = jnp.einsum('kij,kjq->kiq', a_flat, picked, precision=highest)]
    pallas_call x0 -> x23, Pallas kernels: none -> 39.1 us  [call(): pl.pallas_call(body, out_shape=[jax.ShapeDtypeStruct(s, d) for s, d in ou...]
    ppermute x0 -> x26, starting transfers between devices: none -> 25.6 us  [swap(): return lax.ppermute(v, axis, [(i, i ^ mask) for i in range(size)])]
  transfers between devices with their start and end apart: 12 -> 26, of which waited for: 12 -> 20; matrix products, arithmetic and copies ran while one was open for 3% -> 2% of each run, Pallas kernels for 0% -> 2%
where the time goes in v3:
time: 244 us
  waiting for transfers between devices  153 us (63%)
  Pallas kernels  39.1 us (16%)
  starting transfers between devices  25.6 us (10%)
  local copies, waits for them, and re-layouts  23.7 us (10%)
    ppermute x26, waiting for transfers between devices, swap(): return lax.ppermute(v, axis, [(i, i ^ mask) for i in range(size)])  153 us
    pallas_call x23, Pallas kernels, call(): pl.pallas_call(body, out_shape=[jax.ShapeDtypeStruct(s, d) for s, d in ou...  39.1 us
    ppermute x26, starting transfers between devices, swap(): return lax.ppermute(v, axis, [(i, i ^ mask) for i in range(size)])  25.6 us
    unnamed x63, local copies, waits for them, and re-layouts  21.7 us
  transfers between devices with their start and end apart: 26, of which 20 were waited for; matrix products, arithmetic and copies ran while one was open for 2% of the time, Pallas kernels for 2%

profile of v3, /device:TPU:0, one launch (start us, length us, event | category | flops | bytes accessed | tf_op | source)
XLA Modules:
  0.0 243.7 jit_solution(10391337488275661679)
XLA Ops:
  0.6 3.1 %collective-permute-start.4 = (f32[24,128,128]{2,1,0:T(8,128)}, f32[24,128,128]{2,1,0:T(8,128)S(1)}, u32[]{:S(2)}, u32[]{:S(2)}) collective-permute-start(f32[24,128,128]{2,1,0:T(8,128)} %bitcast.7), channel_id=1, source_target_pairs={{0,4},{4,0},{8,12},{12,8},{1,5},{5,1},{9,13},{13,9},{2,6},{6,2},{1... | collective-permute-start | bytes 4718600 | tf_op jit(solution)/shard_map/ppermute | solution.py:361
  5.3 2.0 collective-permute-start.5
  7.4 1.1 copy-done.14
  8.5 1.0 copy-done.16
  9.5 1.0 copy-done.18
  10.5 1.0 copy-done.20
  11.5 0.9 copy-done.27
  12.4 0.9 copy-done.28
  13.3 1.8 shard_map.130
  15.1 2.5 %collective-permute-start.3 = (f32[256,128]{1,0:T(8,128)S(1)}, f32[256,128]{1,0:T(8,128)S(1)}, u32[]{:S(2)}, u32[]{:S(2)}) collective-permute-start(f32[256,128]{1,0:T(8,128)S(1)} %get-tuple-element.63), channel_id=1, source_target_pairs={{0,12},{4,8},{8,4},{12,0},{1,13},{5,9},{9,5},{13,1},{2,14},{6,10},... | collective-permute-start | bytes 393224 | tf_op jit(solution)/shard_map/ppermute | solution.py:361
  18.3 20.9 %collective-permute-done = s32[26]{0:T(128)S(1)} collective-permute-done((s32[26]{0:T(128)S(1)}, s32[26]{0:T(128)S(1)}, u32[]{:S(2)}, u32[]{:S(2)}) %collective-permute-start) | collective-permute-done | bytes 136 | tf_op jit(solution)/shard_map/ppermute | solution.py:361
  39.2 3.1 %collective-permute-start.2 = (f32[256,128]{1,0:T(8,128)S(1)}, f32[256,128]{1,0:T(8,128)S(1)}, u32[]{:S(2)}, u32[]{:S(2)}) collective-permute-start(f32[256,128]{1,0:T(8,128)S(1)} %get-tuple-element.62.refs_0_), channel_id=1, source_target_pairs={{0,8},{4,12},{8,0},{12,4},{1,9},{5,13},{9,1},{13,5},{2,10},{6,14},... | collective-permute-start | bytes 393224 | tf_op jit(solution)/shard_map/ppermute | solution.py:361
  43.2 8.5 %collective-permute-done.2.refs_2_ = f32[256,128]{1,0:T(8,128)S(1)} collective-permute-done((f32[256,128]{1,0:T(8,128)S(1)}, f32[256,128]{1,0:T(8,128)S(1)}, u32[]{:S(2)}, u32[]{:S(2)}) %collective-permute-start.2) | collective-permute-done | bytes 131104 | tf_op jit(solution)/shard_map/ppermute | solution.py:361
  54.6 1.2 copy-done.12
  55.8 1.4 copy-done.13
  57.2 0.9 copy-done.24
  58.2 0.9 copy-done.26
  59.1 3.0 %shard_map.132 = (bf16[1536,1024]{1,0:T(8,128)(2,1)S(1)}, bf16[1536,1024]{1,0:T(8,128)(2,1)S(1)}, bf16[1024,1536]{1,0:T(8,128)(2,1)S(1)}, bf16[1024,1536]{1,0:T(...) custom-call(s32[48]{0:T(128)S(1)} %pad_add_fusion.3.cols, ...), custom_call_target="tpu_custom_call" | custom-call | flops 100000000 | bytes 3670016 | tf_op jit(solution)/shard_map/pallas_call | solution.py:27
  62.2 1.6 copy-done.2
  63.8 1.7 copy-done.5
  65.5 2.7 %shard_map.133 = (f32[768,128]{1,0:T(8,128)S(1)}, f32[256,128]{1,0:T(8,128)S(1)}) custom-call(s32[4]{0:T(128)S(1)} %pad_add_fusion.2.pairs, f32[512,128]{1,0:T(8,128)S(1)} %get-tuple-element.64.x.refs_11_, bf16[1536,1024]{1,0:T(8,128)(2,1)S(1)} %get-tuple-element.65.a_hi.refs_0_.refs_2_, bf16[1536,1024]{1,0:T(8,128)(2,1)S(1)} %get-tuple-element.66.a_lo.refs_1_.refs_3_, ...), custom_call_target="tpu_custom_call" | custom-call | flops 805306368 | bytes 7077888 | tf_op jit(solution)/shard_map/pallas_call | solution.py:27
  68.3 2.8 %collective-permute-start.8 = (f32[768,128]{1,0:T(8,128)}, f32[768,128]{1,0:T(8,128)}, u32[]{:S(2)}, u32[]{:S(2)}) collective-permute-start(f32[768,128]{1,0:T(8,128)} %get-tuple-element.70), channel_id=1, source_target_pairs={{0,4},{4,0},{8,12},{12,8},{1,5},{5,1},{9,13},{13,9},{2,6},{6,2},{1... | collective-permute-start | bytes 1179656 | tf_op jit(solution)/shard_map/ppermute | solution.py:361
  71.9 1.5 collective-permute-start.7
  73.4 1.6 collective-permute-start.9
  75.0 0.9 dynamic_update_slice.6
  75.9 5.2 %collective-permute-done.9 = f32[256]{0:T(256)} collective-permute-done((f32[256]{0:T(256)}, f32[256]{0:T(256)}, u32[]{:S(2)}, u32[]{:S(2)}) %collective-permute-start.9) | collective-permute-done | bytes 1056 | tf_op jit(solution)/shard_map/ppermute | solution.py:361
  81.1 1.0 dynamic_update_slice.7
  82.2 1.0 copy-done.15
  83.1 1.0 copy-done.17
  84.1 1.4 shard_map.135
  85.5 1.9 copy-done.3
  87.4 1.9 copy-done.6
  89.3 3.3 %shard_map.136 = (f32[528,128]{1,0:T(8,128)S(1)}, f32[768,128]{1,0:T(8,128)S(1)}) custom-call(s32[4]{0:T(128)S(1)} %pad_add_fusion.2.pairs, f32[768,128]{1,0:T(8,128)} %shard_map.134.m1, f32[768,128]{1,0:T(8,128)} %collective-permute-done.7.m2, f32[768,128]{1,0:T(8,128)S(1)} %get-tuple-element.71.z.refs_7_, f32[768,128]{1,0:T(8,128)S(1)} %get-tuple-element.72.y.refs_8_, ...), custom_call_target="tpu_custom_call" | custom-call | flops 805306368 | bytes 8003584 | tf_op jit(solution)/shard_map/pallas_call | solution.py:27
  92.6 1.7 collective-permute-start.10
  94.3 13.3 %collective-permute-done.10.m2 = f32[528,128]{1,0:T(8,128)S(1)} collective-permute-done((f32[528,128]{1,0:T(8,128)S(1)}, f32[528,128]{1,0:T(8,128)S(1)}, u32[]{:S(2)}, u32[]{:S(2)}) %collective-permute-start.10) | collective-permute-done | bytes 270368 | tf_op jit(solution)/shard_map/ppermute | solution.py:361
  107.7 3.1 %shard_map.137 = (f32[776,128]{1,0:T(8,128)S(1)}, f32[256,128]{1,0:T(8,128)S(1)}, f32[512,128]{1,0:T(8,128)S(1)}, f32[512,128]{1,0:T(8,128)S(1)}, f32[512,128]{1,0:T(8,128)S(1)}, /*index=5*/f32[512,128]{1,0:T(8,128)S(1)}) custom-call(s32[4]{0:T(128)S(1)} %pad_add_fusion.2.pairs, f32[528,128]{1,0:T(8,128)S(1)} %get-tuple-element.77.m1, ...), custom_call_target="tpu_custom_call" | custom-call | flops 805306368 | bytes 7880704 | tf_op jit(solution)/shard_map/pallas_call | solution.py:27
  110.8 1.7 collective-permute-done.11.b
  112.6 1.6 collective-permute-start.12
  114.1 9.8 %collective-permute-done.12.m2 = f32[776,128]{1,0:T(8,128)S(1)} collective-permute-done((f32[776,128]{1,0:T(8,128)S(1)}, f32[776,128]{1,0:T(8,128)S(1)}, u32[]{:S(2)}, u32[]{:S(2)}) %collective-permute-start.12) | collective-permute-done | bytes 397344 | tf_op jit(solution)/shard_map/ppermute | solution.py:361
  123.9 2.5 %shard_map.139 = (f32[520,128]{1,0:T(8,128)S(1)}, f32[768,128]{1,0:T(8,128)S(1)}, f32[8,128]{1,0:T(8,128)S(1)}) custom-call(s32[4]{0:T(128)S(1)} %pad_add_fusion.2.pairs, f32[776,128]{1,0:T(8,128)S(1)} %shard_map.138.m1, f32[776,128]{1,0:T(8,128)S(1)} %collective-permute-done.12.m2, f32[256,128]{1,0:T(8,128)S(1)} %get-tuple-element.80.pp.pp_first.refs_15_, ...), custom_call_target="tpu_custom_call" | custom-call | flops 805306368 | bytes 7217152 | tf_op jit(solution)/shard_map/pallas_call | solution.py:27
  126.5 13.9 %collective-permute-done.13.m2 = f32[520,128]{1,0:T(8,128)S(1)} collective-permute-done((f32[520,128]{1,0:T(8,128)S(1)}, f32[520,128]{1,0:T(8,128)S(1)}, u32[]{:S(2)}, u32[]{:S(2)}) %collective-permute-start.13) | collective-permute-done | bytes 266272 | tf_op jit(solution)/shard_map/ppermute | solution.py:361
  140.4 2.9 %shard_map.140 = (f32[776,128]{1,0:T(8,128)S(1)}, f32[256,128]{1,0:T(8,128)S(1)}, f32[512,128]{1,0:T(8,128)S(1)}, f32[8,128]{1,0:T(8,128)S(1)}) custom-call(s32[4]{0:T(128)S(1)} %pad_add_fusion.2.pairs, f32[520,128]{1,0:T(8,128)S(1)} %get-tuple-element.81.m1, f32[520,128]{1,0:T(8,128)S(1)} %collective-permute-done.13.m2, ...), custom_call_target="tpu_custom_call" | custom-call | flops 805306368 | bytes 8531968 | tf_op jit(solution)/shard_map/pallas_call | solution.py:27
  143.3 1.7 collective-permute-done.14.b
  145.1 1.6 collective-permute-start.15
  146.6 9.7 %collective-permute-done.15.m2 = f32[776,128]{1,0:T(8,128)S(1)} collective-permute-done((f32[776,128]{1,0:T(8,128)S(1)}, f32[776,128]{1,0:T(8,128)S(1)}, u32[]{:S(2)}, u32[]{:S(2)}) %collective-permute-start.15) | collective-permute-done | bytes 397344 | tf_op jit(solution)/shard_map/ppermute | solution.py:361
  156.7 0.8 collective-permute-done.17.got
  157.5 0.9 shard_map.143
  158.4 2.7 %collective-permute-done.16.refs_1_ = f32[8,128]{1,0:T(8,128)S(1)} collective-permute-done((f32[8,128]{1,0:T(8,128)S(1)}, f32[8,128]{1,0:T(8,128)S(1)}, u32[]{:S(2)}, u32[]{:S(2)}) %collective-permute-start.16) | collective-permute-done | bytes 4128 | tf_op jit(solution)/shard_map/ppermute | solution.py:361
  161.2 3.3 %shard_map.144 = (f32[512,128]{1,0:T(8,128)S(1)}, f32[512,128]{1,0:T(8,128)S(1)}, f32[768,128]{1,0:T(8,128)S(1)}, f32[768,128]{1,0:T(8,128)S(1)}, f32[768,128]{1,0:T(8,128)S(1)}, /*index=5*/f32[256,128]{1,0:T(8,128)}) custom-call(s32[4]{0:T(128)S(1)} %pad_add_fusion.2.pairs, f32[8,128]{1,0:T(8,128)S(1)} %get-tuple-element.89.refs_0_, ...), custom_call_target="tpu_custom_call" | custom-call | flops 805306368 | bytes 10240000 | tf_op jit(solution)/shard_map/pallas_call | solution.py:27
  164.5 11.7 %collective-permute-done.18.m2 = f32[512,128]{1,0:T(8,128)S(1)} collective-permute-done((f32[512,128]{1,0:T(8,128)S(1)}, f32[512,128]{1,0:T(8,128)S(1)}, u32[]{:S(2)}, u32[]{:S(2)}) %collective-permute-start.18) | collective-permute-done | bytes 262176 | tf_op jit(solution)/shard_map/ppermute | solution.py:361
  176.2 3.1 %shard_map.145 = (f32[776,128]{1,0:T(8,128)S(1)}, f32[256,128]{1,0:T(8,128)S(1)}, f32[512,128]{1,0:T(8,128)S(1)}, f32[512,128]{1,0:T(8,128)S(1)}) custom-call(s32[4]{0:T(128)S(1)} %pad_add_fusion.2.pairs, f32[512,128]{1,0:T(8,128)S(1)} %get-tuple-element.99.m1, f32[512,128]{1,0:T(8,128)S(1)} %collective-permute-done.18.m2, ...), custom_call_target="tpu_custom_call" | custom-call | flops 805306368 | bytes 8388608 | tf_op jit(solution)/shard_map/pallas_call | solution.py:27
  179.3 1.7 collective-permute-done.19.b
  181.1 1.6 collective-permute-start.20
  182.7 9.7 %collective-permute-done.20.m2 = f32[776,128]{1,0:T(8,128)S(1)} collective-permute-done((f32[776,128]{1,0:T(8,128)S(1)}, f32[776,128]{1,0:T(8,128)S(1)}, u32[]{:S(2)}, u32[]{:S(2)}) %collective-permute-start.20) | collective-permute-done | bytes 397344 | tf_op jit(solution)/shard_map/ppermute | solution.py:361
  192.4 2.5 %shard_map.147 = (f32[520,128]{1,0:T(8,128)S(1)}, f32[768,128]{1,0:T(8,128)S(1)}, f32[8,128]{1,0:T(8,128)S(1)}) custom-call(s32[4]{0:T(128)S(1)} %pad_add_fusion.2.pairs, f32[776,128]{1,0:T(8,128)S(1)} %shard_map.146.m1, f32[776,128]{1,0:T(8,128)S(1)} %collective-permute-done.20.m2, f32[256,128]{1,0:T(8,128)S(1)} %get-tuple-element.102.pp.pp_first, ...), custom_call_target="tpu_custom_call" | custom-call | flops 805306368 | bytes 7217152 | tf_op jit(solution)/shard_map/pallas_call | solution.py:27
  195.0 13.9 %collective-permute-done.21.m2 = f32[520,128]{1,0:T(8,128)S(1)} collective-permute-done((f32[520,128]{1,0:T(8,128)S(1)}, f32[520,128]{1,0:T(8,128)S(1)}, u32[]{:S(2)}, u32[]{:S(2)}) %collective-permute-start.21) | collective-permute-done | bytes 266272 | tf_op jit(solution)/shard_map/ppermute | solution.py:361
  208.9 3.5 %shard_map.148 = (f32[776,128]{1,0:T(8,128)S(1)}, f32[256,128]{1,0:T(8,128)}, f32[512,128]{1,0:T(8,128)S(1)}, f32[8,128]{1,0:T(8,128)S(1)}) custom-call(s32[4]{0:T(128)S(1)} %pad_add_fusion.2.pairs, f32[520,128]{1,0:T(8,128)S(1)} %get-tuple-element.103.m1, f32[520,128]{1,0:T(8,128)S(1)} %collective-permute-done.21.m2, f32[8,128]{1,0:T(8,128)S(1)} %get-tuple-element.104.scal, ...), custom_call_target="tpu_custom_call" | custom-call | flops 805306368 | bytes 8531968 | tf_op jit(solution)/shard_map/pallas_call | solution.py:27
  212.4 1.7 collective-permute-done.22.b
  214.2 1.6 collective-permute-start.23
  215.7 9.8 %collective-permute-done.23.m2 = f32[776,128]{1,0:T(8,128)S(1)} collective-permute-done((f32[776,128]{1,0:T(8,128)S(1)}, f32[776,128]{1,0:T(8,128)S(1)}, u32[]{:S(2)}, u32[]{:S(2)}) %collective-permute-start.23) | collective-permute-done | bytes 397344 | tf_op jit(solution)/shard_map/ppermute | solution.py:361
  225.8 4.5 %collective-permute-done.24.refs_1_ = f32[8,128]{1,0:T(8,128)S(1)} collective-permute-done((f32[8,128]{1,0:T(8,128)S(1)}, f32[8,128]{1,0:T(8,128)S(1)}, u32[]{:S(2)}, u32[]{:S(2)}) %collective-permute-start.24) | collective-permute-done | bytes 4128 | tf_op jit(solution)/shard_map/ppermute | solution.py:361
  230.2 1.0 shard_map.151
  231.3 10.6 %collective-permute-done.25.got = f32[896,128]{1,0:T(8,128)S(1)} collective-permute-done((f32[896,128]{1,0:T(8,128)S(1)}, f32[896,128]{1,0:T(8,128)S(1)}, u32[]{:S(2)}, u32[]{:S(2)}) %collective-permute-start.25) | collective-permute-done | bytes 458784 | tf_op jit(solution)/shard_map/ppermute | solution.py:361
  241.9 1.8 shard_map.152
  (83 shorter events, 8.1 us)
Async XLA Ops:
  0.6 54.0 %collective-permute-start.4 = (f32[24,128,128]{2,1,0:T(8,128)}, f32[24,128,128]{2,1,0:T(8,128)S(1)}, u32[]{:S(2)}, u32[]{:S(2)}) collective-permute-start(f32[24,128,128]{2,1,0:T(8,128)} %bitcast.7), channel_id=1, source_target_pairs={{0,4},{4,0},{8,12},{12,8},{1,5},{5,1},{9,13},{13,9},{2,6},{6,2},{1... | collective-permute-start | bytes 4718600 | tf_op jit(solution)/shard_map/ppermute | solution.py:361
  5.3 33.9 %collective-permute-start = (s32[26]{0:T(128)S(1)}, s32[26]{0:T(128)S(1)}, u32[]{:S(2)}, u32[]{:S(2)}) collective-permute-start(s32[26]{0:T(128)S(1)} %pad_add_fusion.1), channel_id=1, source_target_pairs={{0,4},{4,0},{8,12},{12,8},{1,5},{5,1},{9,13},{13,9},{2,6},{6,2},{1... | collective-permute-start | bytes 320 | tf_op jit(solution)/shard_map/ppermute | solution.py:361
  5.3 48.5 %collective-permute-start.5 = (f32[4,128,128]{2,1,0:T(8,128)}, f32[4,128,128]{2,1,0:T(8,128)S(1)}, u32[]{:S(2)}, u32[]{:S(2)}) collective-permute-start(f32[4,128,128]{2,1,0:T(8,128)} %bitcast.9), channel_id=1, source_target_pairs={{0,4},{4,0},{8,12},{12,8},{1,5},{5,1},{9,13},{13,9},{2,6},{6,2},{1... | collective-permute-start | bytes 786440 | tf_op jit(solution)/shard_map/ppermute | solution.py:361
  7.3 48.5 %copy-start.11 = (f32[6,4,128,128]{3,2,1,0:T(8,128)S(1)}, f32[6,4,128,128]{3,2,1,0:T(8,128)}, u32[]{:S(2)}) copy-start(f32[6,4,128,128]{3,2,1,0:T(8,128)} %param.18) | copy-start | bytes 4718596
  7.4 1.1 copy-start.14
  8.5 1.0 copy-start.16
  9.5 1.0 copy-start.18
  10.5 1.0 copy-start.20
  11.5 0.9 copy-start.27
  12.4 0.9 copy-start.28
  15.1 38.7 %copy-start.29 = (f32[768,128]{1,0:T(8,128)}, f32[768,128]{1,0:T(8,128)S(1)}, u32[]{:S(2)}) copy-start(f32[768,128]{1,0:T(8,128)S(1)} %get-tuple-element.94) | copy-start | bytes 1179652
  15.1 36.5 %collective-permute-start.3 = (f32[256,128]{1,0:T(8,128)S(1)}, f32[256,128]{1,0:T(8,128)S(1)}, u32[]{:S(2)}, u32[]{:S(2)}) collective-permute-start(f32[256,128]{1,0:T(8,128)S(1)} %get-tuple-element.63), channel_id=1, source_target_pairs={{0,12},{4,8},{8,4},{12,0},{1,13},{5,9},{9,5},{13,1},{2,14},{6,10},... | collective-permute-start | bytes 393224 | tf_op jit(solution)/shard_map/ppermute | solution.py:361
  17.6 34.8 %collective-permute-start.1 = (f32[256,128]{1,0:T(8,128)S(1)}, f32[256,128]{1,0:T(8,128)S(1)}, u32[]{:S(2)}, u32[]{:S(2)}) collective-permute-start(f32[256,128]{1,0:T(8,128)S(1)} %get-tuple-element.63), channel_id=1, source_target_pairs={{0,4},{4,0},{8,12},{12,8},{1,5},{5,1},{9,13},{13,9},{2,6},{6,2},{1... | collective-permute-start | bytes 393224 | tf_op jit(solution)/shard_map/ppermute | solution.py:361
  39.2 12.4 %collective-permute-start.2 = (f32[256,128]{1,0:T(8,128)S(1)}, f32[256,128]{1,0:T(8,128)S(1)}, u32[]{:S(2)}, u32[]{:S(2)}) collective-permute-start(f32[256,128]{1,0:T(8,128)S(1)} %get-tuple-element.62.refs_0_), channel_id=1, source_target_pairs={{0,8},{4,12},{8,0},{12,4},{1,9},{5,13},{9,1},{13,5},{2,10},{6,14},... | collective-permute-start | bytes 393224 | tf_op jit(solution)/shard_map/ppermute | solution.py:361
  53.2 0.7 copy-start.22
  53.9 14.3 %copy-start.9 = (f32[512,128]{1,0:T(8,128)}, f32[512,128]{1,0:T(8,128)S(1)}, u32[]{:S(2)}) copy-start(f32[512,128]{1,0:T(8,128)S(1)} %get-tuple-element.64.x.refs_11_) | copy-start | bytes 786436
  53.9 0.7 copy-start.25
  54.6 1.2 copy-start.12
  55.8 1.4 copy-start.13
  57.2 0.9 copy-start.24
  58.2 0.9 copy-start.26
  62.2 1.6 copy-start.2
  63.8 1.7 copy-start.5
  65.5 2.7 %copy-start = (bf16[1536,1024]{1,0:T(8,128)(2,1)}, bf16[1536,1024]{1,0:T(8,128)(2,1)S(1)}, u32[]{:S(2)}) copy-start(bf16[1536,1024]{1,0:T(8,128)(2,1)S(1)} %get-tuple-element.66.a_lo.refs_1_.refs_3_) | copy-start | bytes 9437188
  65.5 2.7 %copy-start.7 = (bf16[2,256,256]{2,1,0:T(8,128)(2,1)}, bf16[2,256,256]{2,1,0:T(8,128)(2,1)S(1)}, u32[]{:S(2)}) copy-start(bf16[2,256,256]{2,1,0:T(8,128)(2,1)S(1)} %get-tuple-element.68.p_lo.refs_3_.refs_5_) | copy-start | bytes 786436
  68.2 2.9 %collective-permute-start.6 = (f32[768,128]{1,0:T(8,128)S(1)}, f32[768,128]{1,0:T(8,128)S(1)}, u32[]{:S(2)}, u32[]{:S(2)}) collective-permute-start(f32[768,128]{1,0:T(8,128)S(1)} %get-tuple-element.69.a), channel_id=1, source_target_pairs={{0,1},{1,0},{2,3},{3,2},{4,5},{5,4},{6,7},{7,6},{8,9},{9,8},{10,11... | collective-permute-start | bytes 1179656 | tf_op jit(solution)/shard_map/ppermute | solution.py:361
  68.3 13.9 %collective-permute-start.8 = (f32[768,128]{1,0:T(8,128)}, f32[768,128]{1,0:T(8,128)}, u32[]{:S(2)}, u32[]{:S(2)}) collective-permute-start(f32[768,128]{1,0:T(8,128)} %get-tuple-element.70), channel_id=1, source_target_pairs={{0,4},{4,0},{8,12},{12,8},{1,5},{5,1},{9,13},{13,9},{2,6},{6,2},{1... | collective-permute-start | bytes 1179656 | tf_op jit(solution)/shard_map/ppermute | solution.py:361
  71.9 13.6 %collective-permute-start.7 = (f32[768,128]{1,0:T(8,128)}, f32[768,128]{1,0:T(8,128)}, u32[]{:S(2)}, u32[]{:S(2)}) collective-permute-start(f32[768,128]{1,0:T(8,128)} %shard_map.134.m1), channel_id=1, source_target_pairs={{0,2},{1,3},{2,0},{3,1},{4,6},{5,7},{6,4},{7,5},{8,10},{9,11},{10,... | collective-permute-start | bytes 1179656 | tf_op jit(solution)/shard_map/ppermute | solution.py:361
  73.4 7.7 %collective-permute-start.9 = (f32[256]{0:T(256)}, f32[256]{0:T(256)}, u32[]{:S(2)}, u32[]{:S(2)}) collective-permute-start(f32[256]{0:T(256)} %param.13), channel_id=1, source_target_pairs={{0,4},{4,0},{8,12},{12,8},{1,5},{5,1},{9,13},{13,9},{2,6},{6,2},{1... | collective-permute-start | bytes 3080 | tf_op jit(solution)/shard_map/ppermute | solution.py:361
  82.1 1.0 copy-start.15
  83.1 1.0 copy-start.17
  85.5 1.9 copy-start.3
  87.4 1.9 copy-start.6
  89.3 18.3 %copy-start.1 = (bf16[1536,1024]{1,0:T(8,128)(2,1)S(1)}, bf16[1536,1024]{1,0:T(8,128)(2,1)}, u32[]{:S(2)}) copy-start(bf16[1536,1024]{1,0:T(8,128)(2,1)} %copy-done) | copy-start | bytes 9437188
  89.3 18.3 %copy-start.8 = (bf16[2,256,256]{2,1,0:T(8,128)(2,1)S(1)}, bf16[2,256,256]{2,1,0:T(8,128)(2,1)}, u32[]{:S(2)}) copy-start(bf16[2,256,256]{2,1,0:T(8,128)(2,1)} %copy-done.7) | copy-start | bytes 786436
  89.3 18.3 %copy-start.10 = (f32[512,128]{1,0:T(8,128)S(1)}, f32[512,128]{1,0:T(8,128)}, u32[]{:S(2)}) copy-start(f32[512,128]{1,0:T(8,128)} %copy-done.9) | copy-start | bytes 786436
  89.3 18.3 %copy-start.23 = (f32[512,128]{1,0:T(8,128)S(1)}, f32[512,128]{1,0:T(8,128)}, u32[]{:S(2)}) copy-start(f32[512,128]{1,0:T(8,128)} %copy-done.22) | copy-start | bytes 786436
  92.6 15.0 %collective-permute-start.10 = (f32[528,128]{1,0:T(8,128)S(1)}, f32[528,128]{1,0:T(8,128)S(1)}, u32[]{:S(2)}, u32[]{:S(2)}) collective-permute-start(f32[528,128]{1,0:T(8,128)S(1)} %get-tuple-element.77.m1), channel_id=1, source_target_pairs={{0,8},{4,12},{8,0},{12,4},{1,9},{5,13},{9,1},{13,5},{2,10},{6,14},... | collective-permute-start | bytes 811016 | tf_op jit(solution)/shard_map/ppermute | solution.py:361
  107.6 16.2 %copy-start.4 = (bf16[1024,1536]{1,0:T(8,128)(2,1)S(1)}, bf16[1024,1536]{1,0:T(8,128)(2,1)}, u32[]{:S(2)}) copy-start(bf16[1024,1536]{1,0:T(8,128)(2,1)} %copy-done.2) | copy-start | bytes 9437188
  110.8 1.7 collective-permute-start.11
  112.6 11.3 %collective-permute-start.12 = (f32[776,128]{1,0:T(8,128)S(1)}, f32[776,128]{1,0:T(8,128)S(1)}, u32[]{:S(2)}, u32[]{:S(2)}) collective-permute-start(f32[776,128]{1,0:T(8,128)S(1)} %shard_map.138.m1), channel_id=1, source_target_pairs={{0,2},{1,3},{2,0},{3,1},{4,6},{5,7},{6,4},{7,5},{8,10},{9,11},{10,... | collective-permute-start | bytes 1191944 | tf_op jit(solution)/shard_map/ppermute | solution.py:361
  126.4 14.0 %collective-permute-start.13 = (f32[520,128]{1,0:T(8,128)S(1)}, f32[520,128]{1,0:T(8,128)S(1)}, u32[]{:S(2)}, u32[]{:S(2)}) collective-permute-start(f32[520,128]{1,0:T(8,128)S(1)} %get-tuple-element.81.m1), channel_id=1, source_target_pairs={{0,8},{4,12},{8,0},{12,4},{1,9},{5,13},{9,1},{13,5},{2,10},{6,14},... | collective-permute-start | bytes 798728 | tf_op jit(solution)/shard_map/ppermute | solution.py:361
  140.4 6.2 %copy-start.30 = (f32[768,128]{1,0:T(8,128)S(1)}, f32[768,128]{1,0:T(8,128)}, u32[]{:S(2)}) copy-start(f32[768,128]{1,0:T(8,128)} %copy-done.29) | copy-start | bytes 1179652
  140.4 17.1 %copy-start.19 = (f32[768,128]{1,0:T(8,128)S(1)}, f32[768,128]{1,0:T(8,128)}, u32[]{:S(2)}) copy-start(f32[768,128]{1,0:T(8,128)} %a.3) | copy-start | bytes 1179652
  140.4 17.1 %copy-start.21 = (f32[768,128]{1,0:T(8,128)S(1)}, f32[768,128]{1,0:T(8,128)}, u32[]{:S(2)}) copy-start(f32[768,128]{1,0:T(8,128)} %b.3) | copy-start | bytes 1179652
  143.3 1.7 collective-permute-start.14
  145.1 11.3 %collective-permute-start.15 = (f32[776,128]{1,0:T(8,128)S(1)}, f32[776,128]{1,0:T(8,128)S(1)}, u32[]{:S(2)}, u32[]{:S(2)}) collective-permute-start(f32[776,128]{1,0:T(8,128)S(1)} %shard_map.141.m1), channel_id=1, source_target_pairs={{0,2},{1,3},{2,0},{3,1},{4,6},{5,7},{6,4},{7,5},{8,10},{9,11},{10,... | collective-permute-start | bytes 1191944 | tf_op jit(solution)/shard_map/ppermute | solution.py:361
  146.6 10.9 %collective-permute-start.17 = (f32[768,128]{1,0:T(8,128)S(1)}, f32[768,128]{1,0:T(8,128)S(1)}, u32[]{:S(2)}, u32[]{:S(2)}) collective-permute-start(f32[768,128]{1,0:T(8,128)S(1)} %copy-done.30), channel_id=1, source_target_pairs={{0,4},{4,0},{8,12},{12,8},{1,5},{5,1},{9,13},{13,9},{2,6},{6,2},{1... | collective-permute-start | bytes 1179656 | tf_op jit(solution)/shard_map/ppermute | solution.py:361
  156.7 4.5 %collective-permute-start.16 = (f32[8,128]{1,0:T(8,128)S(1)}, f32[8,128]{1,0:T(8,128)S(1)}, u32[]{:S(2)}, u32[]{:S(2)}) collective-permute-start(f32[8,128]{1,0:T(8,128)S(1)} %get-tuple-element.89.refs_0_), channel_id=1, source_target_pairs={{0,8},{4,12},{8,0},{12,4},{1,9},{5,13},{9,1},{13,5},{2,10},{6,14},... | collective-permute-start | bytes 12296 | tf_op jit(solution)/shard_map/ppermute | solution.py:361
  164.5 11.7 %collective-permute-start.18 = (f32[512,128]{1,0:T(8,128)S(1)}, f32[512,128]{1,0:T(8,128)S(1)}, u32[]{:S(2)}, u32[]{:S(2)}) collective-permute-start(f32[512,128]{1,0:T(8,128)S(1)} %get-tuple-element.99.m1), channel_id=1, source_target_pairs={{0,8},{4,12},{8,0},{12,4},{1,9},{5,13},{9,1},{13,5},{2,10},{6,14},... | collective-permute-start | bytes 786440 | tf_op jit(solution)/shard_map/ppermute | solution.py:361
  179.3 1.7 collective-permute-start.19
  181.1 11.3 %collective-permute-start.20 = (f32[776,128]{1,0:T(8,128)S(1)}, f32[776,128]{1,0:T(8,128)S(1)}, u32[]{:S(2)}, u32[]{:S(2)}) collective-permute-start(f32[776,128]{1,0:T(8,128)S(1)} %shard_map.146.m1), channel_id=1, source_target_pairs={{0,2},{1,3},{2,0},{3,1},{4,6},{5,7},{6,4},{7,5},{8,10},{9,11},{10,... | collective-permute-start | bytes 1191944 | tf_op jit(solution)/shard_map/ppermute | solution.py:361
  194.9 14.0 %collective-permute-start.21 = (f32[520,128]{1,0:T(8,128)S(1)}, f32[520,128]{1,0:T(8,128)S(1)}, u32[]{:S(2)}, u32[]{:S(2)}) collective-permute-start(f32[520,128]{1,0:T(8,128)S(1)} %get-tuple-element.103.m1), channel_id=1, source_target_pairs={{0,8},{4,12},{8,0},{12,4},{1,9},{5,13},{9,1},{13,5},{2,10},{6,14},... | collective-permute-start | bytes 798728 | tf_op jit(solution)/shard_map/ppermute | solution.py:361
  212.4 1.7 collective-permute-start.22
  214.2 11.3 %collective-permute-start.23 = (f32[776,128]{1,0:T(8,128)S(1)}, f32[776,128]{1,0:T(8,128)S(1)}, u32[]{:S(2)}, u32[]{:S(2)}) collective-permute-start(f32[776,128]{1,0:T(8,128)S(1)} %shard_map.149.m1), channel_id=1, source_target_pairs={{0,2},{1,3},{2,0},{3,1},{4,6},{5,7},{6,4},{7,5},{8,10},{9,11},{10,... | collective-permute-start | bytes 1191944 | tf_op jit(solution)/shard_map/ppermute | solution.py:361
  225.7 4.5 %collective-permute-start.24 = (f32[8,128]{1,0:T(8,128)S(1)}, f32[8,128]{1,0:T(8,128)S(1)}, u32[]{:S(2)}, u32[]{:S(2)}) collective-permute-start(f32[8,128]{1,0:T(8,128)S(1)} %get-tuple-element.109.refs_0_), channel_id=1, source_target_pairs={{0,8},{4,12},{8,0},{12,4},{1,9},{5,13},{9,1},{13,5},{2,10},{6,14},... | collective-permute-start | bytes 12296 | tf_op jit(solution)/shard_map/ppermute | solution.py:361
  231.2 10.6 %collective-permute-start.25 = (f32[896,128]{1,0:T(8,128)S(1)}, f32[896,128]{1,0:T(8,128)S(1)}, u32[]{:S(2)}, u32[]{:S(2)}) collective-permute-start(f32[896,128]{1,0:T(8,128)S(1)} %get-tuple-element.120), channel_id=1, source_target_pairs={{0,4},{4,0},{8,12},{12,8},{1,5},{5,1},{9,13},{13,9},{2,6},{6,2},{1... | collective-permute-start | bytes 1376264 | tf_op jit(solution)/shard_map/ppermute | solution.py:361

commit v4 on v0

v4 whole, which is shorter than its diff:
```python
import functools

import jax
import jax.numpy as jnp
from jax import lax
from jax.experimental import pallas as pl
from jax.experimental.pallas import tpu as pltpu
from jax.sharding import PartitionSpec as P

ADMM_ITERS = 2
RHO = 0.5
SIGMA = 1e-06
RELAX = 1.6
BLK = 128
LANES = 128
HALF = 64
SC = 8
F32 = jnp.float32
BF16 = jnp.bfloat16

VMEM = pl.BlockSpec(memory_space=pltpu.VMEM)
SMEM = pl.BlockSpec(memory_space=pltpu.SMEM)
ANY = pl.BlockSpec(memory_space=pl.ANY)


def call(body, outs, ins, smem=(), scratch=(), flops=0, after=None):
    n_bytes = sum(v.size * v.dtype.itemsize for v in ins)
    tied = [] if after is None else [after]

    def run(*refs):
        body(*refs[len(tied) :])

    return pl.pallas_call(
        run,
        out_shape=[jax.ShapeDtypeStruct(s, d) for s, d in outs],
        in_specs=[ANY] * len(tied) + [SMEM] * len(smem) + [VMEM] * len(ins),
        out_specs=[VMEM] * len(outs),
        scratch_shapes=list(scratch),
        compiler_params=pltpu.CompilerParams(vmem_limit_bytes=30 * 1024 * 1024),
        cost_estimate=pl.CostEstimate(flops=flops, bytes_accessed=n_bytes, transcendentals=0),
    )(*tied, *smem, *ins)


def low_half(shape):
    return lax.broadcasted_iota(jnp.int32, shape, 1) < HALF


def turn(v):
    return pltpu.roll(v, HALF, 1)


def fold(v):
    return v + turn(v)


def col_sum(v):
    return fold(jnp.sum(v, axis=0, keepdims=True))


def split_bf16(v):
    hi = v.astype(BF16).astype(F32)
    return hi, v - hi


def pair_up(v):
    hi, lo = split_bf16(v)
    low = low_half(v.shape)
    first = jnp.where(low, hi, turn(lo)).astype(BF16)
    second = jnp.where(low, turn(hi), lo).astype(BF16)
    return first, second


def dot(a, b):
    return jnp.dot(a, b, preferred_element_type=F32)


def pack_rows(*rows):
    at = lax.broadcasted_iota(jnp.int32, (SC, LANES), 0)
    tile = jnp.zeros((SC, LANES), F32)
    for k, row in enumerate(rows):
        tile = jnp.where(at == k, row, tile)
    return tile


def add_all(refs, rows=None):
    total = refs[0][...] if rows is None else refs[0][rows]
    for ref in refs[1:]:
        total = total + (ref[...] if rows is None else ref[rows])
    return total


def half_of(part, v):
    rows = v.shape[0] // 2
    first, second = v[:rows], v[rows:]
    low = low_half(first.shape)
    if part == 0:
        return jnp.where(low, first, turn(second))
    return jnp.where(low, turn(first), second)


def join_halves(a, b, out):
    rows = a.shape[0]
    low = low_half(a.shape)
    out[0:rows, :] = jnp.where(low, a, turn(b))
    out[rows:, :] = jnp.where(low, turn(a), b)


def side_by_side(v):
    rows = v.shape[0] // 2
    return jnp.where(low_half((rows, LANES)), v[:rows], v[rows:])


def cut_kernel(*refs):
    count = len(refs) // 3
    for k in range(count):
        v = refs[k][...]
        refs[count + 2 * k][...] = half_of(0, v)
        refs[count + 2 * k + 1][...] = half_of(1, v)


def prep_kernel(slab, per, cols, pairs, a_in, p_in, a_hi, a_lo, t_hi, t_lo, p_hi, p_lo, diag):
    for ref in (a_hi, a_lo, t_hi, t_lo):
        ref[...] = jnp.zeros(ref.shape, BF16)
    diag[...] = jnp.zeros(diag.shape, F32)
    for m in range(slab):
        rows = slice(m * BLK, (m + 1) * BLK)
        for s in range(per):
            k = m * per + s
            col = cols[k]
            at = pl.multiple_of(col * BLK, BLK)
            block = a_in[k]
            hi, lo = split_bf16(block)
            a_hi[rows, pl.ds(at, BLK)] = hi.astype(BF16)
            a_lo[rows, pl.ds(at, BLK)] = lo.astype(BF16)
            hi, lo = split_bf16(block.T)
            t_hi[pl.ds(at, BLK), rows] = hi.astype(BF16)
            t_lo[pl.ds(at, BLK), rows] = lo.astype(BF16)
            diag[pl.ds(col, 1), :] += RHO * jnp.sum(block * block, axis=0, keepdims=True)
    shape = (BLK, BLK)
    eye = lax.broadcasted_iota(jnp.int32, shape, 0) == lax.broadcasted_iota(jnp.int32, shape, 1)
    for e in range(4):
        hi, lo = split_bf16(p_in[e])
        rows = slice((e // 2) * BLK, (e // 2 + 1) * BLK)
        lanes = slice((e % 2) * BLK, (e % 2 + 1) * BLK)
        p_hi[rows, lanes] = hi.astype(BF16)
        p_lo[rows, lanes] = lo.astype(BF16)
    for e in range(2):
        diag[pl.ds(pairs[e], 1), :] += jnp.sum(jnp.where(eye, p_in[3 * e], 0.0), axis=0, keepdims=True)


def forward(pairs, mats, wide, msg, pp, tile=None, pp_first=None):
    a_hi, a_lo, p_hi, p_lo = mats
    x = wide[...]
    total = fold(dot(a_hi[...], x) + dot(a_lo[...], x))
    rows = total.shape[0] // 2
    msg[0:rows, :] = side_by_side(total)
    at_i = pl.ds(pl.multiple_of(pairs[0] * BLK, BLK), BLK)
    at_j = pl.ds(pl.multiple_of(pairs[1] * BLK, BLK), BLK)
    v = jnp.concatenate([wide[at_i, :], wide[at_j, :]], axis=0)
    pp_now = side_by_side(fold(dot(p_hi[...], v) + dot(p_lo[...], v)))
    pp[...] = pp_now
    if tile is not None:
        at = lax.broadcasted_iota(jnp.int32, (SC, LANES), 0)
        here = side_by_side(fold(v.astype(F32)))
        tile = jnp.where(at == 3, col_sum(here * pp_now), tile)
        if pp_first is not None:
            tile = jnp.where(at == 4, col_sum(here * pp_first), tile)
        msg[rows : rows + SC, :] = tile


def first_kernel(n, own, part, place, pairs, *refs):
    msgs, (a_hi, a_lo, p_hi, p_lo, msg, pp, wide) = refs[:n], refs[n:]
    for k in range(n):
        at = pl.multiple_of(lax.bitwise_xor(place[0], k) * own, own)
        wide[pl.ds(at, own), :] = pair_up(msgs[k][...])[part]
    forward(pairs, (a_hi, a_lo, p_hi, p_lo), wide, msg, pp)


def next_kernel(n, oh, second, place, pairs, *refs):
    msgs, mats, rest = refs[:n], refs[n : n + 4], refs[n + 4 :]
    pp_first = None
    if second:
        pp_first, rest = rest[0][...], rest[1:]
    msg, pp, wide = rest
    for k in range(n):
        at = pl.multiple_of(lax.bitwise_xor(place[0], k) * (2 * oh), oh)
        a, b = pair_up(msgs[k][0:oh, :])
        wide[pl.ds(at, oh), :] = a
        wide[pl.ds(pl.multiple_of(at + oh, oh), oh), :] = b
    tile = add_all(msgs, slice(oh, oh + SC))
    forward(pairs, mats, wide, msg, pp, tile, pp_first)


def backward(n, oh, place, pairs, w, pp_now, t_hi, t_lo, full, outs, extra=None):
    wide = jnp.concatenate(pair_up(w), axis=0)
    full[...] = fold(dot(t_hi[...], wide) + dot(t_lo[...], wide))
    turned = turn(pp_now)
    low = low_half(pp_now.shape)
    at_i = pl.ds(pl.multiple_of(pairs[0] * BLK, BLK), BLK)
    at_j = pl.ds(pl.multiple_of(pairs[1] * BLK, BLK), BLK)
    full[at_i, :] += jnp.where(low, pp_now, turned)
    full[at_j, :] += jnp.where(low, turned, pp_now)
    for k in range(n):
        at = pl.multiple_of(lax.bitwise_xor(place[0], k) * (2 * oh), oh)
        outs[k][0:oh, :] = side_by_side(full[pl.ds(at, 2 * oh), :])
        if extra is not None:
            outs[k][oh : oh + extra.shape[0], :] = extra


def add_kernel(a, b, out):
    out[...] = a[...] + b[...]


def start_back_kernel(n, oh, lead, place, pairs, m1, m2, z, y, pp, t_hi, t_lo, *rest):
    extra = None
    if lead:
        extra, rest = rest[0][...], rest[1:]
    outs, (ax, full) = rest[:n], rest[n:]
    ax_now = m1[...] + m2[...]
    ax[...] = ax_now
    w = RHO * ax_now - (RHO * z[...] - y[...])
    backward(n, oh, place, pairs, w, pp[...], t_hi, t_lo, full, outs, extra)


def step_back_kernel(n, oh, place, pairs, m1, m2, pp, t_hi, t_lo, *rest):
    outs, (ad, scal, full) = rest[:n], rest[n:]
    rows = ad.shape[0]
    ad_now = m1[0:rows, :] + m2[0:rows, :]
    tile = m1[rows:, :] + m2[rows:, :]
    ad[...] = ad_now
    scal[...] = tile
    curve = RHO * col_sum(ad_now * ad_now) + tile[3:4]
    backward(n, oh, place, pairs, RHO * ad_now, pp[...], t_hi, t_lo, full, outs, pack_rows(curve))


def residual_kernel(n, oh, fresh, place, *refs):
    msgs, (x, q, pd, *rest) = refs[:n], refs[n:]
    if fresh:
        msg, res, dk, full = rest
        tile = add_all(msgs, slice(oh, msgs[0].shape[0]))
        for b in range(tile.shape[0]):
            full[b * BLK : (b + 1) * BLK, :] = jnp.broadcast_to(tile[b : b + 1], (BLK, LANES)).T
        at = pl.multiple_of(place[0] * (2 * oh), oh)
        diag = pd[...] + SIGMA + side_by_side(full[pl.ds(at, 2 * oh), :])
        dk[...] = diag
    else:
        dk, msg, res = rest
        diag = dk[...]
    r = -q[...] - pd[...] * x[...] - add_all(msgs, slice(0, oh))
    s = r / diag
    res[...] = r
    msg[0:oh, :] = s
    msg[oh : oh + SC, :] = pack_rows(col_sum(r * s), col_sum((pd[...] + SIGMA) * s * s))


def step_kernel(n, oh, *refs):
    msgs, (scal, prev, r, pd, dk, msg, step_out) = refs[:n], refs[n:]
    total = add_all(msgs)
    shift = pd[...] + SIGMA
    d = prev[0:oh, :]
    kd = shift * d + total[:oh]
    curve = total[oh : oh + 1] + scal[1:2, :]
    step = scal[0:1, :] / curve
    r_new = r[...] - step * kd
    s = r_new / dk[...]
    msg[0:oh, :] = s
    msg[oh : oh + SC, :] = pack_rows(col_sum(r_new * s), col_sum(shift * s * s), col_sum(shift * s * d))
    step_out[...] = jnp.broadcast_to(step, step_out.shape)


def curve_kernel(m1, m2, scal, ad, share, ad2, keep):
    rows = ad.shape[0]
    tile = m1[rows:, :] + m2[rows:, :]
    beta = tile[0:1] / scal[0:1, :]
    ad_now = m1[0:rows, :] + m2[0:rows, :] + beta * ad[...]
    ad2[...] = ad_now
    flat = tile[1:2] + 2.0 * beta * tile[2:3] + beta * beta * scal[1:2, :]
    pair = tile[3:4] + 2.0 * beta * tile[4:5] + beta * beta * scal[3:4, :]
    share[...] = pack_rows(RHO * col_sum(ad_now * ad_now) + pair)
    keep[...] = pack_rows(tile[0:1], beta, flat)


def admm_update(n, oh, refs):
    shares, rest = refs[:n], refs[n:]
    keep, step_in, ax, ad, ad2, z, y, lower, upper, x, msg1, msg2 = rest[:12]
    beta = keep[1:2, :]
    step1 = step_in[0:1, :]
    step2 = keep[0:1, :] / (add_all(shares)[0:1] + keep[2:3, :])
    d1 = msg1[0:oh, :]
    d2 = msg2[0:oh, :] + beta * d1
    x_hat = x[...] + step1 * d1 + step2 * d2
    x_new = RELAX * x_hat + (1.0 - RELAX) * x[...]
    ax_hat = ax[...] + step1 * ad[...] + step2 * ad2[...]
    relaxed = RELAX * ax_hat + (1.0 - RELAX) * z[...]
    z_new = jnp.clip(relaxed + y[...] / RHO, lower[...], upper[...])
    y_new = y[...] + RHO * (relaxed - z_new)
    return (beta, step1, step2, ax[...]), x_new, ax_hat, z_new, y_new, rest[12:]


def update_kernel(n, oh, place, pairs, *refs):
    (beta, step1, step2, ax), x_new, ax_hat, z_new, y_new, rest = admm_update(n, oh, refs)
    ppx, pp1, pp2, t_hi, t_lo = rest[:5]
    outs, (x_out, z_out, y_out, ax_out, full) = rest[5 : 5 + n], rest[5 + n :]
    x_out[...] = x_new
    z_out[...] = z_new
    y_out[...] = y_new
    ax_new = RELAX * ax_hat + (1.0 - RELAX) * ax
    ax_out[...] = ax_new
    pp_hat = ppx[...] + step1 * pp1[...] + step2 * (pp2[...] + beta * pp1[...])
    pp_new = RELAX * pp_hat + (1.0 - RELAX) * ppx[...]
    w = RHO * ax_new - (RHO * z_new - y_new)
    backward(n, oh, place, pairs, w, pp_new, t_hi, t_lo, full, outs)


def last_kernel(n, oh, *refs):
    _, x_new, _, z_new, y_new, (x_out, z_out, y_out) = admm_update(n, oh, refs)
    x_out[...] = x_new
    z_out[...] = z_new
    y_out[...] = y_new


def finish_kernel(n, oh, *refs):
    _, x_new, _, z_new, y_new, rest = admm_update(n, oh, refs)
    x_first, z_first, y_first, x_out, z_out, y_out = rest
    join_halves(x_first[...], x_new, x_out)
    join_halves(z_first[...], z_new, z_out)
    join_halves(y_first[...], y_new, y_out)


def local(x_state, q_lin, p_diag, z_state, y_state, lower_bound, upper_bound, a_blocks, a_cols, p_blocks, p_pairs):
    slab, per = a_cols.shape
    n = lax.axis_size("row")
    n_col = lax.axis_size("col")
    own = x_state.shape[0]
    oh = own // 2
    span = own * n
    n_range = span // BLK
    slab_rows = slab * BLK
    half_rows = slab_rows // 2
    place = lax.axis_index("row").astype(jnp.int32).reshape(1)

    def swap(v, axis, size, mask):
        return lax.ppermute(v, axis, [(i, i ^ mask) for i in range(size)])

    swaps = [2, 3, 1] if n == 4 else list(range(1, n))

    def to_row(pieces, order=None):
        got = {0: pieces[0]}
        for k in order or swaps:
            got[k] = swap(pieces[k], "row", n, k)
        return [got[k] for k in range(n)]

    def to_all_rows(v):
        return to_row([v] * n, swaps[::-1])

    cols = a_cols.reshape(-1)
    pairs = p_pairs.reshape(-1)
    pd = jnp.concatenate(
        [jnp.broadcast_to(p_diag[:oh, None], (oh, HALF)), jnp.broadcast_to(p_diag[oh:, None], (oh, HALF))], axis=1
    )
    own_shape = ((oh, LANES), F32)
    msg_shape = ((oh + SC, LANES), F32)
    slab_shape = ((half_rows, LANES), F32)
    out_shape = ((half_rows + SC, LANES), F32)
    tile_shape = ((SC, LANES), F32)
    pp_shape = ((BLK, LANES), F32)
    x_rows = to_all_rows(x_state)
    *mats, t_hi, t_lo, p_hi, p_lo, diag = call(
        functools.partial(prep_kernel, slab, per),
        [((slab_rows, span), BF16)] * 2
        + [((span, slab_rows), BF16)] * 2
        + [((2 * BLK, 2 * BLK), BF16)] * 2
        + [((n_range, LANES), F32)],
        [a_blocks.reshape(slab * per, BLK, BLK), p_blocks.reshape(4, BLK, BLK)],
        [cols, pairs],
        flops=10**8,
    )
    mats = [*mats, p_hi, p_lo]
    backs = [t_hi, t_lo]
    cuts = call(
        cut_kernel,
        [own_shape] * 4 + [slab_shape] * 8,
        [x_state, q_lin, z_state, y_state, lower_bound, upper_bound],
    )
    flops = 4 * span * slab_rows * LANES
    wide = [pltpu.VMEM((span, LANES), BF16)]
    full = [pltpu.VMEM((span, LANES), F32)]
    shared = {"last": None}

    def run(body, *rest, **more):
        outs = call(body, *rest, after=shared["last"], **more)
        shared["last"] = outs[0]
        return outs

    def chain(part):
        x, q, z, y, lower, upper = cuts[part::2]

        def over_col(v):
            mask = 1
            while mask * 2 < n_col:
                (v,) = run(add_kernel, [(v.shape, F32)], [v, swap(v, "col", n_col, mask)])
                mask *= 2
                yield
            return [v, swap(v, "col", n_col, mask)]

        msg, ppx = run(
            functools.partial(first_kernel, n, own, part),
            [slab_shape, pp_shape],
            [*x_rows, *mats],
            [place, pairs],
            wide,
            flops,
        )
        yield
        sums = yield from over_col(msg)
        lead = part == 0
        piece = ((oh + n_range, LANES), F32) if lead else own_shape
        *pieces, ax = run(
            functools.partial(start_back_kernel, n, oh, lead),
            [piece] * n + [slab_shape],
            [*sums, z, y, ppx, *backs] + [diag] * lead,
            [place, pairs],
            full,
            flops,
        )
        pieces = to_row(pieces)
        yield
        for outer in range(ADMM_ITERS):
            fresh = lead and outer == 0
            msg1, r, *made = run(
                functools.partial(residual_kernel, n, oh, fresh),
                [msg_shape, own_shape] + [own_shape] * fresh,
                [*pieces, x, q, pd] + ([] if fresh else [shared["dk"]]),
                [place],
                full * fresh,
            )
            if fresh:
                shared["dk"] = made[0]
            dk = shared["dk"]
            rows1 = to_all_rows(msg1)
            yield
            msg, pp1 = run(
                functools.partial(next_kernel, n, oh, False),
                [out_shape, pp_shape],
                [*rows1, *mats],
                [place, pairs],
                wide,
                flops,
            )
            yield
            sums = yield from over_col(msg)
            *pieces, ad, scal = run(
                functools.partial(step_back_kernel, n, oh),
                [msg_shape] * n + [slab_shape, tile_shape],
                [*sums, pp1, *backs],
                [place, pairs],
                full,
                flops,
            )
            pieces = to_row(pieces)
            yield
            msg2, step = run(
                functools.partial(step_kernel, n, oh),
                [msg_shape, tile_shape],
                [*pieces, scal, msg1, r, pd, dk],
            )
            rows2 = to_all_rows(msg2)
            yield
            msg, pp2 = run(
                functools.partial(next_kernel, n, oh, True),
                [out_shape, pp_shape],
                [*rows2, *mats, pp1],
                [place, pairs],
                wide,
                flops,
            )
            yield
            sums = yield from over_col(msg)
            share, ad2, keep = run(
                curve_kernel, [tile_shape, slab_shape, tile_shape], [*sums, scal, ad]
            )
            shares = to_all_rows(share)
            yield
            state = [*shares, keep, step, ax, ad, ad2, z, y, lower, upper, x, msg1, msg2]
            if outer + 1 < ADMM_ITERS:
                *pieces, x, z, y, ax = run(
                    functools.partial(update_kernel, n, oh),
                    [own_shape] * n + [own_shape, slab_shape, slab_shape, slab_shape],
                    [*state, ppx, pp1, pp2, *backs],
                    [place, pairs],
                    full,
                    flops,
                )
                pieces = to_row(pieces)
                yield
            elif lead:
                shared["first"] = run(
                    functools.partial(last_kernel, n, oh), [own_shape, slab_shape, slab_shape], state
                )
                yield
            else:
                whole = ((slab_rows, LANES), F32)
                shared["out"] = run(
                    functools.partial(finish_kernel, n, oh),
                    [((own, LANES), F32), whole, whole],
                    [*state, *shared["first"]],
                )

    chains = [chain(0), chain(1)]
    while "out" not in shared:
        for one in chains:
            next(one, None)
    return shared["out"]


def solution(mesh):
    placed = (
        P(("col", "row"), "grp"),
        P(("col", "row"), "grp"),
        P(("col", "row")),
        P("row", "grp"),
        P("row", "grp"),
        P("row", "grp"),
        P("row", "grp"),
        P("row", "col", None, None),
        P("row", "col"),
        P("col", "row", None, None),
        P("col", "row", None),
    )

    def run(*args):
        return tuple(local(*args))

    return jax.shard_map(
        run,
        mesh=mesh,
        in_specs=placed,
        out_specs=(P(("col", "row"), "grp"), P("row", "grp"), P("row", "grp")),
        check_vma=False,
    )
```

time: 737 us -> 213 us (0.29); the launches traced: 729 us -> 213 us
  blocking collectives: 287 us -> 0 us
  waiting for transfers between devices: 283 us -> 55.2 us
  starting transfers between devices: 1.14 us -> 112 us
  matrix products: 57.9 us -> 0 us
  local copies, waits for them, and re-layouts: 55.2 us -> 4.06 us
  Pallas kernels: 0 us -> 39.9 us
  other arithmetic: 28.7 us -> 0.1 us
  between operations: 16 us -> 1.23 us
    psum x6 -> x0, blocking collectives: 177 us -> none  [column_sums(): return lax.psum((pieces[0],), ('row', 'col'))]
    psum x6 -> x0, waiting for transfers between devices: 168 us -> none  [products(): slab_sum = lax.psum(slab_part.reshape(slab_blocks * block, qp_count), 'col')]
    reduce_scatter x6 -> x0, waiting for transfers between devices: 114 us -> none  [settle_rows(): return lax.psum_scatter(var_term, 'row', scatter_dimension=0, tiled=True)]
    ppermute x0 -> x83, starting transfers between devices: none -> 112 us  [swap(): return lax.ppermute(v, axis, [(i, i ^ mask) for i in range(size)])]
    all_gather x6 -> x0, blocking collectives: 98.3 us -> none  [reach_range(): return lax.all_gather(vector, 'row', axis=0, tiled=True)]
    dot_general x31 -> x0, matrix products: 57.9 us -> none  [the longest x6 25.5 us: products(): slab_part = jnp.einsum('kij,kjq->kiq', a_flat, picked, precision=highest)]
    ppermute x0 -> x83, waiting for transfers between devices: none -> 55.2 us  [swap(): return lax.ppermute(v, axis, [(i, i ^ mask) for i in range(size)])]
    pallas_call x0 -> x44, Pallas kernels: none -> 39.9 us  [call(): pl.pallas_call(run, out_shape=[jax.ShapeDtypeStruct(s, d) for s, d in out...]
  transfers between devices with their start and end apart: 12 -> 83, of which waited for: 12 -> 23; matrix products, arithmetic and copies ran while one was open for 3% -> 1% of each run, Pallas kernels for 0% -> 17%
where the time goes in v4:
time: 213 us
  starting transfers between devices  112 us (53%)
  waiting for transfers between devices  55.2 us (26%)
  Pallas kernels  39.9 us (19%)
  local copies, waits for them, and re-layouts  4.06 us (2%)
    ppermute x83, starting transfers between devices, swap(): return lax.ppermute(v, axis, [(i, i ^ mask) for i in range(size)])  112 us
    ppermute x83, waiting for transfers between devices, swap(): return lax.ppermute(v, axis, [(i, i ^ mask) for i in range(size)])  55.2 us
    pallas_call x44, Pallas kernels, call(): pl.pallas_call(run, out_shape=[jax.ShapeDtypeStruct(s, d) for s, d in out...  39.9 us
  transfers between devices with their start and end apart: 83, of which 23 were waited for; matrix products, arithmetic and copies ran while one was open for 1% of the time, Pallas kernels for 17%

profile of v4, /device:TPU:0, one launch (start us, length us, event | category | flops | bytes accessed | tf_op | source)
XLA Modules:
  0.0 212.8 jit_solution(18053787370002115977)
XLA Ops:
  0.6 3.1 %collective-permute-start = (f32[256,128]{1,0:T(8,128)}, f32[256,128]{1,0:T(8,128)S(1)}, u32[]{:S(2)}, u32[]{:S(2)}) collective-permute-start(f32[256,128]{1,0:T(8,128)} %refs_0_.1), channel_id=1, source_target_pairs={{0,4},{4,0},{8,12},{12,8},{1,5},{5,1},{9,13},{13,9},{2,6},{6,2},{1... | collective-permute-start | bytes 393224 | tf_op jit(solution)/shard_map/ppermute | solution.py:343
  3.7 2.6 %collective-permute-start.1 = (f32[256,128]{1,0:T(8,128)}, f32[256,128]{1,0:T(8,128)S(1)}, u32[]{:S(2)}, u32[]{:S(2)}) collective-permute-start(f32[256,128]{1,0:T(8,128)} %refs_0_.1), channel_id=1, source_target_pairs={{0,8},{4,12},{8,0},{12,4},{1,9},{5,13},{9,1},{13,5},{2,10},{6,14},... | collective-permute-start | bytes 393224 | tf_op jit(solution)/shard_map/ppermute | solution.py:343
  10.2 1.8 shard_map.130
  12.0 4.9 %collective-permute-done.1.refs_4_.refs_5_ = f32[256,128]{1,0:T(8,128)S(1)} collective-permute-done((f32[256,128]{1,0:T(8,128)}, f32[256,128]{1,0:T(8,128)S(1)}, u32[]{:S(2)}, u32[]{:S(2)}) %collective-permute-start.1) | collective-permute-done | bytes 131104 | tf_op jit(solution)/shard_map/ppermute | solution.py:343
  16.9 1.8 shard_map.131
  18.8 1.8 shard_map.132
  24.0 5.6 %collective-permute-done.5.refs_4_ = f32[384,128]{1,0:T(8,128)S(1)} collective-permute-done((f32[384,128]{1,0:T(8,128)S(1)}, f32[384,128]{1,0:T(8,128)S(1)}, u32[]{:S(2)}, u32[]{:S(2)}) %collective-permute-start.5) | collective-permute-done | bytes 196640 | tf_op jit(solution)/shard_map/ppermute | solution.py:343
  29.7 1.7 shard_map.136
  31.4 2.0 collective-permute-start.7
  35.9 1.7 shard_map.137
  41.8 1.6 collective-permute-start.11
  43.4 2.0 collective-permute-start.12
  47.7 2.5 %collective-permute-done.11.refs_4_ = f32[128,128]{1,0:T(8,128)S(1)} collective-permute-done((f32[128,128]{1,0:T(8,128)S(1)}, f32[128,128]{1,0:T(8,128)S(1)}, u32[]{:S(2)}, u32[]{:S(2)}) %collective-permute-start.11) | collective-permute-done | bytes 65568 | tf_op jit(solution)/shard_map/ppermute | solution.py:343
  50.3 4.8 %collective-permute-start.16 = (f32[136,128]{1,0:T(8,128)S(1)}, f32[136,128]{1,0:T(8,128)S(1)}, u32[]{:S(2)}, u32[]{:S(2)}) collective-permute-start(f32[136,128]{1,0:T(8,128)S(1)} %get-tuple-element.151.refs_0_.refs_3_.refs_6_.refs_17_), channel_id=1, source_target_pairs={{0,4},{4,0},{8,12},{12,8},{1,5},{5,1},{9,13},{13,9},{2,6},{6,2},{1... | collective-permute-start | bytes 208904 | tf_op jit(solution)/shard_map/ppermute | solution.py:343
  57.5 1.9 shard_map.140
  62.2 1.9 shard_map.141
  67.2 4.9 %collective-permute-done.21.refs_4_ = f32[392,128]{1,0:T(8,128)S(1)} collective-permute-done((f32[392,128]{1,0:T(8,128)S(1)}, f32[392,128]{1,0:T(8,128)S(1)}, u32[]{:S(2)}, u32[]{:S(2)}) %collective-permute-start.21) | collective-permute-done | bytes 200736 | tf_op jit(solution)/shard_map/ppermute | solution.py:343
  72.1 1.7 shard_map.144
  75.9 2.3 %collective-permute-start.25 = (f32[136,128]{1,0:T(8,128)S(1)}, f32[136,128]{1,0:T(8,128)S(1)}, u32[]{:S(2)}, u32[]{:S(2)}) collective-permute-start(f32[136,128]{1,0:T(8,128)S(1)} %get-tuple-element.160), channel_id=1, source_target_pairs={{0,12},{4,8},{8,4},{12,0},{1,13},{5,9},{9,5},{13,1},{2,14},{6,10},... | collective-permute-start | bytes 208904 | tf_op jit(solution)/shard_map/ppermute | solution.py:343
  78.2 1.7 shard_map.145
  80.0 2.0 collective-permute-start.27
  82.1 2.3 %collective-permute-start.28 = (f32[136,128]{1,0:T(8,128)S(1)}, f32[136,128]{1,0:T(8,128)S(1)}, u32[]{:S(2)}, u32[]{:S(2)}) collective-permute-start(f32[136,128]{1,0:T(8,128)S(1)} %get-tuple-element.166), channel_id=1, source_target_pairs={{0,12},{4,8},{8,4},{12,0},{1,13},{5,9},{9,5},{13,1},{2,14},{6,10},... | collective-permute-start | bytes 208904 | tf_op jit(solution)/shard_map/ppermute | solution.py:343
  84.6 1.6 collective-permute-start.29
  86.6 2.3 %collective-permute-start.31 = (f32[136,128]{1,0:T(8,128)S(1)}, f32[136,128]{1,0:T(8,128)S(1)}, u32[]{:S(2)}, u32[]{:S(2)}) collective-permute-start(f32[136,128]{1,0:T(8,128)S(1)} %get-tuple-element.163.refs_0_.refs_3_.refs_18_), channel_id=1, source_target_pairs={{0,12},{4,8},{8,4},{12,0},{1,13},{5,9},{9,5},{13,1},{2,14},{6,10},... | collective-permute-start | bytes 208904 | tf_op jit(solution)/shard_map/ppermute | solution.py:343
  90.2 3.6 %collective-permute-start.32 = (f32[136,128]{1,0:T(8,128)S(1)}, f32[136,128]{1,0:T(8,128)S(1)}, u32[]{:S(2)}, u32[]{:S(2)}) collective-permute-start(f32[136,128]{1,0:T(8,128)S(1)} %get-tuple-element.169.refs_0_.refs_3_.refs_18_), channel_id=1, source_target_pairs={{0,4},{4,0},{8,12},{12,8},{1,5},{5,1},{9,13},{13,9},{2,6},{6,2},{1... | collective-permute-start | bytes 208904 | tf_op jit(solution)/shard_map/ppermute | solution.py:343
  93.9 2.4 %collective-permute-start.34 = (f32[136,128]{1,0:T(8,128)S(1)}, f32[136,128]{1,0:T(8,128)S(1)}, u32[]{:S(2)}, u32[]{:S(2)}) collective-permute-start(f32[136,128]{1,0:T(8,128)S(1)} %get-tuple-element.169.refs_0_.refs_3_.refs_18_), channel_id=1, source_target_pairs={{0,12},{4,8},{8,4},{12,0},{1,13},{5,9},{9,5},{13,1},{2,14},{6,10},... | collective-permute-start | bytes 208904 | tf_op jit(solution)/shard_map/ppermute | solution.py:343
  96.3 1.9 shard_map.148
  98.3 2.1 collective-permute-done.33.refs_5_
  100.4 1.9 shard_map.149
  105.4 4.9 %collective-permute-done.37.refs_2_ = f32[392,128]{1,0:T(8,128)S(1)} collective-permute-done((f32[392,128]{1,0:T(8,128)S(1)}, f32[392,128]{1,0:T(8,128)S(1)}, u32[]{:S(2)}, u32[]{:S(2)}) %collective-permute-start.37) | collective-permute-done | bytes 200736 | tf_op jit(solution)/shard_map/ppermute | solution.py:343
  113.1 1.7 collective-permute-start.41
  115.7 2.0 collective-permute-start.43
  117.7 1.7 collective-permute-start.44
  119.4 1.8 shard_map.154
  121.3 2.7 %collective-permute-start.46 = (f32[128,128]{1,0:T(8,128)S(1)}, f32[128,128]{1,0:T(8,128)S(1)}, u32[]{:S(2)}, u32[]{:S(2)}) collective-permute-start(f32[128,128]{1,0:T(8,128)S(1)} %get-tuple-element.193), channel_id=1, source_target_pairs={{0,8},{4,12},{8,0},{12,4},{1,9},{5,13},{9,1},{13,5},{2,10},{6,14},... | collective-permute-start | bytes 196616 | tf_op jit(solution)/shard_map/ppermute | solution.py:343
  124.0 1.7 collective-permute-start.47
  125.7 1.8 shard_map.155
  128.0 2.6 %collective-permute-done.47.refs_5_ = f32[128,128]{1,0:T(8,128)S(1)} collective-permute-done((f32[128,128]{1,0:T(8,128)S(1)}, f32[128,128]{1,0:T(8,128)S(1)}, u32[]{:S(2)}, u32[]{:S(2)}) %collective-permute-start.47) | collective-permute-done | bytes 65568 | tf_op jit(solution)/shard_map/ppermute | solution.py:343
  130.7 2.1 collective-permute-start.49
  132.9 2.3 %collective-permute-start.50 = (f32[128,128]{1,0:T(8,128)S(1)}, f32[128,128]{1,0:T(8,128)S(1)}, u32[]{:S(2)}, u32[]{:S(2)}) collective-permute-start(f32[128,128]{1,0:T(8,128)S(1)} %get-tuple-element.199), channel_id=1, source_target_pairs={{0,12},{4,8},{8,4},{12,0},{1,13},{5,9},{9,5},{13,1},{2,14},{6,10},... | collective-permute-start | bytes 196616 | tf_op jit(solution)/shard_map/ppermute | solution.py:343
  135.1 1.6 collective-permute-start.53
  137.7 1.9 collective-permute-done.50.refs_5_
  139.7 4.0 %collective-permute-start.54 = (f32[136,128]{1,0:T(8,128)S(1)}, f32[136,128]{1,0:T(8,128)S(1)}, u32[]{:S(2)}, u32[]{:S(2)}) collective-permute-start(f32[136,128]{1,0:T(8,128)S(1)} %get-tuple-element.201.refs_0_.refs_3_.refs_6_.refs_15_), channel_id=1, source_target_pairs={{0,4},{4,0},{8,12},{12,8},{1,5},{5,1},{9,13},{13,9},{2,6},{6,2},{1... | collective-permute-start | bytes 208904 | tf_op jit(solution)/shard_map/ppermute | solution.py:343
  144.2 2.0 collective-permute-start.56
  146.1 1.9 shard_map.158
  150.4 1.9 shard_map.159
  155.3 4.9 %collective-permute-done.59.refs_4_ = f32[392,128]{1,0:T(8,128)S(1)} collective-permute-done((f32[392,128]{1,0:T(8,128)S(1)}, f32[392,128]{1,0:T(8,128)S(1)}, u32[]{:S(2)}, u32[]{:S(2)}) %collective-permute-start.59) | collective-permute-done | bytes 200736 | tf_op jit(solution)/shard_map/ppermute | solution.py:343
  160.2 1.7 shard_map.162
  164.5 1.9 collective-permute-start.63
  166.4 1.7 shard_map.163
  168.3 2.4 %collective-permute-start.65 = (f32[136,128]{1,0:T(8,128)S(1)}, f32[136,128]{1,0:T(8,128)S(1)}, u32[]{:S(2)}, u32[]{:S(2)}) collective-permute-start(f32[136,128]{1,0:T(8,128)S(1)} %get-tuple-element.215), channel_id=1, source_target_pairs={{0,8},{4,12},{8,0},{12,4},{1,9},{5,13},{9,1},{13,5},{2,10},{6,14},... | collective-permute-start | bytes 208904 | tf_op jit(solution)/shard_map/ppermute | solution.py:343
  170.7 1.9 collective-permute-start.66
  173.6 1.7 collective-permute-start.68
  175.2 1.9 collective-permute-start.69
  178.2 2.8 %collective-permute-start.70 = (f32[136,128]{1,0:T(8,128)S(1)}, f32[136,128]{1,0:T(8,128)S(1)}, u32[]{:S(2)}, u32[]{:S(2)}) collective-permute-start(f32[136,128]{1,0:T(8,128)S(1)} %get-tuple-element.219.refs_0_.refs_3_.refs_16_), channel_id=1, source_target_pairs={{0,4},{4,0},{8,12},{12,8},{1,5},{5,1},{9,13},{13,9},{2,6},{6,2},{1... | collective-permute-start | bytes 208904 | tf_op jit(solution)/shard_map/ppermute | solution.py:343
  181.7 1.8 collective-permute-start.72
  183.5 2.7 %shard_map.166 = (f32[392,128]{1,0:T(8,128)S(1)}, f32[128,128]{1,0:T(8,128)}) custom-call(f32[136,128]{1,0:T(8,128)S(1)} %get-tuple-element.219.refs_0_.refs_3_.refs_16_, s32[1]{0:T(128)} %bitcast.refs_0_.refs_1_, s32[2]{0:T(128)S(1)} %bitcast.23, f32[136,128]{1,0:T(8,128)S(1)} %get-tuple-element.213.refs_0_.refs_3_.refs_16_, ...), custom_call_target="tpu_custom_call" | custom-call | flops 402653184 | bytes 3751936 | tf_op jit(solution)/shard_map/pallas_call | solution.py:33
  186.1 2.4 %collective-permute-done.71.refs_5_ = f32[136,128]{1,0:T(8,128)S(1)} collective-permute-done((f32[136,128]{1,0:T(8,128)S(1)}, f32[136,128]{1,0:T(8,128)S(1)}, u32[]{:S(2)}, u32[]{:S(2)}) %collective-permute-start.71) | collective-permute-done | bytes 69664 | tf_op jit(solution)/shard_map/ppermute | solution.py:343
  188.5 2.4 %shard_map.167 = (f32[392,128]{1,0:T(8,128)S(1)}, f32[128,128]{1,0:T(8,128)}) custom-call(f32[392,128]{1,0:T(8,128)S(1)} %get-tuple-element.220.refs_0_.refs_1_, s32[1]{0:T(128)} %bitcast.refs_0_.refs_1_, s32[2]{0:T(128)S(1)} %bitcast.24, f32[136,128]{1,0:T(8,128)S(1)} %get-tuple-element.219.refs_0_.refs_3_.refs_16_, ...), custom_call_target="tpu_custom_call" | custom-call | flops 402653184 | bytes 3751936 | tf_op jit(solution)/shard_map/pallas_call | solution.py:33
  194.0 4.8 %collective-permute-done.75.refs_2_ = f32[392,128]{1,0:T(8,128)S(1)} collective-permute-done((f32[392,128]{1,0:T(8,128)S(1)}, f32[392,128]{1,0:T(8,128)S(1)}, u32[]{:S(2)}, u32[]{:S(2)}) %collective-permute-start.75) | collective-permute-done | bytes 200736 | tf_op jit(solution)/shard_map/ppermute | solution.py:343
  201.6 1.8 collective-permute-start.79
  204.4 1.8 collective-permute-start.81
  206.2 1.8 collective-permute-start.82
  208.9 2.7 %collective-permute-done.82.refs_4_ = f32[8,128]{1,0:T(8,128)S(1)} collective-permute-done((f32[8,128]{1,0:T(8,128)S(1)}, f32[8,128]{1,0:T(8,128)S(1)}, u32[]{:S(2)}, u32[]{:S(2)}) %collective-permute-start.82) | collective-permute-done | bytes 4128 | tf_op jit(solution)/shard_map/ppermute | solution.py:343
  (174 shorter events, 57.4 us)
Async XLA Ops:
  0.6 11.3 %collective-permute-start = (f32[256,128]{1,0:T(8,128)}, f32[256,128]{1,0:T(8,128)S(1)}, u32[]{:S(2)}, u32[]{:S(2)}) collective-permute-start(f32[256,128]{1,0:T(8,128)} %refs_0_.1), channel_id=1, source_target_pairs={{0,4},{4,0},{8,12},{12,8},{1,5},{5,1},{9,13},{13,9},{2,6},{6,2},{1... | collective-permute-start | bytes 393224 | tf_op jit(solution)/shard_map/ppermute | solution.py:343
  3.7 13.2 %collective-permute-start.1 = (f32[256,128]{1,0:T(8,128)}, f32[256,128]{1,0:T(8,128)S(1)}, u32[]{:S(2)}, u32[]{:S(2)}) collective-permute-start(f32[256,128]{1,0:T(8,128)} %refs_0_.1), channel_id=1, source_target_pairs={{0,8},{4,12},{8,0},{12,4},{1,9},{5,13},{9,1},{13,5},{2,10},{6,14},... | collective-permute-start | bytes 393224 | tf_op jit(solution)/shard_map/ppermute | solution.py:343
  6.3 10.6 %collective-permute-start.2 = (f32[256,128]{1,0:T(8,128)}, f32[256,128]{1,0:T(8,128)S(1)}, u32[]{:S(2)}, u32[]{:S(2)}) collective-permute-start(f32[256,128]{1,0:T(8,128)} %refs_0_.1), channel_id=1, source_target_pairs={{0,12},{4,8},{8,4},{12,0},{1,13},{5,9},{9,5},{13,1},{2,14},{6,10},... | collective-permute-start | bytes 393224 | tf_op jit(solution)/shard_map/ppermute | solution.py:343
  21.8 7.8 %collective-permute-start.5 = (f32[384,128]{1,0:T(8,128)S(1)}, f32[384,128]{1,0:T(8,128)S(1)}, u32[]{:S(2)}, u32[]{:S(2)}) collective-permute-start(f32[384,128]{1,0:T(8,128)S(1)} %shard_map.133.refs_0_.refs_3_), channel_id=1, source_target_pairs={{0,2},{1,3},{2,0},{3,1},{4,6},{5,7},{6,4},{7,5},{8,10},{9,11},{10,... | collective-permute-start | bytes 589832 | tf_op jit(solution)/shard_map/ppermute | solution.py:343
  23.4 12.5 %collective-permute-start.6 = (f32[384,128]{1,0:T(8,128)S(1)}, f32[384,128]{1,0:T(8,128)S(1)}, u32[]{:S(2)}, u32[]{:S(2)}) collective-permute-start(f32[384,128]{1,0:T(8,128)S(1)} %shard_map.134.refs_0_.refs_3_), channel_id=1, source_target_pairs={{0,2},{1,3},{2,0},{3,1},{4,6},{5,7},{6,4},{7,5},{8,10},{9,11},{10,... | collective-permute-start | bytes 589832 | tf_op jit(solution)/shard_map/ppermute | solution.py:343
  31.4 7.6 %collective-permute-start.7 = (f32[136,128]{1,0:T(8,128)S(1)}, f32[136,128]{1,0:T(8,128)S(1)}, u32[]{:S(2)}, u32[]{:S(2)}) collective-permute-start(f32[136,128]{1,0:T(8,128)S(1)} %get-tuple-element.139), channel_id=1, source_target_pairs={{0,4},{4,0},{8,12},{12,8},{1,5},{5,1},{9,13},{13,9},{2,6},{6,2},{1... | collective-permute-start | bytes 208904 | tf_op jit(solution)/shard_map/ppermute | solution.py:343
  37.6 8.5 %collective-permute-start.10 = (f32[128,128]{1,0:T(8,128)S(1)}, f32[128,128]{1,0:T(8,128)S(1)}, u32[]{:S(2)}, u32[]{:S(2)}) collective-permute-start(f32[128,128]{1,0:T(8,128)S(1)} %get-tuple-element.145), channel_id=1, source_target_pairs={{0,4},{4,0},{8,12},{12,8},{1,5},{5,1},{9,13},{13,9},{2,6},{6,2},{1... | collective-permute-start | bytes 196616 | tf_op jit(solution)/shard_map/ppermute | solution.py:343
  41.0 15.0 %collective-permute-start.13 = (f32[136,128]{1,0:T(8,128)S(1)}, f32[136,128]{1,0:T(8,128)S(1)}, u32[]{:S(2)}, u32[]{:S(2)}) collective-permute-start(f32[136,128]{1,0:T(8,128)S(1)} %get-tuple-element.144.refs_0_.refs_3_.refs_6_.refs_17_), channel_id=1, source_target_pairs={{0,4},{4,0},{8,12},{12,8},{1,5},{5,1},{9,13},{13,9},{2,6},{6,2},{1... | collective-permute-start | bytes 208904 | tf_op jit(solution)/shard_map/ppermute | solution.py:343
  41.8 8.4 %collective-permute-start.11 = (f32[128,128]{1,0:T(8,128)S(1)}, f32[128,128]{1,0:T(8,128)S(1)}, u32[]{:S(2)}, u32[]{:S(2)}) collective-permute-start(f32[128,128]{1,0:T(8,128)S(1)} %get-tuple-element.146), channel_id=1, source_target_pairs={{0,8},{4,12},{8,0},{12,4},{1,9},{5,13},{9,1},{13,5},{2,10},{6,14},... | collective-permute-start | bytes 196616 | tf_op jit(solution)/shard_map/ppermute | solution.py:343
  43.4 6.7 %collective-permute-start.12 = (f32[128,128]{1,0:T(8,128)S(1)}, f32[128,128]{1,0:T(8,128)S(1)}, u32[]{:S(2)}, u32[]{:S(2)}) collective-permute-start(f32[128,128]{1,0:T(8,128)S(1)} %get-tuple-element.147), channel_id=1, source_target_pairs={{0,12},{4,8},{8,4},{12,0},{1,13},{5,9},{9,5},{13,1},{2,14},{6,10},... | collective-permute-start | bytes 196616 | tf_op jit(solution)/shard_map/ppermute | solution.py:343
  45.4 12.1 %collective-permute-start.14 = (f32[136,128]{1,0:T(8,128)S(1)}, f32[136,128]{1,0:T(8,128)S(1)}, u32[]{:S(2)}, u32[]{:S(2)}) collective-permute-start(f32[136,128]{1,0:T(8,128)S(1)} %get-tuple-element.144.refs_0_.refs_3_.refs_6_.refs_17_), channel_id=1, source_target_pairs={{0,8},{4,12},{8,0},{12,4},{1,9},{5,13},{9,1},{13,5},{2,10},{6,14},... | collective-permute-start | bytes 208904 | tf_op jit(solution)/shard_map/ppermute | solution.py:343
  46.1 11.4 %collective-permute-start.15 = (f32[136,128]{1,0:T(8,128)S(1)}, f32[136,128]{1,0:T(8,128)S(1)}, u32[]{:S(2)}, u32[]{:S(2)}) collective-permute-start(f32[136,128]{1,0:T(8,128)S(1)} %get-tuple-element.144.refs_0_.refs_3_.refs_6_.refs_17_), channel_id=1, source_target_pairs={{0,12},{4,8},{8,4},{12,0},{1,13},{5,9},{9,5},{13,1},{2,14},{6,10},... | collective-permute-start | bytes 208904 | tf_op jit(solution)/shard_map/ppermute | solution.py:343
  50.3 9.2 %collective-permute-start.16 = (f32[136,128]{1,0:T(8,128)S(1)}, f32[136,128]{1,0:T(8,128)S(1)}, u32[]{:S(2)}, u32[]{:S(2)}) collective-permute-start(f32[136,128]{1,0:T(8,128)S(1)} %get-tuple-element.151.refs_0_.refs_3_.refs_6_.refs_17_), channel_id=1, source_target_pairs={{0,4},{4,0},{8,12},{12,8},{1,5},{5,1},{9,13},{13,9},{2,6},{6,2},{1... | collective-permute-start | bytes 208904 | tf_op jit(solution)/shard_map/ppermute | solution.py:343
  64.2 7.8 %collective-permute-start.21 = (f32[392,128]{1,0:T(8,128)S(1)}, f32[392,128]{1,0:T(8,128)S(1)}, u32[]{:S(2)}, u32[]{:S(2)}) collective-permute-start(f32[392,128]{1,0:T(8,128)S(1)} %shard_map.142.refs_0_.refs_3_), channel_id=1, source_target_pairs={{0,2},{1,3},{2,0},{3,1},{4,6},{5,7},{6,4},{7,5},{8,10},{9,11},{10,... | collective-permute-start | bytes 602120 | tf_op jit(solution)/shard_map/ppermute | solution.py:343
  65.8 12.4 %collective-permute-start.22 = (f32[392,128]{1,0:T(8,128)S(1)}, f32[392,128]{1,0:T(8,128)S(1)}, u32[]{:S(2)}, u32[]{:S(2)}) collective-permute-start(f32[392,128]{1,0:T(8,128)S(1)} %shard_map.143.refs_0_.refs_3_), channel_id=1, source_target_pairs={{0,2},{1,3},{2,0},{3,1},{4,6},{5,7},{6,4},{7,5},{8,10},{9,11},{10,... | collective-permute-start | bytes 602120 | tf_op jit(solution)/shard_map/ppermute | solution.py:343
  73.8 8.3 %collective-permute-start.23 = (f32[136,128]{1,0:T(8,128)S(1)}, f32[136,128]{1,0:T(8,128)S(1)}, u32[]{:S(2)}, u32[]{:S(2)}) collective-permute-start(f32[136,128]{1,0:T(8,128)S(1)} %get-tuple-element.158), channel_id=1, source_target_pairs={{0,4},{4,0},{8,12},{12,8},{1,5},{5,1},{9,13},{13,9},{2,6},{6,2},{1... | collective-permute-start | bytes 208904 | tf_op jit(solution)/shard_map/ppermute | solution.py:343
  74.7 9.7 %collective-permute-start.24 = (f32[136,128]{1,0:T(8,128)S(1)}, f32[136,128]{1,0:T(8,128)S(1)}, u32[]{:S(2)}, u32[]{:S(2)}) collective-permute-start(f32[136,128]{1,0:T(8,128)S(1)} %get-tuple-element.159), channel_id=1, source_target_pairs={{0,8},{4,12},{8,0},{12,4},{1,9},{5,13},{9,1},{13,5},{2,10},{6,14},... | collective-permute-start | bytes 208904 | tf_op jit(solution)/shard_map/ppermute | solution.py:343
  75.9 8.5 %collective-permute-start.25 = (f32[136,128]{1,0:T(8,128)S(1)}, f32[136,128]{1,0:T(8,128)S(1)}, u32[]{:S(2)}, u32[]{:S(2)}) collective-permute-start(f32[136,128]{1,0:T(8,128)S(1)} %get-tuple-element.160), channel_id=1, source_target_pairs={{0,12},{4,8},{8,4},{12,0},{1,13},{5,9},{9,5},{13,1},{2,14},{6,10},... | collective-permute-start | bytes 208904 | tf_op jit(solution)/shard_map/ppermute | solution.py:343
  80.0 6.7 %collective-permute-start.26 = (f32[136,128]{1,0:T(8,128)S(1)}, f32[136,128]{1,0:T(8,128)S(1)}, u32[]{:S(2)}, u32[]{:S(2)}) collective-permute-start(f32[136,128]{1,0:T(8,128)S(1)} %get-tuple-element.164), channel_id=1, source_target_pairs={{0,4},{4,0},{8,12},{12,8},{1,5},{5,1},{9,13},{13,9},{2,6},{6,2},{1... | collective-permute-start | bytes 208904 | tf_op jit(solution)/shard_map/ppermute | solution.py:343
  80.0 9.9 %collective-permute-start.27 = (f32[136,128]{1,0:T(8,128)S(1)}, f32[136,128]{1,0:T(8,128)S(1)}, u32[]{:S(2)}, u32[]{:S(2)}) collective-permute-start(f32[136,128]{1,0:T(8,128)S(1)} %get-tuple-element.165), channel_id=1, source_target_pairs={{0,8},{4,12},{8,0},{12,4},{1,9},{5,13},{9,1},{13,5},{2,10},{6,14},... | collective-permute-start | bytes 208904 | tf_op jit(solution)/shard_map/ppermute | solution.py:343
  82.1 7.9 %collective-permute-start.28 = (f32[136,128]{1,0:T(8,128)S(1)}, f32[136,128]{1,0:T(8,128)S(1)}, u32[]{:S(2)}, u32[]{:S(2)}) collective-permute-start(f32[136,128]{1,0:T(8,128)S(1)} %get-tuple-element.166), channel_id=1, source_target_pairs={{0,12},{4,8},{8,4},{12,0},{1,13},{5,9},{9,5},{13,1},{2,14},{6,10},... | collective-permute-start | bytes 208904 | tf_op jit(solution)/shard_map/ppermute | solution.py:343
  84.6 9.3 %collective-permute-start.29 = (f32[136,128]{1,0:T(8,128)S(1)}, f32[136,128]{1,0:T(8,128)S(1)}, u32[]{:S(2)}, u32[]{:S(2)}) collective-permute-start(f32[136,128]{1,0:T(8,128)S(1)} %get-tuple-element.163.refs_0_.refs_3_.refs_18_), channel_id=1, source_target_pairs={{0,4},{4,0},{8,12},{12,8},{1,5},{5,1},{9,13},{13,9},{2,6},{6,2},{1... | collective-permute-start | bytes 208904 | tf_op jit(solution)/shard_map/ppermute | solution.py:343
  86.2 10.1 %collective-permute-start.30 = (f32[136,128]{1,0:T(8,128)S(1)}, f32[136,128]{1,0:T(8,128)S(1)}, u32[]{:S(2)}, u32[]{:S(2)}) collective-permute-start(f32[136,128]{1,0:T(8,128)S(1)} %get-tuple-element.163.refs_0_.refs_3_.refs_18_), channel_id=1, source_target_pairs={{0,8},{4,12},{8,0},{12,4},{1,9},{5,13},{9,1},{13,5},{2,10},{6,14},... | collective-permute-start | bytes 208904 | tf_op jit(solution)/shard_map/ppermute | solution.py:343
  86.6 9.7 %collective-permute-start.31 = (f32[136,128]{1,0:T(8,128)S(1)}, f32[136,128]{1,0:T(8,128)S(1)}, u32[]{:S(2)}, u32[]{:S(2)}) collective-permute-start(f32[136,128]{1,0:T(8,128)S(1)} %get-tuple-element.163.refs_0_.refs_3_.refs_18_), channel_id=1, source_target_pairs={{0,12},{4,8},{8,4},{12,0},{1,13},{5,9},{9,5},{13,1},{2,14},{6,10},... | collective-permute-start | bytes 208904 | tf_op jit(solution)/shard_map/ppermute | solution.py:343
  90.2 8.0 %collective-permute-start.32 = (f32[136,128]{1,0:T(8,128)S(1)}, f32[136,128]{1,0:T(8,128)S(1)}, u32[]{:S(2)}, u32[]{:S(2)}) collective-permute-start(f32[136,128]{1,0:T(8,128)S(1)} %get-tuple-element.169.refs_0_.refs_3_.refs_18_), channel_id=1, source_target_pairs={{0,4},{4,0},{8,12},{12,8},{1,5},{5,1},{9,13},{13,9},{2,6},{6,2},{1... | collective-permute-start | bytes 208904 | tf_op jit(solution)/shard_map/ppermute | solution.py:343
  93.8 6.5 %collective-permute-start.33 = (f32[136,128]{1,0:T(8,128)S(1)}, f32[136,128]{1,0:T(8,128)S(1)}, u32[]{:S(2)}, u32[]{:S(2)}) collective-permute-start(f32[136,128]{1,0:T(8,128)S(1)} %get-tuple-element.169.refs_0_.refs_3_.refs_18_), channel_id=1, source_target_pairs={{0,8},{4,12},{8,0},{12,4},{1,9},{5,13},{9,1},{13,5},{2,10},{6,14},... | collective-permute-start | bytes 208904 | tf_op jit(solution)/shard_map/ppermute | solution.py:343
  93.9 6.5 %collective-permute-start.34 = (f32[136,128]{1,0:T(8,128)S(1)}, f32[136,128]{1,0:T(8,128)S(1)}, u32[]{:S(2)}, u32[]{:S(2)}) collective-permute-start(f32[136,128]{1,0:T(8,128)S(1)} %get-tuple-element.169.refs_0_.refs_3_.refs_18_), channel_id=1, source_target_pairs={{0,12},{4,8},{8,4},{12,0},{1,13},{5,9},{9,5},{13,1},{2,14},{6,10},... | collective-permute-start | bytes 208904 | tf_op jit(solution)/shard_map/ppermute | solution.py:343
  102.4 7.8 %collective-permute-start.37 = (f32[392,128]{1,0:T(8,128)S(1)}, f32[392,128]{1,0:T(8,128)S(1)}, u32[]{:S(2)}, u32[]{:S(2)}) collective-permute-start(f32[392,128]{1,0:T(8,128)S(1)} %shard_map.150.refs_0_.refs_1_), channel_id=1, source_target_pairs={{0,2},{1,3},{2,0},{3,1},{4,6},{5,7},{6,4},{7,5},{8,10},{9,11},{10,... | collective-permute-start | bytes 602120 | tf_op jit(solution)/shard_map/ppermute | solution.py:343
  104.0 10.8 %collective-permute-start.38 = (f32[392,128]{1,0:T(8,128)S(1)}, f32[392,128]{1,0:T(8,128)S(1)}, u32[]{:S(2)}, u32[]{:S(2)}) collective-permute-start(f32[392,128]{1,0:T(8,128)S(1)} %shard_map.151.refs_0_.refs_1_), channel_id=1, source_target_pairs={{0,2},{1,3},{2,0},{3,1},{4,6},{5,7},{6,4},{7,5},{8,10},{9,11},{10,... | collective-permute-start | bytes 602120 | tf_op jit(solution)/shard_map/ppermute | solution.py:343
  110.5 7.2 %collective-permute-start.39 = (f32[8,128]{1,0:T(8,128)S(1)}, f32[8,128]{1,0:T(8,128)S(1)}, u32[]{:S(2)}, u32[]{:S(2)}) collective-permute-start(f32[8,128]{1,0:T(8,128)S(1)} %get-tuple-element.173.refs_0_.refs_3_), channel_id=1, source_target_pairs={{0,4},{4,0},{8,12},{12,8},{1,5},{5,1},{9,13},{13,9},{2,6},{6,2},{1... | collective-permute-start | bytes 12296 | tf_op jit(solution)/shard_map/ppermute | solution.py:343
  111.8 7.7 %collective-permute-start.40 = (f32[8,128]{1,0:T(8,128)S(1)}, f32[8,128]{1,0:T(8,128)S(1)}, u32[]{:S(2)}, u32[]{:S(2)}) collective-permute-start(f32[8,128]{1,0:T(8,128)S(1)} %get-tuple-element.173.refs_0_.refs_3_), channel_id=1, source_target_pairs={{0,8},{4,12},{8,0},{12,4},{1,9},{5,13},{9,1},{13,5},{2,10},{6,14},... | collective-permute-start | bytes 12296 | tf_op jit(solution)/shard_map/ppermute | solution.py:343
  113.1 6.3 %collective-permute-start.41 = (f32[8,128]{1,0:T(8,128)S(1)}, f32[8,128]{1,0:T(8,128)S(1)}, u32[]{:S(2)}, u32[]{:S(2)}) collective-permute-start(f32[8,128]{1,0:T(8,128)S(1)} %get-tuple-element.173.refs_0_.refs_3_), channel_id=1, source_target_pairs={{0,12},{4,8},{8,4},{12,0},{1,13},{5,9},{9,5},{13,1},{2,14},{6,10},... | collective-permute-start | bytes 12296 | tf_op jit(solution)/shard_map/ppermute | solution.py:343
  115.0 9.0 %collective-permute-start.42 = (f32[8,128]{1,0:T(8,128)S(1)}, f32[8,128]{1,0:T(8,128)S(1)}, u32[]{:S(2)}, u32[]{:S(2)}) collective-permute-start(f32[8,128]{1,0:T(8,128)S(1)} %get-tuple-element.175.refs_0_.refs_3_), channel_id=1, source_target_pairs={{0,4},{4,0},{8,12},{12,8},{1,5},{5,1},{9,13},{13,9},{2,6},{6,2},{1... | collective-permute-start | bytes 12296 | tf_op jit(solution)/shard_map/ppermute | solution.py:343
  115.7 10.0 %collective-permute-start.43 = (f32[8,128]{1,0:T(8,128)S(1)}, f32[8,128]{1,0:T(8,128)S(1)}, u32[]{:S(2)}, u32[]{:S(2)}) collective-permute-start(f32[8,128]{1,0:T(8,128)S(1)} %get-tuple-element.175.refs_0_.refs_3_), channel_id=1, source_target_pairs={{0,8},{4,12},{8,0},{12,4},{1,9},{5,13},{9,1},{13,5},{2,10},{6,14},... | collective-permute-start | bytes 12296 | tf_op jit(solution)/shard_map/ppermute | solution.py:343
  117.7 8.0 %collective-permute-start.44 = (f32[8,128]{1,0:T(8,128)S(1)}, f32[8,128]{1,0:T(8,128)S(1)}, u32[]{:S(2)}, u32[]{:S(2)}) collective-permute-start(f32[8,128]{1,0:T(8,128)S(1)} %get-tuple-element.175.refs_0_.refs_3_), channel_id=1, source_target_pairs={{0,12},{4,8},{8,4},{12,0},{1,13},{5,9},{9,5},{13,1},{2,14},{6,10},... | collective-permute-start | bytes 12296 | tf_op jit(solution)/shard_map/ppermute | solution.py:343
  121.2 6.4 %collective-permute-start.45 = (f32[128,128]{1,0:T(8,128)S(1)}, f32[128,128]{1,0:T(8,128)S(1)}, u32[]{:S(2)}, u32[]{:S(2)}) collective-permute-start(f32[128,128]{1,0:T(8,128)S(1)} %get-tuple-element.192), channel_id=1, source_target_pairs={{0,4},{4,0},{8,12},{12,8},{1,5},{5,1},{9,13},{13,9},{2,6},{6,2},{1... | collective-permute-start | bytes 196616 | tf_op jit(solution)/shard_map/ppermute | solution.py:343
  121.3 6.7 %collective-permute-start.46 = (f32[128,128]{1,0:T(8,128)S(1)}, f32[128,128]{1,0:T(8,128)S(1)}, u32[]{:S(2)}, u32[]{:S(2)}) collective-permute-start(f32[128,128]{1,0:T(8,128)S(1)} %get-tuple-element.193), channel_id=1, source_target_pairs={{0,8},{4,12},{8,0},{12,4},{1,9},{5,13},{9,1},{13,5},{2,10},{6,14},... | collective-permute-start | bytes 196616 | tf_op jit(solution)/shard_map/ppermute | solution.py:343
  124.0 6.6 %collective-permute-start.47 = (f32[128,128]{1,0:T(8,128)S(1)}, f32[128,128]{1,0:T(8,128)S(1)}, u32[]{:S(2)}, u32[]{:S(2)}) collective-permute-start(f32[128,128]{1,0:T(8,128)S(1)} %get-tuple-element.194), channel_id=1, source_target_pairs={{0,12},{4,8},{8,4},{12,0},{1,13},{5,9},{9,5},{13,1},{2,14},{6,10},... | collective-permute-start | bytes 196616 | tf_op jit(solution)/shard_map/ppermute | solution.py:343
  127.5 7.6 %collective-permute-start.48 = (f32[128,128]{1,0:T(8,128)S(1)}, f32[128,128]{1,0:T(8,128)S(1)}, u32[]{:S(2)}, u32[]{:S(2)}) collective-permute-start(f32[128,128]{1,0:T(8,128)S(1)} %get-tuple-element.197), channel_id=1, source_target_pairs={{0,4},{4,0},{8,12},{12,8},{1,5},{5,1},{9,13},{13,9},{2,6},{6,2},{1... | collective-permute-start | bytes 196616 | tf_op jit(solution)/shard_map/ppermute | solution.py:343
  130.7 13.4 %collective-permute-start.51 = (f32[136,128]{1,0:T(8,128)S(1)}, f32[136,128]{1,0:T(8,128)S(1)}, u32[]{:S(2)}, u32[]{:S(2)}) collective-permute-start(f32[136,128]{1,0:T(8,128)S(1)} %get-tuple-element.196.refs_0_.refs_3_.refs_6_.refs_15_), channel_id=1, source_target_pairs={{0,4},{4,0},{8,12},{12,8},{1,5},{5,1},{9,13},{13,9},{2,6},{6,2},{1... | collective-permute-start | bytes 208904 | tf_op jit(solution)/shard_map/ppermute | solution.py:343
  130.7 7.0 %collective-permute-start.49 = (f32[128,128]{1,0:T(8,128)S(1)}, f32[128,128]{1,0:T(8,128)S(1)}, u32[]{:S(2)}, u32[]{:S(2)}) collective-permute-start(f32[128,128]{1,0:T(8,128)S(1)} %get-tuple-element.198), channel_id=1, source_target_pairs={{0,8},{4,12},{8,0},{12,4},{1,9},{5,13},{9,1},{13,5},{2,10},{6,14},... | collective-permute-start | bytes 196616 | tf_op jit(solution)/shard_map/ppermute | solution.py:343
  132.9 6.7 %collective-permute-start.50 = (f32[128,128]{1,0:T(8,128)S(1)}, f32[128,128]{1,0:T(8,128)S(1)}, u32[]{:S(2)}, u32[]{:S(2)}) collective-permute-start(f32[128,128]{1,0:T(8,128)S(1)} %get-tuple-element.199), channel_id=1, source_target_pairs={{0,12},{4,8},{8,4},{12,0},{1,13},{5,9},{9,5},{13,1},{2,14},{6,10},... | collective-permute-start | bytes 196616 | tf_op jit(solution)/shard_map/ppermute | solution.py:343
  135.1 11.0 %collective-permute-start.52 = (f32[136,128]{1,0:T(8,128)S(1)}, f32[136,128]{1,0:T(8,128)S(1)}, u32[]{:S(2)}, u32[]{:S(2)}) collective-permute-start(f32[136,128]{1,0:T(8,128)S(1)} %get-tuple-element.196.refs_0_.refs_3_.refs_6_.refs_15_), channel_id=1, source_target_pairs={{0,8},{4,12},{8,0},{12,4},{1,9},{5,13},{9,1},{13,5},{2,10},{6,14},... | collective-permute-start | bytes 208904 | tf_op jit(solution)/shard_map/ppermute | solution.py:343
  135.1 11.0 %collective-permute-start.53 = (f32[136,128]{1,0:T(8,128)S(1)}, f32[136,128]{1,0:T(8,128)S(1)}, u32[]{:S(2)}, u32[]{:S(2)}) collective-permute-start(f32[136,128]{1,0:T(8,128)S(1)} %get-tuple-element.196.refs_0_.refs_3_.refs_6_.refs_15_), channel_id=1, source_target_pairs={{0,12},{4,8},{8,4},{12,0},{1,13},{5,9},{9,5},{13,1},{2,14},{6,10},... | collective-permute-start | bytes 208904 | tf_op jit(solution)/shard_map/ppermute | solution.py:343
  139.7 8.4 %collective-permute-start.54 = (f32[136,128]{1,0:T(8,128)S(1)}, f32[136,128]{1,0:T(8,128)S(1)}, u32[]{:S(2)}, u32[]{:S(2)}) collective-permute-start(f32[136,128]{1,0:T(8,128)S(1)} %get-tuple-element.201.refs_0_.refs_3_.refs_6_.refs_15_), channel_id=1, source_target_pairs={{0,4},{4,0},{8,12},{12,8},{1,5},{5,1},{9,13},{13,9},{2,6},{6,2},{1... | collective-permute-start | bytes 208904 | tf_op jit(solution)/shard_map/ppermute | solution.py:343
  152.3 7.8 %collective-permute-start.59 = (f32[392,128]{1,0:T(8,128)S(1)}, f32[392,128]{1,0:T(8,128)S(1)}, u32[]{:S(2)}, u32[]{:S(2)}) collective-permute-start(f32[392,128]{1,0:T(8,128)S(1)} %shard_map.160.refs_0_.refs_3_), channel_id=1, source_target_pairs={{0,2},{1,3},{2,0},{3,1},{4,6},{5,7},{6,4},{7,5},{8,10},{9,11},{10,... | collective-permute-start | bytes 602120 | tf_op jit(solution)/shard_map/ppermute | solution.py:343
  153.9 12.4 %collective-permute-start.60 = (f32[392,128]{1,0:T(8,128)S(1)}, f32[392,128]{1,0:T(8,128)S(1)}, u32[]{:S(2)}, u32[]{:S(2)}) collective-permute-start(f32[392,128]{1,0:T(8,128)S(1)} %shard_map.161.refs_0_.refs_3_), channel_id=1, source_target_pairs={{0,2},{1,3},{2,0},{3,1},{4,6},{5,7},{6,4},{7,5},{8,10},{9,11},{10,... | collective-permute-start | bytes 602120 | tf_op jit(solution)/shard_map/ppermute | solution.py:343
  161.9 8.8 %collective-permute-start.61 = (f32[136,128]{1,0:T(8,128)S(1)}, f32[136,128]{1,0:T(8,128)S(1)}, u32[]{:S(2)}, u32[]{:S(2)}) collective-permute-start(f32[136,128]{1,0:T(8,128)S(1)} %get-tuple-element.208), channel_id=1, source_target_pairs={{0,4},{4,0},{8,12},{12,8},{1,5},{5,1},{9,13},{13,9},{2,6},{6,2},{1... | collective-permute-start | bytes 208904 | tf_op jit(solution)/shard_map/ppermute | solution.py:343
  163.0 9.6 %collective-permute-start.62 = (f32[136,128]{1,0:T(8,128)S(1)}, f32[136,128]{1,0:T(8,128)S(1)}, u32[]{:S(2)}, u32[]{:S(2)}) collective-permute-start(f32[136,128]{1,0:T(8,128)S(1)} %get-tuple-element.209), channel_id=1, source_target_pairs={{0,8},{4,12},{8,0},{12,4},{1,9},{5,13},{9,1},{13,5},{2,10},{6,14},... | collective-permute-start | bytes 208904 | tf_op jit(solution)/shard_map/ppermute | solution.py:343
  164.5 8.0 %collective-permute-start.63 = (f32[136,128]{1,0:T(8,128)S(1)}, f32[136,128]{1,0:T(8,128)S(1)}, u32[]{:S(2)}, u32[]{:S(2)}) collective-permute-start(f32[136,128]{1,0:T(8,128)S(1)} %get-tuple-element.210), channel_id=1, source_target_pairs={{0,12},{4,8},{8,4},{12,0},{1,13},{5,9},{9,5},{13,1},{2,14},{6,10},... | collective-permute-start | bytes 208904 | tf_op jit(solution)/shard_map/ppermute | solution.py:343
  168.1 7.1 %collective-permute-start.64 = (f32[136,128]{1,0:T(8,128)S(1)}, f32[136,128]{1,0:T(8,128)S(1)}, u32[]{:S(2)}, u32[]{:S(2)}) collective-permute-start(f32[136,128]{1,0:T(8,128)S(1)} %get-tuple-element.214), channel_id=1, source_target_pairs={{0,4},{4,0},{8,12},{12,8},{1,5},{5,1},{9,13},{13,9},{2,6},{6,2},{1... | collective-permute-start | bytes 208904 | tf_op jit(solution)/shard_map/ppermute | solution.py:343
  168.3 9.8 %collective-permute-start.65 = (f32[136,128]{1,0:T(8,128)S(1)}, f32[136,128]{1,0:T(8,128)S(1)}, u32[]{:S(2)}, u32[]{:S(2)}) collective-permute-start(f32[136,128]{1,0:T(8,128)S(1)} %get-tuple-element.215), channel_id=1, source_target_pairs={{0,8},{4,12},{8,0},{12,4},{1,9},{5,13},{9,1},{13,5},{2,10},{6,14},... | collective-permute-start | bytes 208904 | tf_op jit(solution)/shard_map/ppermute | solution.py:343
  170.7 7.4 %collective-permute-start.66 = (f32[136,128]{1,0:T(8,128)S(1)}, f32[136,128]{1,0:T(8,128)S(1)}, u32[]{:S(2)}, u32[]{:S(2)}) collective-permute-start(f32[136,128]{1,0:T(8,128)S(1)} %get-tuple-element.216), channel_id=1, source_target_pairs={{0,12},{4,8},{8,4},{12,0},{1,13},{5,9},{9,5},{13,1},{2,14},{6,10},... | collective-permute-start | bytes 208904 | tf_op jit(solution)/shard_map/ppermute | solution.py:343
  172.7 9.0 %collective-permute-start.67 = (f32[136,128]{1,0:T(8,128)S(1)}, f32[136,128]{1,0:T(8,128)S(1)}, u32[]{:S(2)}, u32[]{:S(2)}) collective-permute-start(f32[136,128]{1,0:T(8,128)S(1)} %get-tuple-element.213.refs_0_.refs_3_.refs_16_), channel_id=1, source_target_pairs={{0,4},{4,0},{8,12},{12,8},{1,5},{5,1},{9,13},{13,9},{2,6},{6,2},{1... | collective-permute-start | bytes 208904 | tf_op jit(solution)/shard_map/ppermute | solution.py:343
  173.6 9.9 %collective-permute-start.68 = (f32[136,128]{1,0:T(8,128)S(1)}, f32[136,128]{1,0:T(8,128)S(1)}, u32[]{:S(2)}, u32[]{:S(2)}) collective-permute-start(f32[136,128]{1,0:T(8,128)S(1)} %get-tuple-element.213.refs_0_.refs_3_.refs_16_), channel_id=1, source_target_pairs={{0,8},{4,12},{8,0},{12,4},{1,9},{5,13},{9,1},{13,5},{2,10},{6,14},... | collective-permute-start | bytes 208904 | tf_op jit(solution)/shard_map/ppermute | solution.py:343
  175.2 8.2 %collective-permute-start.69 = (f32[136,128]{1,0:T(8,128)S(1)}, f32[136,128]{1,0:T(8,128)S(1)}, u32[]{:S(2)}, u32[]{:S(2)}) collective-permute-start(f32[136,128]{1,0:T(8,128)S(1)} %get-tuple-element.213.refs_0_.refs_3_.refs_16_), channel_id=1, source_target_pairs={{0,12},{4,8},{8,4},{12,0},{1,13},{5,9},{9,5},{13,1},{2,14},{6,10},... | collective-permute-start | bytes 208904 | tf_op jit(solution)/shard_map/ppermute | solution.py:343
  178.2 7.9 %collective-permute-start.70 = (f32[136,128]{1,0:T(8,128)S(1)}, f32[136,128]{1,0:T(8,128)S(1)}, u32[]{:S(2)}, u32[]{:S(2)}) collective-permute-start(f32[136,128]{1,0:T(8,128)S(1)} %get-tuple-element.219.refs_0_.refs_3_.refs_16_), channel_id=1, source_target_pairs={{0,4},{4,0},{8,12},{12,8},{1,5},{5,1},{9,13},{13,9},{2,6},{6,2},{1... | collective-permute-start | bytes 208904 | tf_op jit(solution)/shard_map/ppermute | solution.py:343
  181.0 7.5 %collective-permute-start.71 = (f32[136,128]{1,0:T(8,128)S(1)}, f32[136,128]{1,0:T(8,128)S(1)}, u32[]{:S(2)}, u32[]{:S(2)}) collective-permute-start(f32[136,128]{1,0:T(8,128)S(1)} %get-tuple-element.219.refs_0_.refs_3_.refs_16_), channel_id=1, source_target_pairs={{0,8},{4,12},{8,0},{12,4},{1,9},{5,13},{9,1},{13,5},{2,10},{6,14},... | collective-permute-start | bytes 208904 | tf_op jit(solution)/shard_map/ppermute | solution.py:343
  181.7 6.9 %collective-permute-start.72 = (f32[136,128]{1,0:T(8,128)S(1)}, f32[136,128]{1,0:T(8,128)S(1)}, u32[]{:S(2)}, u32[]{:S(2)}) collective-permute-start(f32[136,128]{1,0:T(8,128)S(1)} %get-tuple-element.219.refs_0_.refs_3_.refs_16_), channel_id=1, source_target_pairs={{0,12},{4,8},{8,4},{12,0},{1,13},{5,9},{9,5},{13,1},{2,14},{6,10},... | collective-permute-start | bytes 208904 | tf_op jit(solution)/shard_map/ppermute | solution.py:343
  191.0 7.9 %collective-permute-start.75 = (f32[392,128]{1,0:T(8,128)S(1)}, f32[392,128]{1,0:T(8,128)S(1)}, u32[]{:S(2)}, u32[]{:S(2)}) collective-permute-start(f32[392,128]{1,0:T(8,128)S(1)} %shard_map.168.refs_0_.refs_1_), channel_id=1, source_target_pairs={{0,2},{1,3},{2,0},{3,1},{4,6},{5,7},{6,4},{7,5},{8,10},{9,11},{10,... | collective-permute-start | bytes 602120 | tf_op jit(solution)/shard_map/ppermute | solution.py:343
  192.6 10.8 %collective-permute-start.76 = (f32[392,128]{1,0:T(8,128)S(1)}, f32[392,128]{1,0:T(8,128)S(1)}, u32[]{:S(2)}, u32[]{:S(2)}) collective-permute-start(f32[392,128]{1,0:T(8,128)S(1)} %shard_map.169.refs_0_.refs_1_), channel_id=1, source_target_pairs={{0,2},{1,3},{2,0},{3,1},{4,6},{5,7},{6,4},{7,5},{8,10},{9,11},{10,... | collective-permute-start | bytes 602120 | tf_op jit(solution)/shard_map/ppermute | solution.py:343
  199.0 7.2 %collective-permute-start.77 = (f32[8,128]{1,0:T(8,128)S(1)}, f32[8,128]{1,0:T(8,128)S(1)}, u32[]{:S(2)}, u32[]{:S(2)}) collective-permute-start(f32[8,128]{1,0:T(8,128)S(1)} %get-tuple-element.223.refs_0_.refs_1_), channel_id=1, source_target_pairs={{0,4},{4,0},{8,12},{12,8},{1,5},{5,1},{9,13},{13,9},{2,6},{6,2},{1... | collective-permute-start | bytes 12296 | tf_op jit(solution)/shard_map/ppermute | solution.py:343
  200.5 7.4 %collective-permute-start.78 = (f32[8,128]{1,0:T(8,128)S(1)}, f32[8,128]{1,0:T(8,128)S(1)}, u32[]{:S(2)}, u32[]{:S(2)}) collective-permute-start(f32[8,128]{1,0:T(8,128)S(1)} %get-tuple-element.223.refs_0_.refs_1_), channel_id=1, source_target_pairs={{0,8},{4,12},{8,0},{12,4},{1,9},{5,13},{9,1},{13,5},{2,10},{6,14},... | collective-permute-start | bytes 12296 | tf_op jit(solution)/shard_map/ppermute | solution.py:343
  201.6 6.4 %collective-permute-start.79 = (f32[8,128]{1,0:T(8,128)S(1)}, f32[8,128]{1,0:T(8,128)S(1)}, u32[]{:S(2)}, u32[]{:S(2)}) collective-permute-start(f32[8,128]{1,0:T(8,128)S(1)} %get-tuple-element.223.refs_0_.refs_1_), channel_id=1, source_target_pairs={{0,12},{4,8},{8,4},{12,0},{1,13},{5,9},{9,5},{13,1},{2,14},{6,10},... | collective-permute-start | bytes 12296 | tf_op jit(solution)/shard_map/ppermute | solution.py:343
  (30 other events, 112.9 us)

commit v5 on v2

--- a/solution.py
+++ b/solution.py
@@ -98,10 +98,16 @@
         dst[...] = jnp.where(low_half(dst.shape), v[:rows], turn(v[rows:]))
 
 
-def prep_kernel(slab, per, cols, pairs, a_mine, a_other, p_mine, p_other, a_hi, a_lo, t_hi, t_lo, p_hi, p_lo, diag):
-    span = a_hi.shape[1] // 2
-    n_range = span // BLK
-    for ref in (a_hi, a_lo, t_hi, t_lo):
+def flip_of(place, n_half):
+    return place[2] * n_half
+
+
+def prep_kernel(slab, per, place, cols, pairs, a_mine, a_other, p_mine, p_other, *outs):
+    near, far, (p_hi, p_lo, diag) = outs[:4], outs[4:8], outs[8:]
+    span = near[0].shape[1]
+    n_half = span // 2 // BLK
+    n_range = 2 * n_half
+    for ref in outs[:8]:
         ref[...] = jnp.zeros(ref.shape, BF16)
     diag[...] = jnp.zeros(diag.shape, F32)
     for t, src in enumerate((a_mine, a_other)):
@@ -110,14 +116,21 @@
             for s in range(per):
                 k = m * per + s
                 col = cols[t * slab * per + k]
-                at = pl.multiple_of(t * span + col * BLK, BLK)
+                spot = lax.bitwise_xor(col, flip_of(place, n_half))
+                at = pl.multiple_of((t * n_half + lax.rem(spot, n_half)) * BLK, BLK)
                 block = src[k]
                 hi, lo = split_bf16(block)
-                a_hi[rows, pl.ds(at, BLK)] = hi.astype(BF16)
-                a_lo[rows, pl.ds(at, BLK)] = lo.astype(BF16)
-                hi, lo = split_bf16(block.T)
-                t_hi[pl.ds(at, BLK), rows] = hi.astype(BF16)
-                t_lo[pl.ds(at, BLK), rows] = lo.astype(BF16)
+                hi_t, lo_t = split_bf16(block.T)
+                values = [v.astype(BF16) for v in (hi, lo, hi_t, lo_t)]
+
+                def store(refs, at=at, rows=rows, values=values):
+                    refs[0][rows, pl.ds(at, BLK)] = values[0]
+                    refs[1][rows, pl.ds(at, BLK)] = values[1]
+                    refs[2][pl.ds(at, BLK), rows] = values[2]
+                    refs[3][pl.ds(at, BLK), rows] = values[3]
+
+                pl.when(spot < n_half)(functools.partial(store, near))
+                pl.when(spot >= n_half)(functools.partial(store, far))
                 here = pl.ds(t * n_range + col, 1)
                 diag[here, :] += RHO * jnp.sum(block * block, axis=0, keepdims=True)
     shape = (BLK, BLK)
@@ -134,49 +147,70 @@
             diag[here, :] += jnp.sum(jnp.where(eye, src[3 * e], 0.0), axis=0, keepdims=True)
 
 
+def place_pieces(own, place, ks, msgs, others, wide, base):
+    half = wide.shape[0] // 2 if base is None else base
+    start = 0 if base is None else 2 * base
+    for k, msg in zip(ks, msgs):
+        v = msg[0:own, :]
+        if others:
+            v = mix_cores(place[1], v, others[ks.index(k)][...])
+        at = pl.multiple_of(lax.rem(lax.bitwise_xor(place[0], k) * own, half), own)
+        first, second = pair_up(v)
+        wide[pl.ds(start + at, own), :] = first
+        wide[pl.ds(pl.multiple_of(start + half + at, own), own), :] = second
+
+
+def near_kernel(n, own, raw, place, *refs):
+    m = n // 2
+    msgs, rest = refs[:m], refs[m:]
+    others = ()
+    if raw:
+        others, rest = rest[:m], rest[m:]
+    a_hi, a_lo, part, wide = rest
+    place_pieces(own, place, list(range(m)), msgs, others, wide, None)
+    x = wide[...]
+    part[...] = dot(a_hi[...], x) + dot(a_lo[...], x)
+
+
 def forward_kernel(n, own, scalars, place, pairs, *refs):
-    msgs, rest = refs[:n], refs[n:]
-    if scalars == 0:
-        others, rest = rest[:n], rest[n:]
-    a_hi, a_lo, p_hi, p_lo = rest[:4]
-    rest = rest[4:]
+    m = n // 2
+    raw = scalars == 0
+    msgs, rest = refs[:m], refs[m:]
+    if raw:
+        others, rest = rest[:m], rest[m:]
+    else:
+        others, near_msgs, rest = (), rest[:m], rest[m:]
+    part, near_wide, a_hi, a_lo, p_hi, p_lo = rest[:6]
+    rest = rest[6:]
     if scalars == 2:
         pp_first, rest = rest[0], rest[1:]
-    msg, pp, whole, wide = rest
-    row = place[0]
-    span = whole.shape[0]
-    for k in range(n):
-        at = pl.multiple_of(lax.bitwise_xor(row, k) * own, own)
-        v = msgs[k][0:own, :]
-        if scalars == 0:
-            v = mix_cores(place[1], v, others[k][...])
-        whole[pl.ds(at, own), :] = v
-        first, second = pair_up(v)
-        wide[pl.ds(at, own), :] = first
-        wide[pl.ds(pl.multiple_of(span + at, own), own), :] = second
-    x = wide[...]
-    total = fold(dot(a_hi[...], x) + dot(a_lo[...], x))
+    msg, pp, wide = rest
+    half = wide.shape[0] // 4
+    n_half = half // BLK
+    wide[0 : 2 * half, :] = near_wide[...]
+    place_pieces(own, place, list(range(m, n)), msgs, others, wide, half)
+    x = wide[2 * half :, :]
+    total = fold(part[...] + dot(a_hi[...], x) + dot(a_lo[...], x))
     rows = total.shape[0] // 2
     msg[0:rows, :] = jnp.where(low_half((rows, LANES)), total[:rows], total[rows:])
-    parts = []
+    parts, picked = [], []
     for t in range(2):
-        at_i = pl.multiple_of(t * span + pairs[2 * t] * BLK, BLK)
-        at_j = pl.multiple_of(t * span + pairs[2 * t + 1] * BLK, BLK)
-        v = jnp.concatenate([wide[pl.ds(at_i, BLK), :], wide[pl.ds(at_j, BLK), :]], axis=0)
+        blocks = []
+        for e in range(2):
+            spot = lax.bitwise_xor(pairs[2 * t + e], flip_of(place, n_half))
+            at = ((spot // n_half) * 2 + t) * half + lax.rem(spot, n_half) * BLK
+            blocks.append(wide[pl.ds(pl.multiple_of(at, BLK), BLK), :])
+        v = jnp.concatenate(blocks, axis=0)
         parts.append(fold(dot(p_hi[t], v) + dot(p_lo[t], v)))
+        picked.append(fold(v.astype(F32)))
     low2 = low_half((2 * BLK, LANES))
     pp_now = jnp.where(low2, parts[0], parts[1])
     pp[...] = pp_now
     if scalars:
-        picked = []
-        for t in range(2):
-            at_i = pl.multiple_of(pairs[2 * t] * BLK, BLK)
-            at_j = pl.multiple_of(pairs[2 * t + 1] * BLK, BLK)
-            picked.append(jnp.concatenate([whole[pl.ds(at_i, BLK), :], whole[pl.ds(at_j, BLK), :]], axis=0))
         vec = jnp.where(low2, picked[0], picked[1])
-        tile = msgs[0][own : own + SC, :]
-        for k in range(1, n):
-            tile = tile + msgs[k][own : own + SC, :]
+        tile = jnp.zeros((SC, LANES), F32)
+        for ref in (*near_msgs, *msgs):
+            tile = tile + ref[own : own + SC, :]
         tile = fold(tile)
         at = lax.broadcasted_iota(jnp.int32, (SC, LANES), 0)
         tile = jnp.where(at == 3, col_sum(vec * pp_now), tile)
@@ -185,43 +219,54 @@
         msg[rows : rows + SC, :] = tile
 
 
-def back_product(n, own, place, pairs, w, pp_now, t_hi, t_lo, total, outs, extra):
-    row = place[0]
-    span = total.shape[0]
-    first, second = pair_up(w)
-    wide = jnp.concatenate([first, second], axis=0)
+def back_product(own, side, place, pairs, w, pp_now, t_hi, t_lo, total, outs, extra):
+    half = total.shape[0]
+    n_half = half // BLK
+    if w.shape[0] == t_hi.shape[1]:
+        wide = w
+    else:
+        wide = jnp.concatenate(pair_up(w), axis=0)
     part = fold(dot(t_hi[...], wide) + dot(t_lo[...], wide))
-    low = low_half((span, LANES))
-    total[...] = jnp.where(low, part[:span], part[span:])
+    total[...] = jnp.where(low_half((half, LANES)), part[:half], part[half:])
     low1 = low_half((BLK, LANES))
     for t in range(2):
-        side = low1 if t == 0 else jnp.logical_not(low1)
+        lanes = low1 if t == 0 else jnp.logical_not(low1)
         for e in range(2):
-            at = pl.ds(pl.multiple_of(pairs[2 * t + e] * BLK, BLK), BLK)
-            total[at, :] += jnp.where(side, pp_now[e * BLK : (e + 1) * BLK], 0.0)
-    for k in range(n):
-        at = pl.multiple_of(lax.bitwise_xor(row, k) * own, own)
-        outs[k][0:own, :] = total[pl.ds(at, own), :]
+            spot = lax.bitwise_xor(pairs[2 * t + e], flip_of(place, n_half))
+            wanted = jnp.logical_and(lanes, spot // n_half == side)
+            at = pl.ds(pl.multiple_of(lax.rem(spot, n_half) * BLK, BLK), BLK)
+            total[at, :] += jnp.where(wanted, pp_now[e * BLK : (e + 1) * BLK], 0.0)
+    m = len(outs)
+    for k, out in enumerate(outs):
+        at = lax.rem(lax.bitwise_xor(place[0], k + side * m) * own, half)
+        out[0:own, :] = total[pl.ds(pl.multiple_of(at, own), own), :]
         if extra is not None:
-            outs[k][own : own + extra.shape[0], :] = extra
+            out[own : own + extra.shape[0], :] = extra
+
+
+def near_back_kernel(own, place, pairs, w, pp, extra, t_hi, t_lo, *rest):
+    outs, total = rest[:-1], rest[-1]
+    more = extra[...] if outs[0].shape[0] > own else None
+    back_product(own, 0, place, pairs, w[...], pp[...], t_hi, t_lo, total, outs, more)
 
 
 def start_back_kernel(n, nx, own, place, pairs, *refs):
     msgs, rest = refs[:nx], refs[nx:]
     z, y, pp, diag, t_hi, t_lo = rest[:6]
-    outs, (ax, total) = rest[6 : 6 + n], rest[6 + n :]
+    outs, (ax, wide, total) = rest[6 : 6 + n // 2], rest[6 + n // 2 :]
     ax_now = msgs[0][...]
     for k in range(1, nx):
         ax_now = ax_now + msgs[k][...]
     ax[...] = ax_now
-    w = RHO * ax_now - (RHO * z[...] - y[...])
-    back_product(n, own, place, pairs, w, pp[...], t_hi, t_lo, total, outs, diag[...])
+    w = jnp.concatenate(pair_up(RHO * ax_now - (RHO * z[...] - y[...])), axis=0)
+    wide[...] = w
+    back_product(own, 1, place, pairs, w, pp[...], t_hi, t_lo, total, outs, diag[...])
 
 
 def step_back_kernel(n, nx, own, place, pairs, *refs):
     msgs, rest = refs[:nx], refs[nx:]
     pp, t_hi, t_lo = rest[:3]
-    outs, (ad, scal, total) = rest[3 : 3 + n], rest[3 + n :]
+    outs, (ad, scal, share, wide, total) = rest[3 : 3 + n // 2], rest[3 + n // 2 :]
     rows = ad.shape[0]
     v = msgs[0][...]
     for k in range(1, nx):
@@ -230,10 +275,11 @@
     tile = v[rows:]
     ad[...] = ad_now
     scal[...] = tile
-    curve = RHO * col_sum(ad_now * ad_now) + tile[3:4]
-    back_product(
-        n, own, place, pairs, RHO * ad_now, pp[...], t_hi, t_lo, total, outs, pack_rows(curve)
-    )
+    extra = pack_rows(RHO * col_sum(ad_now * ad_now) + tile[3:4])
+    share[...] = extra
+    w = jnp.concatenate(pair_up(RHO * ad_now), axis=0)
+    wide[...] = w
+    back_product(own, 1, place, pairs, w, pp[...], t_hi, t_lo, total, outs, extra)
 
 
 def residual_kernel(n, own, first, place, *refs):
@@ -331,7 +377,8 @@
     beta, step1, step2, x_new, ax_hat, z_new, y_new, rest = admm_update(n, own, refs)
     ax = refs[n + 2]
     ppx, pp1, pp2, t_hi, t_lo = rest[:5]
-    outs, (x_out, z_out, y_out, ax_out, ppx_out, total) = rest[5 : 5 + n], rest[5 + n :]
+    m = n // 2
+    outs, (x_out, z_out, y_out, ax_out, ppx_out, wide, total) = rest[5 : 5 + m], rest[5 + m :]
     x_out[...] = x_new
     z_out[...] = z_new
     y_out[...] = y_new
@@ -340,8 +387,9 @@
     pp_hat = ppx[...] + step1 * pp1[...] + step2 * (pp2[...] + beta * pp1[...])
     pp_new = RELAX * pp_hat + (1.0 - RELAX) * ppx[...]
     ppx_out[...] = pp_new
-    w = RHO * ax_new - (RHO * z_new - y_new)
-    back_product(n, own, place, pairs, w, pp_new, t_hi, t_lo, total, outs, None)
+    w = jnp.concatenate(pair_up(RHO * ax_new - (RHO * z_new - y_new)), axis=0)
+    wide[...] = w
+    back_product(own, 1, place, pairs, w, pp_new, t_hi, t_lo, total, outs, None)
 
 
 def last_kernel(n, own, *refs):
@@ -382,7 +430,7 @@
     half_rows = slab_rows // 2
     row_at = lax.axis_index("row")
     core_at = lax.axis_index("col") % 2
-    place = jnp.stack([row_at, core_at]).astype(jnp.int32)
+    place = jnp.stack([row_at, core_at, row_at // (n // 2)]).astype(jnp.int32)
 
     def to_core(v):
         return lax.ppermute(v, "col", [(c, c ^ 1) for c in range(n_col)])
@@ -390,16 +438,14 @@
     def to_x(v):
         return [v] + [lax.ppermute(v, "col", [(c, c ^ (2 * k)) for c in range(n_col)]) for k in range(1, nx)]
 
-    swaps = [2, 3, 1] if n == 4 else list(range(1, n))
-
-    def to_row(pieces, order=None):
-        got = {0: pieces[0]}
-        for k in order or swaps:
-            got[k] = lax.ppermute(pieces[k], "row", [(i, i ^ k) for i in range(n)])
-        return [got[k] for k in range(n)]
+    m = n // 2
+
+    def to_row(pieces, ks):
+        return [lax.ppermute(v, "row", [(i, i ^ k) for i in range(n)]) for v, k in zip(pieces, ks)]
 
     def to_all_rows(v):
-        return to_row([v] * n, swaps[::-1])
+        ks = list(range(n - 1, 0, -1))
+        return [v] + to_row([v] * (n - 1), ks)[::-1]
 
     a_mine = a_blocks.reshape(slab * per, BLK, BLK)
     p_mine = p_blocks.reshape(4, BLK, BLK)
@@ -415,45 +461,67 @@
     pd = jnp.concatenate(
         [jnp.broadcast_to(p_diag[:, None], (own, HALF)), jnp.broadcast_to(pd_other[:, None], (own, HALF))], axis=1
     )
-    x_others = [to_core(v) for v in x_rows]
-    x, q = call(own_kernel, [((own, LANES), F32)] * 2, [x_state, x_others[0], q_lin, to_core(q_lin)], [place])
     z, y, lower, upper = call(
         slab_kernel, [((half_rows, LANES), F32)] * 4, [z_state, y_state, lower_bound, upper_bound], [place]
     )
-    wide = 2 * span
-    a_hi, a_lo, t_hi, t_lo, p_hi, p_lo, diag = call(
+    sides = [((slab_rows, span), BF16)] * 2 + [((span, slab_rows), BF16)] * 2
+    *halves, p_hi, p_lo, diag = call(
         functools.partial(prep_kernel, slab, per),
-        [((slab_rows, wide), BF16)] * 2
-        + [((wide, slab_rows), BF16)] * 2
-        + [((2, 2 * BLK, 2 * BLK), BF16)] * 2
-        + [((2 * n_range, LANES), F32)],
+        sides * 2 + [((2, 2 * BLK, 2 * BLK), BF16)] * 2 + [((2 * n_range, LANES), F32)],
         [a_mine, a_other, p_mine, p_other],
-        [cols, pairs],
+        [place, cols, pairs],
         flops=10**8,
     )
-    prod_flops = 4 * slab_rows * wide * LANES
-    total_scratch = [pltpu.VMEM((span, LANES), F32)]
-
-    def forward(msgs, scalars, pp_first=()):
+    near_a, near_t, far_a, far_t = halves[0:2], halves[2:4], halves[4:6], halves[6:8]
+    *late, diag = lax.optimization_barrier((*x_rows[m:], diag))
+    x_rows = [*x_rows[:m], *late]
+    x_others = [to_core(v) for v in x_rows]
+    x, q = call(own_kernel, [((own, LANES), F32)] * 2, [x_state, x_others[0], q_lin, to_core(q_lin)], [place])
+    prod_flops = 2 * slab_rows * 2 * span * LANES
+    total_scratch = [pltpu.VMEM((span // 2, LANES), F32)]
+
+    def forward(msgs, scalars, pp_first=(), others=()):
         extra = SC if scalars else 0
+        part, near_wide = call(
+            functools.partial(near_kernel, n, own, scalars == 0),
+            [((slab_rows, LANES), F32), ((span, LANES), BF16)],
+            [*msgs[:m], *others[:m], *near_a],
+            [place],
+            flops=prod_flops,
+        )
         return call(
             functools.partial(forward_kernel, n, own, scalars),
             [((half_rows + extra, LANES), F32), ((2 * BLK, LANES), F32)],
-            [*msgs, a_hi, a_lo, p_hi, p_lo, *pp_first],
+            [*msgs[m:], *(msgs[:m] if scalars else others[m:]), part, near_wide, *far_a, p_hi, p_lo, *pp_first],
             [place, pairs],
-            total_scratch + [pltpu.VMEM((wide, LANES), BF16)],
+            [pltpu.VMEM((2 * span, LANES), BF16)],
             flops=prod_flops,
         )
 
-    msg, ppx = forward(x_rows + x_others, 0)
-    *pieces, ax = call(
+    def backward(far_pieces, w, pp, extra):
+        got = to_row(far_pieces, range(m, n))
+        shape = far_pieces[0].shape
+        near = call(
+            functools.partial(near_back_kernel, own),
+            [(shape, F32)] * m,
+            [w, pp, extra, *near_t],
+            [place, pairs],
+            total_scratch,
+            flops=prod_flops,
+        )
+        return [near[0], *to_row(near[1:], range(1, m)), *got]
+
+    msg, ppx = forward(x_rows, 0, (), x_others)
+    w_shape = ((slab_rows, LANES), BF16)
+    *pieces, ax, w = call(
         functools.partial(start_back_kernel, n, nx, own),
-        [((own + 2 * n_range, LANES), F32)] * n + [((half_rows, LANES), F32)],
-        [*to_x(msg), z, y, ppx, diag, t_hi, t_lo],
+        [((own + 2 * n_range, LANES), F32)] * m + [((half_rows, LANES), F32), w_shape],
+        [*to_x(msg), z, y, ppx, diag, *far_t],
         [place, pairs],
         total_scratch,
         flops=prod_flops,
     )
+    pieces = backward(pieces, w, ppx, diag)
     own_shape = ((own, LANES), F32)
     msg_shape = ((own + SC, LANES), F32)
     tile_shape = ((SC, LANES), F32)
@@ -463,22 +531,22 @@
             msg1, r, dk = call(
                 functools.partial(residual_kernel, n, own, True),
                 [msg_shape, own_shape, own_shape],
-                [*to_row(pieces), x, q, pd],
+                [*pieces, x, q, pd],
                 [place],
-                total_scratch,
+                [pltpu.VMEM((span, LANES), F32)],
             )
         else:
             msg1, r = call(
                 functools.partial(residual_kernel, n, own, False),
                 [msg_shape, own_shape],
-                [*to_row(pieces), x, q, pd, dk],
+                [*pieces, x, q, pd, dk],
                 [place],
             )
         msg, pp1 = forward(to_all_rows(msg1), 1)
-        *pieces, ad, scal = call(
+        *pieces, ad, scal, curve, w = call(
             functools.partial(step_back_kernel, n, nx, own),
-            [msg_shape] * n + [slab_shape, tile_shape],
-            [*to_x(msg), pp1, t_hi, t_lo],
+            [msg_shape] * m + [slab_shape, tile_shape, tile_shape, w_shape],
+            [*to_x(msg), pp1, *far_t],
             [place, pairs],
             total_scratch,
             flops=prod_flops,
@@ -486,7 +554,7 @@
         msg2, step = call(
             functools.partial(step_kernel, n, own),
             [msg_shape, tile_shape],
-            [*to_row(pieces), scal, msg1, r, pd, dk],
+            [*backward(pieces, w, pp1, curve), scal, msg1, r, pd, dk],
         )
         msg, pp2 = forward(to_all_rows(msg2), 2, (pp1,))
         ad2, share, keep = call(
@@ -497,14 +565,15 @@
         shares = to_all_rows(share)
         state = [*shares, keep, step, ax, ad, ad2, z, y, lower, upper, x, msg1, msg2]
         if outer + 1 < ADMM_ITERS:
-            *pieces, x, z, y, ax, ppx = call(
+            *pieces, x, z, y, ax, ppx, w = call(
                 functools.partial(update_kernel, n, own),
-                [own_shape] * n + [own_shape, slab_shape, slab_shape, slab_shape, ((2 * BLK, LANES), F32)],
-                [*state, ppx, pp1, pp2, t_hi, t_lo],
+                [own_shape] * m + [own_shape, slab_shape, slab_shape, slab_shape, ((2 * BLK, LANES), F32), w_shape],
+                [*state, ppx, pp1, pp2, *far_t],
                 [place, pairs],
                 total_scratch,
                 flops=prod_flops,
             )
+            pieces = backward(pieces, w, ppx, share)
         else:
             (out,) = call(
                 functools.partial(last_kernel, n, own), [((2 * half_rows + own, LANES), F32)], state

time: 203 us -> 206 us (1.015)
  Pallas kernels: 35.6 us -> 46.7 us
  waiting for transfers between devices: 99.6 us -> 88.7 us
  starting transfers between devices: 61 us -> 63.9 us
    pallas_call x20 -> x29, Pallas kernels: 35.6 us -> 46.7 us  [call(): pl.pallas_call(body, out_shape=[jax.ShapeDtypeStruct(s, d) for s, d in ou...]
    ppermute x33, waiting for transfers between devices: 74.6 us -> 63.8 us  [to_row(): lax.ppermute(v, 'row', [(i, i ^ k) for i in range(n)])]
    ppermute x33, starting transfers between devices: 51.5 us -> 53.7 us  [to_row(): lax.ppermute(v, 'row', [(i, i ^ k) for i in range(n)])]
  transfers between devices with their start and end apart: 48 -> 48, of which waited for: 30 -> 31; matrix products, arithmetic and copies ran while one was open for 1% -> 1% of each run, Pallas kernels for 2% -> 9%
where the time goes in v5:
time: 206 us; the launch traced here: 205 us
  waiting for transfers between devices  88.7 us (43%)
  starting transfers between devices  63.9 us (31%)
  Pallas kernels  46.7 us (23%)
  local copies, waits for them, and re-layouts  3.5 us (2%)
    ppermute x33, waiting for transfers between devices, to_row(): lax.ppermute(v, 'row', [(i, i ^ k) for i in range(n)])  63.8 us
    ppermute x33, starting transfers between devices, to_row(): lax.ppermute(v, 'row', [(i, i ^ k) for i in range(n)])  53.7 us
    pallas_call x29, Pallas kernels, call(): pl.pallas_call(body, out_shape=[jax.ShapeDtypeStruct(s, d) for s, d in ou...  46.7 us
    ppermute x5, waiting for transfers between devices, to_x(): lax.ppermute(v, 'col', [(c, c ^ 2 * k) for c in range(n_col)])  21.4 us
    ppermute x5, starting transfers between devices, to_x(): lax.ppermute(v, 'col', [(c, c ^ 2 * k) for c in range(n_col)])  7.52 us
  transfers between devices with their start and end apart: 48, of which 31 were waited for; matrix products, arithmetic and copies ran while one was open for 1% of the time, Pallas kernels for 9%

profile of v5, /device:TPU:0, one launch (start us, length us, event | category | flops | bytes accessed | tf_op | source)
XLA Modules:
  0.0 205.4 jit_solution(2436601247336751386)
XLA Ops:
  1.1 2.7 %collective-permute-start.7 = (f32[256,128]{1,0:T(8,128)}, f32[256,128]{1,0:T(8,128)S(1)}, u32[]{:S(2)}, u32[]{:S(2)}) collective-permute-start(f32[256,128]{1,0:T(8,128)} %x.1), channel_id=1, source_target_pairs={{0,4},{4,0},{8,12},{12,8},{1,5},{5,1},{9,13},{13,9},{2,6},{6,2},{1... | collective-permute-start | bytes 393224 | tf_op jit(solution)/shard_map/ppermute | solution.py:444
  3.8 2.5 %collective-permute-start.2 = (f32[256,128]{1,0:T(8,128)}, f32[256,128]{1,0:T(8,128)S(1)}, u32[]{:S(2)}, u32[]{:S(2)}) collective-permute-start(f32[256,128]{1,0:T(8,128)} %x.1), channel_id=1, source_target_pairs={{0,12},{4,8},{8,4},{12,0},{1,13},{5,9},{9,5},{13,1},{2,14},{6,10},... | collective-permute-start | bytes 393224 | tf_op jit(solution)/shard_map/ppermute | solution.py:444
  13.1 7.6 %shard_map.130 = (bf16[768,1024]{1,0:T(8,128)(2,1)S(1)}, bf16[768,1024]{1,0:T(8,128)(2,1)S(1)}, bf16[1024,768]{1,0:T(8,128)(2,1)S(1)}, bf16[1024,768]{1,0:T(8,12...) custom-call(s32[3]{0:T(128)S(1)} %pad_add_fusion.place, ...), custom_call_target="tpu_custom_call" | custom-call | flops 100000000 | bytes 3670016 | tf_op jit(solution)/shard_map/pallas_call | solution.py:27
  21.3 1.8 shard_map.131
  23.2 2.1 %shard_map.132 = (f32[384,128]{1,0:T(8,128)S(1)}, f32[256,128]{1,0:T(8,128)S(1)}) custom-call(s32[3]{0:T(128)S(1)} %pad_add_fusion.place, s32[4]{0:T(128)S(1)} %pad_add_fusion.2.pairs, f32[256,128]{1,0:T(8,128)S(1)} %collective-permute-done.1.refs_0_, f32[256,128]{1,0:T(8,128)S(1)} %collective-permute-done.2.refs_1_, ...), custom_call_target="tpu_custom_call" | custom-call | flops 402653184 | bytes 4849664 | tf_op jit(solution)/shard_map/pallas_call | solution.py:27
  25.3 1.5 collective-permute-start.10
  28.1 4.2 %collective-permute-done.10.refs_1_ = f32[384,128]{1,0:T(8,128)S(1)} collective-permute-done((f32[384,128]{1,0:T(8,128)S(1)}, f32[384,128]{1,0:T(8,128)S(1)}, u32[]{:S(2)}, u32[]{:S(2)}) %collective-permute-start.10) | collective-permute-done | bytes 196640 | tf_op jit(solution)/shard_map/ppermute | solution.py:439
  32.3 1.8 shard_map.134
  34.1 1.7 shard_map.135
  35.8 1.7 collective-permute-start.11
  37.6 4.0 %collective-permute-start.12 = (f32[272,128]{1,0:T(8,128)S(1)}, f32[272,128]{1,0:T(8,128)S(1)}, u32[]{:S(2)}, u32[]{:S(2)}) collective-permute-start(f32[272,128]{1,0:T(8,128)S(1)} %get-tuple-element.112), channel_id=1, source_target_pairs={{0,8},{4,12},{8,0},{12,4},{1,9},{5,13},{9,1},{13,5},{2,10},{6,14},... | collective-permute-start | bytes 417800 | tf_op jit(solution)/shard_map/ppermute | solution.py:444
  44.0 7.8 %collective-permute-done.12.refs_2_ = f32[272,128]{1,0:T(8,128)S(1)} collective-permute-done((f32[272,128]{1,0:T(8,128)S(1)}, f32[272,128]{1,0:T(8,128)S(1)}, u32[]{:S(2)}, u32[]{:S(2)}) %collective-permute-start.12) | collective-permute-done | bytes 139296 | tf_op jit(solution)/shard_map/ppermute | solution.py:444
  52.8 2.1 %collective-permute-start.18 = (f32[264,128]{1,0:T(8,128)S(1)}, f32[264,128]{1,0:T(8,128)S(1)}, u32[]{:S(2)}, u32[]{:S(2)}) collective-permute-start(f32[264,128]{1,0:T(8,128)S(1)} %get-tuple-element.116.refs_0_.refs_2_.refs_5_.refs_14_), channel_id=1, source_target_pairs={{0,4},{4,0},{8,12},{12,8},{1,5},{5,1},{9,13},{13,9},{2,6},{6,2},{1... | collective-permute-start | bytes 405512 | tf_op jit(solution)/shard_map/ppermute | solution.py:444
  54.9 2.5 %collective-permute-start.17 = (f32[264,128]{1,0:T(8,128)S(1)}, f32[264,128]{1,0:T(8,128)S(1)}, u32[]{:S(2)}, u32[]{:S(2)}) collective-permute-start(f32[264,128]{1,0:T(8,128)S(1)} %get-tuple-element.116.refs_0_.refs_2_.refs_5_.refs_14_), channel_id=1, source_target_pairs={{0,12},{4,8},{8,4},{12,0},{1,13},{5,9},{9,5},{13,1},{2,14},{6,10},... | collective-permute-start | bytes 405512 | tf_op jit(solution)/shard_map/ppermute | solution.py:444
  58.8 1.7 shard_map.138
  60.4 3.7 %collective-permute-done.17.refs_1_ = f32[264,128]{1,0:T(8,128)S(1)} collective-permute-done((f32[264,128]{1,0:T(8,128)S(1)}, f32[264,128]{1,0:T(8,128)S(1)}, u32[]{:S(2)}, u32[]{:S(2)}) %collective-permute-start.17) | collective-permute-done | bytes 135200 | tf_op jit(solution)/shard_map/ppermute | solution.py:444
  64.1 4.0 %collective-permute-done.16.refs_0_ = f32[264,128]{1,0:T(8,128)S(1)} collective-permute-done((f32[264,128]{1,0:T(8,128)S(1)}, f32[264,128]{1,0:T(8,128)S(1)}, u32[]{:S(2)}, u32[]{:S(2)}) %collective-permute-start.16) | collective-permute-done | bytes 135200 | tf_op jit(solution)/shard_map/ppermute | solution.py:444
  68.1 2.0 shard_map.139
  70.1 1.5 collective-permute-start.19
  71.6 4.5 %collective-permute-done.19.refs_1_ = f32[392,128]{1,0:T(8,128)S(1)} collective-permute-done((f32[392,128]{1,0:T(8,128)S(1)}, f32[392,128]{1,0:T(8,128)S(1)}, u32[]{:S(2)}, u32[]{:S(2)}) %collective-permute-start.19) | collective-permute-done | bytes 200736 | tf_op jit(solution)/shard_map/ppermute | solution.py:439
  76.1 1.7 shard_map.140
  77.9 1.7 shard_map.141
  79.6 2.2 %collective-permute-start.21 = (f32[264,128]{1,0:T(8,128)S(1)}, f32[264,128]{1,0:T(8,128)S(1)}, u32[]{:S(2)}, u32[]{:S(2)}) collective-permute-start(f32[264,128]{1,0:T(8,128)S(1)} %get-tuple-element.125), channel_id=1, source_target_pairs={{0,8},{4,12},{8,0},{12,4},{1,9},{5,13},{9,1},{13,5},{2,10},{6,14},... | collective-permute-start | bytes 405512 | tf_op jit(solution)/shard_map/ppermute | solution.py:444
  81.9 2.1 %collective-permute-start.22 = (f32[264,128]{1,0:T(8,128)S(1)}, f32[264,128]{1,0:T(8,128)S(1)}, u32[]{:S(2)}, u32[]{:S(2)}) collective-permute-start(f32[264,128]{1,0:T(8,128)S(1)} %get-tuple-element.126), channel_id=1, source_target_pairs={{0,12},{4,8},{8,4},{12,0},{1,13},{5,9},{9,5},{13,1},{2,14},{6,10},... | collective-permute-start | bytes 405512 | tf_op jit(solution)/shard_map/ppermute | solution.py:444
  85.0 6.6 %collective-permute-done.21.refs_2_ = f32[264,128]{1,0:T(8,128)S(1)} collective-permute-done((f32[264,128]{1,0:T(8,128)S(1)}, f32[264,128]{1,0:T(8,128)S(1)}, u32[]{:S(2)}, u32[]{:S(2)}) %collective-permute-start.21) | collective-permute-done | bytes 135200 | tf_op jit(solution)/shard_map/ppermute | solution.py:444
  91.7 2.1 %collective-permute-start.25 = (f32[264,128]{1,0:T(8,128)S(1)}, f32[264,128]{1,0:T(8,128)S(1)}, u32[]{:S(2)}, u32[]{:S(2)}) collective-permute-start(f32[264,128]{1,0:T(8,128)S(1)} %get-tuple-element.130.refs_0_.refs_2_.refs_15_), channel_id=1, source_target_pairs={{0,4},{4,0},{8,12},{12,8},{1,5},{5,1},{9,13},{13,9},{2,6},{6,2},{1... | collective-permute-start | bytes 405512 | tf_op jit(solution)/shard_map/ppermute | solution.py:444
  95.3 3.5 %collective-permute-done.25.refs_1_.refs_3_ = f32[264,128]{1,0:T(8,128)S(1)} collective-permute-done((f32[264,128]{1,0:T(8,128)S(1)}, f32[264,128]{1,0:T(8,128)S(1)}, u32[]{:S(2)}, u32[]{:S(2)}) %collective-permute-start.25) | collective-permute-done | bytes 135200 | tf_op jit(solution)/shard_map/ppermute | solution.py:444
  98.8 1.7 shard_map.143
  101.7 4.4 %collective-permute-done.23.refs_0_ = f32[264,128]{1,0:T(8,128)S(1)} collective-permute-done((f32[264,128]{1,0:T(8,128)S(1)}, f32[264,128]{1,0:T(8,128)S(1)}, u32[]{:S(2)}, u32[]{:S(2)}) %collective-permute-start.23) | collective-permute-done | bytes 135200 | tf_op jit(solution)/shard_map/ppermute | solution.py:444
  106.0 2.0 shard_map.144
  109.5 4.2 %collective-permute-done.26.refs_1_ = f32[392,128]{1,0:T(8,128)S(1)} collective-permute-done((f32[392,128]{1,0:T(8,128)S(1)}, f32[392,128]{1,0:T(8,128)S(1)}, u32[]{:S(2)}, u32[]{:S(2)}) %collective-permute-start.26) | collective-permute-done | bytes 200736 | tf_op jit(solution)/shard_map/ppermute | solution.py:439
  113.9 1.9 collective-permute-start.29
  115.8 2.7 %collective-permute-start.27 = (f32[8,128]{1,0:T(8,128)S(1)}, f32[8,128]{1,0:T(8,128)S(1)}, u32[]{:S(2)}, u32[]{:S(2)}) collective-permute-start(f32[8,128]{1,0:T(8,128)S(1)} %get-tuple-element.135.refs_0_.extra), channel_id=1, source_target_pairs={{0,4},{4,0},{8,12},{12,8},{1,5},{5,1},{9,13},{13,9},{2,6},{6,2},{1... | collective-permute-start | bytes 12296 | tf_op jit(solution)/shard_map/ppermute | solution.py:444
  120.3 1.9 shard_map.146
  122.2 1.7 shard_map.147
  123.9 1.8 collective-permute-start.30
  126.7 1.7 collective-permute-start.32
  128.4 1.6 collective-permute-done.30.refs_1_
  130.0 5.3 %collective-permute-done.31.refs_2_ = f32[256,128]{1,0:T(8,128)S(1)} collective-permute-done((f32[256,128]{1,0:T(8,128)S(1)}, f32[256,128]{1,0:T(8,128)S(1)}, u32[]{:S(2)}, u32[]{:S(2)}) %collective-permute-start.31) | collective-permute-done | bytes 131104 | tf_op jit(solution)/shard_map/ppermute | solution.py:444
  135.9 6.3 %collective-permute-start.35 = (f32[264,128]{1,0:T(8,128)S(1)}, f32[264,128]{1,0:T(8,128)S(1)}, u32[]{:S(2)}, u32[]{:S(2)}) collective-permute-start(f32[264,128]{1,0:T(8,128)S(1)} %get-tuple-element.150.refs_0_.refs_2_.refs_5_.refs_14_), channel_id=1, source_target_pairs={{0,4},{4,0},{8,12},{12,8},{1,5},{5,1},{9,13},{13,9},{2,6},{6,2},{1... | collective-permute-start | bytes 405512 | tf_op jit(solution)/shard_map/ppermute | solution.py:444
  142.3 1.9 collective-permute-start.34
  145.3 1.7 shard_map.149
  146.9 2.2 %collective-permute-done.34.refs_1_ = f32[264,128]{1,0:T(8,128)S(1)} collective-permute-done((f32[264,128]{1,0:T(8,128)S(1)}, f32[264,128]{1,0:T(8,128)S(1)}, u32[]{:S(2)}, u32[]{:S(2)}) %collective-permute-start.34) | collective-permute-done | bytes 135200 | tf_op jit(solution)/shard_map/ppermute | solution.py:444
  149.1 2.8 %collective-permute-done.33.refs_0_ = f32[264,128]{1,0:T(8,128)S(1)} collective-permute-done((f32[264,128]{1,0:T(8,128)S(1)}, f32[264,128]{1,0:T(8,128)S(1)}, u32[]{:S(2)}, u32[]{:S(2)}) %collective-permute-start.33) | collective-permute-done | bytes 135200 | tf_op jit(solution)/shard_map/ppermute | solution.py:444
  152.0 2.0 shard_map.150
  154.0 1.5 collective-permute-start.36
  155.5 4.2 %collective-permute-done.36.refs_1_ = f32[392,128]{1,0:T(8,128)S(1)} collective-permute-done((f32[392,128]{1,0:T(8,128)S(1)}, f32[392,128]{1,0:T(8,128)S(1)}, u32[]{:S(2)}, u32[]{:S(2)}) %collective-permute-start.36) | collective-permute-done | bytes 200736 | tf_op jit(solution)/shard_map/ppermute | solution.py:439
  159.7 1.7 shard_map.151
  161.4 1.7 shard_map.152
  163.2 2.4 %collective-permute-start.38 = (f32[264,128]{1,0:T(8,128)S(1)}, f32[264,128]{1,0:T(8,128)S(1)}, u32[]{:S(2)}, u32[]{:S(2)}) collective-permute-start(f32[264,128]{1,0:T(8,128)S(1)} %get-tuple-element.159), channel_id=1, source_target_pairs={{0,8},{4,12},{8,0},{12,4},{1,9},{5,13},{9,1},{13,5},{2,10},{6,14},... | collective-permute-start | bytes 405512 | tf_op jit(solution)/shard_map/ppermute | solution.py:444
  165.6 2.0 collective-permute-start.39
  167.6 2.8 %collective-permute-done.37.refs_1_ = f32[264,128]{1,0:T(8,128)S(1)} collective-permute-done((f32[264,128]{1,0:T(8,128)S(1)}, f32[264,128]{1,0:T(8,128)S(1)}, u32[]{:S(2)}, u32[]{:S(2)}) %collective-permute-start.37) | collective-permute-done | bytes 135200 | tf_op jit(solution)/shard_map/ppermute | solution.py:444
  170.3 4.3 %collective-permute-done.38.refs_2_ = f32[264,128]{1,0:T(8,128)S(1)} collective-permute-done((f32[264,128]{1,0:T(8,128)S(1)}, f32[264,128]{1,0:T(8,128)S(1)}, u32[]{:S(2)}, u32[]{:S(2)}) %collective-permute-start.38) | collective-permute-done | bytes 135200 | tf_op jit(solution)/shard_map/ppermute | solution.py:444
  174.7 2.1 %collective-permute-start.42 = (f32[264,128]{1,0:T(8,128)S(1)}, f32[264,128]{1,0:T(8,128)S(1)}, u32[]{:S(2)}, u32[]{:S(2)}) collective-permute-start(f32[264,128]{1,0:T(8,128)S(1)} %get-tuple-element.163.refs_0_.refs_2_.refs_15_), channel_id=1, source_target_pairs={{0,4},{4,0},{8,12},{12,8},{1,5},{5,1},{9,13},{13,9},{2,6},{6,2},{1... | collective-permute-start | bytes 405512 | tf_op jit(solution)/shard_map/ppermute | solution.py:444
  176.8 1.9 collective-permute-start.41
  179.8 1.7 shard_map.154
  181.4 2.2 %collective-permute-done.41.refs_1_ = f32[264,128]{1,0:T(8,128)S(1)} collective-permute-done((f32[264,128]{1,0:T(8,128)S(1)}, f32[264,128]{1,0:T(8,128)S(1)}, u32[]{:S(2)}, u32[]{:S(2)}) %collective-permute-start.41) | collective-permute-done | bytes 135200 | tf_op jit(solution)/shard_map/ppermute | solution.py:444
  183.7 3.0 %collective-permute-done.40.refs_0_ = f32[264,128]{1,0:T(8,128)S(1)} collective-permute-done((f32[264,128]{1,0:T(8,128)S(1)}, f32[264,128]{1,0:T(8,128)S(1)}, u32[]{:S(2)}, u32[]{:S(2)}) %collective-permute-start.40) | collective-permute-done | bytes 135200 | tf_op jit(solution)/shard_map/ppermute | solution.py:444
  186.7 2.6 %shard_map.155 = (f32[392,128]{1,0:T(8,128)S(1)}, f32[256,128]{1,0:T(8,128)}) custom-call(s32[3]{0:T(128)S(1)} %pad_add_fusion.place, s32[4]{0:T(128)S(1)} %pad_add_fusion.2.pairs, f32[264,128]{1,0:T(8,128)S(1)} %collective-permute-done.40.refs_0_, f32[264,128]{1,0:T(8,128)S(1)} %collective-permute-done.41.refs_1_, ...), custom_call_target="tpu_custom_call" | custom-call | flops 402653184 | bytes 4997120 | tf_op jit(solution)/shard_map/pallas_call | solution.py:27
  190.7 4.2 %collective-permute-done.43.refs_1_ = f32[392,128]{1,0:T(8,128)S(1)} collective-permute-done((f32[392,128]{1,0:T(8,128)S(1)}, f32[392,128]{1,0:T(8,128)S(1)}, u32[]{:S(2)}, u32[]{:S(2)}) %collective-permute-start.43) | collective-permute-done | bytes 200736 | tf_op jit(solution)/shard_map/ppermute | solution.py:439
  195.1 1.9 collective-permute-start.46
  197.0 2.5 %collective-permute-start.44 = (f32[8,128]{1,0:T(8,128)S(1)}, f32[8,128]{1,0:T(8,128)S(1)}, u32[]{:S(2)}, u32[]{:S(2)}) collective-permute-start(f32[8,128]{1,0:T(8,128)S(1)} %get-tuple-element.168.refs_0_), channel_id=1, source_target_pairs={{0,4},{4,0},{8,12},{12,8},{1,5},{5,1},{9,13},{13,9},{2,6},{6,2},{1... | collective-permute-start | bytes 12296 | tf_op jit(solution)/shard_map/ppermute | solution.py:444
  201.8 1.9 collective-permute-done.47.got
  203.7 1.7 shard_map.158
  (89 shorter events, 29.2 us)
Async XLA Ops:
  0.6 10.1 %collective-permute-start.3 = (f32[24,128,128]{2,1,0:T(8,128)}, f32[24,128,128]{2,1,0:T(8,128)S(1)}, u32[]{:S(2)}, u32[]{:S(2)}) collective-permute-start(f32[24,128,128]{2,1,0:T(8,128)} %bitcast.7), channel_id=1, source_target_pairs={{0,1},{1,0},{2,3},{3,2},{4,5},{5,4},{6,7},{7,6},{8,9},{9,8},{10,11... | collective-permute-start | bytes 4718600 | tf_op jit(solution)/shard_map/ppermute | solution.py:436
  1.1 8.3 %collective-permute-start.7 = (f32[256,128]{1,0:T(8,128)}, f32[256,128]{1,0:T(8,128)S(1)}, u32[]{:S(2)}, u32[]{:S(2)}) collective-permute-start(f32[256,128]{1,0:T(8,128)} %x.1), channel_id=1, source_target_pairs={{0,4},{4,0},{8,12},{12,8},{1,5},{5,1},{9,13},{13,9},{2,6},{6,2},{1... | collective-permute-start | bytes 393224 | tf_op jit(solution)/shard_map/ppermute | solution.py:444
  3.8 16.9 %collective-permute-start.2 = (f32[256,128]{1,0:T(8,128)}, f32[256,128]{1,0:T(8,128)S(1)}, u32[]{:S(2)}, u32[]{:S(2)}) collective-permute-start(f32[256,128]{1,0:T(8,128)} %x.1), channel_id=1, source_target_pairs={{0,12},{4,8},{8,4},{12,0},{1,13},{5,9},{9,5},{13,1},{2,14},{6,10},... | collective-permute-start | bytes 393224 | tf_op jit(solution)/shard_map/ppermute | solution.py:444
  6.3 3.4 %collective-permute-start.4 = (f32[4,128,128]{2,1,0:T(8,128)}, f32[4,128,128]{2,1,0:T(8,128)S(1)}, u32[]{:S(2)}, u32[]{:S(2)}) collective-permute-start(f32[4,128,128]{2,1,0:T(8,128)} %bitcast.9), channel_id=1, source_target_pairs={{0,1},{1,0},{2,3},{3,2},{4,5},{5,4},{6,7},{7,6},{8,9},{9,8},{10,11... | collective-permute-start | bytes 786440 | tf_op jit(solution)/shard_map/ppermute | solution.py:436
  7.9 1.3 collective-permute-start
  9.2 11.5 %collective-permute-start.1 = (f32[256,128]{1,0:T(8,128)}, f32[256,128]{1,0:T(8,128)S(1)}, u32[]{:S(2)}, u32[]{:S(2)}) collective-permute-start(f32[256,128]{1,0:T(8,128)} %x.1), channel_id=1, source_target_pairs={{0,8},{4,12},{8,0},{12,4},{1,9},{5,13},{9,1},{13,5},{2,10},{6,14},... | collective-permute-start | bytes 393224 | tf_op jit(solution)/shard_map/ppermute | solution.py:444
  9.5 11.9 %collective-permute-start.8 = (f32[256,128]{1,0:T(8,128)}, f32[256,128]{1,0:T(8,128)S(1)}, u32[]{:S(2)}, u32[]{:S(2)}) collective-permute-start(f32[256,128]{1,0:T(8,128)} %x.1), channel_id=1, source_target_pairs={{0,1},{1,0},{2,3},{3,2},{4,5},{5,4},{6,7},{7,6},{8,9},{9,8},{10,11... | collective-permute-start | bytes 393224 | tf_op jit(solution)/shard_map/ppermute | solution.py:436
  9.6 11.7 %collective-permute-start.9 = (f32[256,128]{1,0:T(8,128)S(1)}, f32[256,128]{1,0:T(8,128)S(1)}, u32[]{:S(2)}, u32[]{:S(2)}) collective-permute-start(f32[256,128]{1,0:T(8,128)S(1)} %collective-permute-done.7.refs_1_), channel_id=1, source_target_pairs={{0,1},{1,0},{2,3},{3,2},{4,5},{5,4},{6,7},{7,6},{8,9},{9,8},{10,11... | collective-permute-start | bytes 393224 | tf_op jit(solution)/shard_map/ppermute | solution.py:436
  10.7 1.4 copy-start
  12.1 0.9 copy-start.6
  13.1 8.2 %copy-start.1 = (f32[256,128]{1,0:T(8,128)S(1)}, f32[256,128]{1,0:T(8,128)}, u32[]{:S(2)}) copy-start(f32[256,128]{1,0:T(8,128)} %x.1) | copy-start | bytes 393220
  20.7 2.4 %collective-permute-start.5 = (f32[256,128]{1,0:T(8,128)S(1)}, f32[256,128]{1,0:T(8,128)S(1)}, u32[]{:S(2)}, u32[]{:S(2)}) collective-permute-start(f32[256,128]{1,0:T(8,128)S(1)} %collective-permute-done.1.refs_0_), channel_id=1, source_target_pairs={{0,1},{1,0},{2,3},{3,2},{4,5},{5,4},{6,7},{7,6},{8,9},{9,8},{10,11... | collective-permute-start | bytes 393224 | tf_op jit(solution)/shard_map/ppermute | solution.py:436
  21.0 2.2 %collective-permute-start.6 = (f32[256,128]{1,0:T(8,128)S(1)}, f32[256,128]{1,0:T(8,128)S(1)}, u32[]{:S(2)}, u32[]{:S(2)}) collective-permute-start(f32[256,128]{1,0:T(8,128)S(1)} %collective-permute-done.2.refs_1_), channel_id=1, source_target_pairs={{0,1},{1,0},{2,3},{3,2},{4,5},{5,4},{6,7},{7,6},{8,9},{9,8},{10,11... | collective-permute-start | bytes 393224 | tf_op jit(solution)/shard_map/ppermute | solution.py:436
  23.2 3.7 %copy-start.2 = (f32[768,128]{1,0:T(8,128)S(1)}, f32[768,128]{1,0:T(8,128)}, u32[]{:S(2)}) copy-start(f32[768,128]{1,0:T(8,128)} %refs_0_.3) | copy-start | bytes 1179652
  23.2 3.6 %copy-start.3 = (f32[768,128]{1,0:T(8,128)S(1)}, f32[768,128]{1,0:T(8,128)}, u32[]{:S(2)}) copy-start(f32[768,128]{1,0:T(8,128)} %refs_1_.1) | copy-start | bytes 1179652
  23.2 3.6 %copy-start.4 = (f32[768,128]{1,0:T(8,128)S(1)}, f32[768,128]{1,0:T(8,128)}, u32[]{:S(2)}) copy-start(f32[768,128]{1,0:T(8,128)} %refs_2_.1) | copy-start | bytes 1179652
  23.2 3.6 %copy-start.5 = (f32[768,128]{1,0:T(8,128)S(1)}, f32[768,128]{1,0:T(8,128)}, u32[]{:S(2)}) copy-start(f32[768,128]{1,0:T(8,128)} %refs_3_.1) | copy-start | bytes 1179652
  25.3 7.1 %collective-permute-start.10 = (f32[384,128]{1,0:T(8,128)S(1)}, f32[384,128]{1,0:T(8,128)S(1)}, u32[]{:S(2)}, u32[]{:S(2)}) collective-permute-start(f32[384,128]{1,0:T(8,128)S(1)} %get-tuple-element.100.refs_0_), channel_id=1, source_target_pairs={{0,2},{1,3},{2,0},{3,1},{4,6},{5,7},{6,4},{7,5},{8,10},{9,11},{10,... | collective-permute-start | bytes 589832 | tf_op jit(solution)/shard_map/ppermute | solution.py:439
  34.1 7.5 %copy-start.7 = (f32[256,128]{1,0:T(8,128)S(1)}, f32[256,128]{1,0:T(8,128)}, u32[]{:S(2)}) copy-start(f32[256,128]{1,0:T(8,128)} %q.1) | copy-start | bytes 393220
  34.1 7.5 %copy-start.8 = (f32[256]{0:T(256)S(1)}, f32[256]{0:T(256)}, u32[]{:S(2)}) copy-start(f32[256]{0:T(256)} %param.13) | copy-start | bytes 3076
  35.8 8.2 %collective-permute-start.11 = (f32[272,128]{1,0:T(8,128)S(1)}, f32[272,128]{1,0:T(8,128)S(1)}, u32[]{:S(2)}, u32[]{:S(2)}) collective-permute-start(f32[272,128]{1,0:T(8,128)S(1)} %get-tuple-element.111), channel_id=1, source_target_pairs={{0,4},{4,0},{8,12},{12,8},{1,5},{5,1},{9,13},{13,9},{2,6},{6,2},{1... | collective-permute-start | bytes 417800 | tf_op jit(solution)/shard_map/ppermute | solution.py:444
  37.6 14.3 %collective-permute-start.12 = (f32[272,128]{1,0:T(8,128)S(1)}, f32[272,128]{1,0:T(8,128)S(1)}, u32[]{:S(2)}, u32[]{:S(2)}) collective-permute-start(f32[272,128]{1,0:T(8,128)S(1)} %get-tuple-element.112), channel_id=1, source_target_pairs={{0,8},{4,12},{8,0},{12,4},{1,9},{5,13},{9,1},{13,5},{2,10},{6,14},... | collective-permute-start | bytes 417800 | tf_op jit(solution)/shard_map/ppermute | solution.py:444
  41.6 10.2 %collective-permute-start.13 = (f32[272,128]{1,0:T(8,128)S(1)}, f32[272,128]{1,0:T(8,128)S(1)}, u32[]{:S(2)}, u32[]{:S(2)}) collective-permute-start(f32[272,128]{1,0:T(8,128)S(1)} %get-tuple-element.113), channel_id=1, source_target_pairs={{0,12},{4,8},{8,4},{12,0},{1,13},{5,9},{9,5},{13,1},{2,14},{6,10},... | collective-permute-start | bytes 417800 | tf_op jit(solution)/shard_map/ppermute | solution.py:444
  41.6 1.7 collective-permute-start.14
  41.6 1.3 collective-permute-start.15
  52.8 6.0 %collective-permute-start.18 = (f32[264,128]{1,0:T(8,128)S(1)}, f32[264,128]{1,0:T(8,128)S(1)}, u32[]{:S(2)}, u32[]{:S(2)}) collective-permute-start(f32[264,128]{1,0:T(8,128)S(1)} %get-tuple-element.116.refs_0_.refs_2_.refs_5_.refs_14_), channel_id=1, source_target_pairs={{0,4},{4,0},{8,12},{12,8},{1,5},{5,1},{9,13},{13,9},{2,6},{6,2},{1... | collective-permute-start | bytes 405512 | tf_op jit(solution)/shard_map/ppermute | solution.py:444
  54.9 9.2 %collective-permute-start.17 = (f32[264,128]{1,0:T(8,128)S(1)}, f32[264,128]{1,0:T(8,128)S(1)}, u32[]{:S(2)}, u32[]{:S(2)}) collective-permute-start(f32[264,128]{1,0:T(8,128)S(1)} %get-tuple-element.116.refs_0_.refs_2_.refs_5_.refs_14_), channel_id=1, source_target_pairs={{0,12},{4,8},{8,4},{12,0},{1,13},{5,9},{9,5},{13,1},{2,14},{6,10},... | collective-permute-start | bytes 405512 | tf_op jit(solution)/shard_map/ppermute | solution.py:444
  57.4 10.7 %collective-permute-start.16 = (f32[264,128]{1,0:T(8,128)S(1)}, f32[264,128]{1,0:T(8,128)S(1)}, u32[]{:S(2)}, u32[]{:S(2)}) collective-permute-start(f32[264,128]{1,0:T(8,128)S(1)} %get-tuple-element.116.refs_0_.refs_2_.refs_5_.refs_14_), channel_id=1, source_target_pairs={{0,8},{4,12},{8,0},{12,4},{1,9},{5,13},{9,1},{13,5},{2,10},{6,14},... | collective-permute-start | bytes 405512 | tf_op jit(solution)/shard_map/ppermute | solution.py:444
  70.1 6.0 %collective-permute-start.19 = (f32[392,128]{1,0:T(8,128)S(1)}, f32[392,128]{1,0:T(8,128)S(1)}, u32[]{:S(2)}, u32[]{:S(2)}) collective-permute-start(f32[392,128]{1,0:T(8,128)S(1)} %get-tuple-element.119.refs_0_), channel_id=1, source_target_pairs={{0,2},{1,3},{2,0},{3,1},{4,6},{5,7},{6,4},{7,5},{8,10},{9,11},{10,... | collective-permute-start | bytes 602120 | tf_op jit(solution)/shard_map/ppermute | solution.py:439
  79.6 5.4 %collective-permute-start.20 = (f32[264,128]{1,0:T(8,128)S(1)}, f32[264,128]{1,0:T(8,128)S(1)}, u32[]{:S(2)}, u32[]{:S(2)}) collective-permute-start(f32[264,128]{1,0:T(8,128)S(1)} %get-tuple-element.124), channel_id=1, source_target_pairs={{0,4},{4,0},{8,12},{12,8},{1,5},{5,1},{9,13},{13,9},{2,6},{6,2},{1... | collective-permute-start | bytes 405512 | tf_op jit(solution)/shard_map/ppermute | solution.py:444
  79.6 11.9 %collective-permute-start.21 = (f32[264,128]{1,0:T(8,128)S(1)}, f32[264,128]{1,0:T(8,128)S(1)}, u32[]{:S(2)}, u32[]{:S(2)}) collective-permute-start(f32[264,128]{1,0:T(8,128)S(1)} %get-tuple-element.125), channel_id=1, source_target_pairs={{0,8},{4,12},{8,0},{12,4},{1,9},{5,13},{9,1},{13,5},{2,10},{6,14},... | collective-permute-start | bytes 405512 | tf_op jit(solution)/shard_map/ppermute | solution.py:444
  81.9 9.7 %collective-permute-start.22 = (f32[264,128]{1,0:T(8,128)S(1)}, f32[264,128]{1,0:T(8,128)S(1)}, u32[]{:S(2)}, u32[]{:S(2)}) collective-permute-start(f32[264,128]{1,0:T(8,128)S(1)} %get-tuple-element.126), channel_id=1, source_target_pairs={{0,12},{4,8},{8,4},{12,0},{1,13},{5,9},{9,5},{13,1},{2,14},{6,10},... | collective-permute-start | bytes 405512 | tf_op jit(solution)/shard_map/ppermute | solution.py:444
  91.7 7.1 %collective-permute-start.25 = (f32[264,128]{1,0:T(8,128)S(1)}, f32[264,128]{1,0:T(8,128)S(1)}, u32[]{:S(2)}, u32[]{:S(2)}) collective-permute-start(f32[264,128]{1,0:T(8,128)S(1)} %get-tuple-element.130.refs_0_.refs_2_.refs_15_), channel_id=1, source_target_pairs={{0,4},{4,0},{8,12},{12,8},{1,5},{5,1},{9,13},{13,9},{2,6},{6,2},{1... | collective-permute-start | bytes 405512 | tf_op jit(solution)/shard_map/ppermute | solution.py:444
  93.8 7.9 %collective-permute-start.24 = (f32[264,128]{1,0:T(8,128)S(1)}, f32[264,128]{1,0:T(8,128)S(1)}, u32[]{:S(2)}, u32[]{:S(2)}) collective-permute-start(f32[264,128]{1,0:T(8,128)S(1)} %get-tuple-element.130.refs_0_.refs_2_.refs_15_), channel_id=1, source_target_pairs={{0,12},{4,8},{8,4},{12,0},{1,13},{5,9},{9,5},{13,1},{2,14},{6,10},... | collective-permute-start | bytes 405512 | tf_op jit(solution)/shard_map/ppermute | solution.py:444
  95.1 10.9 %collective-permute-start.23 = (f32[264,128]{1,0:T(8,128)S(1)}, f32[264,128]{1,0:T(8,128)S(1)}, u32[]{:S(2)}, u32[]{:S(2)}) collective-permute-start(f32[264,128]{1,0:T(8,128)S(1)} %get-tuple-element.130.refs_0_.refs_2_.refs_15_), channel_id=1, source_target_pairs={{0,8},{4,12},{8,0},{12,4},{1,9},{5,13},{9,1},{13,5},{2,10},{6,14},... | collective-permute-start | bytes 405512 | tf_op jit(solution)/shard_map/ppermute | solution.py:444
  108.0 5.7 %collective-permute-start.26 = (f32[392,128]{1,0:T(8,128)S(1)}, f32[392,128]{1,0:T(8,128)S(1)}, u32[]{:S(2)}, u32[]{:S(2)}) collective-permute-start(f32[392,128]{1,0:T(8,128)S(1)} %get-tuple-element.133.refs_0_), channel_id=1, source_target_pairs={{0,2},{1,3},{2,0},{3,1},{4,6},{5,7},{6,4},{7,5},{8,10},{9,11},{10,... | collective-permute-start | bytes 602120 | tf_op jit(solution)/shard_map/ppermute | solution.py:439
  113.9 5.6 %collective-permute-start.29 = (f32[8,128]{1,0:T(8,128)S(1)}, f32[8,128]{1,0:T(8,128)S(1)}, u32[]{:S(2)}, u32[]{:S(2)}) collective-permute-start(f32[8,128]{1,0:T(8,128)S(1)} %get-tuple-element.135.refs_0_.extra), channel_id=1, source_target_pairs={{0,12},{4,8},{8,4},{12,0},{1,13},{5,9},{9,5},{13,1},{2,14},{6,10},... | collective-permute-start | bytes 12296 | tf_op jit(solution)/shard_map/ppermute | solution.py:444
  115.8 4.5 %collective-permute-start.28 = (f32[8,128]{1,0:T(8,128)S(1)}, f32[8,128]{1,0:T(8,128)S(1)}, u32[]{:S(2)}, u32[]{:S(2)}) collective-permute-start(f32[8,128]{1,0:T(8,128)S(1)} %get-tuple-element.135.refs_0_.extra), channel_id=1, source_target_pairs={{0,8},{4,12},{8,0},{12,4},{1,9},{5,13},{9,1},{13,5},{2,10},{6,14},... | collective-permute-start | bytes 12296 | tf_op jit(solution)/shard_map/ppermute | solution.py:444
  115.8 4.5 %collective-permute-start.27 = (f32[8,128]{1,0:T(8,128)S(1)}, f32[8,128]{1,0:T(8,128)S(1)}, u32[]{:S(2)}, u32[]{:S(2)}) collective-permute-start(f32[8,128]{1,0:T(8,128)S(1)} %get-tuple-element.135.refs_0_.extra), channel_id=1, source_target_pairs={{0,4},{4,0},{8,12},{12,8},{1,5},{5,1},{9,13},{13,9},{2,6},{6,2},{1... | collective-permute-start | bytes 12296 | tf_op jit(solution)/shard_map/ppermute | solution.py:444
  123.9 6.1 %collective-permute-start.30 = (f32[256,128]{1,0:T(8,128)S(1)}, f32[256,128]{1,0:T(8,128)S(1)}, u32[]{:S(2)}, u32[]{:S(2)}) collective-permute-start(f32[256,128]{1,0:T(8,128)S(1)} %get-tuple-element.146), channel_id=1, source_target_pairs={{0,4},{4,0},{8,12},{12,8},{1,5},{5,1},{9,13},{13,9},{2,6},{6,2},{1... | collective-permute-start | bytes 393224 | tf_op jit(solution)/shard_map/ppermute | solution.py:444
  125.8 9.5 %collective-permute-start.31 = (f32[256,128]{1,0:T(8,128)S(1)}, f32[256,128]{1,0:T(8,128)S(1)}, u32[]{:S(2)}, u32[]{:S(2)}) collective-permute-start(f32[256,128]{1,0:T(8,128)S(1)} %get-tuple-element.147), channel_id=1, source_target_pairs={{0,8},{4,12},{8,0},{12,4},{1,9},{5,13},{9,1},{13,5},{2,10},{6,14},... | collective-permute-start | bytes 393224 | tf_op jit(solution)/shard_map/ppermute | solution.py:444
  126.7 8.6 %collective-permute-start.32 = (f32[256,128]{1,0:T(8,128)S(1)}, f32[256,128]{1,0:T(8,128)S(1)}, u32[]{:S(2)}, u32[]{:S(2)}) collective-permute-start(f32[256,128]{1,0:T(8,128)S(1)} %get-tuple-element.148), channel_id=1, source_target_pairs={{0,12},{4,8},{8,4},{12,0},{1,13},{5,9},{9,5},{13,1},{2,14},{6,10},... | collective-permute-start | bytes 393224 | tf_op jit(solution)/shard_map/ppermute | solution.py:444
  135.9 9.3 %collective-permute-start.35 = (f32[264,128]{1,0:T(8,128)S(1)}, f32[264,128]{1,0:T(8,128)S(1)}, u32[]{:S(2)}, u32[]{:S(2)}) collective-permute-start(f32[264,128]{1,0:T(8,128)S(1)} %get-tuple-element.150.refs_0_.refs_2_.refs_5_.refs_14_), channel_id=1, source_target_pairs={{0,4},{4,0},{8,12},{12,8},{1,5},{5,1},{9,13},{13,9},{2,6},{6,2},{1... | collective-permute-start | bytes 405512 | tf_op jit(solution)/shard_map/ppermute | solution.py:444
  142.3 6.9 %collective-permute-start.34 = (f32[264,128]{1,0:T(8,128)S(1)}, f32[264,128]{1,0:T(8,128)S(1)}, u32[]{:S(2)}, u32[]{:S(2)}) collective-permute-start(f32[264,128]{1,0:T(8,128)S(1)} %get-tuple-element.150.refs_0_.refs_2_.refs_5_.refs_14_), channel_id=1, source_target_pairs={{0,12},{4,8},{8,4},{12,0},{1,13},{5,9},{9,5},{13,1},{2,14},{6,10},... | collective-permute-start | bytes 405512 | tf_op jit(solution)/shard_map/ppermute | solution.py:444
  144.1 7.9 %collective-permute-start.33 = (f32[264,128]{1,0:T(8,128)S(1)}, f32[264,128]{1,0:T(8,128)S(1)}, u32[]{:S(2)}, u32[]{:S(2)}) collective-permute-start(f32[264,128]{1,0:T(8,128)S(1)} %get-tuple-element.150.refs_0_.refs_2_.refs_5_.refs_14_), channel_id=1, source_target_pairs={{0,8},{4,12},{8,0},{12,4},{1,9},{5,13},{9,1},{13,5},{2,10},{6,14},... | collective-permute-start | bytes 405512 | tf_op jit(solution)/shard_map/ppermute | solution.py:444
  154.0 5.7 %collective-permute-start.36 = (f32[392,128]{1,0:T(8,128)S(1)}, f32[392,128]{1,0:T(8,128)S(1)}, u32[]{:S(2)}, u32[]{:S(2)}) collective-permute-start(f32[392,128]{1,0:T(8,128)S(1)} %get-tuple-element.153.refs_0_), channel_id=1, source_target_pairs={{0,2},{1,3},{2,0},{3,1},{4,6},{5,7},{6,4},{7,5},{8,10},{9,11},{10,... | collective-permute-start | bytes 602120 | tf_op jit(solution)/shard_map/ppermute | solution.py:439
  163.1 7.2 %collective-permute-start.37 = (f32[264,128]{1,0:T(8,128)S(1)}, f32[264,128]{1,0:T(8,128)S(1)}, u32[]{:S(2)}, u32[]{:S(2)}) collective-permute-start(f32[264,128]{1,0:T(8,128)S(1)} %get-tuple-element.158), channel_id=1, source_target_pairs={{0,4},{4,0},{8,12},{12,8},{1,5},{5,1},{9,13},{13,9},{2,6},{6,2},{1... | collective-permute-start | bytes 405512 | tf_op jit(solution)/shard_map/ppermute | solution.py:444
  163.2 11.4 %collective-permute-start.38 = (f32[264,128]{1,0:T(8,128)S(1)}, f32[264,128]{1,0:T(8,128)S(1)}, u32[]{:S(2)}, u32[]{:S(2)}) collective-permute-start(f32[264,128]{1,0:T(8,128)S(1)} %get-tuple-element.159), channel_id=1, source_target_pairs={{0,8},{4,12},{8,0},{12,4},{1,9},{5,13},{9,1},{13,5},{2,10},{6,14},... | collective-permute-start | bytes 405512 | tf_op jit(solution)/shard_map/ppermute | solution.py:444
  165.6 9.0 %collective-permute-start.39 = (f32[264,128]{1,0:T(8,128)S(1)}, f32[264,128]{1,0:T(8,128)S(1)}, u32[]{:S(2)}, u32[]{:S(2)}) collective-permute-start(f32[264,128]{1,0:T(8,128)S(1)} %get-tuple-element.160), channel_id=1, source_target_pairs={{0,12},{4,8},{8,4},{12,0},{1,13},{5,9},{9,5},{13,1},{2,14},{6,10},... | collective-permute-start | bytes 405512 | tf_op jit(solution)/shard_map/ppermute | solution.py:444
  174.7 5.1 %collective-permute-start.42 = (f32[264,128]{1,0:T(8,128)S(1)}, f32[264,128]{1,0:T(8,128)S(1)}, u32[]{:S(2)}, u32[]{:S(2)}) collective-permute-start(f32[264,128]{1,0:T(8,128)S(1)} %get-tuple-element.163.refs_0_.refs_2_.refs_15_), channel_id=1, source_target_pairs={{0,4},{4,0},{8,12},{12,8},{1,5},{5,1},{9,13},{13,9},{2,6},{6,2},{1... | collective-permute-start | bytes 405512 | tf_op jit(solution)/shard_map/ppermute | solution.py:444
  176.8 6.9 %collective-permute-start.41 = (f32[264,128]{1,0:T(8,128)S(1)}, f32[264,128]{1,0:T(8,128)S(1)}, u32[]{:S(2)}, u32[]{:S(2)}) collective-permute-start(f32[264,128]{1,0:T(8,128)S(1)} %get-tuple-element.163.refs_0_.refs_2_.refs_15_), channel_id=1, source_target_pairs={{0,12},{4,8},{8,4},{12,0},{1,13},{5,9},{9,5},{13,1},{2,14},{6,10},... | collective-permute-start | bytes 405512 | tf_op jit(solution)/shard_map/ppermute | solution.py:444
  178.7 8.0 %collective-permute-start.40 = (f32[264,128]{1,0:T(8,128)S(1)}, f32[264,128]{1,0:T(8,128)S(1)}, u32[]{:S(2)}, u32[]{:S(2)}) collective-permute-start(f32[264,128]{1,0:T(8,128)S(1)} %get-tuple-element.163.refs_0_.refs_2_.refs_15_), channel_id=1, source_target_pairs={{0,8},{4,12},{8,0},{12,4},{1,9},{5,13},{9,1},{13,5},{2,10},{6,14},... | collective-permute-start | bytes 405512 | tf_op jit(solution)/shard_map/ppermute | solution.py:444
  189.2 5.7 %collective-permute-start.43 = (f32[392,128]{1,0:T(8,128)S(1)}, f32[392,128]{1,0:T(8,128)S(1)}, u32[]{:S(2)}, u32[]{:S(2)}) collective-permute-start(f32[392,128]{1,0:T(8,128)S(1)} %get-tuple-element.166.refs_0_), channel_id=1, source_target_pairs={{0,2},{1,3},{2,0},{3,1},{4,6},{5,7},{6,4},{7,5},{8,10},{9,11},{10,... | collective-permute-start | bytes 602120 | tf_op jit(solution)/shard_map/ppermute | solution.py:439
  195.1 5.4 %collective-permute-start.46 = (f32[8,128]{1,0:T(8,128)S(1)}, f32[8,128]{1,0:T(8,128)S(1)}, u32[]{:S(2)}, u32[]{:S(2)}) collective-permute-start(f32[8,128]{1,0:T(8,128)S(1)} %get-tuple-element.168.refs_0_), channel_id=1, source_target_pairs={{0,12},{4,8},{8,4},{12,0},{1,13},{5,9},{9,5},{13,1},{2,14},{6,10},... | collective-permute-start | bytes 12296 | tf_op jit(solution)/shard_map/ppermute | solution.py:444
  197.0 4.5 %collective-permute-start.45 = (f32[8,128]{1,0:T(8,128)S(1)}, f32[8,128]{1,0:T(8,128)S(1)}, u32[]{:S(2)}, u32[]{:S(2)}) collective-permute-start(f32[8,128]{1,0:T(8,128)S(1)} %get-tuple-element.168.refs_0_), channel_id=1, source_target_pairs={{0,8},{4,12},{8,0},{12,4},{1,9},{5,13},{9,1},{13,5},{2,10},{6,14},... | collective-permute-start | bytes 12296 | tf_op jit(solution)/shard_map/ppermute | solution.py:444
  197.0 4.5 %collective-permute-start.44 = (f32[8,128]{1,0:T(8,128)S(1)}, f32[8,128]{1,0:T(8,128)S(1)}, u32[]{:S(2)}, u32[]{:S(2)}) collective-permute-start(f32[8,128]{1,0:T(8,128)S(1)} %get-tuple-element.168.refs_0_), channel_id=1, source_target_pairs={{0,4},{4,0},{8,12},{12,8},{1,5},{5,1},{9,13},{13,9},{2,6},{6,2},{1... | collective-permute-start | bytes 12296 | tf_op jit(solution)/shard_map/ppermute | solution.py:444
  201.7 2.0 collective-permute-start.47

commit v6 on v2

--- a/solution.py
+++ b/solution.py
@@ -134,7 +134,8 @@
             diag[here, :] += jnp.sum(jnp.where(eye, src[3 * e], 0.0), axis=0, keepdims=True)
 
 
-def forward_kernel(n, own, scalars, place, pairs, *refs):
+def forward_kernel(ks, own, scalars, place, pairs, *refs):
+    n = len(ks)
     msgs, rest = refs[:n], refs[n:]
     if scalars == 0:
         others, rest = rest[:n], rest[n:]
@@ -145,11 +146,11 @@
     msg, pp, whole, wide = rest
     row = place[0]
     span = whole.shape[0]
-    for k in range(n):
+    for i, k in enumerate(ks):
         at = pl.multiple_of(lax.bitwise_xor(row, k) * own, own)
-        v = msgs[k][0:own, :]
+        v = msgs[i][0:own, :]
         if scalars == 0:
-            v = mix_cores(place[1], v, others[k][...])
+            v = mix_cores(place[1], v, others[i][...])
         whole[pl.ds(at, own), :] = v
         first, second = pair_up(v)
         wide[pl.ds(at, own), :] = first
@@ -390,21 +391,22 @@
     def to_x(v):
         return [v] + [lax.ppermute(v, "col", [(c, c ^ (2 * k)) for c in range(n_col)]) for k in range(1, nx)]
 
-    swaps = [2, 3, 1] if n == 4 else list(range(1, n))
-
-    def to_row(pieces, order=None):
-        got = {0: pieces[0]}
-        for k in order or swaps:
-            got[k] = lax.ppermute(pieces[k], "row", [(i, i ^ k) for i in range(n)])
-        return [got[k] for k in range(n)]
-
-    def to_all_rows(v):
-        return to_row([v] * n, swaps[::-1])
+    scalar_ks = list(range(1, n))
+    row_ks = [2, 1, 3] if n == 4 else scalar_ks
+
+    def over_row(v, k):
+        return lax.ppermute(v, "row", [(i, i ^ k) for i in range(n)])
+
+    def to_row(pieces):
+        return [pieces[0]] + [over_row(pieces[k], k) for k in row_ks]
+
+    def to_all_rows(v, ks):
+        return [v] + [over_row(v, k) for k in ks]
 
     a_mine = a_blocks.reshape(slab * per, BLK, BLK)
     p_mine = p_blocks.reshape(4, BLK, BLK)
     ints = jnp.concatenate([a_cols.reshape(-1), p_pairs.reshape(-1)])
-    x_rows = to_all_rows(x_state)
+    x_rows = to_all_rows(x_state, row_ks)
     a_other = to_core(a_mine)
     ints_other = to_core(ints)
     p_other = to_core(p_mine)
@@ -415,8 +417,6 @@
     pd = jnp.concatenate(
         [jnp.broadcast_to(p_diag[:, None], (own, HALF)), jnp.broadcast_to(pd_other[:, None], (own, HALF))], axis=1
     )
-    x_others = [to_core(v) for v in x_rows]
-    x, q = call(own_kernel, [((own, LANES), F32)] * 2, [x_state, x_others[0], q_lin, to_core(q_lin)], [place])
     z, y, lower, upper = call(
         slab_kernel, [((half_rows, LANES), F32)] * 4, [z_state, y_state, lower_bound, upper_bound], [place]
     )
@@ -431,13 +431,17 @@
         [cols, pairs],
         flops=10**8,
     )
+    *late, diag = lax.optimization_barrier((*x_rows[1:], diag))
+    x_rows = [x_state, *late]
+    x_others = [to_core(v) for v in x_rows]
+    x, q = call(own_kernel, [((own, LANES), F32)] * 2, [x_state, x_others[0], q_lin, to_core(q_lin)], [place])
     prod_flops = 4 * slab_rows * wide * LANES
     total_scratch = [pltpu.VMEM((span, LANES), F32)]
 
     def forward(msgs, scalars, pp_first=()):
         extra = SC if scalars else 0
         return call(
-            functools.partial(forward_kernel, n, own, scalars),
+            functools.partial(forward_kernel, (0, *row_ks), own, scalars),
             [((half_rows + extra, LANES), F32), ((2 * BLK, LANES), F32)],
             [*msgs, a_hi, a_lo, p_hi, p_lo, *pp_first],
             [place, pairs],
@@ -474,7 +478,7 @@
                 [*to_row(pieces), x, q, pd, dk],
                 [place],
             )
-        msg, pp1 = forward(to_all_rows(msg1), 1)
+        msg, pp1 = forward(to_all_rows(msg1, row_ks), 1)
         *pieces, ad, scal = call(
             functools.partial(step_back_kernel, n, nx, own),
             [msg_shape] * n + [slab_shape, tile_shape],
@@ -488,13 +492,13 @@
             [msg_shape, tile_shape],
             [*to_row(pieces), scal, msg1, r, pd, dk],
         )
-        msg, pp2 = forward(to_all_rows(msg2), 2, (pp1,))
+        msg, pp2 = forward(to_all_rows(msg2, row_ks), 2, (pp1,))
         ad2, share, keep = call(
             functools.partial(curve_kernel, nx),
             [slab_shape, tile_shape, tile_shape],
             [*to_x(msg), scal, ad],
         )
-        shares = to_all_rows(share)
+        shares = to_all_rows(share, scalar_ks)
         state = [*shares, keep, step, ax, ad, ad2, z, y, lower, upper, x, msg1, msg2]
         if outer + 1 < ADMM_ITERS:
             *pieces, x, z, y, ax, ppx = call(

time: 203 us -> 209 us (1.030)
  local copies, waits for them, and re-layouts: 3.49 us -> 16.3 us
  waiting for transfers between devices: 99.6 us -> 90.7 us
    unnamed x19 -> x45, local copies, waits for them, and re-layouts: 3.16 us -> 15.9 us
    ppermute x33, waiting for transfers between devices: 74.6 us -> 65 us  [over_row(): return lax.ppermute(v, 'row', [(i, i ^ k) for i in range(n)])]
  transfers between devices with their start and end apart: 48 -> 48, of which waited for: 30 -> 31; matrix products, arithmetic and copies ran while one was open for 1% -> 1% of each run, Pallas kernels for 2% -> 3%
where the time goes in v6:
time: 209 us; the launch traced here: 208 us
  waiting for transfers between devices  90.7 us (43%)
  starting transfers between devices  61.9 us (30%)
  Pallas kernels  36.8 us (18%)
  local copies, waits for them, and re-layouts  16.3 us (8%)
    ppermute x33, waiting for transfers between devices, over_row(): return lax.ppermute(v, 'row', [(i, i ^ k) for i in range(n)])  65 us
    ppermute x33, starting transfers between devices, over_row(): return lax.ppermute(v, 'row', [(i, i ^ k) for i in range(n)])  51.3 us
    pallas_call x20, Pallas kernels, call(): pl.pallas_call(body, out_shape=[jax.ShapeDtypeStruct(s, d) for s, d in ou...  36.8 us
    ppermute x5, waiting for transfers between devices, to_x(): lax.ppermute(v, 'col', [(c, c ^ 2 * k) for c in range(n_col)])  21.7 us
    unnamed x45, local copies, waits for them, and re-layouts  15.9 us
    ppermute x5, starting transfers between devices, to_x(): lax.ppermute(v, 'col', [(c, c ^ 2 * k) for c in range(n_col)])  7.89 us
  transfers between devices with their start and end apart: 48, of which 31 were waited for; matrix products, arithmetic and copies ran while one was open for 1% of the time, Pallas kernels for 3%

profile of v6, /device:TPU:0, one launch (start us, length us, event | category | flops | bytes accessed | tf_op | source)
XLA Modules:
  0.0 208.3 jit_solution(1051823920802829377)
XLA Ops:
  3.2 4.7 %collective-permute-start.3 = (f32[256,128]{1,0:T(8,128)}, f32[256,128]{1,0:T(8,128)}, u32[]{:S(2)}, u32[]{:S(2)}) collective-permute-start(f32[256,128]{1,0:T(8,128)} %x.1), channel_id=1, source_target_pairs={{0,12},{4,8},{8,4},{12,0},{1,13},{5,9},{9,5},{13,1},{2,14},{6,10},... | collective-permute-start | bytes 393224 | tf_op jit(solution)/shard_map/ppermute | solution.py:398
  11.2 1.4 copy-done.9
  12.6 1.4 copy-done.11
  15.9 3.0 %shard_map.130 = (bf16[768,2048]{1,0:T(8,128)(2,1)S(1)}, bf16[768,2048]{1,0:T(8,128)(2,1)S(1)}, bf16[2048,768]{1,0:T(8,128)(2,1)S(1)}, bf16[2048,768]{1,0:T(8,12...) custom-call(s32[48]{0:T(128)S(1)} %pad_add_fusion.3.cols, ...), custom_call_target="tpu_custom_call" | custom-call | flops 100000000 | bytes 3670016 | tf_op jit(solution)/shard_map/pallas_call | solution.py:27
  19.0 1.6 copy-done
  20.6 1.7 copy-done.3
  22.3 1.7 copy-done.5
  27.2 1.9 copy-done.1
  30.1 3.9 %shard_map.131 = (f32[384,128]{1,0:T(8,128)S(1)}, f32[256,128]{1,0:T(8,128)S(1)}) custom-call(s32[2]{0:T(128)S(1)} %pad_add_fusion.place, s32[4]{0:T(128)S(1)} %pad_add_fusion.2.pairs, f32[256,128]{1,0:T(8,128)S(1)} %copy-done.12, f32[256,128]{1,0:T(8,128)} %collective-permute-done.1.refs_1_, f32[256,128]{1,0:T(8,128)} %collective-permute-done.2.refs_2_, ...), custom_call_target="tpu_custom_call" | custom-call | flops 805306368 | bytes 7864320 | tf_op jit(solution)/shard_map/pallas_call | solution.py:27
  33.9 1.8 collective-permute-start.10
  35.7 1.3 shard_map.132
  37.0 4.1 %collective-permute-done.10.refs_1_ = f32[384,128]{1,0:T(8,128)S(1)} collective-permute-done((f32[384,128]{1,0:T(8,128)S(1)}, f32[384,128]{1,0:T(8,128)S(1)}, u32[]{:S(2)}, u32[]{:S(2)}) %collective-permute-start.10) | collective-permute-done | bytes 196640 | tf_op jit(solution)/shard_map/ppermute | solution.py:392
  41.2 2.6 %shard_map.133 = (f32[272,128]{1,0:T(8,128)S(1)}, f32[272,128]{1,0:T(8,128)S(1)}, f32[272,128]{1,0:T(8,128)S(1)}, f32[272,128]{1,0:T(8,128)S(1)}, f32[384,128]{1,0:T(8,128)S(1)}) custom-call(s32[2]{0:T(128)S(1)} %pad_add_fusion.place, s32[4]{0:T(128)S(1)} %pad_add_fusion.2.pairs, f32[384,128]{1,0:T(8,128)S(1)} %get-tuple-element.77.refs_0_, ...), custom_call_target="tpu_custom_call" | custom-call | flops 805306368 | bytes 7217152 | tf_op jit(solution)/shard_map/pallas_call | solution.py:27
  43.8 2.4 %collective-permute-start.11 = (f32[272,128]{1,0:T(8,128)S(1)}, f32[272,128]{1,0:T(8,128)S(1)}, u32[]{:S(2)}, u32[]{:S(2)}) collective-permute-start(f32[272,128]{1,0:T(8,128)S(1)} %get-tuple-element.85), channel_id=1, source_target_pairs={{0,8},{4,12},{8,0},{12,4},{1,9},{5,13},{9,1},{13,5},{2,10},{6,14},... | collective-permute-start | bytes 417800 | tf_op jit(solution)/shard_map/ppermute | solution.py:398
  46.2 2.0 collective-permute-start.12
  51.1 6.1 %collective-permute-done.11.refs_1_ = f32[272,128]{1,0:T(8,128)S(1)} collective-permute-done((f32[272,128]{1,0:T(8,128)S(1)}, f32[272,128]{1,0:T(8,128)S(1)}, u32[]{:S(2)}, u32[]{:S(2)}) %collective-permute-start.11) | collective-permute-done | bytes 139296 | tf_op jit(solution)/shard_map/ppermute | solution.py:398
  58.1 2.1 %collective-permute-start.18 = (f32[264,128]{1,0:T(8,128)S(1)}, f32[264,128]{1,0:T(8,128)S(1)}, u32[]{:S(2)}, u32[]{:S(2)}) collective-permute-start(f32[264,128]{1,0:T(8,128)S(1)} %get-tuple-element.90.refs_0_.refs_5_.refs_14_), channel_id=1, source_target_pairs={{0,12},{4,8},{8,4},{12,0},{1,13},{5,9},{9,5},{13,1},{2,14},{6,10},... | collective-permute-start | bytes 405512 | tf_op jit(solution)/shard_map/ppermute | solution.py:398
  60.3 2.5 %collective-permute-start.17 = (f32[264,128]{1,0:T(8,128)S(1)}, f32[264,128]{1,0:T(8,128)S(1)}, u32[]{:S(2)}, u32[]{:S(2)}) collective-permute-start(f32[264,128]{1,0:T(8,128)S(1)} %get-tuple-element.90.refs_0_.refs_5_.refs_14_), channel_id=1, source_target_pairs={{0,4},{4,0},{8,12},{12,8},{1,5},{5,1},{9,13},{13,9},{2,6},{6,2},{1... | collective-permute-start | bytes 405512 | tf_op jit(solution)/shard_map/ppermute | solution.py:398
  62.8 3.0 %collective-permute-done.18.refs_3_ = f32[264,128]{1,0:T(8,128)S(1)} collective-permute-done((f32[264,128]{1,0:T(8,128)S(1)}, f32[264,128]{1,0:T(8,128)S(1)}, u32[]{:S(2)}, u32[]{:S(2)}) %collective-permute-start.18) | collective-permute-done | bytes 135200 | tf_op jit(solution)/shard_map/ppermute | solution.py:398
  65.8 2.3 %collective-permute-done.17.refs_2_ = f32[264,128]{1,0:T(8,128)S(1)} collective-permute-done((f32[264,128]{1,0:T(8,128)S(1)}, f32[264,128]{1,0:T(8,128)S(1)}, u32[]{:S(2)}, u32[]{:S(2)}) %collective-permute-start.17) | collective-permute-done | bytes 135200 | tf_op jit(solution)/shard_map/ppermute | solution.py:398
  68.1 5.1 %collective-permute-done.16.refs_1_ = f32[264,128]{1,0:T(8,128)S(1)} collective-permute-done((f32[264,128]{1,0:T(8,128)S(1)}, f32[264,128]{1,0:T(8,128)S(1)}, u32[]{:S(2)}, u32[]{:S(2)}) %collective-permute-start.16) | collective-permute-done | bytes 135200 | tf_op jit(solution)/shard_map/ppermute | solution.py:398
  73.2 2.9 %shard_map.136 = (f32[392,128]{1,0:T(8,128)S(1)}, f32[256,128]{1,0:T(8,128)S(1)}) custom-call(s32[2]{0:T(128)S(1)} %pad_add_fusion.place, s32[4]{0:T(128)S(1)} %pad_add_fusion.2.pairs, f32[264,128]{1,0:T(8,128)S(1)} %get-tuple-element.90.refs_0_.refs_5_.refs_14_, f32[264,128]{1,0:T(8,128)S(1)} %collective-permute-done.16.refs_1_, ...), custom_call_target="tpu_custom_call" | custom-call | flops 805306368 | bytes 7356416 | tf_op jit(solution)/shard_map/pallas_call | solution.py:27
  76.0 1.5 collective-permute-start.19
  77.6 4.9 %collective-permute-done.19.refs_1_ = f32[392,128]{1,0:T(8,128)S(1)} collective-permute-done((f32[392,128]{1,0:T(8,128)S(1)}, f32[392,128]{1,0:T(8,128)S(1)}, u32[]{:S(2)}, u32[]{:S(2)}) %collective-permute-start.19) | collective-permute-done | bytes 200736 | tf_op jit(solution)/shard_map/ppermute | solution.py:392
  82.5 2.8 %shard_map.137 = (f32[264,128]{1,0:T(8,128)S(1)}, f32[264,128]{1,0:T(8,128)S(1)}, f32[264,128]{1,0:T(8,128)S(1)}, f32[264,128]{1,0:T(8,128)S(1)}, f32[384,128]{1,0:T(8,128)S(1)}, /*index=5*/f32[8,128]{1,0:T(8,128)S(1)}) custom-call(s32[2]{0:T(128)S(1)} %pad_add_fusion.place, s32[4]{0:T(128)S(1)} %pad_add_fusion.2.pairs, ...), custom_call_target="tpu_custom_call" | custom-call | flops 805306368 | bytes 6823936 | tf_op jit(solution)/shard_map/pallas_call | solution.py:27
  85.4 3.6 %collective-permute-start.21 = (f32[264,128]{1,0:T(8,128)S(1)}, f32[264,128]{1,0:T(8,128)S(1)}, u32[]{:S(2)}, u32[]{:S(2)}) collective-permute-start(f32[264,128]{1,0:T(8,128)S(1)} %get-tuple-element.95), channel_id=1, source_target_pairs={{0,4},{4,0},{8,12},{12,8},{1,5},{5,1},{9,13},{13,9},{2,6},{6,2},{1... | collective-permute-start | bytes 405512 | tf_op jit(solution)/shard_map/ppermute | solution.py:398
  89.8 7.6 %collective-permute-done.20.refs_1_ = f32[264,128]{1,0:T(8,128)S(1)} collective-permute-done((f32[264,128]{1,0:T(8,128)S(1)}, f32[264,128]{1,0:T(8,128)S(1)}, u32[]{:S(2)}, u32[]{:S(2)}) %collective-permute-start.20) | collective-permute-done | bytes 135200 | tf_op jit(solution)/shard_map/ppermute | solution.py:398
  97.5 2.0 collective-permute-start.25
  99.4 2.8 %collective-permute-start.24 = (f32[264,128]{1,0:T(8,128)S(1)}, f32[264,128]{1,0:T(8,128)S(1)}, u32[]{:S(2)}, u32[]{:S(2)}) collective-permute-start(f32[264,128]{1,0:T(8,128)S(1)} %get-tuple-element.100.refs_0_.refs_15_), channel_id=1, source_target_pairs={{0,4},{4,0},{8,12},{12,8},{1,5},{5,1},{9,13},{13,9},{2,6},{6,2},{1... | collective-permute-start | bytes 405512 | tf_op jit(solution)/shard_map/ppermute | solution.py:398
  102.2 3.6 %collective-permute-done.25.refs_3_ = f32[264,128]{1,0:T(8,128)S(1)} collective-permute-done((f32[264,128]{1,0:T(8,128)S(1)}, f32[264,128]{1,0:T(8,128)S(1)}, u32[]{:S(2)}, u32[]{:S(2)}) %collective-permute-start.25) | collective-permute-done | bytes 135200 | tf_op jit(solution)/shard_map/ppermute | solution.py:398
  106.4 5.2 %collective-permute-done.23.refs_1_ = f32[264,128]{1,0:T(8,128)S(1)} collective-permute-done((f32[264,128]{1,0:T(8,128)S(1)}, f32[264,128]{1,0:T(8,128)S(1)}, u32[]{:S(2)}, u32[]{:S(2)}) %collective-permute-start.23) | collective-permute-done | bytes 135200 | tf_op jit(solution)/shard_map/ppermute | solution.py:398
  111.6 2.9 %shard_map.139 = (f32[392,128]{1,0:T(8,128)S(1)}, f32[256,128]{1,0:T(8,128)S(1)}) custom-call(s32[2]{0:T(128)S(1)} %pad_add_fusion.place, s32[4]{0:T(128)S(1)} %pad_add_fusion.2.pairs, f32[264,128]{1,0:T(8,128)S(1)} %get-tuple-element.100.refs_0_.refs_15_, f32[264,128]{1,0:T(8,128)S(1)} %collective-permute-done.23.refs_1_, ...), custom_call_target="tpu_custom_call" | custom-call | flops 805306368 | bytes 7487488 | tf_op jit(solution)/shard_map/pallas_call | solution.py:27
  114.5 1.5 collective-permute-start.26
  116.0 4.2 %collective-permute-done.26.refs_1_ = f32[392,128]{1,0:T(8,128)S(1)} collective-permute-done((f32[392,128]{1,0:T(8,128)S(1)}, f32[392,128]{1,0:T(8,128)S(1)}, u32[]{:S(2)}, u32[]{:S(2)}) %collective-permute-start.26) | collective-permute-done | bytes 200736 | tf_op jit(solution)/shard_map/ppermute | solution.py:392
  120.4 1.6 collective-permute-start.29
  122.1 2.8 %collective-permute-start.27 = (f32[8,128]{1,0:T(8,128)S(1)}, f32[8,128]{1,0:T(8,128)S(1)}, u32[]{:S(2)}, u32[]{:S(2)}) collective-permute-start(f32[8,128]{1,0:T(8,128)S(1)} %get-tuple-element.103.refs_0_), channel_id=1, source_target_pairs={{0,4},{4,0},{8,12},{12,8},{1,5},{5,1},{9,13},{13,9},{2,6},{6,2},{1... | collective-permute-start | bytes 12296 | tf_op jit(solution)/shard_map/ppermute | solution.py:398
  126.6 3.3 %shard_map.141 = (f32[256,128]{1,0:T(8,128)S(1)}, f32[256,128]{1,0:T(8,128)S(1)}, f32[256,128]{1,0:T(8,128)S(1)}, f32[256,128]{1,0:T(8,128)S(1)}, f32[256,128]{1...) custom-call(s32[2]{0:T(128)S(1)} %pad_add_fusion.place, ...), custom_call_target="tpu_custom_call" | custom-call | flops 805306368 | bytes 8486912 | tf_op jit(solution)/shard_map/pallas_call | solution.py:27
  129.9 2.0 collective-permute-start.30
  132.7 1.6 collective-permute-start.32
  134.3 3.1 %collective-permute-done.30.refs_1_ = f32[256,128]{1,0:T(8,128)S(1)} collective-permute-done((f32[256,128]{1,0:T(8,128)S(1)}, f32[256,128]{1,0:T(8,128)S(1)}, u32[]{:S(2)}, u32[]{:S(2)}) %collective-permute-start.30) | collective-permute-done | bytes 131104 | tf_op jit(solution)/shard_map/ppermute | solution.py:398
  137.4 3.1 %collective-permute-done.32.refs_3_ = f32[256,128]{1,0:T(8,128)S(1)} collective-permute-done((f32[256,128]{1,0:T(8,128)S(1)}, f32[256,128]{1,0:T(8,128)S(1)}, u32[]{:S(2)}, u32[]{:S(2)}) %collective-permute-start.32) | collective-permute-done | bytes 131104 | tf_op jit(solution)/shard_map/ppermute | solution.py:398
  141.2 1.8 collective-permute-start.35
  143.0 3.9 %collective-permute-start.34 = (f32[264,128]{1,0:T(8,128)S(1)}, f32[264,128]{1,0:T(8,128)S(1)}, u32[]{:S(2)}, u32[]{:S(2)}) collective-permute-start(f32[264,128]{1,0:T(8,128)S(1)} %get-tuple-element.116.refs_0_.refs_5_.refs_14_), channel_id=1, source_target_pairs={{0,4},{4,0},{8,12},{12,8},{1,5},{5,1},{9,13},{13,9},{2,6},{6,2},{1... | collective-permute-start | bytes 405512 | tf_op jit(solution)/shard_map/ppermute | solution.py:398
  148.1 1.8 collective-permute-done.34.refs_2_
  149.9 3.9 %collective-permute-done.33.refs_1_ = f32[264,128]{1,0:T(8,128)S(1)} collective-permute-done((f32[264,128]{1,0:T(8,128)S(1)}, f32[264,128]{1,0:T(8,128)S(1)}, u32[]{:S(2)}, u32[]{:S(2)}) %collective-permute-start.33) | collective-permute-done | bytes 135200 | tf_op jit(solution)/shard_map/ppermute | solution.py:398
  153.7 2.9 %shard_map.143 = (f32[392,128]{1,0:T(8,128)S(1)}, f32[256,128]{1,0:T(8,128)S(1)}) custom-call(s32[2]{0:T(128)S(1)} %pad_add_fusion.place, s32[4]{0:T(128)S(1)} %pad_add_fusion.2.pairs, f32[264,128]{1,0:T(8,128)S(1)} %get-tuple-element.116.refs_0_.refs_5_.refs_14_, f32[264,128]{1,0:T(8,128)S(1)} %collective-permute-done.33.refs_1_, ...), custom_call_target="tpu_custom_call" | custom-call | flops 805306368 | bytes 7356416 | tf_op jit(solution)/shard_map/pallas_call | solution.py:27
  156.6 1.6 collective-permute-start.36
  158.2 4.2 %collective-permute-done.36.refs_1_ = f32[392,128]{1,0:T(8,128)S(1)} collective-permute-done((f32[392,128]{1,0:T(8,128)S(1)}, f32[392,128]{1,0:T(8,128)S(1)}, u32[]{:S(2)}, u32[]{:S(2)}) %collective-permute-start.36) | collective-permute-done | bytes 200736 | tf_op jit(solution)/shard_map/ppermute | solution.py:392
  162.4 2.6 %shard_map.144 = (f32[264,128]{1,0:T(8,128)S(1)}, f32[264,128]{1,0:T(8,128)S(1)}, f32[264,128]{1,0:T(8,128)S(1)}, f32[264,128]{1,0:T(8,128)S(1)}, f32[384,128]{1,0:T(8,128)S(1)}, /*index=5*/f32[8,128]{1,0:T(8,128)S(1)}) custom-call(s32[2]{0:T(128)S(1)} %pad_add_fusion.place, s32[4]{0:T(128)S(1)} %pad_add_fusion.2.pairs, ...), custom_call_target="tpu_custom_call" | custom-call | flops 805306368 | bytes 6823936 | tf_op jit(solution)/shard_map/pallas_call | solution.py:27
  165.6 3.8 %collective-permute-start.39 = (f32[264,128]{1,0:T(8,128)S(1)}, f32[264,128]{1,0:T(8,128)S(1)}, u32[]{:S(2)}, u32[]{:S(2)}) collective-permute-start(f32[264,128]{1,0:T(8,128)S(1)} %get-tuple-element.122), channel_id=1, source_target_pairs={{0,12},{4,8},{8,4},{12,0},{1,13},{5,9},{9,5},{13,1},{2,14},{6,10},... | collective-permute-start | bytes 405512 | tf_op jit(solution)/shard_map/ppermute | solution.py:398
  169.4 7.6 %collective-permute-done.37.refs_1_ = f32[264,128]{1,0:T(8,128)S(1)} collective-permute-done((f32[264,128]{1,0:T(8,128)S(1)}, f32[264,128]{1,0:T(8,128)S(1)}, u32[]{:S(2)}, u32[]{:S(2)}) %collective-permute-start.37) | collective-permute-done | bytes 135200 | tf_op jit(solution)/shard_map/ppermute | solution.py:398
  177.1 2.3 %collective-permute-start.42 = (f32[264,128]{1,0:T(8,128)S(1)}, f32[264,128]{1,0:T(8,128)S(1)}, u32[]{:S(2)}, u32[]{:S(2)}) collective-permute-start(f32[264,128]{1,0:T(8,128)S(1)} %get-tuple-element.125.refs_0_.refs_15_), channel_id=1, source_target_pairs={{0,12},{4,8},{8,4},{12,0},{1,13},{5,9},{9,5},{13,1},{2,14},{6,10},... | collective-permute-start | bytes 405512 | tf_op jit(solution)/shard_map/ppermute | solution.py:398
  179.4 1.4 collective-permute-start.41
  181.6 2.6 %collective-permute-done.42.refs_3_ = f32[264,128]{1,0:T(8,128)S(1)} collective-permute-done((f32[264,128]{1,0:T(8,128)S(1)}, f32[264,128]{1,0:T(8,128)S(1)}, u32[]{:S(2)}, u32[]{:S(2)}) %collective-permute-start.42) | collective-permute-done | bytes 135200 | tf_op jit(solution)/shard_map/ppermute | solution.py:398
  184.2 1.3 collective-permute-done.41.refs_2_
  185.5 2.8 %collective-permute-done.40.refs_1_ = f32[264,128]{1,0:T(8,128)S(1)} collective-permute-done((f32[264,128]{1,0:T(8,128)S(1)}, f32[264,128]{1,0:T(8,128)S(1)}, u32[]{:S(2)}, u32[]{:S(2)}) %collective-permute-start.40) | collective-permute-done | bytes 135200 | tf_op jit(solution)/shard_map/ppermute | solution.py:398
  188.3 3.5 %shard_map.146 = (f32[392,128]{1,0:T(8,128)S(1)}, f32[256,128]{1,0:T(8,128)}) custom-call(s32[2]{0:T(128)S(1)} %pad_add_fusion.place, s32[4]{0:T(128)S(1)} %pad_add_fusion.2.pairs, f32[264,128]{1,0:T(8,128)S(1)} %get-tuple-element.125.refs_0_.refs_15_, f32[264,128]{1,0:T(8,128)S(1)} %collective-permute-done.40.refs_1_, ...), custom_call_target="tpu_custom_call" | custom-call | flops 805306368 | bytes 7487488 | tf_op jit(solution)/shard_map/pallas_call | solution.py:27
  191.8 1.5 collective-permute-start.43
  193.3 4.2 %collective-permute-done.43.refs_1_ = f32[392,128]{1,0:T(8,128)S(1)} collective-permute-done((f32[392,128]{1,0:T(8,128)S(1)}, f32[392,128]{1,0:T(8,128)S(1)}, u32[]{:S(2)}, u32[]{:S(2)}) %collective-permute-start.43) | collective-permute-done | bytes 200736 | tf_op jit(solution)/shard_map/ppermute | solution.py:392
  197.7 2.2 %collective-permute-start.46 = (f32[8,128]{1,0:T(8,128)S(1)}, f32[8,128]{1,0:T(8,128)S(1)}, u32[]{:S(2)}, u32[]{:S(2)}) collective-permute-start(f32[8,128]{1,0:T(8,128)S(1)} %get-tuple-element.128.refs_0_), channel_id=1, source_target_pairs={{0,12},{4,8},{8,4},{12,0},{1,13},{5,9},{9,5},{13,1},{2,14},{6,10},... | collective-permute-start | bytes 12296 | tf_op jit(solution)/shard_map/ppermute | solution.py:398
  199.9 2.2 %collective-permute-start.44 = (f32[8,128]{1,0:T(8,128)S(1)}, f32[8,128]{1,0:T(8,128)S(1)}, u32[]{:S(2)}, u32[]{:S(2)}) collective-permute-start(f32[8,128]{1,0:T(8,128)S(1)} %get-tuple-element.128.refs_0_), channel_id=1, source_target_pairs={{0,4},{4,0},{8,12},{12,8},{1,5},{5,1},{9,13},{13,9},{2,6},{6,2},{1... | collective-permute-start | bytes 12296 | tf_op jit(solution)/shard_map/ppermute | solution.py:398
  203.1 1.3 collective-permute-done.45.refs_2_
  204.7 1.9 collective-permute-done.47.got
  206.6 1.7 shard_map.149
  (106 shorter events, 24.8 us)
Async XLA Ops:
  0.6 9.5 %collective-permute-start.4 = (f32[24,128,128]{2,1,0:T(8,128)}, f32[24,128,128]{2,1,0:T(8,128)S(1)}, u32[]{:S(2)}, u32[]{:S(2)}) collective-permute-start(f32[24,128,128]{2,1,0:T(8,128)} %bitcast.6), channel_id=1, source_target_pairs={{0,1},{1,0},{2,3},{3,2},{4,5},{5,4},{6,7},{7,6},{8,9},{9,8},{10,11... | collective-permute-start | bytes 4718600 | tf_op jit(solution)/shard_map/ppermute | solution.py:389
  1.1 8.2 %collective-permute-start.5 = (f32[4,128,128]{2,1,0:T(8,128)}, f32[4,128,128]{2,1,0:T(8,128)S(1)}, u32[]{:S(2)}, u32[]{:S(2)}) collective-permute-start(f32[4,128,128]{2,1,0:T(8,128)} %bitcast.8), channel_id=1, source_target_pairs={{0,1},{1,0},{2,3},{3,2},{4,5},{5,4},{6,7},{7,6},{8,9},{9,8},{10,11... | collective-permute-start | bytes 786440 | tf_op jit(solution)/shard_map/ppermute | solution.py:389
  2.8 5.1 %collective-permute-start = (s32[26]{0:T(128)S(1)}, s32[26]{0:T(128)S(1)}, u32[]{:S(2)}, u32[]{:S(2)}) collective-permute-start(s32[26]{0:T(128)S(1)} %pad_add_fusion.1), channel_id=1, source_target_pairs={{0,1},{1,0},{2,3},{3,2},{4,5},{5,4},{6,7},{7,6},{8,9},{9,8},{10,11... | collective-permute-start | bytes 320 | tf_op jit(solution)/shard_map/ppermute | solution.py:389
  3.2 21.5 %collective-permute-start.3 = (f32[256,128]{1,0:T(8,128)}, f32[256,128]{1,0:T(8,128)}, u32[]{:S(2)}, u32[]{:S(2)}) collective-permute-start(f32[256,128]{1,0:T(8,128)} %x.1), channel_id=1, source_target_pairs={{0,12},{4,8},{8,4},{12,0},{1,13},{5,9},{9,5},{13,1},{2,14},{6,10},... | collective-permute-start | bytes 393224 | tf_op jit(solution)/shard_map/ppermute | solution.py:398
  7.9 16.8 %collective-permute-start.2 = (f32[256,128]{1,0:T(8,128)}, f32[256,128]{1,0:T(8,128)}, u32[]{:S(2)}, u32[]{:S(2)}) collective-permute-start(f32[256,128]{1,0:T(8,128)} %x.1), channel_id=1, source_target_pairs={{0,4},{4,0},{8,12},{12,8},{1,5},{5,1},{9,13},{13,9},{2,6},{6,2},{1... | collective-permute-start | bytes 393224 | tf_op jit(solution)/shard_map/ppermute | solution.py:398
  7.9 16.8 %collective-permute-start.1 = (f32[256,128]{1,0:T(8,128)}, f32[256,128]{1,0:T(8,128)}, u32[]{:S(2)}, u32[]{:S(2)}) collective-permute-start(f32[256,128]{1,0:T(8,128)} %x.1), channel_id=1, source_target_pairs={{0,8},{4,12},{8,0},{12,4},{1,9},{5,13},{9,1},{13,5},{2,10},{6,14},... | collective-permute-start | bytes 393224 | tf_op jit(solution)/shard_map/ppermute | solution.py:398
  10.1 15.8 %collective-permute-start.6 = (f32[256,128]{1,0:T(8,128)}, f32[256,128]{1,0:T(8,128)}, u32[]{:S(2)}, u32[]{:S(2)}) collective-permute-start(f32[256,128]{1,0:T(8,128)} %x.1), channel_id=1, source_target_pairs={{0,1},{1,0},{2,3},{3,2},{4,5},{5,4},{6,7},{7,6},{8,9},{9,8},{10,11... | collective-permute-start | bytes 393224 | tf_op jit(solution)/shard_map/ppermute | solution.py:389
  11.2 1.4 copy-start.9
  12.6 1.4 copy-start.11
  15.9 11.3 %copy-start.12 = (f32[256,128]{1,0:T(8,128)S(1)}, f32[256,128]{1,0:T(8,128)}, u32[]{:S(2)}) copy-start(f32[256,128]{1,0:T(8,128)} %x.1) | copy-start | bytes 393220
  19.0 1.6 copy-start
  20.6 1.7 copy-start.3
  22.3 1.8 copy-start.5
  24.7 1.9 collective-permute-start.7
  25.3 1.7 collective-permute-start.8
  25.4 1.8 collective-permute-start.9
  27.2 1.9 copy-start.1
  30.0 5.7 %copy-start.13 = (f32[768,128]{1,0:T(8,128)S(1)}, f32[768,128]{1,0:T(8,128)}, u32[]{:S(2)}) copy-start(f32[768,128]{1,0:T(8,128)} %refs_0_.3) | copy-start | bytes 1179652
  30.0 5.7 %copy-start.14 = (f32[768,128]{1,0:T(8,128)S(1)}, f32[768,128]{1,0:T(8,128)}, u32[]{:S(2)}) copy-start(f32[768,128]{1,0:T(8,128)} %refs_1_.1) | copy-start | bytes 1179652
  30.0 5.7 %copy-start.15 = (f32[768,128]{1,0:T(8,128)S(1)}, f32[768,128]{1,0:T(8,128)}, u32[]{:S(2)}) copy-start(f32[768,128]{1,0:T(8,128)} %refs_2_.1) | copy-start | bytes 1179652
  30.0 5.7 %copy-start.16 = (f32[768,128]{1,0:T(8,128)S(1)}, f32[768,128]{1,0:T(8,128)}, u32[]{:S(2)}) copy-start(f32[768,128]{1,0:T(8,128)} %refs_3_.1) | copy-start | bytes 1179652
  30.0 11.1 %copy-start.4 = (bf16[2048,768]{1,0:T(8,128)(2,1)S(1)}, bf16[2048,768]{1,0:T(8,128)(2,1)}, u32[]{:S(2)}) copy-start(bf16[2048,768]{1,0:T(8,128)(2,1)} %copy-done.3) | copy-start | bytes 9437188
  30.1 11.1 %copy-start.6 = (bf16[2048,768]{1,0:T(8,128)(2,1)S(1)}, bf16[2048,768]{1,0:T(8,128)(2,1)}, u32[]{:S(2)}) copy-start(bf16[2048,768]{1,0:T(8,128)(2,1)} %copy-done.5) | copy-start | bytes 9437188
  33.9 7.2 %collective-permute-start.10 = (f32[384,128]{1,0:T(8,128)S(1)}, f32[384,128]{1,0:T(8,128)S(1)}, u32[]{:S(2)}, u32[]{:S(2)}) collective-permute-start(f32[384,128]{1,0:T(8,128)S(1)} %get-tuple-element.77.refs_0_), channel_id=1, source_target_pairs={{0,2},{1,3},{2,0},{3,1},{4,6},{5,7},{6,4},{7,5},{8,10},{9,11},{10,... | collective-permute-start | bytes 589832 | tf_op jit(solution)/shard_map/ppermute | solution.py:392
  41.1 7.1 %copy-start.20 = (f32[256,128]{1,0:T(8,128)S(1)}, f32[256,128]{1,0:T(8,128)}, u32[]{:S(2)}) copy-start(f32[256,128]{1,0:T(8,128)} %q.1) | copy-start | bytes 393220
  41.2 7.1 %copy-start.21 = (f32[256]{0:T(256)S(1)}, f32[256]{0:T(256)}, u32[]{:S(2)}) copy-start(f32[256]{0:T(256)} %param.13) | copy-start | bytes 3076
  41.2 32.0 %copy-start.2 = (bf16[768,2048]{1,0:T(8,128)(2,1)S(1)}, bf16[768,2048]{1,0:T(8,128)(2,1)}, u32[]{:S(2)}) copy-start(bf16[768,2048]{1,0:T(8,128)(2,1)} %copy-done) | copy-start | bytes 9437188
  43.8 13.3 %collective-permute-start.11 = (f32[272,128]{1,0:T(8,128)S(1)}, f32[272,128]{1,0:T(8,128)S(1)}, u32[]{:S(2)}, u32[]{:S(2)}) collective-permute-start(f32[272,128]{1,0:T(8,128)S(1)} %get-tuple-element.85), channel_id=1, source_target_pairs={{0,8},{4,12},{8,0},{12,4},{1,9},{5,13},{9,1},{13,5},{2,10},{6,14},... | collective-permute-start | bytes 417800 | tf_op jit(solution)/shard_map/ppermute | solution.py:398
  46.2 10.9 %collective-permute-start.12 = (f32[272,128]{1,0:T(8,128)S(1)}, f32[272,128]{1,0:T(8,128)S(1)}, u32[]{:S(2)}, u32[]{:S(2)}) collective-permute-start(f32[272,128]{1,0:T(8,128)S(1)} %get-tuple-element.86), channel_id=1, source_target_pairs={{0,4},{4,0},{8,12},{12,8},{1,5},{5,1},{9,13},{13,9},{2,6},{6,2},{1... | collective-permute-start | bytes 417800 | tf_op jit(solution)/shard_map/ppermute | solution.py:398
  48.3 8.9 %collective-permute-start.13 = (f32[272,128]{1,0:T(8,128)S(1)}, f32[272,128]{1,0:T(8,128)S(1)}, u32[]{:S(2)}, u32[]{:S(2)}) collective-permute-start(f32[272,128]{1,0:T(8,128)S(1)} %get-tuple-element.87), channel_id=1, source_target_pairs={{0,12},{4,8},{8,4},{12,0},{1,13},{5,9},{9,5},{13,1},{2,14},{6,10},... | collective-permute-start | bytes 417800 | tf_op jit(solution)/shard_map/ppermute | solution.py:398
  48.3 1.7 collective-permute-start.14
  48.3 1.3 collective-permute-start.15
  58.1 7.6 %collective-permute-start.18 = (f32[264,128]{1,0:T(8,128)S(1)}, f32[264,128]{1,0:T(8,128)S(1)}, u32[]{:S(2)}, u32[]{:S(2)}) collective-permute-start(f32[264,128]{1,0:T(8,128)S(1)} %get-tuple-element.90.refs_0_.refs_5_.refs_14_), channel_id=1, source_target_pairs={{0,12},{4,8},{8,4},{12,0},{1,13},{5,9},{9,5},{13,1},{2,14},{6,10},... | collective-permute-start | bytes 405512 | tf_op jit(solution)/shard_map/ppermute | solution.py:398
  60.3 7.8 %collective-permute-start.17 = (f32[264,128]{1,0:T(8,128)S(1)}, f32[264,128]{1,0:T(8,128)S(1)}, u32[]{:S(2)}, u32[]{:S(2)}) collective-permute-start(f32[264,128]{1,0:T(8,128)S(1)} %get-tuple-element.90.refs_0_.refs_5_.refs_14_), channel_id=1, source_target_pairs={{0,4},{4,0},{8,12},{12,8},{1,5},{5,1},{9,13},{13,9},{2,6},{6,2},{1... | collective-permute-start | bytes 405512 | tf_op jit(solution)/shard_map/ppermute | solution.py:398
  62.8 10.4 %collective-permute-start.16 = (f32[264,128]{1,0:T(8,128)S(1)}, f32[264,128]{1,0:T(8,128)S(1)}, u32[]{:S(2)}, u32[]{:S(2)}) collective-permute-start(f32[264,128]{1,0:T(8,128)S(1)} %get-tuple-element.90.refs_0_.refs_5_.refs_14_), channel_id=1, source_target_pairs={{0,8},{4,12},{8,0},{12,4},{1,9},{5,13},{9,1},{13,5},{2,10},{6,14},... | collective-permute-start | bytes 405512 | tf_op jit(solution)/shard_map/ppermute | solution.py:398
  76.0 6.5 %collective-permute-start.19 = (f32[392,128]{1,0:T(8,128)S(1)}, f32[392,128]{1,0:T(8,128)S(1)}, u32[]{:S(2)}, u32[]{:S(2)}) collective-permute-start(f32[392,128]{1,0:T(8,128)S(1)} %get-tuple-element.91.refs_0_), channel_id=1, source_target_pairs={{0,2},{1,3},{2,0},{3,1},{4,6},{5,7},{6,4},{7,5},{8,10},{9,11},{10,... | collective-permute-start | bytes 602120 | tf_op jit(solution)/shard_map/ppermute | solution.py:392
  85.3 12.0 %collective-permute-start.20 = (f32[264,128]{1,0:T(8,128)S(1)}, f32[264,128]{1,0:T(8,128)S(1)}, u32[]{:S(2)}, u32[]{:S(2)}) collective-permute-start(f32[264,128]{1,0:T(8,128)S(1)} %get-tuple-element.94), channel_id=1, source_target_pairs={{0,8},{4,12},{8,0},{12,4},{1,9},{5,13},{9,1},{13,5},{2,10},{6,14},... | collective-permute-start | bytes 405512 | tf_op jit(solution)/shard_map/ppermute | solution.py:398
  85.4 12.0 %collective-permute-start.21 = (f32[264,128]{1,0:T(8,128)S(1)}, f32[264,128]{1,0:T(8,128)S(1)}, u32[]{:S(2)}, u32[]{:S(2)}) collective-permute-start(f32[264,128]{1,0:T(8,128)S(1)} %get-tuple-element.95), channel_id=1, source_target_pairs={{0,4},{4,0},{8,12},{12,8},{1,5},{5,1},{9,13},{13,9},{2,6},{6,2},{1... | collective-permute-start | bytes 405512 | tf_op jit(solution)/shard_map/ppermute | solution.py:398
  89.0 8.3 %collective-permute-start.22 = (f32[264,128]{1,0:T(8,128)S(1)}, f32[264,128]{1,0:T(8,128)S(1)}, u32[]{:S(2)}, u32[]{:S(2)}) collective-permute-start(f32[264,128]{1,0:T(8,128)S(1)} %get-tuple-element.96), channel_id=1, source_target_pairs={{0,12},{4,8},{8,4},{12,0},{1,13},{5,9},{9,5},{13,1},{2,14},{6,10},... | collective-permute-start | bytes 405512 | tf_op jit(solution)/shard_map/ppermute | solution.py:398
  97.5 8.3 %collective-permute-start.25 = (f32[264,128]{1,0:T(8,128)S(1)}, f32[264,128]{1,0:T(8,128)S(1)}, u32[]{:S(2)}, u32[]{:S(2)}) collective-permute-start(f32[264,128]{1,0:T(8,128)S(1)} %get-tuple-element.100.refs_0_.refs_15_), channel_id=1, source_target_pairs={{0,12},{4,8},{8,4},{12,0},{1,13},{5,9},{9,5},{13,1},{2,14},{6,10},... | collective-permute-start | bytes 405512 | tf_op jit(solution)/shard_map/ppermute | solution.py:398
  99.4 7.0 %collective-permute-start.24 = (f32[264,128]{1,0:T(8,128)S(1)}, f32[264,128]{1,0:T(8,128)S(1)}, u32[]{:S(2)}, u32[]{:S(2)}) collective-permute-start(f32[264,128]{1,0:T(8,128)S(1)} %get-tuple-element.100.refs_0_.refs_15_), channel_id=1, source_target_pairs={{0,4},{4,0},{8,12},{12,8},{1,5},{5,1},{9,13},{13,9},{2,6},{6,2},{1... | collective-permute-start | bytes 405512 | tf_op jit(solution)/shard_map/ppermute | solution.py:398
  102.2 9.4 %collective-permute-start.23 = (f32[264,128]{1,0:T(8,128)S(1)}, f32[264,128]{1,0:T(8,128)S(1)}, u32[]{:S(2)}, u32[]{:S(2)}) collective-permute-start(f32[264,128]{1,0:T(8,128)S(1)} %get-tuple-element.100.refs_0_.refs_15_), channel_id=1, source_target_pairs={{0,8},{4,12},{8,0},{12,4},{1,9},{5,13},{9,1},{13,5},{2,10},{6,14},... | collective-permute-start | bytes 405512 | tf_op jit(solution)/shard_map/ppermute | solution.py:398
  114.5 5.8 %collective-permute-start.26 = (f32[392,128]{1,0:T(8,128)S(1)}, f32[392,128]{1,0:T(8,128)S(1)}, u32[]{:S(2)}, u32[]{:S(2)}) collective-permute-start(f32[392,128]{1,0:T(8,128)S(1)} %get-tuple-element.101.refs_0_), channel_id=1, source_target_pairs={{0,2},{1,3},{2,0},{3,1},{4,6},{5,7},{6,4},{7,5},{8,10},{9,11},{10,... | collective-permute-start | bytes 602120 | tf_op jit(solution)/shard_map/ppermute | solution.py:392
  120.4 5.4 %collective-permute-start.29 = (f32[8,128]{1,0:T(8,128)S(1)}, f32[8,128]{1,0:T(8,128)S(1)}, u32[]{:S(2)}, u32[]{:S(2)}) collective-permute-start(f32[8,128]{1,0:T(8,128)S(1)} %get-tuple-element.103.refs_0_), channel_id=1, source_target_pairs={{0,12},{4,8},{8,4},{12,0},{1,13},{5,9},{9,5},{13,1},{2,14},{6,10},... | collective-permute-start | bytes 12296 | tf_op jit(solution)/shard_map/ppermute | solution.py:398
  122.1 4.5 %collective-permute-start.28 = (f32[8,128]{1,0:T(8,128)S(1)}, f32[8,128]{1,0:T(8,128)S(1)}, u32[]{:S(2)}, u32[]{:S(2)}) collective-permute-start(f32[8,128]{1,0:T(8,128)S(1)} %get-tuple-element.103.refs_0_), channel_id=1, source_target_pairs={{0,8},{4,12},{8,0},{12,4},{1,9},{5,13},{9,1},{13,5},{2,10},{6,14},... | collective-permute-start | bytes 12296 | tf_op jit(solution)/shard_map/ppermute | solution.py:398
  122.1 4.5 %collective-permute-start.27 = (f32[8,128]{1,0:T(8,128)S(1)}, f32[8,128]{1,0:T(8,128)S(1)}, u32[]{:S(2)}, u32[]{:S(2)}) collective-permute-start(f32[8,128]{1,0:T(8,128)S(1)} %get-tuple-element.103.refs_0_), channel_id=1, source_target_pairs={{0,4},{4,0},{8,12},{12,8},{1,5},{5,1},{9,13},{13,9},{2,6},{6,2},{1... | collective-permute-start | bytes 12296 | tf_op jit(solution)/shard_map/ppermute | solution.py:398
  129.9 7.5 %collective-permute-start.30 = (f32[256,128]{1,0:T(8,128)S(1)}, f32[256,128]{1,0:T(8,128)S(1)}, u32[]{:S(2)}, u32[]{:S(2)}) collective-permute-start(f32[256,128]{1,0:T(8,128)S(1)} %get-tuple-element.112), channel_id=1, source_target_pairs={{0,8},{4,12},{8,0},{12,4},{1,9},{5,13},{9,1},{13,5},{2,10},{6,14},... | collective-permute-start | bytes 393224 | tf_op jit(solution)/shard_map/ppermute | solution.py:398
  131.9 5.5 %collective-permute-start.31 = (f32[256,128]{1,0:T(8,128)S(1)}, f32[256,128]{1,0:T(8,128)S(1)}, u32[]{:S(2)}, u32[]{:S(2)}) collective-permute-start(f32[256,128]{1,0:T(8,128)S(1)} %get-tuple-element.113), channel_id=1, source_target_pairs={{0,4},{4,0},{8,12},{12,8},{1,5},{5,1},{9,13},{13,9},{2,6},{6,2},{1... | collective-permute-start | bytes 393224 | tf_op jit(solution)/shard_map/ppermute | solution.py:398
  132.7 7.9 %collective-permute-start.32 = (f32[256,128]{1,0:T(8,128)S(1)}, f32[256,128]{1,0:T(8,128)S(1)}, u32[]{:S(2)}, u32[]{:S(2)}) collective-permute-start(f32[256,128]{1,0:T(8,128)S(1)} %get-tuple-element.114), channel_id=1, source_target_pairs={{0,12},{4,8},{8,4},{12,0},{1,13},{5,9},{9,5},{13,1},{2,14},{6,10},... | collective-permute-start | bytes 393224 | tf_op jit(solution)/shard_map/ppermute | solution.py:398
  141.2 6.9 %collective-permute-start.35 = (f32[264,128]{1,0:T(8,128)S(1)}, f32[264,128]{1,0:T(8,128)S(1)}, u32[]{:S(2)}, u32[]{:S(2)}) collective-permute-start(f32[264,128]{1,0:T(8,128)S(1)} %get-tuple-element.116.refs_0_.refs_5_.refs_14_), channel_id=1, source_target_pairs={{0,12},{4,8},{8,4},{12,0},{1,13},{5,9},{9,5},{13,1},{2,14},{6,10},... | collective-permute-start | bytes 405512 | tf_op jit(solution)/shard_map/ppermute | solution.py:398
  143.0 6.9 %collective-permute-start.34 = (f32[264,128]{1,0:T(8,128)S(1)}, f32[264,128]{1,0:T(8,128)S(1)}, u32[]{:S(2)}, u32[]{:S(2)}) collective-permute-start(f32[264,128]{1,0:T(8,128)S(1)} %get-tuple-element.116.refs_0_.refs_5_.refs_14_), channel_id=1, source_target_pairs={{0,4},{4,0},{8,12},{12,8},{1,5},{5,1},{9,13},{13,9},{2,6},{6,2},{1... | collective-permute-start | bytes 405512 | tf_op jit(solution)/shard_map/ppermute | solution.py:398
  146.9 6.9 %collective-permute-start.33 = (f32[264,128]{1,0:T(8,128)S(1)}, f32[264,128]{1,0:T(8,128)S(1)}, u32[]{:S(2)}, u32[]{:S(2)}) collective-permute-start(f32[264,128]{1,0:T(8,128)S(1)} %get-tuple-element.116.refs_0_.refs_5_.refs_14_), channel_id=1, source_target_pairs={{0,8},{4,12},{8,0},{12,4},{1,9},{5,13},{9,1},{13,5},{2,10},{6,14},... | collective-permute-start | bytes 405512 | tf_op jit(solution)/shard_map/ppermute | solution.py:398
  156.6 5.8 %collective-permute-start.36 = (f32[392,128]{1,0:T(8,128)S(1)}, f32[392,128]{1,0:T(8,128)S(1)}, u32[]{:S(2)}, u32[]{:S(2)}) collective-permute-start(f32[392,128]{1,0:T(8,128)S(1)} %get-tuple-element.117.refs_0_), channel_id=1, source_target_pairs={{0,2},{1,3},{2,0},{3,1},{4,6},{5,7},{6,4},{7,5},{8,10},{9,11},{10,... | collective-permute-start | bytes 602120 | tf_op jit(solution)/shard_map/ppermute | solution.py:392
  165.0 12.0 %collective-permute-start.37 = (f32[264,128]{1,0:T(8,128)S(1)}, f32[264,128]{1,0:T(8,128)S(1)}, u32[]{:S(2)}, u32[]{:S(2)}) collective-permute-start(f32[264,128]{1,0:T(8,128)S(1)} %get-tuple-element.120), channel_id=1, source_target_pairs={{0,8},{4,12},{8,0},{12,4},{1,9},{5,13},{9,1},{13,5},{2,10},{6,14},... | collective-permute-start | bytes 405512 | tf_op jit(solution)/shard_map/ppermute | solution.py:398
  165.6 11.4 %collective-permute-start.38 = (f32[264,128]{1,0:T(8,128)S(1)}, f32[264,128]{1,0:T(8,128)S(1)}, u32[]{:S(2)}, u32[]{:S(2)}) collective-permute-start(f32[264,128]{1,0:T(8,128)S(1)} %get-tuple-element.121), channel_id=1, source_target_pairs={{0,4},{4,0},{8,12},{12,8},{1,5},{5,1},{9,13},{13,9},{2,6},{6,2},{1... | collective-permute-start | bytes 405512 | tf_op jit(solution)/shard_map/ppermute | solution.py:398
  165.6 11.4 %collective-permute-start.39 = (f32[264,128]{1,0:T(8,128)S(1)}, f32[264,128]{1,0:T(8,128)S(1)}, u32[]{:S(2)}, u32[]{:S(2)}) collective-permute-start(f32[264,128]{1,0:T(8,128)S(1)} %get-tuple-element.122), channel_id=1, source_target_pairs={{0,12},{4,8},{8,4},{12,0},{1,13},{5,9},{9,5},{13,1},{2,14},{6,10},... | collective-permute-start | bytes 405512 | tf_op jit(solution)/shard_map/ppermute | solution.py:398
  177.1 7.0 %collective-permute-start.42 = (f32[264,128]{1,0:T(8,128)S(1)}, f32[264,128]{1,0:T(8,128)S(1)}, u32[]{:S(2)}, u32[]{:S(2)}) collective-permute-start(f32[264,128]{1,0:T(8,128)S(1)} %get-tuple-element.125.refs_0_.refs_15_), channel_id=1, source_target_pairs={{0,12},{4,8},{8,4},{12,0},{1,13},{5,9},{9,5},{13,1},{2,14},{6,10},... | collective-permute-start | bytes 405512 | tf_op jit(solution)/shard_map/ppermute | solution.py:398
  179.4 6.1 %collective-permute-start.41 = (f32[264,128]{1,0:T(8,128)S(1)}, f32[264,128]{1,0:T(8,128)S(1)}, u32[]{:S(2)}, u32[]{:S(2)}) collective-permute-start(f32[264,128]{1,0:T(8,128)S(1)} %get-tuple-element.125.refs_0_.refs_15_), channel_id=1, source_target_pairs={{0,4},{4,0},{8,12},{12,8},{1,5},{5,1},{9,13},{13,9},{2,6},{6,2},{1... | collective-permute-start | bytes 405512 | tf_op jit(solution)/shard_map/ppermute | solution.py:398
  180.8 7.5 %collective-permute-start.40 = (f32[264,128]{1,0:T(8,128)S(1)}, f32[264,128]{1,0:T(8,128)S(1)}, u32[]{:S(2)}, u32[]{:S(2)}) collective-permute-start(f32[264,128]{1,0:T(8,128)S(1)} %get-tuple-element.125.refs_0_.refs_15_), channel_id=1, source_target_pairs={{0,8},{4,12},{8,0},{12,4},{1,9},{5,13},{9,1},{13,5},{2,10},{6,14},... | collective-permute-start | bytes 405512 | tf_op jit(solution)/shard_map/ppermute | solution.py:398
  191.8 5.7 %collective-permute-start.43 = (f32[392,128]{1,0:T(8,128)S(1)}, f32[392,128]{1,0:T(8,128)S(1)}, u32[]{:S(2)}, u32[]{:S(2)}) collective-permute-start(f32[392,128]{1,0:T(8,128)S(1)} %get-tuple-element.126.refs_0_), channel_id=1, source_target_pairs={{0,2},{1,3},{2,0},{3,1},{4,6},{5,7},{6,4},{7,5},{8,10},{9,11},{10,... | collective-permute-start | bytes 602120 | tf_op jit(solution)/shard_map/ppermute | solution.py:392
  197.7 5.4 %collective-permute-start.46 = (f32[8,128]{1,0:T(8,128)S(1)}, f32[8,128]{1,0:T(8,128)S(1)}, u32[]{:S(2)}, u32[]{:S(2)}) collective-permute-start(f32[8,128]{1,0:T(8,128)S(1)} %get-tuple-element.128.refs_0_), channel_id=1, source_target_pairs={{0,12},{4,8},{8,4},{12,0},{1,13},{5,9},{9,5},{13,1},{2,14},{6,10},... | collective-permute-start | bytes 12296 | tf_op jit(solution)/shard_map/ppermute | solution.py:398
  199.9 4.5 %collective-permute-start.45 = (f32[8,128]{1,0:T(8,128)S(1)}, f32[8,128]{1,0:T(8,128)S(1)}, u32[]{:S(2)}, u32[]{:S(2)}) collective-permute-start(f32[8,128]{1,0:T(8,128)S(1)} %get-tuple-element.128.refs_0_), channel_id=1, source_target_pairs={{0,8},{4,12},{8,0},{12,4},{1,9},{5,13},{9,1},{13,5},{2,10},{6,14},... | collective-permute-start | bytes 12296 | tf_op jit(solution)/shard_map/ppermute | solution.py:398
  199.9 4.5 %collective-permute-start.44 = (f32[8,128]{1,0:T(8,128)S(1)}, f32[8,128]{1,0:T(8,128)S(1)}, u32[]{:S(2)}, u32[]{:S(2)}) collective-permute-start(f32[8,128]{1,0:T(8,128)S(1)} %get-tuple-element.128.refs_0_), channel_id=1, source_target_pairs={{0,4},{4,0},{8,12},{12,8},{1,5},{5,1},{9,13},{13,9},{2,6},{6,2},{1... | collective-permute-start | bytes 12296 | tf_op jit(solution)/shard_map/ppermute | solution.py:398
  204.6 2.0 collective-permute-start.47
  (6 other events, 5.4 us)

commit v7 on v2

--- a/solution.py
+++ b/solution.py
@@ -21,18 +21,25 @@
 VMEM = pl.BlockSpec(memory_space=pltpu.VMEM)
 SMEM = pl.BlockSpec(memory_space=pltpu.SMEM)
 
-
-def call(body, outs, ins, smem=(), scratch=(), flops=0):
+ANY = pl.BlockSpec(memory_space=pl.ANY)
+
+
+def call(body, outs, ins, smem=(), scratch=(), flops=0, after=None):
     n_bytes = sum(v.size * v.dtype.itemsize for v in ins)
+    tied = [] if after is None else [after]
+
+    def run(*refs):
+        body(*refs[len(tied) :])
+
     return pl.pallas_call(
-        body,
+        run,
         out_shape=[jax.ShapeDtypeStruct(s, d) for s, d in outs],
-        in_specs=[SMEM] * len(smem) + [VMEM] * len(ins),
+        in_specs=[ANY] * len(tied) + [SMEM] * len(smem) + [VMEM] * len(ins),
         out_specs=[VMEM] * len(outs),
         scratch_shapes=list(scratch),
         compiler_params=pltpu.CompilerParams(vmem_limit_bytes=30 * 1024 * 1024),
         cost_estimate=pl.CostEstimate(flops=flops, bytes_accessed=n_bytes, transcendentals=0),
-    )(*smem, *ins)
+    )(*tied, *smem, *ins)
 
 
 def low_half(shape):
@@ -98,48 +105,69 @@
         dst[...] = jnp.where(low_half(dst.shape), v[:rows], turn(v[rows:]))
 
 
-def prep_kernel(slab, per, cols, pairs, a_mine, a_other, p_mine, p_other, a_hi, a_lo, t_hi, t_lo, p_hi, p_lo, diag):
-    span = a_hi.shape[1] // 2
-    n_range = span // BLK
+def prep_kernel(slab, per, cols, pairs, a_in, p_in, a_hi, a_lo, t_hi, t_lo, p_hi, p_lo, diag):
     for ref in (a_hi, a_lo, t_hi, t_lo):
         ref[...] = jnp.zeros(ref.shape, BF16)
     diag[...] = jnp.zeros(diag.shape, F32)
-    for t, src in enumerate((a_mine, a_other)):
-        for m in range(slab):
-            rows = slice(m * BLK, (m + 1) * BLK)
-            for s in range(per):
-                k = m * per + s
-                col = cols[t * slab * per + k]
-                at = pl.multiple_of(t * span + col * BLK, BLK)
-                block = src[k]
-                hi, lo = split_bf16(block)
-                a_hi[rows, pl.ds(at, BLK)] = hi.astype(BF16)
-                a_lo[rows, pl.ds(at, BLK)] = lo.astype(BF16)
-                hi, lo = split_bf16(block.T)
-                t_hi[pl.ds(at, BLK), rows] = hi.astype(BF16)
-                t_lo[pl.ds(at, BLK), rows] = lo.astype(BF16)
-                here = pl.ds(t * n_range + col, 1)
-                diag[here, :] += RHO * jnp.sum(block * block, axis=0, keepdims=True)
+    for m in range(slab):
+        rows = slice(m * BLK, (m + 1) * BLK)
+        for s in range(per):
+            k = m * per + s
+            col = cols[k]
+            at = pl.multiple_of(col * BLK, BLK)
+            block = a_in[k]
+            hi, lo = split_bf16(block)
+            a_hi[rows, pl.ds(at, BLK)] = hi.astype(BF16)
+            a_lo[rows, pl.ds(at, BLK)] = lo.astype(BF16)
+            hi, lo = split_bf16(block.T)
+            t_hi[pl.ds(at, BLK), rows] = hi.astype(BF16)
+            t_lo[pl.ds(at, BLK), rows] = lo.astype(BF16)
+            diag[pl.ds(col, 1), :] += RHO * jnp.sum(block * block, axis=0, keepdims=True)
     shape = (BLK, BLK)
     eye = lax.broadcasted_iota(jnp.int32, shape, 0) == lax.broadcasted_iota(jnp.int32, shape, 1)
-    for t, src in enumerate((p_mine, p_other)):
-        for e in range(4):
-            hi, lo = split_bf16(src[e])
-            rows = slice((e // 2) * BLK, (e // 2 + 1) * BLK)
-            lanes = slice((e % 2) * BLK, (e % 2 + 1) * BLK)
-            p_hi[t, rows, lanes] = hi.astype(BF16)
-            p_lo[t, rows, lanes] = lo.astype(BF16)
-        for e in range(2):
-            here = pl.ds(t * n_range + pairs[2 * t + e], 1)
-            diag[here, :] += jnp.sum(jnp.where(eye, src[3 * e], 0.0), axis=0, keepdims=True)
+    for e in range(4):
+        hi, lo = split_bf16(p_in[e])
+        rows = slice((e // 2) * BLK, (e // 2 + 1) * BLK)
+        lanes = slice((e % 2) * BLK, (e % 2 + 1) * BLK)
+        p_hi[rows, lanes] = hi.astype(BF16)
+        p_lo[rows, lanes] = lo.astype(BF16)
+    for e in range(2):
+        diag[pl.ds(pairs[e], 1), :] += jnp.sum(jnp.where(eye, p_in[3 * e], 0.0), axis=0, keepdims=True)
+
+
+def first_kernel(n, own, place, pairs, *refs):
+    msgs, (a_hi, a_lo, p_hi, p_lo, keep, send, wide) = refs[:n], refs[n:]
+    core = place[1]
+    for k in range(n):
+        at = pl.multiple_of(lax.bitwise_xor(place[0], k) * own, own)
+        hi, lo = split_bf16(msgs[k][...])
+        wide[pl.ds(at, own), 0:LANES] = hi.astype(BF16)
+        wide[pl.ds(at, own), LANES:] = lo.astype(BF16)
+    x = wide[...]
+    total = dot(a_hi[...], x) + dot(a_lo[...], x)
+    total = total[:, :LANES] + total[:, LANES:]
+    rows = total.shape[0] // 2
+    keep[0:rows, :] = mix_cores(core, total[:rows], total[rows:])
+    send[0:rows, :] = mix_cores(1 - core, total[:rows], total[rows:])
+    at_i = pl.ds(pl.multiple_of(pairs[0] * BLK, BLK), BLK)
+    at_j = pl.ds(pl.multiple_of(pairs[1] * BLK, BLK), BLK)
+    v = jnp.concatenate([wide[at_i, :], wide[at_j, :]], axis=0)
+    part = dot(p_hi[...], v) + dot(p_lo[...], v)
+    part = part[:, :LANES] + part[:, LANES:]
+    part = jnp.where(core == 0, part, turn(part))
+    keep[rows:, :] = part
+    send[rows:, :] = part
+
+
+def meet_kernel(keep, got, msg, pp):
+    rows = msg.shape[0]
+    msg[...] = keep[0:rows, :] + got[0:rows, :]
+    pp[...] = jnp.where(low_half(pp.shape), keep[rows:, :], got[rows:, :])
 
 
 def forward_kernel(n, own, scalars, place, pairs, *refs):
     msgs, rest = refs[:n], refs[n:]
-    if scalars == 0:
-        others, rest = rest[:n], rest[n:]
-    a_hi, a_lo, p_hi, p_lo = rest[:4]
-    rest = rest[4:]
+    a_mats, p_mats, rest = rest[:4], rest[4:8], rest[8:]
     if scalars == 2:
         pp_first, rest = rest[0], rest[1:]
     msg, pp, whole, wide = rest
@@ -148,14 +176,15 @@
     for k in range(n):
         at = pl.multiple_of(lax.bitwise_xor(row, k) * own, own)
         v = msgs[k][0:own, :]
-        if scalars == 0:
-            v = mix_cores(place[1], v, others[k][...])
         whole[pl.ds(at, own), :] = v
         first, second = pair_up(v)
         wide[pl.ds(at, own), :] = first
         wide[pl.ds(pl.multiple_of(span + at, own), own), :] = second
-    x = wide[...]
-    total = fold(dot(a_hi[...], x) + dot(a_lo[...], x))
+    total = jnp.zeros((a_mats[0].shape[0], LANES), F32)
+    for t in range(2):
+        x = wide[t * span : (t + 1) * span, :]
+        total = total + (dot(a_mats[2 * t][...], x) + dot(a_mats[2 * t + 1][...], x))
+    total = fold(total)
     rows = total.shape[0] // 2
     msg[0:rows, :] = jnp.where(low_half((rows, LANES)), total[:rows], total[rows:])
     parts = []
@@ -163,36 +192,35 @@
         at_i = pl.multiple_of(t * span + pairs[2 * t] * BLK, BLK)
         at_j = pl.multiple_of(t * span + pairs[2 * t + 1] * BLK, BLK)
         v = jnp.concatenate([wide[pl.ds(at_i, BLK), :], wide[pl.ds(at_j, BLK), :]], axis=0)
-        parts.append(fold(dot(p_hi[t], v) + dot(p_lo[t], v)))
+        parts.append(fold(dot(p_mats[2 * t][...], v) + dot(p_mats[2 * t + 1][...], v)))
     low2 = low_half((2 * BLK, LANES))
     pp_now = jnp.where(low2, parts[0], parts[1])
     pp[...] = pp_now
-    if scalars:
-        picked = []
-        for t in range(2):
-            at_i = pl.multiple_of(pairs[2 * t] * BLK, BLK)
-            at_j = pl.multiple_of(pairs[2 * t + 1] * BLK, BLK)
-            picked.append(jnp.concatenate([whole[pl.ds(at_i, BLK), :], whole[pl.ds(at_j, BLK), :]], axis=0))
-        vec = jnp.where(low2, picked[0], picked[1])
-        tile = msgs[0][own : own + SC, :]
-        for k in range(1, n):
-            tile = tile + msgs[k][own : own + SC, :]
-        tile = fold(tile)
-        at = lax.broadcasted_iota(jnp.int32, (SC, LANES), 0)
-        tile = jnp.where(at == 3, col_sum(vec * pp_now), tile)
-        if scalars == 2:
-            tile = jnp.where(at == 4, col_sum(vec * pp_first[...]), tile)
-        msg[rows : rows + SC, :] = tile
-
-
-def back_product(n, own, place, pairs, w, pp_now, t_hi, t_lo, total, outs, extra):
+    picked = []
+    for t in range(2):
+        at_i = pl.multiple_of(pairs[2 * t] * BLK, BLK)
+        at_j = pl.multiple_of(pairs[2 * t + 1] * BLK, BLK)
+        picked.append(jnp.concatenate([whole[pl.ds(at_i, BLK), :], whole[pl.ds(at_j, BLK), :]], axis=0))
+    vec = jnp.where(low2, picked[0], picked[1])
+    tile = msgs[0][own : own + SC, :]
+    for k in range(1, n):
+        tile = tile + msgs[k][own : own + SC, :]
+    tile = fold(tile)
+    at = lax.broadcasted_iota(jnp.int32, (SC, LANES), 0)
+    tile = jnp.where(at == 3, col_sum(vec * pp_now), tile)
+    if scalars == 2:
+        tile = jnp.where(at == 4, col_sum(vec * pp_first[...]), tile)
+    msg[rows : rows + SC, :] = tile
+
+
+def back_product(n, own, place, pairs, w, pp_now, t_mats, total, outs, extra=()):
     row = place[0]
     span = total.shape[0]
     first, second = pair_up(w)
     wide = jnp.concatenate([first, second], axis=0)
-    part = fold(dot(t_hi[...], wide) + dot(t_lo[...], wide))
-    low = low_half((span, LANES))
-    total[...] = jnp.where(low, part[:span], part[span:])
+    mine = fold(dot(t_mats[0][...], wide) + dot(t_mats[1][...], wide))
+    other = fold(dot(t_mats[2][...], wide) + dot(t_mats[3][...], wide))
+    total[...] = jnp.where(low_half((span, LANES)), mine, other)
     low1 = low_half((BLK, LANES))
     for t in range(2):
         side = low1 if t == 0 else jnp.logical_not(low1)
@@ -202,26 +230,28 @@
     for k in range(n):
         at = pl.multiple_of(lax.bitwise_xor(row, k) * own, own)
         outs[k][0:own, :] = total[pl.ds(at, own), :]
-        if extra is not None:
-            outs[k][own : own + extra.shape[0], :] = extra
+        at = own
+        for rows in extra:
+            outs[k][at : at + rows.shape[0], :] = rows
+            at += rows.shape[0]
 
 
 def start_back_kernel(n, nx, own, place, pairs, *refs):
     msgs, rest = refs[:nx], refs[nx:]
-    z, y, pp, diag, t_hi, t_lo = rest[:6]
-    outs, (ax, total) = rest[6 : 6 + n], rest[6 + n :]
+    z, y, pp, diag, diag_other, *t_mats = rest[:9]
+    outs, (ax, total) = rest[9 : 9 + n], rest[9 + n :]
     ax_now = msgs[0][...]
     for k in range(1, nx):
         ax_now = ax_now + msgs[k][...]
     ax[...] = ax_now
     w = RHO * ax_now - (RHO * z[...] - y[...])
-    back_product(n, own, place, pairs, w, pp[...], t_hi, t_lo, total, outs, diag[...])
+    back_product(n, own, place, pairs, w, pp[...], t_mats, total, outs, (diag[...], diag_other[...]))
 
 
 def step_back_kernel(n, nx, own, place, pairs, *refs):
     msgs, rest = refs[:nx], refs[nx:]
-    pp, t_hi, t_lo = rest[:3]
-    outs, (ad, scal, total) = rest[3 : 3 + n], rest[3 + n :]
+    pp, *t_mats = rest[:5]
+    outs, (ad, scal, total) = rest[5 : 5 + n], rest[5 + n :]
     rows = ad.shape[0]
     v = msgs[0][...]
     for k in range(1, nx):
@@ -231,9 +261,7 @@
     ad[...] = ad_now
     scal[...] = tile
     curve = RHO * col_sum(ad_now * ad_now) + tile[3:4]
-    back_product(
-        n, own, place, pairs, RHO * ad_now, pp[...], t_hi, t_lo, total, outs, pack_rows(curve)
-    )
+    back_product(n, own, place, pairs, RHO * ad_now, pp[...], t_mats, total, outs, (pack_rows(curve),))
 
 
 def residual_kernel(n, own, first, place, *refs):
@@ -330,8 +358,8 @@
 def update_kernel(n, own, place, pairs, *refs):
     beta, step1, step2, x_new, ax_hat, z_new, y_new, rest = admm_update(n, own, refs)
     ax = refs[n + 2]
-    ppx, pp1, pp2, t_hi, t_lo = rest[:5]
-    outs, (x_out, z_out, y_out, ax_out, ppx_out, total) = rest[5 : 5 + n], rest[5 + n :]
+    ppx, pp1, pp2, *t_mats = rest[:7]
+    outs, (x_out, z_out, y_out, ax_out, ppx_out, total) = rest[7 : 7 + n], rest[7 + n :]
     x_out[...] = x_new
     z_out[...] = z_new
     y_out[...] = y_new
@@ -341,7 +369,7 @@
     pp_new = RELAX * pp_hat + (1.0 - RELAX) * ppx[...]
     ppx_out[...] = pp_new
     w = RHO * ax_new - (RHO * z_new - y_new)
-    back_product(n, own, place, pairs, w, pp_new, t_hi, t_lo, total, outs, None)
+    back_product(n, own, place, pairs, w, pp_new, t_mats, total, outs)
 
 
 def last_kernel(n, own, *refs):
@@ -410,54 +438,72 @@
     p_other = to_core(p_mine)
     pd_other = to_core(p_diag)
     count = slab * per
-    cols = jnp.concatenate([ints[:count], ints_other[:count]])
-    pairs = jnp.concatenate([ints[count:], ints_other[count:]])
     pd = jnp.concatenate(
         [jnp.broadcast_to(p_diag[:, None], (own, HALF)), jnp.broadcast_to(pd_other[:, None], (own, HALF))], axis=1
     )
-    x_others = [to_core(v) for v in x_rows]
-    x, q = call(own_kernel, [((own, LANES), F32)] * 2, [x_state, x_others[0], q_lin, to_core(q_lin)], [place])
+    x, q = call(
+        own_kernel, [((own, LANES), F32)] * 2, [x_state, to_core(x_state), q_lin, to_core(q_lin)], [place]
+    )
     z, y, lower, upper = call(
         slab_kernel, [((half_rows, LANES), F32)] * 4, [z_state, y_state, lower_bound, upper_bound], [place]
-    )
-    wide = 2 * span
-    a_hi, a_lo, t_hi, t_lo, p_hi, p_lo, diag = call(
-        functools.partial(prep_kernel, slab, per),
-        [((slab_rows, wide), BF16)] * 2
-        + [((wide, slab_rows), BF16)] * 2
-        + [((2, 2 * BLK, 2 * BLK), BF16)] * 2
-        + [((2 * n_range, LANES), F32)],
-        [a_mine, a_other, p_mine, p_other],
-        [cols, pairs],
-        flops=10**8,
-    )
-    prod_flops = 4 * slab_rows * wide * LANES
-    total_scratch = [pltpu.VMEM((span, LANES), F32)]
-
-    def forward(msgs, scalars, pp_first=()):
-        extra = SC if scalars else 0
-        return call(
-            functools.partial(forward_kernel, n, own, scalars),
-            [((half_rows + extra, LANES), F32), ((2 * BLK, LANES), F32)],
-            [*msgs, a_hi, a_lo, p_hi, p_lo, *pp_first],
-            [place, pairs],
-            total_scratch + [pltpu.VMEM((wide, LANES), BF16)],
-            flops=prod_flops,
-        )
-
-    msg, ppx = forward(x_rows + x_others, 0)
-    *pieces, ax = call(
-        functools.partial(start_back_kernel, n, nx, own),
-        [((own + 2 * n_range, LANES), F32)] * n + [((half_rows, LANES), F32)],
-        [*to_x(msg), z, y, ppx, diag, t_hi, t_lo],
-        [place, pairs],
-        total_scratch,
-        flops=prod_flops,
     )
     own_shape = ((own, LANES), F32)
     msg_shape = ((own + SC, LANES), F32)
     tile_shape = ((SC, LANES), F32)
     slab_shape = ((half_rows, LANES), F32)
+    pp_shape = ((2 * BLK, LANES), F32)
+
+    def prepare(a, p, at_cols, at_pairs, after=None):
+        *mats, diag = call(
+            functools.partial(prep_kernel, slab, per),
+            [((slab_rows, span), BF16)] * 2
+            + [((span, slab_rows), BF16)] * 2
+            + [((2 * BLK, 2 * BLK), BF16)] * 2
+            + [((n_range, LANES), F32)],
+            [a, p],
+            [at_cols, at_pairs],
+            flops=10**8,
+            after=after,
+        )
+        return mats[0:2], mats[2:4], mats[4:6], diag
+
+    prod_flops = 4 * slab_rows * 2 * span * LANES
+    total_scratch = [pltpu.VMEM((span, LANES), F32)]
+    a_own, t_own, p_own, diag = prepare(a_mine, p_mine, a_cols.reshape(-1), p_pairs.reshape(-1))
+    both_shape = ((half_rows + 2 * BLK, LANES), F32)
+    keep, send = call(
+        functools.partial(first_kernel, n, own),
+        [both_shape, both_shape],
+        [*x_rows, *a_own, *p_own],
+        [place, p_pairs.reshape(-1)],
+        [pltpu.VMEM((span, 2 * LANES), BF16)],
+        flops=prod_flops,
+    )
+    msg, ppx = call(meet_kernel, [slab_shape, pp_shape], [keep, to_core(send)])
+    a_far, t_far, p_far, diag_other = prepare(
+        a_other, p_other, ints_other[:count], ints_other[count:], after=msg
+    )
+    a_mats, t_mats, p_mats = [*a_own, *a_far], [*t_own, *t_far], [*p_own, *p_far]
+    pairs = jnp.concatenate([p_pairs.reshape(-1), ints_other[count:]])
+
+    def forward(msgs, scalars, pp_first=()):
+        return call(
+            functools.partial(forward_kernel, n, own, scalars),
+            [((half_rows + SC, LANES), F32), pp_shape],
+            [*msgs, *a_mats, *p_mats, *pp_first],
+            [place, pairs],
+            total_scratch + [pltpu.VMEM((2 * span, LANES), BF16)],
+            flops=prod_flops,
+        )
+
+    *pieces, ax = call(
+        functools.partial(start_back_kernel, n, nx, own),
+        [((own + 2 * n_range, LANES), F32)] * n + [((half_rows, LANES), F32)],
+        [*to_x(msg), z, y, ppx, diag, diag_other, *t_mats],
+        [place, pairs],
+        total_scratch,
+        flops=prod_flops,
+    )
     for outer in range(ADMM_ITERS):
         if outer == 0:
             msg1, r, dk = call(
@@ -478,7 +524,7 @@
         *pieces, ad, scal = call(
             functools.partial(step_back_kernel, n, nx, own),
             [msg_shape] * n + [slab_shape, tile_shape],
-            [*to_x(msg), pp1, t_hi, t_lo],
+            [*to_x(msg), pp1, *t_mats],
             [place, pairs],
             total_scratch,
             flops=prod_flops,
@@ -500,7 +546,7 @@
             *pieces, x, z, y, ax, ppx = call(
                 functools.partial(update_kernel, n, own),
                 [own_shape] * n + [own_shape, slab_shape, slab_shape, slab_shape, ((2 * BLK, LANES), F32)],
-                [*state, ppx, pp1, pp2, t_hi, t_lo],
+                [*state, ppx, pp1, pp2, *t_mats],
                 [place, pairs],
                 total_scratch,
                 flops=prod_flops,

time: 203 us -> 193 us (0.951)
  waiting for transfers between devices: 99.6 us -> 89.8 us
  starting transfers between devices: 61 us -> 63.2 us
    ppermute x33, waiting for transfers between devices: 74.6 us -> 66.1 us  [to_row(): got[k] = lax.ppermute(pieces[k], 'row', [(i, i ^ k) for i in range(n)])]
    ppermute x33, starting transfers between devices: 51.5 us -> 54 us  [to_row(): got[k] = lax.ppermute(pieces[k], 'row', [(i, i ^ k) for i in range(n)])]
    pallas_call x20 -> x22, Pallas kernels: 35.6 us -> 34.7 us  [call(): pl.pallas_call(run, out_shape=[jax.ShapeDtypeStruct(s, d) for s, d in out...]
    ppermute x10 -> x8, waiting for transfers between devices: 3.85 us -> 4.49 us  [to_core(): return lax.ppermute(v, 'col', [(c, c ^ 1) for c in range(n_col)])]
  transfers between devices with their start and end apart: 48 -> 46, of which waited for: 30 -> 30; matrix products, arithmetic and copies ran while one was open for 1% -> 1% of each run, Pallas kernels for 2% -> 4%
where the time goes in v7:
time: 193 us
  waiting for transfers between devices  89.8 us (47%)
  starting transfers between devices  63.2 us (33%)
  Pallas kernels  34.7 us (18%)
  local copies, waits for them, and re-layouts  4.16 us (2%)
    ppermute x33, waiting for transfers between devices, to_row(): got[k] = lax.ppermute(pieces[k], 'row', [(i, i ^ k) for i in range(n)])  66.1 us
    ppermute x33, starting transfers between devices, to_row(): got[k] = lax.ppermute(pieces[k], 'row', [(i, i ^ k) for i in range(n)])  54 us
    pallas_call x22, Pallas kernels, call(): pl.pallas_call(run, out_shape=[jax.ShapeDtypeStruct(s, d) for s, d in out...  34.7 us
    ppermute x5, waiting for transfers between devices, to_x(): lax.ppermute(v, 'col', [(c, c ^ 2 * k) for c in range(n_col)])  19.2 us
    ppermute x5, starting transfers between devices, to_x(): lax.ppermute(v, 'col', [(c, c ^ 2 * k) for c in range(n_col)])  7.4 us
    ppermute x8, waiting for transfers between devices, to_core(): return lax.ppermute(v, 'col', [(c, c ^ 1) for c in range(n_col)])  4.49 us
  transfers between devices with their start and end apart: 46, of which 30 were waited for; matrix products, arithmetic and copies ran while one was open for 1% of the time, Pallas kernels for 4%

profile of v7, /device:TPU:0, one launch (start us, length us, event | category | flops | bytes accessed | tf_op | source)
XLA Modules:
  0.0 193.2 jit_solution(2629867880607392243)
XLA Ops:
  1.1 4.7 %collective-permute-start.3 = (f32[256,128]{1,0:T(8,128)}, f32[256,128]{1,0:T(8,128)S(1)}, u32[]{:S(2)}, u32[]{:S(2)}) collective-permute-start(f32[256,128]{1,0:T(8,128)} %refs_1_.3), channel_id=1, source_target_pairs={{0,12},{4,8},{8,4},{12,0},{1,13},{5,9},{9,5},{13,1},{2,14},{6,10},... | collective-permute-start | bytes 393224 | tf_op jit(solution)/shard_map/ppermute | solution.py:426
  7.3 1.4 copy-done
  10.3 1.8 shard_map.130
  12.2 5.5 %collective-permute-done.2.refs_4_ = f32[256,128]{1,0:T(8,128)S(1)} collective-permute-done((f32[256,128]{1,0:T(8,128)}, f32[256,128]{1,0:T(8,128)S(1)}, u32[]{:S(2)}, u32[]{:S(2)}) %collective-permute-start.2) | collective-permute-done | bytes 131104 | tf_op jit(solution)/shard_map/ppermute | solution.py:426
  17.8 1.8 shard_map.131
  20.2 1.1 collective-permute-done.4.refs_1_
  21.3 1.6 collective-permute-start.5
  23.0 1.3 shard_map.133
  24.5 1.8 shard_map.134
  26.2 2.1 %collective-permute-done.5.refs_3_ = f32[384,128]{1,0:T(8,128)S(1)} collective-permute-done((f32[384,128]{1,0:T(8,128)S(1)}, f32[384,128]{1,0:T(8,128)S(1)}, u32[]{:S(2)}, u32[]{:S(2)}) %collective-permute-start.5) | collective-permute-done | bytes 196640 | tf_op jit(solution)/shard_map/ppermute | solution.py:419
  28.3 2.6 %shard_map.135 = (f32[272,128]{1,0:T(8,128)S(1)}, f32[272,128]{1,0:T(8,128)S(1)}, f32[272,128]{1,0:T(8,128)S(1)}, f32[272,128]{1,0:T(8,128)S(1)}, f32[384,128]{1,0:T(8,128)S(1)}) custom-call(s32[2]{0:T(128)S(1)} %pad_add_fusion.refs_0_, s32[4]{0:T(128)S(1)} %pad_add_fusion.2.refs_1_, f32[384,128]{1,0:T(8,128)S(1)} %get-tuple-element.80.refs_0_.refs_2_, ...), custom_call_target="tpu_custom_call" | custom-call | flops 805306368 | bytes 7217152 | tf_op jit(solution)/shard_map/pallas_call | solution.py:34
  31.0 3.0 %collective-permute-start.9 = (f32[272,128]{1,0:T(8,128)S(1)}, f32[272,128]{1,0:T(8,128)S(1)}, u32[]{:S(2)}, u32[]{:S(2)}) collective-permute-start(f32[272,128]{1,0:T(8,128)S(1)} %get-tuple-element.92), channel_id=1, source_target_pairs={{0,8},{4,12},{8,0},{12,4},{1,9},{5,13},{9,1},{13,5},{2,10},{6,14},... | collective-permute-start | bytes 417800 | tf_op jit(solution)/shard_map/ppermute | solution.py:426
  34.0 1.4 collective-permute-start.10
  38.6 5.8 %collective-permute-done.9.refs_3_ = f32[272,128]{1,0:T(8,128)S(1)} collective-permute-done((f32[272,128]{1,0:T(8,128)S(1)}, f32[272,128]{1,0:T(8,128)S(1)}, u32[]{:S(2)}, u32[]{:S(2)}) %collective-permute-start.9) | collective-permute-done | bytes 139296 | tf_op jit(solution)/shard_map/ppermute | solution.py:426
  45.3 2.4 %collective-permute-start.16 = (f32[264,128]{1,0:T(8,128)S(1)}, f32[264,128]{1,0:T(8,128)S(1)}, u32[]{:S(2)}, u32[]{:S(2)}) collective-permute-start(f32[264,128]{1,0:T(8,128)S(1)} %get-tuple-element.96.refs_2_.refs_5_.refs_16_), channel_id=1, source_target_pairs={{0,12},{4,8},{8,4},{12,0},{1,13},{5,9},{9,5},{13,1},{2,14},{6,10},... | collective-permute-start | bytes 405512 | tf_op jit(solution)/shard_map/ppermute | solution.py:426
  47.8 2.2 %collective-permute-start.15 = (f32[264,128]{1,0:T(8,128)S(1)}, f32[264,128]{1,0:T(8,128)S(1)}, u32[]{:S(2)}, u32[]{:S(2)}) collective-permute-start(f32[264,128]{1,0:T(8,128)S(1)} %get-tuple-element.96.refs_2_.refs_5_.refs_16_), channel_id=1, source_target_pairs={{0,8},{4,12},{8,0},{12,4},{1,9},{5,13},{9,1},{13,5},{2,10},{6,14},... | collective-permute-start | bytes 405512 | tf_op jit(solution)/shard_map/ppermute | solution.py:426
  50.5 3.2 %collective-permute-done.16.refs_5_ = f32[264,128]{1,0:T(8,128)S(1)} collective-permute-done((f32[264,128]{1,0:T(8,128)S(1)}, f32[264,128]{1,0:T(8,128)S(1)}, u32[]{:S(2)}, u32[]{:S(2)}) %collective-permute-start.16) | collective-permute-done | bytes 135200 | tf_op jit(solution)/shard_map/ppermute | solution.py:426
  53.6 4.7 %collective-permute-done.15.refs_4_ = f32[264,128]{1,0:T(8,128)S(1)} collective-permute-done((f32[264,128]{1,0:T(8,128)S(1)}, f32[264,128]{1,0:T(8,128)S(1)}, u32[]{:S(2)}, u32[]{:S(2)}) %collective-permute-start.15) | collective-permute-done | bytes 135200 | tf_op jit(solution)/shard_map/ppermute | solution.py:426
  58.3 2.9 %shard_map.138 = (f32[392,128]{1,0:T(8,128)S(1)}, f32[256,128]{1,0:T(8,128)S(1)}) custom-call(s32[2]{0:T(128)S(1)} %pad_add_fusion.refs_0_, s32[4]{0:T(128)S(1)} %pad_add_fusion.2.refs_1_, f32[264,128]{1,0:T(8,128)S(1)} %get-tuple-element.96.refs_2_.refs_5_.refs_16_, f32[264,128]{1,0:T(8,128)S(1)} %collective-permute-done.14.refs_3_, ...), custom_call_target="tpu_custom_call" | custom-call | flops 805306368 | bytes 7356416 | tf_op jit(solution)/shard_map/pallas_call | solution.py:34
  61.2 1.5 collective-permute-start.17
  62.7 4.3 %collective-permute-done.17.refs_3_ = f32[392,128]{1,0:T(8,128)S(1)} collective-permute-done((f32[392,128]{1,0:T(8,128)S(1)}, f32[392,128]{1,0:T(8,128)S(1)}, u32[]{:S(2)}, u32[]{:S(2)}) %collective-permute-start.17) | collective-permute-done | bytes 200736 | tf_op jit(solution)/shard_map/ppermute | solution.py:419
  67.0 2.5 %shard_map.139 = (f32[264,128]{1,0:T(8,128)S(1)}, f32[264,128]{1,0:T(8,128)S(1)}, f32[264,128]{1,0:T(8,128)S(1)}, f32[264,128]{1,0:T(8,128)S(1)}, f32[384,128]{1,0:T(8,128)S(1)}, /*index=5*/f32[8,128]{1,0:T(8,128)S(1)}) custom-call(s32[2]{0:T(128)S(1)} %pad_add_fusion.refs_0_, s32[4]{0:T(128)S(1)} %pad_add_fusion.2.refs_1_, ...), custom_call_target="tpu_custom_call" | custom-call | flops 805306368 | bytes 6823936 | tf_op jit(solution)/shard_map/pallas_call | solution.py:34
  69.6 3.0 %collective-permute-start.19 = (f32[264,128]{1,0:T(8,128)S(1)}, f32[264,128]{1,0:T(8,128)S(1)}, u32[]{:S(2)}, u32[]{:S(2)}) collective-permute-start(f32[264,128]{1,0:T(8,128)S(1)} %get-tuple-element.105), channel_id=1, source_target_pairs={{0,8},{4,12},{8,0},{12,4},{1,9},{5,13},{9,1},{13,5},{2,10},{6,14},... | collective-permute-start | bytes 405512 | tf_op jit(solution)/shard_map/ppermute | solution.py:426
  72.6 1.4 collective-permute-start.20
  74.0 2.6 %collective-permute-done.18.refs_1_ = f32[264,128]{1,0:T(8,128)S(1)} collective-permute-done((f32[264,128]{1,0:T(8,128)S(1)}, f32[264,128]{1,0:T(8,128)S(1)}, u32[]{:S(2)}, u32[]{:S(2)}) %collective-permute-start.18) | collective-permute-done | bytes 135200 | tf_op jit(solution)/shard_map/ppermute | solution.py:426
  76.6 3.7 %collective-permute-done.19.refs_2_ = f32[264,128]{1,0:T(8,128)S(1)} collective-permute-done((f32[264,128]{1,0:T(8,128)S(1)}, f32[264,128]{1,0:T(8,128)S(1)}, u32[]{:S(2)}, u32[]{:S(2)}) %collective-permute-start.19) | collective-permute-done | bytes 135200 | tf_op jit(solution)/shard_map/ppermute | solution.py:426
  80.4 4.0 %collective-permute-start.23 = (f32[264,128]{1,0:T(8,128)S(1)}, f32[264,128]{1,0:T(8,128)S(1)}, u32[]{:S(2)}, u32[]{:S(2)}) collective-permute-start(f32[264,128]{1,0:T(8,128)S(1)} %get-tuple-element.110.refs_2_.refs_17_), channel_id=1, source_target_pairs={{0,12},{4,8},{8,4},{12,0},{1,13},{5,9},{9,5},{13,1},{2,14},{6,10},... | collective-permute-start | bytes 405512 | tf_op jit(solution)/shard_map/ppermute | solution.py:426
  84.4 2.8 %collective-permute-start.22 = (f32[264,128]{1,0:T(8,128)S(1)}, f32[264,128]{1,0:T(8,128)S(1)}, u32[]{:S(2)}, u32[]{:S(2)}) collective-permute-start(f32[264,128]{1,0:T(8,128)S(1)} %get-tuple-element.110.refs_2_.refs_17_), channel_id=1, source_target_pairs={{0,8},{4,12},{8,0},{12,4},{1,9},{5,13},{9,1},{13,5},{2,10},{6,14},... | collective-permute-start | bytes 405512 | tf_op jit(solution)/shard_map/ppermute | solution.py:426
  87.7 1.2 collective-permute-done.23.refs_5_
  88.9 4.4 %collective-permute-done.22.refs_4_ = f32[264,128]{1,0:T(8,128)S(1)} collective-permute-done((f32[264,128]{1,0:T(8,128)S(1)}, f32[264,128]{1,0:T(8,128)S(1)}, u32[]{:S(2)}, u32[]{:S(2)}) %collective-permute-start.22) | collective-permute-done | bytes 135200 | tf_op jit(solution)/shard_map/ppermute | solution.py:426
  93.3 3.1 %shard_map.141 = (f32[392,128]{1,0:T(8,128)S(1)}, f32[256,128]{1,0:T(8,128)S(1)}) custom-call(s32[2]{0:T(128)S(1)} %pad_add_fusion.refs_0_, s32[4]{0:T(128)S(1)} %pad_add_fusion.2.refs_1_, f32[264,128]{1,0:T(8,128)S(1)} %get-tuple-element.110.refs_2_.refs_17_, f32[264,128]{1,0:T(8,128)S(1)} %collective-permute-done.21.refs_3_, ...), custom_call_target="tpu_custom_call" | custom-call | flops 805306368 | bytes 7487488 | tf_op jit(solution)/shard_map/pallas_call | solution.py:34
  96.4 1.5 collective-permute-start.24
  97.8 4.3 %collective-permute-done.24.refs_1_ = f32[392,128]{1,0:T(8,128)S(1)} collective-permute-done((f32[392,128]{1,0:T(8,128)S(1)}, f32[392,128]{1,0:T(8,128)S(1)}, u32[]{:S(2)}, u32[]{:S(2)}) %collective-permute-start.24) | collective-permute-done | bytes 200736 | tf_op jit(solution)/shard_map/ppermute | solution.py:419
  102.3 3.2 %collective-permute-start.27 = (f32[8,128]{1,0:T(8,128)S(1)}, f32[8,128]{1,0:T(8,128)S(1)}, u32[]{:S(2)}, u32[]{:S(2)}) collective-permute-start(f32[8,128]{1,0:T(8,128)S(1)} %get-tuple-element.113.refs_2_), channel_id=1, source_target_pairs={{0,12},{4,8},{8,4},{12,0},{1,13},{5,9},{9,5},{13,1},{2,14},{6,10},... | collective-permute-start | bytes 12296 | tf_op jit(solution)/shard_map/ppermute | solution.py:426
  105.5 1.2 collective-permute-start.25
  106.7 1.0 collective-permute-done.27.refs_5_
  107.7 2.3 %collective-permute-done.26.refs_4_ = f32[8,128]{1,0:T(8,128)S(1)} collective-permute-done((f32[8,128]{1,0:T(8,128)S(1)}, f32[8,128]{1,0:T(8,128)S(1)}, u32[]{:S(2)}, u32[]{:S(2)}) %collective-permute-start.26) | collective-permute-done | bytes 4128 | tf_op jit(solution)/shard_map/ppermute | solution.py:426
  110.0 3.2 %shard_map.143 = (f32[256,128]{1,0:T(8,128)S(1)}, f32[256,128]{1,0:T(8,128)S(1)}, f32[256,128]{1,0:T(8,128)S(1)}, f32[256,128]{1,0:T(8,128)S(1)}, f32[256,128]{1...) custom-call(s32[2]{0:T(128)S(1)} %pad_add_fusion.refs_0_, ...), custom_call_target="tpu_custom_call" | custom-call | flops 805306368 | bytes 8486912 | tf_op jit(solution)/shard_map/pallas_call | solution.py:34
  113.6 1.8 collective-permute-start.29
  115.4 2.3 %collective-permute-start.30 = (f32[256,128]{1,0:T(8,128)S(1)}, f32[256,128]{1,0:T(8,128)S(1)}, u32[]{:S(2)}, u32[]{:S(2)}) collective-permute-start(f32[256,128]{1,0:T(8,128)S(1)} %get-tuple-element.124), channel_id=1, source_target_pairs={{0,12},{4,8},{8,4},{12,0},{1,13},{5,9},{9,5},{13,1},{2,14},{6,10},... | collective-permute-start | bytes 393224 | tf_op jit(solution)/shard_map/ppermute | solution.py:426
  118.7 7.4 %collective-permute-done.29.refs_3_ = f32[256,128]{1,0:T(8,128)S(1)} collective-permute-done((f32[256,128]{1,0:T(8,128)S(1)}, f32[256,128]{1,0:T(8,128)S(1)}, u32[]{:S(2)}, u32[]{:S(2)}) %collective-permute-start.29) | collective-permute-done | bytes 131104 | tf_op jit(solution)/shard_map/ppermute | solution.py:426
  127.2 2.9 %collective-permute-start.33 = (f32[264,128]{1,0:T(8,128)S(1)}, f32[264,128]{1,0:T(8,128)S(1)}, u32[]{:S(2)}, u32[]{:S(2)}) collective-permute-start(f32[264,128]{1,0:T(8,128)S(1)} %get-tuple-element.126.refs_2_.refs_5_.refs_14_), channel_id=1, source_target_pairs={{0,12},{4,8},{8,4},{12,0},{1,13},{5,9},{9,5},{13,1},{2,14},{6,10},... | collective-permute-start | bytes 405512 | tf_op jit(solution)/shard_map/ppermute | solution.py:426
  130.1 1.9 collective-permute-start.32
  132.5 1.6 collective-permute-done.33.refs_5_
  134.2 4.3 %collective-permute-done.32.refs_4_ = f32[264,128]{1,0:T(8,128)S(1)} collective-permute-done((f32[264,128]{1,0:T(8,128)S(1)}, f32[264,128]{1,0:T(8,128)S(1)}, u32[]{:S(2)}, u32[]{:S(2)}) %collective-permute-start.32) | collective-permute-done | bytes 135200 | tf_op jit(solution)/shard_map/ppermute | solution.py:426
  138.4 2.9 %shard_map.145 = (f32[392,128]{1,0:T(8,128)S(1)}, f32[256,128]{1,0:T(8,128)S(1)}) custom-call(s32[2]{0:T(128)S(1)} %pad_add_fusion.refs_0_, s32[4]{0:T(128)S(1)} %pad_add_fusion.2.refs_1_, f32[264,128]{1,0:T(8,128)S(1)} %get-tuple-element.126.refs_2_.refs_5_.refs_14_, f32[264,128]{1,0:T(8,128)S(1)} %collective-permute-done.31.refs_3_, ...), custom_call_target="tpu_custom_call" | custom-call | flops 805306368 | bytes 7356416 | tf_op jit(solution)/shard_map/pallas_call | solution.py:34
  141.3 1.5 collective-permute-start.34
  142.8 4.3 %collective-permute-done.34.refs_3_ = f32[392,128]{1,0:T(8,128)S(1)} collective-permute-done((f32[392,128]{1,0:T(8,128)S(1)}, f32[392,128]{1,0:T(8,128)S(1)}, u32[]{:S(2)}, u32[]{:S(2)}) %collective-permute-start.34) | collective-permute-done | bytes 200736 | tf_op jit(solution)/shard_map/ppermute | solution.py:419
  147.1 2.5 %shard_map.146 = (f32[264,128]{1,0:T(8,128)S(1)}, f32[264,128]{1,0:T(8,128)S(1)}, f32[264,128]{1,0:T(8,128)S(1)}, f32[264,128]{1,0:T(8,128)S(1)}, f32[384,128]{1,0:T(8,128)S(1)}, /*index=5*/f32[8,128]{1,0:T(8,128)S(1)}) custom-call(s32[2]{0:T(128)S(1)} %pad_add_fusion.refs_0_, s32[4]{0:T(128)S(1)} %pad_add_fusion.2.refs_1_, ...), custom_call_target="tpu_custom_call" | custom-call | flops 805306368 | bytes 6823936 | tf_op jit(solution)/shard_map/pallas_call | solution.py:34
  149.8 3.4 %collective-permute-start.36 = (f32[264,128]{1,0:T(8,128)S(1)}, f32[264,128]{1,0:T(8,128)S(1)}, u32[]{:S(2)}, u32[]{:S(2)}) collective-permute-start(f32[264,128]{1,0:T(8,128)S(1)} %get-tuple-element.131), channel_id=1, source_target_pairs={{0,8},{4,12},{8,0},{12,4},{1,9},{5,13},{9,1},{13,5},{2,10},{6,14},... | collective-permute-start | bytes 405512 | tf_op jit(solution)/shard_map/ppermute | solution.py:426
  154.1 4.8 %collective-permute-done.35.refs_1_ = f32[264,128]{1,0:T(8,128)S(1)} collective-permute-done((f32[264,128]{1,0:T(8,128)S(1)}, f32[264,128]{1,0:T(8,128)S(1)}, u32[]{:S(2)}, u32[]{:S(2)}) %collective-permute-start.35) | collective-permute-done | bytes 135200 | tf_op jit(solution)/shard_map/ppermute | solution.py:426
  158.8 2.8 %collective-permute-done.36.refs_2_ = f32[264,128]{1,0:T(8,128)S(1)} collective-permute-done((f32[264,128]{1,0:T(8,128)S(1)}, f32[264,128]{1,0:T(8,128)S(1)}, u32[]{:S(2)}, u32[]{:S(2)}) %collective-permute-start.36) | collective-permute-done | bytes 135200 | tf_op jit(solution)/shard_map/ppermute | solution.py:426
  161.7 2.8 %collective-permute-start.40 = (f32[264,128]{1,0:T(8,128)S(1)}, f32[264,128]{1,0:T(8,128)S(1)}, u32[]{:S(2)}, u32[]{:S(2)}) collective-permute-start(f32[264,128]{1,0:T(8,128)S(1)} %get-tuple-element.135.refs_2_.refs_15_), channel_id=1, source_target_pairs={{0,12},{4,8},{8,4},{12,0},{1,13},{5,9},{9,5},{13,1},{2,14},{6,10},... | collective-permute-start | bytes 405512 | tf_op jit(solution)/shard_map/ppermute | solution.py:426
  164.6 1.0 collective-permute-start.39
  166.2 2.5 %collective-permute-done.40.refs_5_ = f32[264,128]{1,0:T(8,128)S(1)} collective-permute-done((f32[264,128]{1,0:T(8,128)S(1)}, f32[264,128]{1,0:T(8,128)S(1)}, u32[]{:S(2)}, u32[]{:S(2)}) %collective-permute-start.40) | collective-permute-done | bytes 135200 | tf_op jit(solution)/shard_map/ppermute | solution.py:426
  168.7 4.3 %collective-permute-done.39.refs_4_ = f32[264,128]{1,0:T(8,128)S(1)} collective-permute-done((f32[264,128]{1,0:T(8,128)S(1)}, f32[264,128]{1,0:T(8,128)S(1)}, u32[]{:S(2)}, u32[]{:S(2)}) %collective-permute-start.39) | collective-permute-done | bytes 135200 | tf_op jit(solution)/shard_map/ppermute | solution.py:426
  173.0 3.5 %shard_map.148 = (f32[392,128]{1,0:T(8,128)S(1)}, f32[256,128]{1,0:T(8,128)}) custom-call(s32[2]{0:T(128)S(1)} %pad_add_fusion.refs_0_, s32[4]{0:T(128)S(1)} %pad_add_fusion.2.refs_1_, f32[264,128]{1,0:T(8,128)S(1)} %get-tuple-element.135.refs_2_.refs_15_, f32[264,128]{1,0:T(8,128)S(1)} %collective-permute-done.38.refs_3_, ...), custom_call_target="tpu_custom_call" | custom-call | flops 805306368 | bytes 7487488 | tf_op jit(solution)/shard_map/pallas_call | solution.py:34
  176.5 1.4 collective-permute-start.41
  177.9 4.3 %collective-permute-done.41.refs_1_ = f32[392,128]{1,0:T(8,128)S(1)} collective-permute-done((f32[392,128]{1,0:T(8,128)S(1)}, f32[392,128]{1,0:T(8,128)S(1)}, u32[]{:S(2)}, u32[]{:S(2)}) %collective-permute-start.41) | collective-permute-done | bytes 200736 | tf_op jit(solution)/shard_map/ppermute | solution.py:419
  182.4 2.4 %collective-permute-start.44 = (f32[8,128]{1,0:T(8,128)S(1)}, f32[8,128]{1,0:T(8,128)S(1)}, u32[]{:S(2)}, u32[]{:S(2)}) collective-permute-start(f32[8,128]{1,0:T(8,128)S(1)} %get-tuple-element.138.refs_0_), channel_id=1, source_target_pairs={{0,12},{4,8},{8,4},{12,0},{1,13},{5,9},{9,5},{13,1},{2,14},{6,10},... | collective-permute-start | bytes 12296 | tf_op jit(solution)/shard_map/ppermute | solution.py:426
  184.8 1.9 %collective-permute-start.42 = (f32[8,128]{1,0:T(8,128)S(1)}, f32[8,128]{1,0:T(8,128)S(1)}, u32[]{:S(2)}, u32[]{:S(2)}) collective-permute-start(f32[8,128]{1,0:T(8,128)S(1)} %get-tuple-element.138.refs_0_), channel_id=1, source_target_pairs={{0,4},{4,0},{8,12},{12,8},{1,5},{5,1},{9,13},{13,9},{2,6},{6,2},{1... | collective-permute-start | bytes 12296 | tf_op jit(solution)/shard_map/ppermute | solution.py:426
  187.8 1.5 collective-permute-done.43.refs_2_
  189.6 1.9 collective-permute-done.45.refs_2_
  191.5 1.7 shard_map.151
  (83 shorter events, 16.4 us)
Async XLA Ops:
  0.6 23.8 %collective-permute-start.6 = (f32[24,128,128]{2,1,0:T(8,128)}, f32[24,128,128]{2,1,0:T(8,128)S(1)}, u32[]{:S(2)}, u32[]{:S(2)}) collective-permute-start(f32[24,128,128]{2,1,0:T(8,128)} %bitcast.6), channel_id=1, source_target_pairs={{0,1},{1,0},{2,3},{3,2},{4,5},{5,4},{6,7},{7,6},{8,9},{9,8},{10,11... | collective-permute-start | bytes 4718600 | tf_op jit(solution)/shard_map/ppermute | solution.py:416
  1.1 11.1 %collective-permute-start.3 = (f32[256,128]{1,0:T(8,128)}, f32[256,128]{1,0:T(8,128)S(1)}, u32[]{:S(2)}, u32[]{:S(2)}) collective-permute-start(f32[256,128]{1,0:T(8,128)} %refs_1_.3), channel_id=1, source_target_pairs={{0,12},{4,8},{8,4},{12,0},{1,13},{5,9},{9,5},{13,1},{2,14},{6,10},... | collective-permute-start | bytes 393224 | tf_op jit(solution)/shard_map/ppermute | solution.py:426
  5.8 11.9 %collective-permute-start.2 = (f32[256,128]{1,0:T(8,128)}, f32[256,128]{1,0:T(8,128)S(1)}, u32[]{:S(2)}, u32[]{:S(2)}) collective-permute-start(f32[256,128]{1,0:T(8,128)} %refs_1_.3), channel_id=1, source_target_pairs={{0,8},{4,12},{8,0},{12,4},{1,9},{5,13},{9,1},{13,5},{2,10},{6,14},... | collective-permute-start | bytes 393224 | tf_op jit(solution)/shard_map/ppermute | solution.py:426
  5.8 11.9 %collective-permute-start.1 = (f32[256,128]{1,0:T(8,128)}, f32[256,128]{1,0:T(8,128)S(1)}, u32[]{:S(2)}, u32[]{:S(2)}) collective-permute-start(f32[256,128]{1,0:T(8,128)} %refs_1_.3), channel_id=1, source_target_pairs={{0,4},{4,0},{8,12},{12,8},{1,5},{5,1},{9,13},{13,9},{2,6},{6,2},{1... | collective-permute-start | bytes 393224 | tf_op jit(solution)/shard_map/ppermute | solution.py:426
  7.3 1.4 copy-start
  8.7 0.9 copy-start.6
  9.7 0.7 copy-start.9
  10.3 7.4 %copy-start.1 = (f32[256,128]{1,0:T(8,128)S(1)}, f32[256,128]{1,0:T(8,128)}, u32[]{:S(2)}) copy-start(f32[256,128]{1,0:T(8,128)} %refs_1_.3) | copy-start | bytes 393220
  17.7 1.9 %copy-start.7 = (f32[1,4,128,128]{3,2,1,0:T(8,128)S(1)}, f32[1,4,128,128]{3,2,1,0:T(8,128)}, u32[]{:S(2)}) copy-start(f32[1,4,128,128]{3,2,1,0:T(8,128)} %param.20) | copy-start | bytes 786436
  17.7 5.2 %copy-start.10 = (s32[1,1,2]{2,1,0:T(1,128)S(1)}, s32[1,1,2]{2,1,0:T(1,128)}, u32[]{:S(2)}) copy-start(s32[1,1,2]{2,1,0:T(1,128)} %param.21) | copy-start | bytes 28
  17.7 5.2 %copy-start.2 = (f32[768,128]{1,0:T(8,128)S(1)}, f32[768,128]{1,0:T(8,128)}, u32[]{:S(2)}) copy-start(f32[768,128]{1,0:T(8,128)} %refs_1_.2) | copy-start | bytes 1179652
  17.8 5.2 %copy-start.3 = (f32[768,128]{1,0:T(8,128)S(1)}, f32[768,128]{1,0:T(8,128)}, u32[]{:S(2)}) copy-start(f32[768,128]{1,0:T(8,128)} %refs_2_.3) | copy-start | bytes 1179652
  17.8 5.2 %copy-start.4 = (f32[768,128]{1,0:T(8,128)S(1)}, f32[768,128]{1,0:T(8,128)}, u32[]{:S(2)}) copy-start(f32[768,128]{1,0:T(8,128)} %refs_3_.2) | copy-start | bytes 1179652
  17.8 5.2 %copy-start.5 = (f32[768,128]{1,0:T(8,128)S(1)}, f32[768,128]{1,0:T(8,128)}, u32[]{:S(2)}) copy-start(f32[768,128]{1,0:T(8,128)} %refs_4_.1) | copy-start | bytes 1179652
  19.6 1.7 collective-permute-start.4
  19.7 4.8 %collective-permute-start.7 = (f32[4,128,128]{2,1,0:T(8,128)S(1)}, f32[4,128,128]{2,1,0:T(8,128)S(1)}, u32[]{:S(2)}, u32[]{:S(2)}) collective-permute-start(f32[4,128,128]{2,1,0:T(8,128)S(1)} %bitcast.9), channel_id=1, source_target_pairs={{0,1},{1,0},{2,3},{3,2},{4,5},{5,4},{6,7},{7,6},{8,9},{9,8},{10,11... | collective-permute-start | bytes 786440 | tf_op jit(solution)/shard_map/ppermute | solution.py:416
  21.3 7.0 %collective-permute-start.5 = (f32[384,128]{1,0:T(8,128)S(1)}, f32[384,128]{1,0:T(8,128)S(1)}, u32[]{:S(2)}, u32[]{:S(2)}) collective-permute-start(f32[384,128]{1,0:T(8,128)S(1)} %get-tuple-element.80.refs_0_.refs_2_), channel_id=1, source_target_pairs={{0,2},{1,3},{2,0},{3,1},{4,6},{5,7},{6,4},{7,5},{8,10},{9,11},{10,... | collective-permute-start | bytes 589832 | tf_op jit(solution)/shard_map/ppermute | solution.py:419
  23.0 1.4 collective-permute-start
  28.3 7.0 %copy-start.11 = (f32[256]{0:T(256)S(1)}, f32[256]{0:T(256)}, u32[]{:S(2)}) copy-start(f32[256]{0:T(256)} %param.13) | copy-start | bytes 3076
  28.3 7.0 %copy-start.8 = (f32[256,128]{1,0:T(8,128)S(1)}, f32[256,128]{1,0:T(8,128)}, u32[]{:S(2)}) copy-start(f32[256,128]{1,0:T(8,128)} %refs_3_.3) | copy-start | bytes 393220
  30.9 7.7 %collective-permute-start.8 = (f32[272,128]{1,0:T(8,128)S(1)}, f32[272,128]{1,0:T(8,128)S(1)}, u32[]{:S(2)}, u32[]{:S(2)}) collective-permute-start(f32[272,128]{1,0:T(8,128)S(1)} %get-tuple-element.91), channel_id=1, source_target_pairs={{0,4},{4,0},{8,12},{12,8},{1,5},{5,1},{9,13},{13,9},{2,6},{6,2},{1... | collective-permute-start | bytes 417800 | tf_op jit(solution)/shard_map/ppermute | solution.py:426
  31.0 13.4 %collective-permute-start.9 = (f32[272,128]{1,0:T(8,128)S(1)}, f32[272,128]{1,0:T(8,128)S(1)}, u32[]{:S(2)}, u32[]{:S(2)}) collective-permute-start(f32[272,128]{1,0:T(8,128)S(1)} %get-tuple-element.92), channel_id=1, source_target_pairs={{0,8},{4,12},{8,0},{12,4},{1,9},{5,13},{9,1},{13,5},{2,10},{6,14},... | collective-permute-start | bytes 417800 | tf_op jit(solution)/shard_map/ppermute | solution.py:426
  34.0 10.4 %collective-permute-start.10 = (f32[272,128]{1,0:T(8,128)S(1)}, f32[272,128]{1,0:T(8,128)S(1)}, u32[]{:S(2)}, u32[]{:S(2)}) collective-permute-start(f32[272,128]{1,0:T(8,128)S(1)} %get-tuple-element.93), channel_id=1, source_target_pairs={{0,12},{4,8},{8,4},{12,0},{1,13},{5,9},{9,5},{13,1},{2,14},{6,10},... | collective-permute-start | bytes 417800 | tf_op jit(solution)/shard_map/ppermute | solution.py:426
  35.4 1.1 collective-permute-start.13
  35.4 1.6 collective-permute-start.12
  36.5 1.3 collective-permute-start.11
  45.3 8.3 %collective-permute-start.16 = (f32[264,128]{1,0:T(8,128)S(1)}, f32[264,128]{1,0:T(8,128)S(1)}, u32[]{:S(2)}, u32[]{:S(2)}) collective-permute-start(f32[264,128]{1,0:T(8,128)S(1)} %get-tuple-element.96.refs_2_.refs_5_.refs_16_), channel_id=1, source_target_pairs={{0,12},{4,8},{8,4},{12,0},{1,13},{5,9},{9,5},{13,1},{2,14},{6,10},... | collective-permute-start | bytes 405512 | tf_op jit(solution)/shard_map/ppermute | solution.py:426
  47.8 10.6 %collective-permute-start.15 = (f32[264,128]{1,0:T(8,128)S(1)}, f32[264,128]{1,0:T(8,128)S(1)}, u32[]{:S(2)}, u32[]{:S(2)}) collective-permute-start(f32[264,128]{1,0:T(8,128)S(1)} %get-tuple-element.96.refs_2_.refs_5_.refs_16_), channel_id=1, source_target_pairs={{0,8},{4,12},{8,0},{12,4},{1,9},{5,13},{9,1},{13,5},{2,10},{6,14},... | collective-permute-start | bytes 405512 | tf_op jit(solution)/shard_map/ppermute | solution.py:426
  50.0 8.4 %collective-permute-start.14 = (f32[264,128]{1,0:T(8,128)S(1)}, f32[264,128]{1,0:T(8,128)S(1)}, u32[]{:S(2)}, u32[]{:S(2)}) collective-permute-start(f32[264,128]{1,0:T(8,128)S(1)} %get-tuple-element.96.refs_2_.refs_5_.refs_16_), channel_id=1, source_target_pairs={{0,4},{4,0},{8,12},{12,8},{1,5},{5,1},{9,13},{13,9},{2,6},{6,2},{1... | collective-permute-start | bytes 405512 | tf_op jit(solution)/shard_map/ppermute | solution.py:426
  61.2 5.8 %collective-permute-start.17 = (f32[392,128]{1,0:T(8,128)S(1)}, f32[392,128]{1,0:T(8,128)S(1)}, u32[]{:S(2)}, u32[]{:S(2)}) collective-permute-start(f32[392,128]{1,0:T(8,128)S(1)} %get-tuple-element.101.refs_2_), channel_id=1, source_target_pairs={{0,2},{1,3},{2,0},{3,1},{4,6},{5,7},{6,4},{7,5},{8,10},{9,11},{10,... | collective-permute-start | bytes 602120 | tf_op jit(solution)/shard_map/ppermute | solution.py:419
  69.5 7.1 %collective-permute-start.18 = (f32[264,128]{1,0:T(8,128)S(1)}, f32[264,128]{1,0:T(8,128)S(1)}, u32[]{:S(2)}, u32[]{:S(2)}) collective-permute-start(f32[264,128]{1,0:T(8,128)S(1)} %get-tuple-element.104), channel_id=1, source_target_pairs={{0,4},{4,0},{8,12},{12,8},{1,5},{5,1},{9,13},{13,9},{2,6},{6,2},{1... | collective-permute-start | bytes 405512 | tf_op jit(solution)/shard_map/ppermute | solution.py:426
  69.6 10.7 %collective-permute-start.19 = (f32[264,128]{1,0:T(8,128)S(1)}, f32[264,128]{1,0:T(8,128)S(1)}, u32[]{:S(2)}, u32[]{:S(2)}) collective-permute-start(f32[264,128]{1,0:T(8,128)S(1)} %get-tuple-element.105), channel_id=1, source_target_pairs={{0,8},{4,12},{8,0},{12,4},{1,9},{5,13},{9,1},{13,5},{2,10},{6,14},... | collective-permute-start | bytes 405512 | tf_op jit(solution)/shard_map/ppermute | solution.py:426
  72.6 7.7 %collective-permute-start.20 = (f32[264,128]{1,0:T(8,128)S(1)}, f32[264,128]{1,0:T(8,128)S(1)}, u32[]{:S(2)}, u32[]{:S(2)}) collective-permute-start(f32[264,128]{1,0:T(8,128)S(1)} %get-tuple-element.106), channel_id=1, source_target_pairs={{0,12},{4,8},{8,4},{12,0},{1,13},{5,9},{9,5},{13,1},{2,14},{6,10},... | collective-permute-start | bytes 405512 | tf_op jit(solution)/shard_map/ppermute | solution.py:426
  80.4 8.5 %collective-permute-start.23 = (f32[264,128]{1,0:T(8,128)S(1)}, f32[264,128]{1,0:T(8,128)S(1)}, u32[]{:S(2)}, u32[]{:S(2)}) collective-permute-start(f32[264,128]{1,0:T(8,128)S(1)} %get-tuple-element.110.refs_2_.refs_17_), channel_id=1, source_target_pairs={{0,12},{4,8},{8,4},{12,0},{1,13},{5,9},{9,5},{13,1},{2,14},{6,10},... | collective-permute-start | bytes 405512 | tf_op jit(solution)/shard_map/ppermute | solution.py:426
  84.4 8.9 %collective-permute-start.22 = (f32[264,128]{1,0:T(8,128)S(1)}, f32[264,128]{1,0:T(8,128)S(1)}, u32[]{:S(2)}, u32[]{:S(2)}) collective-permute-start(f32[264,128]{1,0:T(8,128)S(1)} %get-tuple-element.110.refs_2_.refs_17_), channel_id=1, source_target_pairs={{0,8},{4,12},{8,0},{12,4},{1,9},{5,13},{9,1},{13,5},{2,10},{6,14},... | collective-permute-start | bytes 405512 | tf_op jit(solution)/shard_map/ppermute | solution.py:426
  87.2 6.1 %collective-permute-start.21 = (f32[264,128]{1,0:T(8,128)S(1)}, f32[264,128]{1,0:T(8,128)S(1)}, u32[]{:S(2)}, u32[]{:S(2)}) collective-permute-start(f32[264,128]{1,0:T(8,128)S(1)} %get-tuple-element.110.refs_2_.refs_17_), channel_id=1, source_target_pairs={{0,4},{4,0},{8,12},{12,8},{1,5},{5,1},{9,13},{13,9},{2,6},{6,2},{1... | collective-permute-start | bytes 405512 | tf_op jit(solution)/shard_map/ppermute | solution.py:426
  96.4 5.8 %collective-permute-start.24 = (f32[392,128]{1,0:T(8,128)S(1)}, f32[392,128]{1,0:T(8,128)S(1)}, u32[]{:S(2)}, u32[]{:S(2)}) collective-permute-start(f32[392,128]{1,0:T(8,128)S(1)} %get-tuple-element.111.refs_0_), channel_id=1, source_target_pairs={{0,2},{1,3},{2,0},{3,1},{4,6},{5,7},{6,4},{7,5},{8,10},{9,11},{10,... | collective-permute-start | bytes 602120 | tf_op jit(solution)/shard_map/ppermute | solution.py:419
  102.3 5.4 %collective-permute-start.27 = (f32[8,128]{1,0:T(8,128)S(1)}, f32[8,128]{1,0:T(8,128)S(1)}, u32[]{:S(2)}, u32[]{:S(2)}) collective-permute-start(f32[8,128]{1,0:T(8,128)S(1)} %get-tuple-element.113.refs_2_), channel_id=1, source_target_pairs={{0,12},{4,8},{8,4},{12,0},{1,13},{5,9},{9,5},{13,1},{2,14},{6,10},... | collective-permute-start | bytes 12296 | tf_op jit(solution)/shard_map/ppermute | solution.py:426
  105.5 4.5 %collective-permute-start.26 = (f32[8,128]{1,0:T(8,128)S(1)}, f32[8,128]{1,0:T(8,128)S(1)}, u32[]{:S(2)}, u32[]{:S(2)}) collective-permute-start(f32[8,128]{1,0:T(8,128)S(1)} %get-tuple-element.113.refs_2_), channel_id=1, source_target_pairs={{0,8},{4,12},{8,0},{12,4},{1,9},{5,13},{9,1},{13,5},{2,10},{6,14},... | collective-permute-start | bytes 12296 | tf_op jit(solution)/shard_map/ppermute | solution.py:426
  105.5 4.5 %collective-permute-start.25 = (f32[8,128]{1,0:T(8,128)S(1)}, f32[8,128]{1,0:T(8,128)S(1)}, u32[]{:S(2)}, u32[]{:S(2)}) collective-permute-start(f32[8,128]{1,0:T(8,128)S(1)} %get-tuple-element.113.refs_2_), channel_id=1, source_target_pairs={{0,4},{4,0},{8,12},{12,8},{1,5},{5,1},{9,13},{13,9},{2,6},{6,2},{1... | collective-permute-start | bytes 12296 | tf_op jit(solution)/shard_map/ppermute | solution.py:426
  113.3 5.4 %collective-permute-start.28 = (f32[256,128]{1,0:T(8,128)S(1)}, f32[256,128]{1,0:T(8,128)S(1)}, u32[]{:S(2)}, u32[]{:S(2)}) collective-permute-start(f32[256,128]{1,0:T(8,128)S(1)} %get-tuple-element.122), channel_id=1, source_target_pairs={{0,4},{4,0},{8,12},{12,8},{1,5},{5,1},{9,13},{13,9},{2,6},{6,2},{1... | collective-permute-start | bytes 393224 | tf_op jit(solution)/shard_map/ppermute | solution.py:426
  113.6 12.5 %collective-permute-start.29 = (f32[256,128]{1,0:T(8,128)S(1)}, f32[256,128]{1,0:T(8,128)S(1)}, u32[]{:S(2)}, u32[]{:S(2)}) collective-permute-start(f32[256,128]{1,0:T(8,128)S(1)} %get-tuple-element.123), channel_id=1, source_target_pairs={{0,8},{4,12},{8,0},{12,4},{1,9},{5,13},{9,1},{13,5},{2,10},{6,14},... | collective-permute-start | bytes 393224 | tf_op jit(solution)/shard_map/ppermute | solution.py:426
  115.4 11.2 %collective-permute-start.30 = (f32[256,128]{1,0:T(8,128)S(1)}, f32[256,128]{1,0:T(8,128)S(1)}, u32[]{:S(2)}, u32[]{:S(2)}) collective-permute-start(f32[256,128]{1,0:T(8,128)S(1)} %get-tuple-element.124), channel_id=1, source_target_pairs={{0,12},{4,8},{8,4},{12,0},{1,13},{5,9},{9,5},{13,1},{2,14},{6,10},... | collective-permute-start | bytes 393224 | tf_op jit(solution)/shard_map/ppermute | solution.py:426
  127.2 6.9 %collective-permute-start.33 = (f32[264,128]{1,0:T(8,128)S(1)}, f32[264,128]{1,0:T(8,128)S(1)}, u32[]{:S(2)}, u32[]{:S(2)}) collective-permute-start(f32[264,128]{1,0:T(8,128)S(1)} %get-tuple-element.126.refs_2_.refs_5_.refs_14_), channel_id=1, source_target_pairs={{0,12},{4,8},{8,4},{12,0},{1,13},{5,9},{9,5},{13,1},{2,14},{6,10},... | collective-permute-start | bytes 405512 | tf_op jit(solution)/shard_map/ppermute | solution.py:426
  130.1 8.3 %collective-permute-start.32 = (f32[264,128]{1,0:T(8,128)S(1)}, f32[264,128]{1,0:T(8,128)S(1)}, u32[]{:S(2)}, u32[]{:S(2)}) collective-permute-start(f32[264,128]{1,0:T(8,128)S(1)} %get-tuple-element.126.refs_2_.refs_5_.refs_14_), channel_id=1, source_target_pairs={{0,8},{4,12},{8,0},{12,4},{1,9},{5,13},{9,1},{13,5},{2,10},{6,14},... | collective-permute-start | bytes 405512 | tf_op jit(solution)/shard_map/ppermute | solution.py:426
  132.0 6.4 %collective-permute-start.31 = (f32[264,128]{1,0:T(8,128)S(1)}, f32[264,128]{1,0:T(8,128)S(1)}, u32[]{:S(2)}, u32[]{:S(2)}) collective-permute-start(f32[264,128]{1,0:T(8,128)S(1)} %get-tuple-element.126.refs_2_.refs_5_.refs_14_), channel_id=1, source_target_pairs={{0,4},{4,0},{8,12},{12,8},{1,5},{5,1},{9,13},{13,9},{2,6},{6,2},{1... | collective-permute-start | bytes 405512 | tf_op jit(solution)/shard_map/ppermute | solution.py:426
  141.3 5.8 %collective-permute-start.34 = (f32[392,128]{1,0:T(8,128)S(1)}, f32[392,128]{1,0:T(8,128)S(1)}, u32[]{:S(2)}, u32[]{:S(2)}) collective-permute-start(f32[392,128]{1,0:T(8,128)S(1)} %get-tuple-element.127.refs_2_), channel_id=1, source_target_pairs={{0,2},{1,3},{2,0},{3,1},{4,6},{5,7},{6,4},{7,5},{8,10},{9,11},{10,... | collective-permute-start | bytes 602120 | tf_op jit(solution)/shard_map/ppermute | solution.py:419
  149.6 9.2 %collective-permute-start.35 = (f32[264,128]{1,0:T(8,128)S(1)}, f32[264,128]{1,0:T(8,128)S(1)}, u32[]{:S(2)}, u32[]{:S(2)}) collective-permute-start(f32[264,128]{1,0:T(8,128)S(1)} %get-tuple-element.130), channel_id=1, source_target_pairs={{0,4},{4,0},{8,12},{12,8},{1,5},{5,1},{9,13},{13,9},{2,6},{6,2},{1... | collective-permute-start | bytes 405512 | tf_op jit(solution)/shard_map/ppermute | solution.py:426
  149.8 11.9 %collective-permute-start.36 = (f32[264,128]{1,0:T(8,128)S(1)}, f32[264,128]{1,0:T(8,128)S(1)}, u32[]{:S(2)}, u32[]{:S(2)}) collective-permute-start(f32[264,128]{1,0:T(8,128)S(1)} %get-tuple-element.131), channel_id=1, source_target_pairs={{0,8},{4,12},{8,0},{12,4},{1,9},{5,13},{9,1},{13,5},{2,10},{6,14},... | collective-permute-start | bytes 405512 | tf_op jit(solution)/shard_map/ppermute | solution.py:426
  153.1 8.5 %collective-permute-start.37 = (f32[264,128]{1,0:T(8,128)S(1)}, f32[264,128]{1,0:T(8,128)S(1)}, u32[]{:S(2)}, u32[]{:S(2)}) collective-permute-start(f32[264,128]{1,0:T(8,128)S(1)} %get-tuple-element.132), channel_id=1, source_target_pairs={{0,12},{4,8},{8,4},{12,0},{1,13},{5,9},{9,5},{13,1},{2,14},{6,10},... | collective-permute-start | bytes 405512 | tf_op jit(solution)/shard_map/ppermute | solution.py:426
  161.7 7.0 %collective-permute-start.40 = (f32[264,128]{1,0:T(8,128)S(1)}, f32[264,128]{1,0:T(8,128)S(1)}, u32[]{:S(2)}, u32[]{:S(2)}) collective-permute-start(f32[264,128]{1,0:T(8,128)S(1)} %get-tuple-element.135.refs_2_.refs_15_), channel_id=1, source_target_pairs={{0,12},{4,8},{8,4},{12,0},{1,13},{5,9},{9,5},{13,1},{2,14},{6,10},... | collective-permute-start | bytes 405512 | tf_op jit(solution)/shard_map/ppermute | solution.py:426
  164.6 8.4 %collective-permute-start.39 = (f32[264,128]{1,0:T(8,128)S(1)}, f32[264,128]{1,0:T(8,128)S(1)}, u32[]{:S(2)}, u32[]{:S(2)}) collective-permute-start(f32[264,128]{1,0:T(8,128)S(1)} %get-tuple-element.135.refs_2_.refs_15_), channel_id=1, source_target_pairs={{0,8},{4,12},{8,0},{12,4},{1,9},{5,13},{9,1},{13,5},{2,10},{6,14},... | collective-permute-start | bytes 405512 | tf_op jit(solution)/shard_map/ppermute | solution.py:426
  165.6 7.4 %collective-permute-start.38 = (f32[264,128]{1,0:T(8,128)S(1)}, f32[264,128]{1,0:T(8,128)S(1)}, u32[]{:S(2)}, u32[]{:S(2)}) collective-permute-start(f32[264,128]{1,0:T(8,128)S(1)} %get-tuple-element.135.refs_2_.refs_15_), channel_id=1, source_target_pairs={{0,4},{4,0},{8,12},{12,8},{1,5},{5,1},{9,13},{13,9},{2,6},{6,2},{1... | collective-permute-start | bytes 405512 | tf_op jit(solution)/shard_map/ppermute | solution.py:426
  176.5 5.7 %collective-permute-start.41 = (f32[392,128]{1,0:T(8,128)S(1)}, f32[392,128]{1,0:T(8,128)S(1)}, u32[]{:S(2)}, u32[]{:S(2)}) collective-permute-start(f32[392,128]{1,0:T(8,128)S(1)} %get-tuple-element.136.refs_0_), channel_id=1, source_target_pairs={{0,2},{1,3},{2,0},{3,1},{4,6},{5,7},{6,4},{7,5},{8,10},{9,11},{10,... | collective-permute-start | bytes 602120 | tf_op jit(solution)/shard_map/ppermute | solution.py:419
  182.4 5.4 %collective-permute-start.44 = (f32[8,128]{1,0:T(8,128)S(1)}, f32[8,128]{1,0:T(8,128)S(1)}, u32[]{:S(2)}, u32[]{:S(2)}) collective-permute-start(f32[8,128]{1,0:T(8,128)S(1)} %get-tuple-element.138.refs_0_), channel_id=1, source_target_pairs={{0,12},{4,8},{8,4},{12,0},{1,13},{5,9},{9,5},{13,1},{2,14},{6,10},... | collective-permute-start | bytes 12296 | tf_op jit(solution)/shard_map/ppermute | solution.py:426
  184.8 4.5 %collective-permute-start.43 = (f32[8,128]{1,0:T(8,128)S(1)}, f32[8,128]{1,0:T(8,128)S(1)}, u32[]{:S(2)}, u32[]{:S(2)}) collective-permute-start(f32[8,128]{1,0:T(8,128)S(1)} %get-tuple-element.138.refs_0_), channel_id=1, source_target_pairs={{0,8},{4,12},{8,0},{12,4},{1,9},{5,13},{9,1},{13,5},{2,10},{6,14},... | collective-permute-start | bytes 12296 | tf_op jit(solution)/shard_map/ppermute | solution.py:426
  184.8 4.5 %collective-permute-start.42 = (f32[8,128]{1,0:T(8,128)S(1)}, f32[8,128]{1,0:T(8,128)S(1)}, u32[]{:S(2)}, u32[]{:S(2)}) collective-permute-start(f32[8,128]{1,0:T(8,128)S(1)} %get-tuple-element.138.refs_0_), channel_id=1, source_target_pairs={{0,4},{4,0},{8,12},{12,8},{1,5},{5,1},{9,13},{13,9},{2,6},{6,2},{1... | collective-permute-start | bytes 12296 | tf_op jit(solution)/shard_map/ppermute | solution.py:426
  189.5 2.0 %collective-permute-start.45 = (f32[1024,128]{1,0:T(8,128)S(1)}, f32[1024,128]{1,0:T(8,128)S(1)}, u32[]{:S(2)}, u32[]{:S(2)}) collective-permute-start(f32[1024,128]{1,0:T(8,128)S(1)} %shard_map.150.refs_1_), channel_id=1, source_target_pairs={{0,1},{1,0},{2,3},{3,2},{4,5},{5,4},{6,7},{7,6},{8,9},{9,8},{10,11... | collective-permute-start | bytes 1572872 | tf_op jit(solution)/shard_map/ppermute | solution.py:416

commit v8 on v7

--- a/solution.py
+++ b/solution.py
@@ -105,8 +105,8 @@
         dst[...] = jnp.where(low_half(dst.shape), v[:rows], turn(v[rows:]))
 
 
-def prep_kernel(slab, per, cols, pairs, a_in, p_in, a_hi, a_lo, t_hi, t_lo, p_hi, p_lo, diag):
-    for ref in (a_hi, a_lo, t_hi, t_lo):
+def prep_kernel(slab, per, cols, pairs, a_in, p_in, a_both, t_hi, t_lo, p_hi, p_lo, diag):
+    for ref in (t_hi, t_lo):
         ref[...] = jnp.zeros(ref.shape, BF16)
     diag[...] = jnp.zeros(diag.shape, F32)
     for m in range(slab):
@@ -117,8 +117,8 @@
             at = pl.multiple_of(col * BLK, BLK)
             block = a_in[k]
             hi, lo = split_bf16(block)
-            a_hi[rows, pl.ds(at, BLK)] = hi.astype(BF16)
-            a_lo[rows, pl.ds(at, BLK)] = lo.astype(BF16)
+            a_both[2 * m * BLK : (2 * m + 1) * BLK, s * BLK : (s + 1) * BLK] = hi.astype(BF16)
+            a_both[(2 * m + 1) * BLK : (2 * m + 2) * BLK, s * BLK : (s + 1) * BLK] = lo.astype(BF16)
             hi, lo = split_bf16(block.T)
             t_hi[pl.ds(at, BLK), rows] = hi.astype(BF16)
             t_lo[pl.ds(at, BLK), rows] = lo.astype(BF16)
@@ -135,16 +135,31 @@
         diag[pl.ds(pairs[e], 1), :] += jnp.sum(jnp.where(eye, p_in[3 * e], 0.0), axis=0, keepdims=True)
 
 
-def first_kernel(n, own, place, pairs, *refs):
-    msgs, (a_hi, a_lo, p_hi, p_lo, keep, send, wide) = refs[:n], refs[n:]
+def slab_product(slab, cols, a_refs, starts, wide):
+    per = cols.shape[0] // (slab * len(a_refs))
+    sums = []
+    for m in range(slab):
+        total = None
+        for t, a_ref in enumerate(a_refs):
+            blocks = []
+            for s in range(per):
+                at = starts[t] + cols[(t * slab + m) * per + s] * BLK
+                blocks.append(wide[pl.ds(pl.multiple_of(at, BLK), BLK), :])
+            part = dot(a_ref[2 * m * BLK : (2 * m + 2) * BLK, :], jnp.concatenate(blocks, axis=0))
+            total = part if total is None else total + part
+        sums.append(total[:BLK] + total[BLK:])
+    return jnp.concatenate(sums, axis=0)
+
+
+def first_kernel(n, own, slab, place, pairs, cols, *refs):
+    msgs, (a_both, p_hi, p_lo, keep, send, wide) = refs[:n], refs[n:]
     core = place[1]
     for k in range(n):
         at = pl.multiple_of(lax.bitwise_xor(place[0], k) * own, own)
         hi, lo = split_bf16(msgs[k][...])
         wide[pl.ds(at, own), 0:LANES] = hi.astype(BF16)
         wide[pl.ds(at, own), LANES:] = lo.astype(BF16)
-    x = wide[...]
-    total = dot(a_hi[...], x) + dot(a_lo[...], x)
+    total = slab_product(slab, cols, [a_both], [0], wide)
     total = total[:, :LANES] + total[:, LANES:]
     rows = total.shape[0] // 2
     keep[0:rows, :] = mix_cores(core, total[:rows], total[rows:])
@@ -165,9 +180,9 @@
     pp[...] = jnp.where(low_half(pp.shape), keep[rows:, :], got[rows:, :])
 
 
-def forward_kernel(n, own, scalars, place, pairs, *refs):
+def forward_kernel(n, own, slab, scalars, place, pairs, cols, *refs):
     msgs, rest = refs[:n], refs[n:]
-    a_mats, p_mats, rest = rest[:4], rest[4:8], rest[8:]
+    a_mats, p_mats, rest = rest[:2], rest[2:6], rest[6:]
     if scalars == 2:
         pp_first, rest = rest[0], rest[1:]
     msg, pp, whole, wide = rest
@@ -180,11 +195,7 @@
         first, second = pair_up(v)
         wide[pl.ds(at, own), :] = first
         wide[pl.ds(pl.multiple_of(span + at, own), own), :] = second
-    total = jnp.zeros((a_mats[0].shape[0], LANES), F32)
-    for t in range(2):
-        x = wide[t * span : (t + 1) * span, :]
-        total = total + (dot(a_mats[2 * t][...], x) + dot(a_mats[2 * t + 1][...], x))
-    total = fold(total)
+    total = fold(slab_product(slab, cols, a_mats, [0, span], wide))
     rows = total.shape[0] // 2
     msg[0:rows, :] = jnp.where(low_half((rows, LANES)), total[:rows], total[rows:])
     parts = []
@@ -418,16 +429,16 @@
     def to_x(v):
         return [v] + [lax.ppermute(v, "col", [(c, c ^ (2 * k)) for c in range(n_col)]) for k in range(1, nx)]
 
-    swaps = [2, 3, 1] if n == 4 else list(range(1, n))
-
-    def to_row(pieces, order=None):
-        got = {0: pieces[0]}
-        for k in order or swaps:
-            got[k] = lax.ppermute(pieces[k], "row", [(i, i ^ k) for i in range(n)])
-        return [got[k] for k in range(n)]
+    ks = range(1, n)
+
+    def over_row(v, k):
+        return lax.ppermute(v, "row", [(i, i ^ k) for i in range(n)])
+
+    def to_row(pieces):
+        return [pieces[0]] + [over_row(pieces[k], k) for k in ks]
 
     def to_all_rows(v):
-        return to_row([v] * n, swaps[::-1])
+        return [v] + [over_row(v, k) for k in ks]
 
     a_mine = a_blocks.reshape(slab * per, BLK, BLK)
     p_mine = p_blocks.reshape(4, BLK, BLK)
@@ -456,7 +467,7 @@
     def prepare(a, p, at_cols, at_pairs, after=None):
         *mats, diag = call(
             functools.partial(prep_kernel, slab, per),
-            [((slab_rows, span), BF16)] * 2
+            [((2 * slab_rows, per * BLK), BF16)]
             + [((span, slab_rows), BF16)] * 2
             + [((2 * BLK, 2 * BLK), BF16)] * 2
             + [((n_range, LANES), F32)],
@@ -465,17 +476,17 @@
             flops=10**8,
             after=after,
         )
-        return mats[0:2], mats[2:4], mats[4:6], diag
+        return mats[0:1], mats[1:3], mats[3:5], diag
 
     prod_flops = 4 * slab_rows * 2 * span * LANES
     total_scratch = [pltpu.VMEM((span, LANES), F32)]
     a_own, t_own, p_own, diag = prepare(a_mine, p_mine, a_cols.reshape(-1), p_pairs.reshape(-1))
     both_shape = ((half_rows + 2 * BLK, LANES), F32)
     keep, send = call(
-        functools.partial(first_kernel, n, own),
+        functools.partial(first_kernel, n, own, slab),
         [both_shape, both_shape],
         [*x_rows, *a_own, *p_own],
-        [place, p_pairs.reshape(-1)],
+        [place, p_pairs.reshape(-1), a_cols.reshape(-1)],
         [pltpu.VMEM((span, 2 * LANES), BF16)],
         flops=prod_flops,
     )
@@ -485,13 +496,14 @@
     )
     a_mats, t_mats, p_mats = [*a_own, *a_far], [*t_own, *t_far], [*p_own, *p_far]
     pairs = jnp.concatenate([p_pairs.reshape(-1), ints_other[count:]])
+    cols = jnp.concatenate([a_cols.reshape(-1), ints_other[:count]])
 
     def forward(msgs, scalars, pp_first=()):
         return call(
-            functools.partial(forward_kernel, n, own, scalars),
+            functools.partial(forward_kernel, n, own, slab, scalars),
             [((half_rows + SC, LANES), F32), pp_shape],
             [*msgs, *a_mats, *p_mats, *pp_first],
-            [place, pairs],
+            [place, pairs, cols],
             total_scratch + [pltpu.VMEM((2 * span, LANES), BF16)],
             flops=prod_flops,
         )

time: 193 us -> 190 us (0.984)
  Pallas kernels: 34.7 us -> 30.3 us
    pallas_call x22, Pallas kernels: 34.7 us -> 30.3 us  [call(): pl.pallas_call(run, out_shape=[jax.ShapeDtypeStruct(s, d) for s, d in out...]
  transfers between devices with their start and end apart: 46 -> 46, of which waited for: 30 -> 30; matrix products, arithmetic and copies ran while one was open for 1% -> 1% of each run, Pallas kernels for 4% -> 3%
where the time goes in v8:
time: 190 us; the launch traced here: 189 us
  waiting for transfers between devices  90.2 us (47%)
  starting transfers between devices  63.4 us (33%)
  Pallas kernels  30.3 us (16%)
  local copies, waits for them, and re-layouts  4.15 us (2%)
    ppermute x33, waiting for transfers between devices, over_row(): return lax.ppermute(v, 'row', [(i, i ^ k) for i in range(n)])  66.3 us
    ppermute x33, starting transfers between devices, over_row(): return lax.ppermute(v, 'row', [(i, i ^ k) for i in range(n)])  54 us
    pallas_call x22, Pallas kernels, call(): pl.pallas_call(run, out_shape=[jax.ShapeDtypeStruct(s, d) for s, d in out...  30.3 us
    ppermute x5, waiting for transfers between devices, to_x(): lax.ppermute(v, 'col', [(c, c ^ 2 * k) for c in range(n_col)])  19.4 us
    ppermute x5, starting transfers between devices, to_x(): lax.ppermute(v, 'col', [(c, c ^ 2 * k) for c in range(n_col)])  7.56 us
    ppermute x8, waiting for transfers between devices, to_core(): return lax.ppermute(v, 'col', [(c, c ^ 1) for c in range(n_col)])  4.49 us
    unnamed x23, local copies, waits for them, and re-layouts  3.82 us
  transfers between devices with their start and end apart: 46, of which 30 were waited for; matrix products, arithmetic and copies ran while one was open for 1% of the time, Pallas kernels for 3%

profile of v8, /device:TPU:0, one launch (start us, length us, event | category | flops | bytes accessed | tf_op | source)
XLA Modules:
  0.0 189.4 jit_solution(6516365362226125639)
XLA Ops:
  1.1 4.7 %collective-permute-start.3 = (f32[256,128]{1,0:T(8,128)}, f32[256,128]{1,0:T(8,128)S(1)}, u32[]{:S(2)}, u32[]{:S(2)}) collective-permute-start(f32[256,128]{1,0:T(8,128)} %refs_1_.3), channel_id=1, source_target_pairs={{0,12},{4,8},{8,4},{12,0},{1,13},{5,9},{9,5},{13,1},{2,14},{6,10},... | collective-permute-start | bytes 393224 | tf_op jit(solution)/shard_map/ppermute | solution.py:435
  7.3 1.4 copy-done
  10.3 1.5 shard_map.130
  11.9 5.8 %collective-permute-done.2.refs_5_ = f32[256,128]{1,0:T(8,128)S(1)} collective-permute-done((f32[256,128]{1,0:T(8,128)}, f32[256,128]{1,0:T(8,128)S(1)}, u32[]{:S(2)}, u32[]{:S(2)}) %collective-permute-start.2) | collective-permute-done | bytes 131104 | tf_op jit(solution)/shard_map/ppermute | solution.py:435
  17.8 1.4 shard_map.131
  19.7 1.1 collective-permute-done.4.refs_1_
  20.9 1.6 collective-permute-start.5
  22.6 1.3 shard_map.133
  24.1 1.4 shard_map.134
  25.5 2.4 %collective-permute-done.5.refs_3_ = f32[384,128]{1,0:T(8,128)S(1)} collective-permute-done((f32[384,128]{1,0:T(8,128)S(1)}, f32[384,128]{1,0:T(8,128)S(1)}, u32[]{:S(2)}, u32[]{:S(2)}) %collective-permute-start.5) | collective-permute-done | bytes 196640 | tf_op jit(solution)/shard_map/ppermute | solution.py:430
  27.9 2.5 %shard_map.135 = (f32[272,128]{1,0:T(8,128)S(1)}, f32[272,128]{1,0:T(8,128)S(1)}, f32[272,128]{1,0:T(8,128)S(1)}, f32[272,128]{1,0:T(8,128)S(1)}, f32[384,128]{1,0:T(8,128)S(1)}) custom-call(s32[2]{0:T(128)S(1)} %pad_add_fusion.refs_0_, s32[4]{0:T(128)S(1)} %pad_add_fusion.2.refs_1_, f32[384,128]{1,0:T(8,128)S(1)} %get-tuple-element.77.refs_0_.refs_2_, ...), custom_call_target="tpu_custom_call" | custom-call | flops 805306368 | bytes 7217152 | tf_op jit(solution)/shard_map/pallas_call | solution.py:34
  30.5 3.0 %collective-permute-start.9 = (f32[272,128]{1,0:T(8,128)S(1)}, f32[272,128]{1,0:T(8,128)S(1)}, u32[]{:S(2)}, u32[]{:S(2)}) collective-permute-start(f32[272,128]{1,0:T(8,128)S(1)} %get-tuple-element.89), channel_id=1, source_target_pairs={{0,8},{4,12},{8,0},{12,4},{1,9},{5,13},{9,1},{13,5},{2,10},{6,14},... | collective-permute-start | bytes 417800 | tf_op jit(solution)/shard_map/ppermute | solution.py:435
  33.6 1.3 collective-permute-start.10
  38.2 5.8 %collective-permute-done.9.refs_3_ = f32[272,128]{1,0:T(8,128)S(1)} collective-permute-done((f32[272,128]{1,0:T(8,128)S(1)}, f32[272,128]{1,0:T(8,128)S(1)}, u32[]{:S(2)}, u32[]{:S(2)}) %collective-permute-start.9) | collective-permute-done | bytes 139296 | tf_op jit(solution)/shard_map/ppermute | solution.py:435
  44.9 2.4 %collective-permute-start.16 = (f32[264,128]{1,0:T(8,128)S(1)}, f32[264,128]{1,0:T(8,128)S(1)}, u32[]{:S(2)}, u32[]{:S(2)}) collective-permute-start(f32[264,128]{1,0:T(8,128)S(1)} %get-tuple-element.93.refs_3_.refs_5_.refs_16_), channel_id=1, source_target_pairs={{0,12},{4,8},{8,4},{12,0},{1,13},{5,9},{9,5},{13,1},{2,14},{6,10},... | collective-permute-start | bytes 405512 | tf_op jit(solution)/shard_map/ppermute | solution.py:435
  47.3 2.2 %collective-permute-start.15 = (f32[264,128]{1,0:T(8,128)S(1)}, f32[264,128]{1,0:T(8,128)S(1)}, u32[]{:S(2)}, u32[]{:S(2)}) collective-permute-start(f32[264,128]{1,0:T(8,128)S(1)} %get-tuple-element.93.refs_3_.refs_5_.refs_16_), channel_id=1, source_target_pairs={{0,8},{4,12},{8,0},{12,4},{1,9},{5,13},{9,1},{13,5},{2,10},{6,14},... | collective-permute-start | bytes 405512 | tf_op jit(solution)/shard_map/ppermute | solution.py:435
  50.1 3.1 %collective-permute-done.16.refs_6_ = f32[264,128]{1,0:T(8,128)S(1)} collective-permute-done((f32[264,128]{1,0:T(8,128)S(1)}, f32[264,128]{1,0:T(8,128)S(1)}, u32[]{:S(2)}, u32[]{:S(2)}) %collective-permute-start.16) | collective-permute-done | bytes 135200 | tf_op jit(solution)/shard_map/ppermute | solution.py:435
  53.2 4.7 %collective-permute-done.15.refs_5_ = f32[264,128]{1,0:T(8,128)S(1)} collective-permute-done((f32[264,128]{1,0:T(8,128)S(1)}, f32[264,128]{1,0:T(8,128)S(1)}, u32[]{:S(2)}, u32[]{:S(2)}) %collective-permute-start.15) | collective-permute-done | bytes 135200 | tf_op jit(solution)/shard_map/ppermute | solution.py:435
  57.9 2.0 %shard_map.138 = (f32[392,128]{1,0:T(8,128)S(1)}, f32[256,128]{1,0:T(8,128)S(1)}) custom-call(s32[2]{0:T(128)S(1)} %pad_add_fusion.refs_0_, s32[4]{0:T(128)S(1)} %pad_add_fusion.2.refs_1_, s32[48]{0:T(128)S(1)} %pad_add_fusion.3.refs_2_, f32[264,128]{1,0:T(8,128)S(1)} %get-tuple-element.93.refs_3_.refs_5_.refs_16_, ...), custom_call_target="tpu_custom_call" | custom-call | flops 805306368 | bytes 4210688 | tf_op jit(solution)/shard_map/pallas_call | solution.py:34
  59.9 1.5 collective-permute-start.17
  61.4 4.2 %collective-permute-done.17.refs_3_ = f32[392,128]{1,0:T(8,128)S(1)} collective-permute-done((f32[392,128]{1,0:T(8,128)S(1)}, f32[392,128]{1,0:T(8,128)S(1)}, u32[]{:S(2)}, u32[]{:S(2)}) %collective-permute-start.17) | collective-permute-done | bytes 200736 | tf_op jit(solution)/shard_map/ppermute | solution.py:430
  65.7 2.5 %shard_map.139 = (f32[264,128]{1,0:T(8,128)S(1)}, f32[264,128]{1,0:T(8,128)S(1)}, f32[264,128]{1,0:T(8,128)S(1)}, f32[264,128]{1,0:T(8,128)S(1)}, f32[384,128]{1,0:T(8,128)S(1)}, /*index=5*/f32[8,128]{1,0:T(8,128)S(1)}) custom-call(s32[2]{0:T(128)S(1)} %pad_add_fusion.refs_0_, s32[4]{0:T(128)S(1)} %pad_add_fusion.2.refs_1_, ...), custom_call_target="tpu_custom_call" | custom-call | flops 805306368 | bytes 6823936 | tf_op jit(solution)/shard_map/pallas_call | solution.py:34
  68.3 3.0 %collective-permute-start.19 = (f32[264,128]{1,0:T(8,128)S(1)}, f32[264,128]{1,0:T(8,128)S(1)}, u32[]{:S(2)}, u32[]{:S(2)}) collective-permute-start(f32[264,128]{1,0:T(8,128)S(1)} %get-tuple-element.101), channel_id=1, source_target_pairs={{0,8},{4,12},{8,0},{12,4},{1,9},{5,13},{9,1},{13,5},{2,10},{6,14},... | collective-permute-start | bytes 405512 | tf_op jit(solution)/shard_map/ppermute | solution.py:435
  71.3 1.3 collective-permute-start.20
  72.7 2.6 %collective-permute-done.18.refs_1_ = f32[264,128]{1,0:T(8,128)S(1)} collective-permute-done((f32[264,128]{1,0:T(8,128)S(1)}, f32[264,128]{1,0:T(8,128)S(1)}, u32[]{:S(2)}, u32[]{:S(2)}) %collective-permute-start.18) | collective-permute-done | bytes 135200 | tf_op jit(solution)/shard_map/ppermute | solution.py:435
  75.3 3.7 %collective-permute-done.19.refs_2_ = f32[264,128]{1,0:T(8,128)S(1)} collective-permute-done((f32[264,128]{1,0:T(8,128)S(1)}, f32[264,128]{1,0:T(8,128)S(1)}, u32[]{:S(2)}, u32[]{:S(2)}) %collective-permute-start.19) | collective-permute-done | bytes 135200 | tf_op jit(solution)/shard_map/ppermute | solution.py:435
  79.1 4.0 %collective-permute-start.23 = (f32[264,128]{1,0:T(8,128)S(1)}, f32[264,128]{1,0:T(8,128)S(1)}, u32[]{:S(2)}, u32[]{:S(2)}) collective-permute-start(f32[264,128]{1,0:T(8,128)S(1)} %get-tuple-element.106.refs_3_.refs_17_), channel_id=1, source_target_pairs={{0,12},{4,8},{8,4},{12,0},{1,13},{5,9},{9,5},{13,1},{2,14},{6,10},... | collective-permute-start | bytes 405512 | tf_op jit(solution)/shard_map/ppermute | solution.py:435
  83.1 2.8 %collective-permute-start.22 = (f32[264,128]{1,0:T(8,128)S(1)}, f32[264,128]{1,0:T(8,128)S(1)}, u32[]{:S(2)}, u32[]{:S(2)}) collective-permute-start(f32[264,128]{1,0:T(8,128)S(1)} %get-tuple-element.106.refs_3_.refs_17_), channel_id=1, source_target_pairs={{0,8},{4,12},{8,0},{12,4},{1,9},{5,13},{9,1},{13,5},{2,10},{6,14},... | collective-permute-start | bytes 405512 | tf_op jit(solution)/shard_map/ppermute | solution.py:435
  86.4 1.2 collective-permute-done.23.refs_6_
  87.6 4.4 %collective-permute-done.22.refs_5_ = f32[264,128]{1,0:T(8,128)S(1)} collective-permute-done((f32[264,128]{1,0:T(8,128)S(1)}, f32[264,128]{1,0:T(8,128)S(1)}, u32[]{:S(2)}, u32[]{:S(2)}) %collective-permute-start.22) | collective-permute-done | bytes 135200 | tf_op jit(solution)/shard_map/ppermute | solution.py:435
  92.0 2.0 %shard_map.141 = (f32[392,128]{1,0:T(8,128)S(1)}, f32[256,128]{1,0:T(8,128)S(1)}) custom-call(s32[2]{0:T(128)S(1)} %pad_add_fusion.refs_0_, s32[4]{0:T(128)S(1)} %pad_add_fusion.2.refs_1_, s32[48]{0:T(128)S(1)} %pad_add_fusion.3.refs_2_, f32[264,128]{1,0:T(8,128)S(1)} %get-tuple-element.106.refs_3_.refs_17_, f32[264,128]{1,0:T(8,128)S(1)} %collective-permute-done.21.refs_4_, ...), custom_call_target="tpu_custom_call" | custom-call | flops 805306368 | bytes 4341760 | tf_op jit(solution)/shard_map/pallas_call | solution.py:34
  94.0 1.5 collective-permute-start.24
  95.5 4.3 %collective-permute-done.24.refs_1_ = f32[392,128]{1,0:T(8,128)S(1)} collective-permute-done((f32[392,128]{1,0:T(8,128)S(1)}, f32[392,128]{1,0:T(8,128)S(1)}, u32[]{:S(2)}, u32[]{:S(2)}) %collective-permute-start.24) | collective-permute-done | bytes 200736 | tf_op jit(solution)/shard_map/ppermute | solution.py:430
  100.0 3.2 %collective-permute-start.27 = (f32[8,128]{1,0:T(8,128)S(1)}, f32[8,128]{1,0:T(8,128)S(1)}, u32[]{:S(2)}, u32[]{:S(2)}) collective-permute-start(f32[8,128]{1,0:T(8,128)S(1)} %get-tuple-element.109.refs_2_), channel_id=1, source_target_pairs={{0,12},{4,8},{8,4},{12,0},{1,13},{5,9},{9,5},{13,1},{2,14},{6,10},... | collective-permute-start | bytes 12296 | tf_op jit(solution)/shard_map/ppermute | solution.py:435
  103.2 1.2 collective-permute-start.25
  105.4 2.4 %collective-permute-done.26.refs_4_ = f32[8,128]{1,0:T(8,128)S(1)} collective-permute-done((f32[8,128]{1,0:T(8,128)S(1)}, f32[8,128]{1,0:T(8,128)S(1)}, u32[]{:S(2)}, u32[]{:S(2)}) %collective-permute-start.26) | collective-permute-done | bytes 4128 | tf_op jit(solution)/shard_map/ppermute | solution.py:435
  107.7 3.4 %shard_map.143 = (f32[256,128]{1,0:T(8,128)S(1)}, f32[256,128]{1,0:T(8,128)S(1)}, f32[256,128]{1,0:T(8,128)S(1)}, f32[256,128]{1,0:T(8,128)S(1)}, f32[256,128]{1...) custom-call(s32[2]{0:T(128)S(1)} %pad_add_fusion.refs_0_, ...), custom_call_target="tpu_custom_call" | custom-call | flops 805306368 | bytes 8486912 | tf_op jit(solution)/shard_map/pallas_call | solution.py:34
  111.4 1.8 collective-permute-start.29
  113.3 2.3 %collective-permute-start.30 = (f32[256,128]{1,0:T(8,128)S(1)}, f32[256,128]{1,0:T(8,128)S(1)}, u32[]{:S(2)}, u32[]{:S(2)}) collective-permute-start(f32[256,128]{1,0:T(8,128)S(1)} %get-tuple-element.120), channel_id=1, source_target_pairs={{0,12},{4,8},{8,4},{12,0},{1,13},{5,9},{9,5},{13,1},{2,14},{6,10},... | collective-permute-start | bytes 393224 | tf_op jit(solution)/shard_map/ppermute | solution.py:435
  115.6 1.2 collective-permute-done.28.refs_2_
  116.7 7.0 %collective-permute-done.29.refs_3_ = f32[256,128]{1,0:T(8,128)S(1)} collective-permute-done((f32[256,128]{1,0:T(8,128)S(1)}, f32[256,128]{1,0:T(8,128)S(1)}, u32[]{:S(2)}, u32[]{:S(2)}) %collective-permute-start.29) | collective-permute-done | bytes 131104 | tf_op jit(solution)/shard_map/ppermute | solution.py:435
  125.1 2.9 %collective-permute-start.33 = (f32[264,128]{1,0:T(8,128)S(1)}, f32[264,128]{1,0:T(8,128)S(1)}, u32[]{:S(2)}, u32[]{:S(2)}) collective-permute-start(f32[264,128]{1,0:T(8,128)S(1)} %get-tuple-element.122.refs_3_.refs_5_.refs_14_), channel_id=1, source_target_pairs={{0,12},{4,8},{8,4},{12,0},{1,13},{5,9},{9,5},{13,1},{2,14},{6,10},... | collective-permute-start | bytes 405512 | tf_op jit(solution)/shard_map/ppermute | solution.py:435
  128.0 1.9 %collective-permute-start.32 = (f32[264,128]{1,0:T(8,128)S(1)}, f32[264,128]{1,0:T(8,128)S(1)}, u32[]{:S(2)}, u32[]{:S(2)}) collective-permute-start(f32[264,128]{1,0:T(8,128)S(1)} %get-tuple-element.122.refs_3_.refs_5_.refs_14_), channel_id=1, source_target_pairs={{0,8},{4,12},{8,0},{12,4},{1,9},{5,13},{9,1},{13,5},{2,10},{6,14},... | collective-permute-start | bytes 405512 | tf_op jit(solution)/shard_map/ppermute | solution.py:435
  130.4 1.6 collective-permute-done.33.refs_6_
  132.0 4.3 %collective-permute-done.32.refs_5_ = f32[264,128]{1,0:T(8,128)S(1)} collective-permute-done((f32[264,128]{1,0:T(8,128)S(1)}, f32[264,128]{1,0:T(8,128)S(1)}, u32[]{:S(2)}, u32[]{:S(2)}) %collective-permute-start.32) | collective-permute-done | bytes 135200 | tf_op jit(solution)/shard_map/ppermute | solution.py:435
  136.3 2.0 %shard_map.145 = (f32[392,128]{1,0:T(8,128)S(1)}, f32[256,128]{1,0:T(8,128)S(1)}) custom-call(s32[2]{0:T(128)S(1)} %pad_add_fusion.refs_0_, s32[4]{0:T(128)S(1)} %pad_add_fusion.2.refs_1_, s32[48]{0:T(128)S(1)} %pad_add_fusion.3.refs_2_, f32[264,128]{1,0:T(8,128)S(1)} %get-tuple-element.122.refs_3_.refs_5_.refs_14_, ...), custom_call_target="tpu_custom_call" | custom-call | flops 805306368 | bytes 4210688 | tf_op jit(solution)/shard_map/pallas_call | solution.py:34
  138.3 1.5 collective-permute-start.34
  139.8 4.3 %collective-permute-done.34.refs_3_ = f32[392,128]{1,0:T(8,128)S(1)} collective-permute-done((f32[392,128]{1,0:T(8,128)S(1)}, f32[392,128]{1,0:T(8,128)S(1)}, u32[]{:S(2)}, u32[]{:S(2)}) %collective-permute-start.34) | collective-permute-done | bytes 200736 | tf_op jit(solution)/shard_map/ppermute | solution.py:430
  144.1 2.5 %shard_map.146 = (f32[264,128]{1,0:T(8,128)S(1)}, f32[264,128]{1,0:T(8,128)S(1)}, f32[264,128]{1,0:T(8,128)S(1)}, f32[264,128]{1,0:T(8,128)S(1)}, f32[384,128]{1,0:T(8,128)S(1)}, /*index=5*/f32[8,128]{1,0:T(8,128)S(1)}) custom-call(s32[2]{0:T(128)S(1)} %pad_add_fusion.refs_0_, s32[4]{0:T(128)S(1)} %pad_add_fusion.2.refs_1_, ...), custom_call_target="tpu_custom_call" | custom-call | flops 805306368 | bytes 6823936 | tf_op jit(solution)/shard_map/pallas_call | solution.py:34
  146.8 3.4 %collective-permute-start.36 = (f32[264,128]{1,0:T(8,128)S(1)}, f32[264,128]{1,0:T(8,128)S(1)}, u32[]{:S(2)}, u32[]{:S(2)}) collective-permute-start(f32[264,128]{1,0:T(8,128)S(1)} %get-tuple-element.127), channel_id=1, source_target_pairs={{0,8},{4,12},{8,0},{12,4},{1,9},{5,13},{9,1},{13,5},{2,10},{6,14},... | collective-permute-start | bytes 405512 | tf_op jit(solution)/shard_map/ppermute | solution.py:435
  151.1 4.8 %collective-permute-done.35.refs_1_ = f32[264,128]{1,0:T(8,128)S(1)} collective-permute-done((f32[264,128]{1,0:T(8,128)S(1)}, f32[264,128]{1,0:T(8,128)S(1)}, u32[]{:S(2)}, u32[]{:S(2)}) %collective-permute-start.35) | collective-permute-done | bytes 135200 | tf_op jit(solution)/shard_map/ppermute | solution.py:435
  155.9 2.8 %collective-permute-done.36.refs_2_ = f32[264,128]{1,0:T(8,128)S(1)} collective-permute-done((f32[264,128]{1,0:T(8,128)S(1)}, f32[264,128]{1,0:T(8,128)S(1)}, u32[]{:S(2)}, u32[]{:S(2)}) %collective-permute-start.36) | collective-permute-done | bytes 135200 | tf_op jit(solution)/shard_map/ppermute | solution.py:435
  158.8 2.8 %collective-permute-start.40 = (f32[264,128]{1,0:T(8,128)S(1)}, f32[264,128]{1,0:T(8,128)S(1)}, u32[]{:S(2)}, u32[]{:S(2)}) collective-permute-start(f32[264,128]{1,0:T(8,128)S(1)} %get-tuple-element.131.refs_3_.refs_15_), channel_id=1, source_target_pairs={{0,12},{4,8},{8,4},{12,0},{1,13},{5,9},{9,5},{13,1},{2,14},{6,10},... | collective-permute-start | bytes 405512 | tf_op jit(solution)/shard_map/ppermute | solution.py:435
  161.6 1.0 collective-permute-start.39
  163.2 2.5 %collective-permute-done.40.refs_6_ = f32[264,128]{1,0:T(8,128)S(1)} collective-permute-done((f32[264,128]{1,0:T(8,128)S(1)}, f32[264,128]{1,0:T(8,128)S(1)}, u32[]{:S(2)}, u32[]{:S(2)}) %collective-permute-start.40) | collective-permute-done | bytes 135200 | tf_op jit(solution)/shard_map/ppermute | solution.py:435
  165.8 4.3 %collective-permute-done.39.refs_5_ = f32[264,128]{1,0:T(8,128)S(1)} collective-permute-done((f32[264,128]{1,0:T(8,128)S(1)}, f32[264,128]{1,0:T(8,128)S(1)}, u32[]{:S(2)}, u32[]{:S(2)}) %collective-permute-start.39) | collective-permute-done | bytes 135200 | tf_op jit(solution)/shard_map/ppermute | solution.py:435
  170.0 2.6 %shard_map.148 = (f32[392,128]{1,0:T(8,128)S(1)}, f32[256,128]{1,0:T(8,128)}) custom-call(s32[2]{0:T(128)S(1)} %pad_add_fusion.refs_0_, s32[4]{0:T(128)S(1)} %pad_add_fusion.2.refs_1_, s32[48]{0:T(128)S(1)} %pad_add_fusion.3.refs_2_, f32[264,128]{1,0:T(8,128)S(1)} %get-tuple-element.131.refs_3_.refs_15_, f32[264,128]{1,0:T(8,128)S(1)} %collective-permute-done.38.refs_4_, ...), custom_call_target="tpu_custom_call" | custom-call | flops 805306368 | bytes 4341760 | tf_op jit(solution)/shard_map/pallas_call | solution.py:34
  172.7 1.5 collective-permute-start.41
  174.1 4.2 %collective-permute-done.41.refs_1_ = f32[392,128]{1,0:T(8,128)S(1)} collective-permute-done((f32[392,128]{1,0:T(8,128)S(1)}, f32[392,128]{1,0:T(8,128)S(1)}, u32[]{:S(2)}, u32[]{:S(2)}) %collective-permute-start.41) | collective-permute-done | bytes 200736 | tf_op jit(solution)/shard_map/ppermute | solution.py:430
  178.6 2.4 %collective-permute-start.44 = (f32[8,128]{1,0:T(8,128)S(1)}, f32[8,128]{1,0:T(8,128)S(1)}, u32[]{:S(2)}, u32[]{:S(2)}) collective-permute-start(f32[8,128]{1,0:T(8,128)S(1)} %get-tuple-element.134.refs_0_), channel_id=1, source_target_pairs={{0,12},{4,8},{8,4},{12,0},{1,13},{5,9},{9,5},{13,1},{2,14},{6,10},... | collective-permute-start | bytes 12296 | tf_op jit(solution)/shard_map/ppermute | solution.py:435
  181.0 1.9 %collective-permute-start.42 = (f32[8,128]{1,0:T(8,128)S(1)}, f32[8,128]{1,0:T(8,128)S(1)}, u32[]{:S(2)}, u32[]{:S(2)}) collective-permute-start(f32[8,128]{1,0:T(8,128)S(1)} %get-tuple-element.134.refs_0_), channel_id=1, source_target_pairs={{0,4},{4,0},{8,12},{12,8},{1,5},{5,1},{9,13},{13,9},{2,6},{6,2},{1... | collective-permute-start | bytes 12296 | tf_op jit(solution)/shard_map/ppermute | solution.py:435
  184.0 1.5 collective-permute-done.43.refs_2_
  185.8 1.9 %collective-permute-done.45.refs_2_ = f32[1024,128]{1,0:T(8,128)S(1)} collective-permute-done((f32[1024,128]{1,0:T(8,128)S(1)}, f32[1024,128]{1,0:T(8,128)S(1)}, u32[]{:S(2)}, u32[]{:S(2)}) %collective-permute-start.45) | collective-permute-done | bytes 524320 | tf_op jit(solution)/shard_map/ppermute | solution.py:427
  187.7 1.7 shard_map.151
  (82 shorter events, 16.6 us)
Async XLA Ops:
  0.6 23.4 %collective-permute-start.6 = (f32[24,128,128]{2,1,0:T(8,128)}, f32[24,128,128]{2,1,0:T(8,128)S(1)}, u32[]{:S(2)}, u32[]{:S(2)}) collective-permute-start(f32[24,128,128]{2,1,0:T(8,128)} %bitcast.6), channel_id=1, source_target_pairs={{0,1},{1,0},{2,3},{3,2},{4,5},{5,4},{6,7},{7,6},{8,9},{9,8},{10,11... | collective-permute-start | bytes 4718600 | tf_op jit(solution)/shard_map/ppermute | solution.py:427
  1.1 10.7 %collective-permute-start.3 = (f32[256,128]{1,0:T(8,128)}, f32[256,128]{1,0:T(8,128)S(1)}, u32[]{:S(2)}, u32[]{:S(2)}) collective-permute-start(f32[256,128]{1,0:T(8,128)} %refs_1_.3), channel_id=1, source_target_pairs={{0,12},{4,8},{8,4},{12,0},{1,13},{5,9},{9,5},{13,1},{2,14},{6,10},... | collective-permute-start | bytes 393224 | tf_op jit(solution)/shard_map/ppermute | solution.py:435
  5.8 11.9 %collective-permute-start.2 = (f32[256,128]{1,0:T(8,128)}, f32[256,128]{1,0:T(8,128)S(1)}, u32[]{:S(2)}, u32[]{:S(2)}) collective-permute-start(f32[256,128]{1,0:T(8,128)} %refs_1_.3), channel_id=1, source_target_pairs={{0,8},{4,12},{8,0},{12,4},{1,9},{5,13},{9,1},{13,5},{2,10},{6,14},... | collective-permute-start | bytes 393224 | tf_op jit(solution)/shard_map/ppermute | solution.py:435
  5.8 11.9 %collective-permute-start.1 = (f32[256,128]{1,0:T(8,128)}, f32[256,128]{1,0:T(8,128)S(1)}, u32[]{:S(2)}, u32[]{:S(2)}) collective-permute-start(f32[256,128]{1,0:T(8,128)} %refs_1_.3), channel_id=1, source_target_pairs={{0,4},{4,0},{8,12},{12,8},{1,5},{5,1},{9,13},{13,9},{2,6},{6,2},{1... | collective-permute-start | bytes 393224 | tf_op jit(solution)/shard_map/ppermute | solution.py:435
  7.3 1.4 copy-start
  8.7 0.9 copy-start.5
  9.7 0.7 copy-start.8
  10.3 7.4 %copy-start.6 = (f32[256,128]{1,0:T(8,128)S(1)}, f32[256,128]{1,0:T(8,128)}, u32[]{:S(2)}) copy-start(f32[256,128]{1,0:T(8,128)} %refs_1_.3) | copy-start | bytes 393220
  17.7 4.7 %copy-start.9 = (s32[1,1,2]{2,1,0:T(1,128)S(1)}, s32[1,1,2]{2,1,0:T(1,128)}, u32[]{:S(2)}) copy-start(s32[1,1,2]{2,1,0:T(1,128)} %param.21) | copy-start | bytes 28
  17.7 4.8 %copy-start.1 = (f32[768,128]{1,0:T(8,128)S(1)}, f32[768,128]{1,0:T(8,128)}, u32[]{:S(2)}) copy-start(f32[768,128]{1,0:T(8,128)} %refs_1_.2) | copy-start | bytes 1179652
  17.7 4.8 %copy-start.2 = (f32[768,128]{1,0:T(8,128)S(1)}, f32[768,128]{1,0:T(8,128)}, u32[]{:S(2)}) copy-start(f32[768,128]{1,0:T(8,128)} %refs_2_.1) | copy-start | bytes 1179652
  17.8 4.8 %copy-start.3 = (f32[768,128]{1,0:T(8,128)S(1)}, f32[768,128]{1,0:T(8,128)}, u32[]{:S(2)}) copy-start(f32[768,128]{1,0:T(8,128)} %refs_3_.4) | copy-start | bytes 1179652
  17.8 4.8 %copy-start.4 = (f32[768,128]{1,0:T(8,128)S(1)}, f32[768,128]{1,0:T(8,128)}, u32[]{:S(2)}) copy-start(f32[768,128]{1,0:T(8,128)} %refs_4_.1) | copy-start | bytes 1179652
  19.2 1.7 collective-permute-start.4
  19.2 4.8 %collective-permute-start.7 = (f32[4,128,128]{2,1,0:T(8,128)S(1)}, f32[4,128,128]{2,1,0:T(8,128)S(1)}, u32[]{:S(2)}, u32[]{:S(2)}) collective-permute-start(f32[4,128,128]{2,1,0:T(8,128)S(1)} %bitcast.9), channel_id=1, source_target_pairs={{0,1},{1,0},{2,3},{3,2},{4,5},{5,4},{6,7},{7,6},{8,9},{9,8},{10,11... | collective-permute-start | bytes 786440 | tf_op jit(solution)/shard_map/ppermute | solution.py:427
  20.9 7.0 %collective-permute-start.5 = (f32[384,128]{1,0:T(8,128)S(1)}, f32[384,128]{1,0:T(8,128)S(1)}, u32[]{:S(2)}, u32[]{:S(2)}) collective-permute-start(f32[384,128]{1,0:T(8,128)S(1)} %get-tuple-element.77.refs_0_.refs_2_), channel_id=1, source_target_pairs={{0,2},{1,3},{2,0},{3,1},{4,6},{5,7},{6,4},{7,5},{8,10},{9,11},{10,... | collective-permute-start | bytes 589832 | tf_op jit(solution)/shard_map/ppermute | solution.py:430
  22.5 1.4 collective-permute-start
  27.9 7.0 %copy-start.10 = (f32[256]{0:T(256)S(1)}, f32[256]{0:T(256)}, u32[]{:S(2)}) copy-start(f32[256]{0:T(256)} %param.13) | copy-start | bytes 3076
  27.9 7.0 %copy-start.7 = (f32[256,128]{1,0:T(8,128)S(1)}, f32[256,128]{1,0:T(8,128)}, u32[]{:S(2)}) copy-start(f32[256,128]{1,0:T(8,128)} %refs_3_.5) | copy-start | bytes 393220
  30.5 7.7 %collective-permute-start.8 = (f32[272,128]{1,0:T(8,128)S(1)}, f32[272,128]{1,0:T(8,128)S(1)}, u32[]{:S(2)}, u32[]{:S(2)}) collective-permute-start(f32[272,128]{1,0:T(8,128)S(1)} %get-tuple-element.88), channel_id=1, source_target_pairs={{0,4},{4,0},{8,12},{12,8},{1,5},{5,1},{9,13},{13,9},{2,6},{6,2},{1... | collective-permute-start | bytes 417800 | tf_op jit(solution)/shard_map/ppermute | solution.py:435
  30.5 13.4 %collective-permute-start.9 = (f32[272,128]{1,0:T(8,128)S(1)}, f32[272,128]{1,0:T(8,128)S(1)}, u32[]{:S(2)}, u32[]{:S(2)}) collective-permute-start(f32[272,128]{1,0:T(8,128)S(1)} %get-tuple-element.89), channel_id=1, source_target_pairs={{0,8},{4,12},{8,0},{12,4},{1,9},{5,13},{9,1},{13,5},{2,10},{6,14},... | collective-permute-start | bytes 417800 | tf_op jit(solution)/shard_map/ppermute | solution.py:435
  33.6 10.4 %collective-permute-start.10 = (f32[272,128]{1,0:T(8,128)S(1)}, f32[272,128]{1,0:T(8,128)S(1)}, u32[]{:S(2)}, u32[]{:S(2)}) collective-permute-start(f32[272,128]{1,0:T(8,128)S(1)} %get-tuple-element.90), channel_id=1, source_target_pairs={{0,12},{4,8},{8,4},{12,0},{1,13},{5,9},{9,5},{13,1},{2,14},{6,10},... | collective-permute-start | bytes 417800 | tf_op jit(solution)/shard_map/ppermute | solution.py:435
  34.9 1.1 collective-permute-start.13
  34.9 1.6 collective-permute-start.12
  36.1 1.3 collective-permute-start.11
  44.9 8.3 %collective-permute-start.16 = (f32[264,128]{1,0:T(8,128)S(1)}, f32[264,128]{1,0:T(8,128)S(1)}, u32[]{:S(2)}, u32[]{:S(2)}) collective-permute-start(f32[264,128]{1,0:T(8,128)S(1)} %get-tuple-element.93.refs_3_.refs_5_.refs_16_), channel_id=1, source_target_pairs={{0,12},{4,8},{8,4},{12,0},{1,13},{5,9},{9,5},{13,1},{2,14},{6,10},... | collective-permute-start | bytes 405512 | tf_op jit(solution)/shard_map/ppermute | solution.py:435
  47.3 10.5 %collective-permute-start.15 = (f32[264,128]{1,0:T(8,128)S(1)}, f32[264,128]{1,0:T(8,128)S(1)}, u32[]{:S(2)}, u32[]{:S(2)}) collective-permute-start(f32[264,128]{1,0:T(8,128)S(1)} %get-tuple-element.93.refs_3_.refs_5_.refs_16_), channel_id=1, source_target_pairs={{0,8},{4,12},{8,0},{12,4},{1,9},{5,13},{9,1},{13,5},{2,10},{6,14},... | collective-permute-start | bytes 405512 | tf_op jit(solution)/shard_map/ppermute | solution.py:435
  49.5 8.3 %collective-permute-start.14 = (f32[264,128]{1,0:T(8,128)S(1)}, f32[264,128]{1,0:T(8,128)S(1)}, u32[]{:S(2)}, u32[]{:S(2)}) collective-permute-start(f32[264,128]{1,0:T(8,128)S(1)} %get-tuple-element.93.refs_3_.refs_5_.refs_16_), channel_id=1, source_target_pairs={{0,4},{4,0},{8,12},{12,8},{1,5},{5,1},{9,13},{13,9},{2,6},{6,2},{1... | collective-permute-start | bytes 405512 | tf_op jit(solution)/shard_map/ppermute | solution.py:435
  59.9 5.8 %collective-permute-start.17 = (f32[392,128]{1,0:T(8,128)S(1)}, f32[392,128]{1,0:T(8,128)S(1)}, u32[]{:S(2)}, u32[]{:S(2)}) collective-permute-start(f32[392,128]{1,0:T(8,128)S(1)} %get-tuple-element.97.refs_2_), channel_id=1, source_target_pairs={{0,2},{1,3},{2,0},{3,1},{4,6},{5,7},{6,4},{7,5},{8,10},{9,11},{10,... | collective-permute-start | bytes 602120 | tf_op jit(solution)/shard_map/ppermute | solution.py:430
  68.2 7.1 %collective-permute-start.18 = (f32[264,128]{1,0:T(8,128)S(1)}, f32[264,128]{1,0:T(8,128)S(1)}, u32[]{:S(2)}, u32[]{:S(2)}) collective-permute-start(f32[264,128]{1,0:T(8,128)S(1)} %get-tuple-element.100), channel_id=1, source_target_pairs={{0,4},{4,0},{8,12},{12,8},{1,5},{5,1},{9,13},{13,9},{2,6},{6,2},{1... | collective-permute-start | bytes 405512 | tf_op jit(solution)/shard_map/ppermute | solution.py:435
  68.3 10.7 %collective-permute-start.19 = (f32[264,128]{1,0:T(8,128)S(1)}, f32[264,128]{1,0:T(8,128)S(1)}, u32[]{:S(2)}, u32[]{:S(2)}) collective-permute-start(f32[264,128]{1,0:T(8,128)S(1)} %get-tuple-element.101), channel_id=1, source_target_pairs={{0,8},{4,12},{8,0},{12,4},{1,9},{5,13},{9,1},{13,5},{2,10},{6,14},... | collective-permute-start | bytes 405512 | tf_op jit(solution)/shard_map/ppermute | solution.py:435
  71.3 7.6 %collective-permute-start.20 = (f32[264,128]{1,0:T(8,128)S(1)}, f32[264,128]{1,0:T(8,128)S(1)}, u32[]{:S(2)}, u32[]{:S(2)}) collective-permute-start(f32[264,128]{1,0:T(8,128)S(1)} %get-tuple-element.102), channel_id=1, source_target_pairs={{0,12},{4,8},{8,4},{12,0},{1,13},{5,9},{9,5},{13,1},{2,14},{6,10},... | collective-permute-start | bytes 405512 | tf_op jit(solution)/shard_map/ppermute | solution.py:435
  79.1 8.5 %collective-permute-start.23 = (f32[264,128]{1,0:T(8,128)S(1)}, f32[264,128]{1,0:T(8,128)S(1)}, u32[]{:S(2)}, u32[]{:S(2)}) collective-permute-start(f32[264,128]{1,0:T(8,128)S(1)} %get-tuple-element.106.refs_3_.refs_17_), channel_id=1, source_target_pairs={{0,12},{4,8},{8,4},{12,0},{1,13},{5,9},{9,5},{13,1},{2,14},{6,10},... | collective-permute-start | bytes 405512 | tf_op jit(solution)/shard_map/ppermute | solution.py:435
  83.1 8.9 %collective-permute-start.22 = (f32[264,128]{1,0:T(8,128)S(1)}, f32[264,128]{1,0:T(8,128)S(1)}, u32[]{:S(2)}, u32[]{:S(2)}) collective-permute-start(f32[264,128]{1,0:T(8,128)S(1)} %get-tuple-element.106.refs_3_.refs_17_), channel_id=1, source_target_pairs={{0,8},{4,12},{8,0},{12,4},{1,9},{5,13},{9,1},{13,5},{2,10},{6,14},... | collective-permute-start | bytes 405512 | tf_op jit(solution)/shard_map/ppermute | solution.py:435
  85.9 6.1 %collective-permute-start.21 = (f32[264,128]{1,0:T(8,128)S(1)}, f32[264,128]{1,0:T(8,128)S(1)}, u32[]{:S(2)}, u32[]{:S(2)}) collective-permute-start(f32[264,128]{1,0:T(8,128)S(1)} %get-tuple-element.106.refs_3_.refs_17_), channel_id=1, source_target_pairs={{0,4},{4,0},{8,12},{12,8},{1,5},{5,1},{9,13},{13,9},{2,6},{6,2},{1... | collective-permute-start | bytes 405512 | tf_op jit(solution)/shard_map/ppermute | solution.py:435
  94.0 5.8 %collective-permute-start.24 = (f32[392,128]{1,0:T(8,128)S(1)}, f32[392,128]{1,0:T(8,128)S(1)}, u32[]{:S(2)}, u32[]{:S(2)}) collective-permute-start(f32[392,128]{1,0:T(8,128)S(1)} %get-tuple-element.107.refs_0_), channel_id=1, source_target_pairs={{0,2},{1,3},{2,0},{3,1},{4,6},{5,7},{6,4},{7,5},{8,10},{9,11},{10,... | collective-permute-start | bytes 602120 | tf_op jit(solution)/shard_map/ppermute | solution.py:430
  100.0 5.4 %collective-permute-start.27 = (f32[8,128]{1,0:T(8,128)S(1)}, f32[8,128]{1,0:T(8,128)S(1)}, u32[]{:S(2)}, u32[]{:S(2)}) collective-permute-start(f32[8,128]{1,0:T(8,128)S(1)} %get-tuple-element.109.refs_2_), channel_id=1, source_target_pairs={{0,12},{4,8},{8,4},{12,0},{1,13},{5,9},{9,5},{13,1},{2,14},{6,10},... | collective-permute-start | bytes 12296 | tf_op jit(solution)/shard_map/ppermute | solution.py:435
  103.2 4.5 %collective-permute-start.26 = (f32[8,128]{1,0:T(8,128)S(1)}, f32[8,128]{1,0:T(8,128)S(1)}, u32[]{:S(2)}, u32[]{:S(2)}) collective-permute-start(f32[8,128]{1,0:T(8,128)S(1)} %get-tuple-element.109.refs_2_), channel_id=1, source_target_pairs={{0,8},{4,12},{8,0},{12,4},{1,9},{5,13},{9,1},{13,5},{2,10},{6,14},... | collective-permute-start | bytes 12296 | tf_op jit(solution)/shard_map/ppermute | solution.py:435
  103.2 4.5 %collective-permute-start.25 = (f32[8,128]{1,0:T(8,128)S(1)}, f32[8,128]{1,0:T(8,128)S(1)}, u32[]{:S(2)}, u32[]{:S(2)}) collective-permute-start(f32[8,128]{1,0:T(8,128)S(1)} %get-tuple-element.109.refs_2_), channel_id=1, source_target_pairs={{0,4},{4,0},{8,12},{12,8},{1,5},{5,1},{9,13},{13,9},{2,6},{6,2},{1... | collective-permute-start | bytes 12296 | tf_op jit(solution)/shard_map/ppermute | solution.py:435
  111.2 5.5 %collective-permute-start.28 = (f32[256,128]{1,0:T(8,128)S(1)}, f32[256,128]{1,0:T(8,128)S(1)}, u32[]{:S(2)}, u32[]{:S(2)}) collective-permute-start(f32[256,128]{1,0:T(8,128)S(1)} %get-tuple-element.118), channel_id=1, source_target_pairs={{0,4},{4,0},{8,12},{12,8},{1,5},{5,1},{9,13},{13,9},{2,6},{6,2},{1... | collective-permute-start | bytes 393224 | tf_op jit(solution)/shard_map/ppermute | solution.py:435
  111.4 12.3 %collective-permute-start.29 = (f32[256,128]{1,0:T(8,128)S(1)}, f32[256,128]{1,0:T(8,128)S(1)}, u32[]{:S(2)}, u32[]{:S(2)}) collective-permute-start(f32[256,128]{1,0:T(8,128)S(1)} %get-tuple-element.119), channel_id=1, source_target_pairs={{0,8},{4,12},{8,0},{12,4},{1,9},{5,13},{9,1},{13,5},{2,10},{6,14},... | collective-permute-start | bytes 393224 | tf_op jit(solution)/shard_map/ppermute | solution.py:435
  113.3 11.1 %collective-permute-start.30 = (f32[256,128]{1,0:T(8,128)S(1)}, f32[256,128]{1,0:T(8,128)S(1)}, u32[]{:S(2)}, u32[]{:S(2)}) collective-permute-start(f32[256,128]{1,0:T(8,128)S(1)} %get-tuple-element.120), channel_id=1, source_target_pairs={{0,12},{4,8},{8,4},{12,0},{1,13},{5,9},{9,5},{13,1},{2,14},{6,10},... | collective-permute-start | bytes 393224 | tf_op jit(solution)/shard_map/ppermute | solution.py:435
  125.1 6.9 %collective-permute-start.33 = (f32[264,128]{1,0:T(8,128)S(1)}, f32[264,128]{1,0:T(8,128)S(1)}, u32[]{:S(2)}, u32[]{:S(2)}) collective-permute-start(f32[264,128]{1,0:T(8,128)S(1)} %get-tuple-element.122.refs_3_.refs_5_.refs_14_), channel_id=1, source_target_pairs={{0,12},{4,8},{8,4},{12,0},{1,13},{5,9},{9,5},{13,1},{2,14},{6,10},... | collective-permute-start | bytes 405512 | tf_op jit(solution)/shard_map/ppermute | solution.py:435
  128.0 8.3 %collective-permute-start.32 = (f32[264,128]{1,0:T(8,128)S(1)}, f32[264,128]{1,0:T(8,128)S(1)}, u32[]{:S(2)}, u32[]{:S(2)}) collective-permute-start(f32[264,128]{1,0:T(8,128)S(1)} %get-tuple-element.122.refs_3_.refs_5_.refs_14_), channel_id=1, source_target_pairs={{0,8},{4,12},{8,0},{12,4},{1,9},{5,13},{9,1},{13,5},{2,10},{6,14},... | collective-permute-start | bytes 405512 | tf_op jit(solution)/shard_map/ppermute | solution.py:435
  129.9 6.4 %collective-permute-start.31 = (f32[264,128]{1,0:T(8,128)S(1)}, f32[264,128]{1,0:T(8,128)S(1)}, u32[]{:S(2)}, u32[]{:S(2)}) collective-permute-start(f32[264,128]{1,0:T(8,128)S(1)} %get-tuple-element.122.refs_3_.refs_5_.refs_14_), channel_id=1, source_target_pairs={{0,4},{4,0},{8,12},{12,8},{1,5},{5,1},{9,13},{13,9},{2,6},{6,2},{1... | collective-permute-start | bytes 405512 | tf_op jit(solution)/shard_map/ppermute | solution.py:435
  138.3 5.8 %collective-permute-start.34 = (f32[392,128]{1,0:T(8,128)S(1)}, f32[392,128]{1,0:T(8,128)S(1)}, u32[]{:S(2)}, u32[]{:S(2)}) collective-permute-start(f32[392,128]{1,0:T(8,128)S(1)} %get-tuple-element.123.refs_2_), channel_id=1, source_target_pairs={{0,2},{1,3},{2,0},{3,1},{4,6},{5,7},{6,4},{7,5},{8,10},{9,11},{10,... | collective-permute-start | bytes 602120 | tf_op jit(solution)/shard_map/ppermute | solution.py:430
  146.7 9.2 %collective-permute-start.35 = (f32[264,128]{1,0:T(8,128)S(1)}, f32[264,128]{1,0:T(8,128)S(1)}, u32[]{:S(2)}, u32[]{:S(2)}) collective-permute-start(f32[264,128]{1,0:T(8,128)S(1)} %get-tuple-element.126), channel_id=1, source_target_pairs={{0,4},{4,0},{8,12},{12,8},{1,5},{5,1},{9,13},{13,9},{2,6},{6,2},{1... | collective-permute-start | bytes 405512 | tf_op jit(solution)/shard_map/ppermute | solution.py:435
  146.8 11.9 %collective-permute-start.36 = (f32[264,128]{1,0:T(8,128)S(1)}, f32[264,128]{1,0:T(8,128)S(1)}, u32[]{:S(2)}, u32[]{:S(2)}) collective-permute-start(f32[264,128]{1,0:T(8,128)S(1)} %get-tuple-element.127), channel_id=1, source_target_pairs={{0,8},{4,12},{8,0},{12,4},{1,9},{5,13},{9,1},{13,5},{2,10},{6,14},... | collective-permute-start | bytes 405512 | tf_op jit(solution)/shard_map/ppermute | solution.py:435
  150.2 8.5 %collective-permute-start.37 = (f32[264,128]{1,0:T(8,128)S(1)}, f32[264,128]{1,0:T(8,128)S(1)}, u32[]{:S(2)}, u32[]{:S(2)}) collective-permute-start(f32[264,128]{1,0:T(8,128)S(1)} %get-tuple-element.128), channel_id=1, source_target_pairs={{0,12},{4,8},{8,4},{12,0},{1,13},{5,9},{9,5},{13,1},{2,14},{6,10},... | collective-permute-start | bytes 405512 | tf_op jit(solution)/shard_map/ppermute | solution.py:435
  158.8 7.0 %collective-permute-start.40 = (f32[264,128]{1,0:T(8,128)S(1)}, f32[264,128]{1,0:T(8,128)S(1)}, u32[]{:S(2)}, u32[]{:S(2)}) collective-permute-start(f32[264,128]{1,0:T(8,128)S(1)} %get-tuple-element.131.refs_3_.refs_15_), channel_id=1, source_target_pairs={{0,12},{4,8},{8,4},{12,0},{1,13},{5,9},{9,5},{13,1},{2,14},{6,10},... | collective-permute-start | bytes 405512 | tf_op jit(solution)/shard_map/ppermute | solution.py:435
  161.6 8.4 %collective-permute-start.39 = (f32[264,128]{1,0:T(8,128)S(1)}, f32[264,128]{1,0:T(8,128)S(1)}, u32[]{:S(2)}, u32[]{:S(2)}) collective-permute-start(f32[264,128]{1,0:T(8,128)S(1)} %get-tuple-element.131.refs_3_.refs_15_), channel_id=1, source_target_pairs={{0,8},{4,12},{8,0},{12,4},{1,9},{5,13},{9,1},{13,5},{2,10},{6,14},... | collective-permute-start | bytes 405512 | tf_op jit(solution)/shard_map/ppermute | solution.py:435
  162.6 7.4 %collective-permute-start.38 = (f32[264,128]{1,0:T(8,128)S(1)}, f32[264,128]{1,0:T(8,128)S(1)}, u32[]{:S(2)}, u32[]{:S(2)}) collective-permute-start(f32[264,128]{1,0:T(8,128)S(1)} %get-tuple-element.131.refs_3_.refs_15_), channel_id=1, source_target_pairs={{0,4},{4,0},{8,12},{12,8},{1,5},{5,1},{9,13},{13,9},{2,6},{6,2},{1... | collective-permute-start | bytes 405512 | tf_op jit(solution)/shard_map/ppermute | solution.py:435
  172.7 5.7 %collective-permute-start.41 = (f32[392,128]{1,0:T(8,128)S(1)}, f32[392,128]{1,0:T(8,128)S(1)}, u32[]{:S(2)}, u32[]{:S(2)}) collective-permute-start(f32[392,128]{1,0:T(8,128)S(1)} %get-tuple-element.132.refs_0_), channel_id=1, source_target_pairs={{0,2},{1,3},{2,0},{3,1},{4,6},{5,7},{6,4},{7,5},{8,10},{9,11},{10,... | collective-permute-start | bytes 602120 | tf_op jit(solution)/shard_map/ppermute | solution.py:430
  178.6 5.4 %collective-permute-start.44 = (f32[8,128]{1,0:T(8,128)S(1)}, f32[8,128]{1,0:T(8,128)S(1)}, u32[]{:S(2)}, u32[]{:S(2)}) collective-permute-start(f32[8,128]{1,0:T(8,128)S(1)} %get-tuple-element.134.refs_0_), channel_id=1, source_target_pairs={{0,12},{4,8},{8,4},{12,0},{1,13},{5,9},{9,5},{13,1},{2,14},{6,10},... | collective-permute-start | bytes 12296 | tf_op jit(solution)/shard_map/ppermute | solution.py:435
  181.0 4.5 %collective-permute-start.43 = (f32[8,128]{1,0:T(8,128)S(1)}, f32[8,128]{1,0:T(8,128)S(1)}, u32[]{:S(2)}, u32[]{:S(2)}) collective-permute-start(f32[8,128]{1,0:T(8,128)S(1)} %get-tuple-element.134.refs_0_), channel_id=1, source_target_pairs={{0,8},{4,12},{8,0},{12,4},{1,9},{5,13},{9,1},{13,5},{2,10},{6,14},... | collective-permute-start | bytes 12296 | tf_op jit(solution)/shard_map/ppermute | solution.py:435
  181.0 4.5 %collective-permute-start.42 = (f32[8,128]{1,0:T(8,128)S(1)}, f32[8,128]{1,0:T(8,128)S(1)}, u32[]{:S(2)}, u32[]{:S(2)}) collective-permute-start(f32[8,128]{1,0:T(8,128)S(1)} %get-tuple-element.134.refs_0_), channel_id=1, source_target_pairs={{0,4},{4,0},{8,12},{12,8},{1,5},{5,1},{9,13},{13,9},{2,6},{6,2},{1... | collective-permute-start | bytes 12296 | tf_op jit(solution)/shard_map/ppermute | solution.py:435
  185.7 2.0 %collective-permute-start.45 = (f32[1024,128]{1,0:T(8,128)S(1)}, f32[1024,128]{1,0:T(8,128)S(1)}, u32[]{:S(2)}, u32[]{:S(2)}) collective-permute-start(f32[1024,128]{1,0:T(8,128)S(1)} %shard_map.150.refs_1_), channel_id=1, source_target_pairs={{0,1},{1,0},{2,3},{3,2},{4,5},{5,4},{6,7},{7,6},{8,9},{9,8},{10,11... | collective-permute-start | bytes 1572872 | tf_op jit(solution)/shard_map/ppermute | solution.py:427

commit v9 on v8

--- a/solution.py
+++ b/solution.py
@@ -105,23 +105,19 @@
         dst[...] = jnp.where(low_half(dst.shape), v[:rows], turn(v[rows:]))
 
 
-def prep_kernel(slab, per, cols, pairs, a_in, p_in, a_both, t_hi, t_lo, p_hi, p_lo, diag):
-    for ref in (t_hi, t_lo):
-        ref[...] = jnp.zeros(ref.shape, BF16)
+def prep_kernel(slab, per, cols, pairs, a_in, p_in, a_both, t_both, p_hi, p_lo, diag):
     diag[...] = jnp.zeros(diag.shape, F32)
     for m in range(slab):
-        rows = slice(m * BLK, (m + 1) * BLK)
         for s in range(per):
             k = m * per + s
             col = cols[k]
-            at = pl.multiple_of(col * BLK, BLK)
             block = a_in[k]
             hi, lo = split_bf16(block)
             a_both[2 * m * BLK : (2 * m + 1) * BLK, s * BLK : (s + 1) * BLK] = hi.astype(BF16)
             a_both[(2 * m + 1) * BLK : (2 * m + 2) * BLK, s * BLK : (s + 1) * BLK] = lo.astype(BF16)
             hi, lo = split_bf16(block.T)
-            t_hi[pl.ds(at, BLK), rows] = hi.astype(BF16)
-            t_lo[pl.ds(at, BLK), rows] = lo.astype(BF16)
+            t_both[k * BLK : (k + 1) * BLK, :BLK] = hi.astype(BF16)
+            t_both[k * BLK : (k + 1) * BLK, BLK:] = lo.astype(BF16)
             diag[pl.ds(col, 1), :] += RHO * jnp.sum(block * block, axis=0, keepdims=True)
     shape = (BLK, BLK)
     eye = lax.broadcasted_iota(jnp.int32, shape, 0) == lax.broadcasted_iota(jnp.int32, shape, 1)
@@ -224,14 +220,23 @@
     msg[rows : rows + SC, :] = tile
 
 
-def back_product(n, own, place, pairs, w, pp_now, t_mats, total, outs, extra=()):
+def back_product(n, own, place, pairs, cols, w, pp_now, t_mats, total, outs, extra=()):
     row = place[0]
-    span = total.shape[0]
-    first, second = pair_up(w)
-    wide = jnp.concatenate([first, second], axis=0)
-    mine = fold(dot(t_mats[0][...], wide) + dot(t_mats[1][...], wide))
-    other = fold(dot(t_mats[2][...], wide) + dot(t_mats[3][...], wide))
-    total[...] = jnp.where(low_half((span, LANES)), mine, other)
+    span = total.shape[0] // 2
+    wide = jnp.concatenate(pair_up(w), axis=0)
+    slab = wide.shape[0] // BLK
+    per = t_mats[0].shape[0] // wide.shape[0]
+    for t in range(2):
+        total[t * span : (t + 1) * span, :] = jnp.zeros((span, LANES), F32)
+    for m in range(slab):
+        v = wide[m * BLK : (m + 1) * BLK]
+        v = jnp.concatenate([v, v], axis=0)
+        for t in range(2):
+            part = dot(t_mats[t][m * per * BLK : (m + 1) * per * BLK, :], v)
+            for s in range(per):
+                at = t * span + cols[(t * slab + m) * per + s] * BLK
+                total[pl.ds(pl.multiple_of(at, BLK), BLK), :] += part[s * BLK : (s + 1) * BLK]
+    total[0:span, :] = jnp.where(low_half((span, LANES)), fold(total[0:span, :]), fold(total[span:, :]))
     low1 = low_half((BLK, LANES))
     for t in range(2):
         side = low1 if t == 0 else jnp.logical_not(low1)
@@ -247,22 +252,22 @@
             at += rows.shape[0]
 
 
-def start_back_kernel(n, nx, own, place, pairs, *refs):
+def start_back_kernel(n, nx, own, place, pairs, cols, *refs):
     msgs, rest = refs[:nx], refs[nx:]
-    z, y, pp, diag, diag_other, *t_mats = rest[:9]
-    outs, (ax, total) = rest[9 : 9 + n], rest[9 + n :]
+    z, y, pp, diag, diag_other, *t_mats = rest[:7]
+    outs, (ax, total) = rest[7 : 7 + n], rest[7 + n :]
     ax_now = msgs[0][...]
     for k in range(1, nx):
         ax_now = ax_now + msgs[k][...]
     ax[...] = ax_now
     w = RHO * ax_now - (RHO * z[...] - y[...])
-    back_product(n, own, place, pairs, w, pp[...], t_mats, total, outs, (diag[...], diag_other[...]))
-
-
-def step_back_kernel(n, nx, own, place, pairs, *refs):
+    back_product(n, own, place, pairs, cols, w, pp[...], t_mats, total, outs, (diag[...], diag_other[...]))
+
+
+def step_back_kernel(n, nx, own, place, pairs, cols, *refs):
     msgs, rest = refs[:nx], refs[nx:]
-    pp, *t_mats = rest[:5]
-    outs, (ad, scal, total) = rest[5 : 5 + n], rest[5 + n :]
+    pp, *t_mats = rest[:3]
+    outs, (ad, scal, total) = rest[3 : 3 + n], rest[3 + n :]
     rows = ad.shape[0]
     v = msgs[0][...]
     for k in range(1, nx):
@@ -272,7 +277,7 @@
     ad[...] = ad_now
     scal[...] = tile
     curve = RHO * col_sum(ad_now * ad_now) + tile[3:4]
-    back_product(n, own, place, pairs, RHO * ad_now, pp[...], t_mats, total, outs, (pack_rows(curve),))
+    back_product(n, own, place, pairs, cols, RHO * ad_now, pp[...], t_mats, total, outs, (pack_rows(curve),))
 
 
 def residual_kernel(n, own, first, place, *refs):
@@ -366,11 +371,11 @@
     return beta, step1, step2, x_new, ax_hat, z_new, y_new, rest[12:]
 
 
-def update_kernel(n, own, place, pairs, *refs):
+def update_kernel(n, own, place, pairs, cols, *refs):
     beta, step1, step2, x_new, ax_hat, z_new, y_new, rest = admm_update(n, own, refs)
     ax = refs[n + 2]
-    ppx, pp1, pp2, *t_mats = rest[:7]
-    outs, (x_out, z_out, y_out, ax_out, ppx_out, total) = rest[7 : 7 + n], rest[7 + n :]
+    ppx, pp1, pp2, *t_mats = rest[:5]
+    outs, (x_out, z_out, y_out, ax_out, ppx_out, total) = rest[5 : 5 + n], rest[5 + n :]
     x_out[...] = x_new
     z_out[...] = z_new
     y_out[...] = y_new
@@ -380,7 +385,7 @@
     pp_new = RELAX * pp_hat + (1.0 - RELAX) * ppx[...]
     ppx_out[...] = pp_new
     w = RHO * ax_new - (RHO * z_new - y_new)
-    back_product(n, own, place, pairs, w, pp_new, t_mats, total, outs)
+    back_product(n, own, place, pairs, cols, w, pp_new, t_mats, total, outs)
 
 
 def last_kernel(n, own, *refs):
@@ -430,12 +435,13 @@
         return [v] + [lax.ppermute(v, "col", [(c, c ^ (2 * k)) for c in range(n_col)]) for k in range(1, nx)]
 
     ks = range(1, n)
+    scatter_ks = (2, 1, 3) if n == 4 else ks
 
     def over_row(v, k):
         return lax.ppermute(v, "row", [(i, i ^ k) for i in range(n)])
 
     def to_row(pieces):
-        return [pieces[0]] + [over_row(pieces[k], k) for k in ks]
+        return [pieces[0]] + [over_row(pieces[k], k) for k in scatter_ks]
 
     def to_all_rows(v):
         return [v] + [over_row(v, k) for k in ks]
@@ -468,7 +474,7 @@
         *mats, diag = call(
             functools.partial(prep_kernel, slab, per),
             [((2 * slab_rows, per * BLK), BF16)]
-            + [((span, slab_rows), BF16)] * 2
+            + [((slab * per * BLK, 2 * BLK), BF16)]
             + [((2 * BLK, 2 * BLK), BF16)] * 2
             + [((n_range, LANES), F32)],
             [a, p],
@@ -476,10 +482,11 @@
             flops=10**8,
             after=after,
         )
-        return mats[0:1], mats[1:3], mats[3:5], diag
+        return mats[0:1], mats[1:2], mats[2:4], diag
 
     prod_flops = 4 * slab_rows * 2 * span * LANES
     total_scratch = [pltpu.VMEM((span, LANES), F32)]
+    back_scratch = [pltpu.VMEM((2 * span, LANES), F32)]
     a_own, t_own, p_own, diag = prepare(a_mine, p_mine, a_cols.reshape(-1), p_pairs.reshape(-1))
     both_shape = ((half_rows + 2 * BLK, LANES), F32)
     keep, send = call(
@@ -512,8 +519,8 @@
         functools.partial(start_back_kernel, n, nx, own),
         [((own + 2 * n_range, LANES), F32)] * n + [((half_rows, LANES), F32)],
         [*to_x(msg), z, y, ppx, diag, diag_other, *t_mats],
-        [place, pairs],
-        total_scratch,
+        [place, pairs, cols],
+        back_scratch,
         flops=prod_flops,
     )
     for outer in range(ADMM_ITERS):
@@ -537,8 +544,8 @@
             functools.partial(step_back_kernel, n, nx, own),
             [msg_shape] * n + [slab_shape, tile_shape],
             [*to_x(msg), pp1, *t_mats],
-            [place, pairs],
-            total_scratch,
+            [place, pairs, cols],
+            back_scratch,
             flops=prod_flops,
         )
         msg2, step = call(
@@ -559,8 +566,8 @@
                 functools.partial(update_kernel, n, own),
                 [own_shape] * n + [own_shape, slab_shape, slab_shape, slab_shape, ((2 * BLK, LANES), F32)],
                 [*state, ppx, pp1, pp2, *t_mats],
-                [place, pairs],
-                total_scratch,
+                [place, pairs, cols],
+                back_scratch,
                 flops=prod_flops,
             )
         else:

time: 190 us -> 191 us (level)
  waiting for transfers between devices: 90.2 us -> 95.2 us
    ppermute x5, waiting for transfers between devices: 19.4 us -> 25 us  [to_x(): lax.ppermute(v, 'col', [(c, c ^ 2 * k) for c in range(n_col)])]
    ppermute x5, starting transfers between devices: 7.56 us -> 5.19 us  [to_x(): lax.ppermute(v, 'col', [(c, c ^ 2 * k) for c in range(n_col)])]
  transfers between devices with their start and end apart: 46 -> 46, of which waited for: 30 -> 26; matrix products, arithmetic and copies ran while one was open for 1% -> 1% of each run, Pallas kernels for 3% -> 3%
where the time goes in v9:
time: 191 us
  waiting for transfers between devices  95.2 us (50%)
  starting transfers between devices  61.5 us (32%)
  Pallas kernels  28.4 us (15%)
  local copies, waits for them, and re-layouts  4.15 us (2%)
    ppermute x33, waiting for transfers between devices, over_row(): return lax.ppermute(v, 'row', [(i, i ^ k) for i in range(n)])  66.8 us
    ppermute x33, starting transfers between devices, over_row(): return lax.ppermute(v, 'row', [(i, i ^ k) for i in range(n)])  54.4 us
    pallas_call x22, Pallas kernels, call(): pl.pallas_call(run, out_shape=[jax.ShapeDtypeStruct(s, d) for s, d in out...  28.4 us
    ppermute x5, waiting for transfers between devices, to_x(): lax.ppermute(v, 'col', [(c, c ^ 2 * k) for c in range(n_col)])  25 us
    ppermute x5, starting transfers between devices, to_x(): lax.ppermute(v, 'col', [(c, c ^ 2 * k) for c in range(n_col)])  5.19 us
    unnamed x23, local copies, waits for them, and re-layouts  3.82 us
  transfers between devices with their start and end apart: 46, of which 26 were waited for; matrix products, arithmetic and copies ran while one was open for 1% of the time, Pallas kernels for 3%

profile of v9, /device:TPU:0, one launch (start us, length us, event | category | flops | bytes accessed | tf_op | source)
XLA Modules:
  0.0 190.6 jit_solution(2538823921560381128)
XLA Ops:
  1.1 4.7 %collective-permute-start.3 = (f32[256,128]{1,0:T(8,128)}, f32[256,128]{1,0:T(8,128)S(1)}, u32[]{:S(2)}, u32[]{:S(2)}) collective-permute-start(f32[256,128]{1,0:T(8,128)} %refs_1_.3), channel_id=1, source_target_pairs={{0,12},{4,8},{8,4},{12,0},{1,13},{5,9},{9,5},{13,1},{2,14},{6,10},... | collective-permute-start | bytes 393224 | tf_op jit(solution)/shard_map/ppermute | solution.py:441
  6.5 0.8 copy.15
  7.3 1.4 copy-done
  8.7 0.9 copy-done.5
  10.3 1.2 shard_map.130
  11.7 6.0 %collective-permute-done.2.refs_5_ = f32[256,128]{1,0:T(8,128)S(1)} collective-permute-done((f32[256,128]{1,0:T(8,128)}, f32[256,128]{1,0:T(8,128)S(1)}, u32[]{:S(2)}, u32[]{:S(2)}) %collective-permute-start.2) | collective-permute-done | bytes 131104 | tf_op jit(solution)/shard_map/ppermute | solution.py:441
  17.7 1.4 shard_map.131
  19.9 1.3 shard_map.133
  21.3 1.6 collective-permute-start.5
  23.0 1.2 shard_map.134
  24.3 4.3 %collective-permute-done.5.refs_4_ = f32[384,128]{1,0:T(8,128)S(1)} collective-permute-done((f32[384,128]{1,0:T(8,128)S(1)}, f32[384,128]{1,0:T(8,128)S(1)}, u32[]{:S(2)}, u32[]{:S(2)}) %collective-permute-start.5) | collective-permute-done | bytes 196640 | tf_op jit(solution)/shard_map/ppermute | solution.py:435
  28.6 2.1 %shard_map.135 = (f32[272,128]{1,0:T(8,128)S(1)}, f32[272,128]{1,0:T(8,128)S(1)}, f32[272,128]{1,0:T(8,128)S(1)}, f32[272,128]{1,0:T(8,128)S(1)}, f32[384,128]{1,0:T(8,128)S(1)}) custom-call(s32[2]{0:T(128)S(1)} %pad_add_fusion.refs_0_, s32[4]{0:T(128)S(1)} %pad_add_fusion.2.refs_1_, s32[48]{0:T(128)S(1)} %pad_add_fusion.3.refs_2_, ...), custom_call_target="tpu_custom_call" | custom-call | flops 805306368 | bytes 4071424 | tf_op jit(solution)/shard_map/pallas_call | solution.py:34
  30.8 3.0 %collective-permute-start.9 = (f32[272,128]{1,0:T(8,128)S(1)}, f32[272,128]{1,0:T(8,128)S(1)}, u32[]{:S(2)}, u32[]{:S(2)}) collective-permute-start(f32[272,128]{1,0:T(8,128)S(1)} %get-tuple-element.85), channel_id=1, source_target_pairs={{0,4},{4,0},{8,12},{12,8},{1,5},{5,1},{9,13},{13,9},{2,6},{6,2},{1... | collective-permute-start | bytes 417800 | tf_op jit(solution)/shard_map/ppermute | solution.py:441
  33.8 1.3 collective-permute-start.10
  36.8 0.8 collective-permute-done.11.refs_2_
  38.4 4.4 %collective-permute-done.8.refs_2_ = f32[272,128]{1,0:T(8,128)S(1)} collective-permute-done((f32[272,128]{1,0:T(8,128)S(1)}, f32[272,128]{1,0:T(8,128)S(1)}, u32[]{:S(2)}, u32[]{:S(2)}) %collective-permute-start.8) | collective-permute-done | bytes 139296 | tf_op jit(solution)/shard_map/ppermute | solution.py:441
  43.0 1.0 shard_map.137
  44.0 1.6 collective-permute-start.16
  45.6 3.2 %collective-permute-start.15 = (f32[264,128]{1,0:T(8,128)S(1)}, f32[264,128]{1,0:T(8,128)S(1)}, u32[]{:S(2)}, u32[]{:S(2)}) collective-permute-start(f32[264,128]{1,0:T(8,128)S(1)} %get-tuple-element.89.refs_3_.refs_5_.refs_17_), channel_id=1, source_target_pairs={{0,8},{4,12},{8,0},{12,4},{1,9},{5,13},{9,1},{13,5},{2,10},{6,14},... | collective-permute-start | bytes 405512 | tf_op jit(solution)/shard_map/ppermute | solution.py:441
  48.8 2.5 %collective-permute-done.16.refs_6_ = f32[264,128]{1,0:T(8,128)S(1)} collective-permute-done((f32[264,128]{1,0:T(8,128)S(1)}, f32[264,128]{1,0:T(8,128)S(1)}, u32[]{:S(2)}, u32[]{:S(2)}) %collective-permute-start.16) | collective-permute-done | bytes 135200 | tf_op jit(solution)/shard_map/ppermute | solution.py:441
  51.3 8.2 %collective-permute-done.15.refs_5_ = f32[264,128]{1,0:T(8,128)S(1)} collective-permute-done((f32[264,128]{1,0:T(8,128)S(1)}, f32[264,128]{1,0:T(8,128)S(1)}, u32[]{:S(2)}, u32[]{:S(2)}) %collective-permute-start.15) | collective-permute-done | bytes 135200 | tf_op jit(solution)/shard_map/ppermute | solution.py:441
  59.5 2.1 %shard_map.138 = (f32[392,128]{1,0:T(8,128)S(1)}, f32[256,128]{1,0:T(8,128)S(1)}) custom-call(s32[2]{0:T(128)S(1)} %pad_add_fusion.refs_0_, s32[4]{0:T(128)S(1)} %pad_add_fusion.2.refs_1_, s32[48]{0:T(128)S(1)} %pad_add_fusion.3.refs_2_, f32[264,128]{1,0:T(8,128)S(1)} %get-tuple-element.89.refs_3_.refs_5_.refs_17_, ...), custom_call_target="tpu_custom_call" | custom-call | flops 805306368 | bytes 4210688 | tf_op jit(solution)/shard_map/pallas_call | solution.py:34
  61.6 1.5 collective-permute-start.17
  63.1 5.4 %collective-permute-done.17.refs_4_ = f32[392,128]{1,0:T(8,128)S(1)} collective-permute-done((f32[392,128]{1,0:T(8,128)S(1)}, f32[392,128]{1,0:T(8,128)S(1)}, u32[]{:S(2)}, u32[]{:S(2)}) %collective-permute-start.17) | collective-permute-done | bytes 200736 | tf_op jit(solution)/shard_map/ppermute | solution.py:435
  68.6 2.1 %shard_map.139 = (f32[264,128]{1,0:T(8,128)S(1)}, f32[264,128]{1,0:T(8,128)S(1)}, f32[264,128]{1,0:T(8,128)S(1)}, f32[264,128]{1,0:T(8,128)S(1)}, f32[384,128]{1,0:T(8,128)S(1)}, /*index=5*/f32[8,128]{1,0:T(8,128)S(1)}) custom-call(s32[2]{0:T(128)S(1)} %pad_add_fusion.refs_0_, s32[4]{0:T(128)S(1)} %pad_add_fusion.2.refs_1_, s32[48]{0:T(128)S(1)} %pad_add_fusion.3.refs_2_, ...), custom_call_target="tpu_custom_call" | custom-call | flops 805306368 | bytes 3678208 | tf_op jit(solution)/shard_map/pallas_call | solution.py:34
  70.8 1.7 collective-permute-start.19
  72.5 2.7 %collective-permute-start.20 = (f32[264,128]{1,0:T(8,128)S(1)}, f32[264,128]{1,0:T(8,128)S(1)}, u32[]{:S(2)}, u32[]{:S(2)}) collective-permute-start(f32[264,128]{1,0:T(8,128)S(1)} %get-tuple-element.98), channel_id=1, source_target_pairs={{0,12},{4,8},{8,4},{12,0},{1,13},{5,9},{9,5},{13,1},{2,14},{6,10},... | collective-permute-start | bytes 405512 | tf_op jit(solution)/shard_map/ppermute | solution.py:441
  75.2 6.0 %collective-permute-done.18.refs_1_ = f32[264,128]{1,0:T(8,128)S(1)} collective-permute-done((f32[264,128]{1,0:T(8,128)S(1)}, f32[264,128]{1,0:T(8,128)S(1)}, u32[]{:S(2)}, u32[]{:S(2)}) %collective-permute-start.18) | collective-permute-done | bytes 135200 | tf_op jit(solution)/shard_map/ppermute | solution.py:441
  81.6 2.1 %collective-permute-start.23 = (f32[264,128]{1,0:T(8,128)S(1)}, f32[264,128]{1,0:T(8,128)S(1)}, u32[]{:S(2)}, u32[]{:S(2)}) collective-permute-start(f32[264,128]{1,0:T(8,128)S(1)} %get-tuple-element.102.refs_3_.refs_18_), channel_id=1, source_target_pairs={{0,12},{4,8},{8,4},{12,0},{1,13},{5,9},{9,5},{13,1},{2,14},{6,10},... | collective-permute-start | bytes 405512 | tf_op jit(solution)/shard_map/ppermute | solution.py:441
  83.8 3.5 %collective-permute-start.22 = (f32[264,128]{1,0:T(8,128)S(1)}, f32[264,128]{1,0:T(8,128)S(1)}, u32[]{:S(2)}, u32[]{:S(2)}) collective-permute-start(f32[264,128]{1,0:T(8,128)S(1)} %get-tuple-element.102.refs_3_.refs_18_), channel_id=1, source_target_pairs={{0,8},{4,12},{8,0},{12,4},{1,9},{5,13},{9,1},{13,5},{2,10},{6,14},... | collective-permute-start | bytes 405512 | tf_op jit(solution)/shard_map/ppermute | solution.py:441
  87.3 1.9 collective-permute-done.23.refs_6_
  89.1 7.1 %collective-permute-done.22.refs_5_ = f32[264,128]{1,0:T(8,128)S(1)} collective-permute-done((f32[264,128]{1,0:T(8,128)S(1)}, f32[264,128]{1,0:T(8,128)S(1)}, u32[]{:S(2)}, u32[]{:S(2)}) %collective-permute-start.22) | collective-permute-done | bytes 135200 | tf_op jit(solution)/shard_map/ppermute | solution.py:441
  96.2 2.1 %shard_map.141 = (f32[392,128]{1,0:T(8,128)S(1)}, f32[256,128]{1,0:T(8,128)S(1)}) custom-call(s32[2]{0:T(128)S(1)} %pad_add_fusion.refs_0_, s32[4]{0:T(128)S(1)} %pad_add_fusion.2.refs_1_, s32[48]{0:T(128)S(1)} %pad_add_fusion.3.refs_2_, f32[264,128]{1,0:T(8,128)S(1)} %get-tuple-element.102.refs_3_.refs_18_, f32[264,128]{1,0:T(8,128)S(1)} %collective-permute-done.21.refs_4_, ...), custom_call_target="tpu_custom_call" | custom-call | flops 805306368 | bytes 4341760 | tf_op jit(solution)/shard_map/pallas_call | solution.py:34
  98.3 1.5 collective-permute-start.24
  99.8 4.4 %collective-permute-done.24.refs_1_ = f32[392,128]{1,0:T(8,128)S(1)} collective-permute-done((f32[392,128]{1,0:T(8,128)S(1)}, f32[392,128]{1,0:T(8,128)S(1)}, u32[]{:S(2)}, u32[]{:S(2)}) %collective-permute-start.24) | collective-permute-done | bytes 200736 | tf_op jit(solution)/shard_map/ppermute | solution.py:435
  104.4 2.3 %collective-permute-start.27 = (f32[8,128]{1,0:T(8,128)S(1)}, f32[8,128]{1,0:T(8,128)S(1)}, u32[]{:S(2)}, u32[]{:S(2)}) collective-permute-start(f32[8,128]{1,0:T(8,128)S(1)} %get-tuple-element.105.refs_3_), channel_id=1, source_target_pairs={{0,12},{4,8},{8,4},{12,0},{1,13},{5,9},{9,5},{13,1},{2,14},{6,10},... | collective-permute-start | bytes 12296 | tf_op jit(solution)/shard_map/ppermute | solution.py:441
  106.7 2.0 %collective-permute-start.25 = (f32[8,128]{1,0:T(8,128)S(1)}, f32[8,128]{1,0:T(8,128)S(1)}, u32[]{:S(2)}, u32[]{:S(2)}) collective-permute-start(f32[8,128]{1,0:T(8,128)S(1)} %get-tuple-element.105.refs_3_), channel_id=1, source_target_pairs={{0,4},{4,0},{8,12},{12,8},{1,5},{5,1},{9,13},{13,9},{2,6},{6,2},{1... | collective-permute-start | bytes 12296 | tf_op jit(solution)/shard_map/ppermute | solution.py:441
  108.7 1.0 collective-permute-done.27.refs_6_
  109.8 1.4 collective-permute-done.26.refs_5_
  111.2 3.1 %shard_map.143 = (f32[256,128]{1,0:T(8,128)S(1)}, f32[256,128]{1,0:T(8,128)S(1)}, f32[256,128]{1,0:T(8,128)S(1)}, f32[256,128]{1,0:T(8,128)S(1)}, f32[256,128]{1...) custom-call(s32[2]{0:T(128)S(1)} %pad_add_fusion.refs_0_, ...), custom_call_target="tpu_custom_call" | custom-call | flops 805306368 | bytes 5341184 | tf_op jit(solution)/shard_map/pallas_call | solution.py:34
  114.3 2.0 %collective-permute-start.28 = (f32[256,128]{1,0:T(8,128)S(1)}, f32[256,128]{1,0:T(8,128)S(1)}, u32[]{:S(2)}, u32[]{:S(2)}) collective-permute-start(f32[256,128]{1,0:T(8,128)S(1)} %get-tuple-element.114), channel_id=1, source_target_pairs={{0,8},{4,12},{8,0},{12,4},{1,9},{5,13},{9,1},{13,5},{2,10},{6,14},... | collective-permute-start | bytes 393224 | tf_op jit(solution)/shard_map/ppermute | solution.py:441
  116.4 2.3 %collective-permute-start.30 = (f32[256,128]{1,0:T(8,128)S(1)}, f32[256,128]{1,0:T(8,128)S(1)}, u32[]{:S(2)}, u32[]{:S(2)}) collective-permute-start(f32[256,128]{1,0:T(8,128)S(1)} %get-tuple-element.116), channel_id=1, source_target_pairs={{0,12},{4,8},{8,4},{12,0},{1,13},{5,9},{9,5},{13,1},{2,14},{6,10},... | collective-permute-start | bytes 393224 | tf_op jit(solution)/shard_map/ppermute | solution.py:441
  118.7 7.2 %collective-permute-done.28.refs_2_ = f32[256,128]{1,0:T(8,128)S(1)} collective-permute-done((f32[256,128]{1,0:T(8,128)S(1)}, f32[256,128]{1,0:T(8,128)S(1)}, u32[]{:S(2)}, u32[]{:S(2)}) %collective-permute-start.28) | collective-permute-done | bytes 131104 | tf_op jit(solution)/shard_map/ppermute | solution.py:441
  126.7 3.3 %collective-permute-start.32 = (f32[264,128]{1,0:T(8,128)S(1)}, f32[264,128]{1,0:T(8,128)S(1)}, u32[]{:S(2)}, u32[]{:S(2)}) collective-permute-start(f32[264,128]{1,0:T(8,128)S(1)} %get-tuple-element.118.refs_3_.refs_5_.refs_14_), channel_id=1, source_target_pairs={{0,8},{4,12},{8,0},{12,4},{1,9},{5,13},{9,1},{13,5},{2,10},{6,14},... | collective-permute-start | bytes 405512 | tf_op jit(solution)/shard_map/ppermute | solution.py:441
  130.0 1.0 collective-permute-start.31
  130.9 3.2 %collective-permute-done.33.refs_6_ = f32[264,128]{1,0:T(8,128)S(1)} collective-permute-done((f32[264,128]{1,0:T(8,128)S(1)}, f32[264,128]{1,0:T(8,128)S(1)}, u32[]{:S(2)}, u32[]{:S(2)}) %collective-permute-start.33) | collective-permute-done | bytes 135200 | tf_op jit(solution)/shard_map/ppermute | solution.py:441
  134.1 4.6 %collective-permute-done.32.refs_5_ = f32[264,128]{1,0:T(8,128)S(1)} collective-permute-done((f32[264,128]{1,0:T(8,128)S(1)}, f32[264,128]{1,0:T(8,128)S(1)}, u32[]{:S(2)}, u32[]{:S(2)}) %collective-permute-start.32) | collective-permute-done | bytes 135200 | tf_op jit(solution)/shard_map/ppermute | solution.py:441
  138.7 2.1 %shard_map.145 = (f32[392,128]{1,0:T(8,128)S(1)}, f32[256,128]{1,0:T(8,128)S(1)}) custom-call(s32[2]{0:T(128)S(1)} %pad_add_fusion.refs_0_, s32[4]{0:T(128)S(1)} %pad_add_fusion.2.refs_1_, s32[48]{0:T(128)S(1)} %pad_add_fusion.3.refs_2_, f32[264,128]{1,0:T(8,128)S(1)} %get-tuple-element.118.refs_3_.refs_5_.refs_14_, ...), custom_call_target="tpu_custom_call" | custom-call | flops 805306368 | bytes 4210688 | tf_op jit(solution)/shard_map/pallas_call | solution.py:34
  141.1 5.5 %collective-permute-done.34.refs_4_ = f32[392,128]{1,0:T(8,128)S(1)} collective-permute-done((f32[392,128]{1,0:T(8,128)S(1)}, f32[392,128]{1,0:T(8,128)S(1)}, u32[]{:S(2)}, u32[]{:S(2)}) %collective-permute-start.34) | collective-permute-done | bytes 200736 | tf_op jit(solution)/shard_map/ppermute | solution.py:435
  146.6 2.1 %shard_map.146 = (f32[264,128]{1,0:T(8,128)S(1)}, f32[264,128]{1,0:T(8,128)S(1)}, f32[264,128]{1,0:T(8,128)S(1)}, f32[264,128]{1,0:T(8,128)S(1)}, f32[384,128]{1,0:T(8,128)S(1)}, /*index=5*/f32[8,128]{1,0:T(8,128)S(1)}) custom-call(s32[2]{0:T(128)S(1)} %pad_add_fusion.refs_0_, s32[4]{0:T(128)S(1)} %pad_add_fusion.2.refs_1_, s32[48]{0:T(128)S(1)} %pad_add_fusion.3.refs_2_, ...), custom_call_target="tpu_custom_call" | custom-call | flops 805306368 | bytes 3678208 | tf_op jit(solution)/shard_map/pallas_call | solution.py:34
  148.8 1.7 collective-permute-start.36
  150.5 2.6 %collective-permute-start.37 = (f32[264,128]{1,0:T(8,128)S(1)}, f32[264,128]{1,0:T(8,128)S(1)}, u32[]{:S(2)}, u32[]{:S(2)}) collective-permute-start(f32[264,128]{1,0:T(8,128)S(1)} %get-tuple-element.124), channel_id=1, source_target_pairs={{0,12},{4,8},{8,4},{12,0},{1,13},{5,9},{9,5},{13,1},{2,14},{6,10},... | collective-permute-start | bytes 405512 | tf_op jit(solution)/shard_map/ppermute | solution.py:441
  153.2 5.0 %collective-permute-done.35.refs_1_ = f32[264,128]{1,0:T(8,128)S(1)} collective-permute-done((f32[264,128]{1,0:T(8,128)S(1)}, f32[264,128]{1,0:T(8,128)S(1)}, u32[]{:S(2)}, u32[]{:S(2)}) %collective-permute-start.35) | collective-permute-done | bytes 135200 | tf_op jit(solution)/shard_map/ppermute | solution.py:441
  158.3 2.1 %collective-permute-start.40 = (f32[264,128]{1,0:T(8,128)S(1)}, f32[264,128]{1,0:T(8,128)S(1)}, u32[]{:S(2)}, u32[]{:S(2)}) collective-permute-start(f32[264,128]{1,0:T(8,128)S(1)} %get-tuple-element.127.refs_3_.refs_15_), channel_id=1, source_target_pairs={{0,12},{4,8},{8,4},{12,0},{1,13},{5,9},{9,5},{13,1},{2,14},{6,10},... | collective-permute-start | bytes 405512 | tf_op jit(solution)/shard_map/ppermute | solution.py:441
  160.4 5.6 %collective-permute-start.39 = (f32[264,128]{1,0:T(8,128)S(1)}, f32[264,128]{1,0:T(8,128)S(1)}, u32[]{:S(2)}, u32[]{:S(2)}) collective-permute-start(f32[264,128]{1,0:T(8,128)S(1)} %get-tuple-element.127.refs_3_.refs_15_), channel_id=1, source_target_pairs={{0,8},{4,12},{8,0},{12,4},{1,9},{5,13},{9,1},{13,5},{2,10},{6,14},... | collective-permute-start | bytes 405512 | tf_op jit(solution)/shard_map/ppermute | solution.py:441
  166.0 6.0 %collective-permute-done.39.refs_5_ = f32[264,128]{1,0:T(8,128)S(1)} collective-permute-done((f32[264,128]{1,0:T(8,128)S(1)}, f32[264,128]{1,0:T(8,128)S(1)}, u32[]{:S(2)}, u32[]{:S(2)}) %collective-permute-start.39) | collective-permute-done | bytes 135200 | tf_op jit(solution)/shard_map/ppermute | solution.py:441
  172.0 2.7 %shard_map.148 = (f32[392,128]{1,0:T(8,128)S(1)}, f32[256,128]{1,0:T(8,128)}) custom-call(s32[2]{0:T(128)S(1)} %pad_add_fusion.refs_0_, s32[4]{0:T(128)S(1)} %pad_add_fusion.2.refs_1_, s32[48]{0:T(128)S(1)} %pad_add_fusion.3.refs_2_, f32[264,128]{1,0:T(8,128)S(1)} %get-tuple-element.127.refs_3_.refs_15_, f32[264,128]{1,0:T(8,128)S(1)} %collective-permute-done.38.refs_4_, ...), custom_call_target="tpu_custom_call" | custom-call | flops 805306368 | bytes 4341760 | tf_op jit(solution)/shard_map/pallas_call | solution.py:34
  174.9 5.4 %collective-permute-done.41.refs_1_ = f32[392,128]{1,0:T(8,128)S(1)} collective-permute-done((f32[392,128]{1,0:T(8,128)S(1)}, f32[392,128]{1,0:T(8,128)S(1)}, u32[]{:S(2)}, u32[]{:S(2)}) %collective-permute-start.41) | collective-permute-done | bytes 200736 | tf_op jit(solution)/shard_map/ppermute | solution.py:435
  180.5 1.6 collective-permute-start.44
  182.5 2.5 %collective-permute-start.42 = (f32[8,128]{1,0:T(8,128)S(1)}, f32[8,128]{1,0:T(8,128)S(1)}, u32[]{:S(2)}, u32[]{:S(2)}) collective-permute-start(f32[8,128]{1,0:T(8,128)S(1)} %get-tuple-element.130.refs_0_), channel_id=1, source_target_pairs={{0,4},{4,0},{8,12},{12,8},{1,5},{5,1},{9,13},{13,9},{2,6},{6,2},{1... | collective-permute-start | bytes 12296 | tf_op jit(solution)/shard_map/ppermute | solution.py:441
  184.9 1.0 collective-permute-done.44.refs_3_
  185.9 0.7 collective-permute-done.43.refs_2_
  186.9 1.9 collective-permute-done.45.refs_2_
  188.8 1.7 shard_map.151
  (82 shorter events, 8.8 us)
Async XLA Ops:
  0.6 22.4 %collective-permute-start.6 = (f32[24,128,128]{2,1,0:T(8,128)}, f32[24,128,128]{2,1,0:T(8,128)S(1)}, u32[]{:S(2)}, u32[]{:S(2)}) collective-permute-start(f32[24,128,128]{2,1,0:T(8,128)} %bitcast.6), channel_id=1, source_target_pairs={{0,1},{1,0},{2,3},{3,2},{4,5},{5,4},{6,7},{7,6},{8,9},{9,8},{10,11... | collective-permute-start | bytes 4718600 | tf_op jit(solution)/shard_map/ppermute | solution.py:432
  1.1 10.6 %collective-permute-start.3 = (f32[256,128]{1,0:T(8,128)}, f32[256,128]{1,0:T(8,128)S(1)}, u32[]{:S(2)}, u32[]{:S(2)}) collective-permute-start(f32[256,128]{1,0:T(8,128)} %refs_1_.3), channel_id=1, source_target_pairs={{0,12},{4,8},{8,4},{12,0},{1,13},{5,9},{9,5},{13,1},{2,14},{6,10},... | collective-permute-start | bytes 393224 | tf_op jit(solution)/shard_map/ppermute | solution.py:441
  5.8 11.9 %collective-permute-start.2 = (f32[256,128]{1,0:T(8,128)}, f32[256,128]{1,0:T(8,128)S(1)}, u32[]{:S(2)}, u32[]{:S(2)}) collective-permute-start(f32[256,128]{1,0:T(8,128)} %refs_1_.3), channel_id=1, source_target_pairs={{0,8},{4,12},{8,0},{12,4},{1,9},{5,13},{9,1},{13,5},{2,10},{6,14},... | collective-permute-start | bytes 393224 | tf_op jit(solution)/shard_map/ppermute | solution.py:441
  5.8 11.9 %collective-permute-start.1 = (f32[256,128]{1,0:T(8,128)}, f32[256,128]{1,0:T(8,128)S(1)}, u32[]{:S(2)}, u32[]{:S(2)}) collective-permute-start(f32[256,128]{1,0:T(8,128)} %refs_1_.3), channel_id=1, source_target_pairs={{0,4},{4,0},{8,12},{12,8},{1,5},{5,1},{9,13},{13,9},{2,6},{6,2},{1... | collective-permute-start | bytes 393224 | tf_op jit(solution)/shard_map/ppermute | solution.py:441
  7.3 1.4 copy-start
  8.7 0.9 copy-start.5
  9.7 0.7 copy-start.8
  10.3 7.4 %copy-start.6 = (f32[256,128]{1,0:T(8,128)S(1)}, f32[256,128]{1,0:T(8,128)}, u32[]{:S(2)}) copy-start(f32[256,128]{1,0:T(8,128)} %refs_1_.3) | copy-start | bytes 393220
  11.6 8.3 %copy-start.1 = (f32[768,128]{1,0:T(8,128)S(1)}, f32[768,128]{1,0:T(8,128)}, u32[]{:S(2)}) copy-start(f32[768,128]{1,0:T(8,128)} %refs_1_.2) | copy-start | bytes 1179652
  11.6 8.3 %copy-start.2 = (f32[768,128]{1,0:T(8,128)S(1)}, f32[768,128]{1,0:T(8,128)}, u32[]{:S(2)}) copy-start(f32[768,128]{1,0:T(8,128)} %refs_2_.1) | copy-start | bytes 1179652
  11.6 8.2 %copy-start.3 = (f32[768,128]{1,0:T(8,128)S(1)}, f32[768,128]{1,0:T(8,128)}, u32[]{:S(2)}) copy-start(f32[768,128]{1,0:T(8,128)} %refs_3_.4) | copy-start | bytes 1179652
  11.6 8.2 %copy-start.4 = (f32[768,128]{1,0:T(8,128)S(1)}, f32[768,128]{1,0:T(8,128)}, u32[]{:S(2)}) copy-start(f32[768,128]{1,0:T(8,128)} %refs_4_.1) | copy-start | bytes 1179652
  19.1 3.8 %copy-start.9 = (s32[1,1,2]{2,1,0:T(1,128)S(1)}, s32[1,1,2]{2,1,0:T(1,128)}, u32[]{:S(2)}) copy-start(s32[1,1,2]{2,1,0:T(1,128)} %param.21) | copy-start | bytes 28
  19.1 2.1 %collective-permute-start.4 = (f32[640,128]{1,0:T(8,128)S(1)}, f32[640,128]{1,0:T(8,128)S(1)}, u32[]{:S(2)}, u32[]{:S(2)}) collective-permute-start(f32[640,128]{1,0:T(8,128)S(1)} %get-tuple-element.74), channel_id=1, source_target_pairs={{0,1},{1,0},{2,3},{3,2},{4,5},{5,4},{6,7},{7,6},{8,9},{9,8},{10,11... | collective-permute-start | bytes 983048 | tf_op jit(solution)/shard_map/ppermute | solution.py:432
  19.2 3.8 %collective-permute-start.7 = (f32[4,128,128]{2,1,0:T(8,128)S(1)}, f32[4,128,128]{2,1,0:T(8,128)S(1)}, u32[]{:S(2)}, u32[]{:S(2)}) collective-permute-start(f32[4,128,128]{2,1,0:T(8,128)S(1)} %bitcast.9), channel_id=1, source_target_pairs={{0,1},{1,0},{2,3},{3,2},{4,5},{5,4},{6,7},{7,6},{8,9},{9,8},{10,11... | collective-permute-start | bytes 786440 | tf_op jit(solution)/shard_map/ppermute | solution.py:432
  19.8 1.4 collective-permute-start
  21.3 7.3 %collective-permute-start.5 = (f32[384,128]{1,0:T(8,128)S(1)}, f32[384,128]{1,0:T(8,128)S(1)}, u32[]{:S(2)}, u32[]{:S(2)}) collective-permute-start(f32[384,128]{1,0:T(8,128)S(1)} %get-tuple-element.75.refs_0_.refs_3_), channel_id=1, source_target_pairs={{0,2},{1,3},{2,0},{3,1},{4,6},{5,7},{6,4},{7,5},{8,10},{9,11},{10,... | collective-permute-start | bytes 589832 | tf_op jit(solution)/shard_map/ppermute | solution.py:435
  28.6 6.6 %copy-start.10 = (f32[256]{0:T(256)S(1)}, f32[256]{0:T(256)}, u32[]{:S(2)}) copy-start(f32[256]{0:T(256)} %param.13) | copy-start | bytes 3076
  28.6 6.6 %copy-start.7 = (f32[256,128]{1,0:T(8,128)S(1)}, f32[256,128]{1,0:T(8,128)}, u32[]{:S(2)}) copy-start(f32[256,128]{1,0:T(8,128)} %refs_3_.5) | copy-start | bytes 393220
  30.7 12.1 %collective-permute-start.8 = (f32[272,128]{1,0:T(8,128)S(1)}, f32[272,128]{1,0:T(8,128)S(1)}, u32[]{:S(2)}, u32[]{:S(2)}) collective-permute-start(f32[272,128]{1,0:T(8,128)S(1)} %get-tuple-element.84), channel_id=1, source_target_pairs={{0,8},{4,12},{8,0},{12,4},{1,9},{5,13},{9,1},{13,5},{2,10},{6,14},... | collective-permute-start | bytes 417800 | tf_op jit(solution)/shard_map/ppermute | solution.py:441
  30.8 12.2 %collective-permute-start.9 = (f32[272,128]{1,0:T(8,128)S(1)}, f32[272,128]{1,0:T(8,128)S(1)}, u32[]{:S(2)}, u32[]{:S(2)}) collective-permute-start(f32[272,128]{1,0:T(8,128)S(1)} %get-tuple-element.85), channel_id=1, source_target_pairs={{0,4},{4,0},{8,12},{12,8},{1,5},{5,1},{9,13},{13,9},{2,6},{6,2},{1... | collective-permute-start | bytes 417800 | tf_op jit(solution)/shard_map/ppermute | solution.py:441
  33.8 9.1 %collective-permute-start.10 = (f32[272,128]{1,0:T(8,128)S(1)}, f32[272,128]{1,0:T(8,128)S(1)}, u32[]{:S(2)}, u32[]{:S(2)}) collective-permute-start(f32[272,128]{1,0:T(8,128)S(1)} %get-tuple-element.86), channel_id=1, source_target_pairs={{0,12},{4,8},{8,4},{12,0},{1,13},{5,9},{9,5},{13,1},{2,14},{6,10},... | collective-permute-start | bytes 417800 | tf_op jit(solution)/shard_map/ppermute | solution.py:441
  35.2 1.1 collective-permute-start.13
  35.2 1.6 collective-permute-start.12
  36.3 1.3 collective-permute-start.11
  44.0 7.3 %collective-permute-start.16 = (f32[264,128]{1,0:T(8,128)S(1)}, f32[264,128]{1,0:T(8,128)S(1)}, u32[]{:S(2)}, u32[]{:S(2)}) collective-permute-start(f32[264,128]{1,0:T(8,128)S(1)} %get-tuple-element.89.refs_3_.refs_5_.refs_17_), channel_id=1, source_target_pairs={{0,12},{4,8},{8,4},{12,0},{1,13},{5,9},{9,5},{13,1},{2,14},{6,10},... | collective-permute-start | bytes 405512 | tf_op jit(solution)/shard_map/ppermute | solution.py:441
  45.6 13.9 %collective-permute-start.15 = (f32[264,128]{1,0:T(8,128)S(1)}, f32[264,128]{1,0:T(8,128)S(1)}, u32[]{:S(2)}, u32[]{:S(2)}) collective-permute-start(f32[264,128]{1,0:T(8,128)S(1)} %get-tuple-element.89.refs_3_.refs_5_.refs_17_), channel_id=1, source_target_pairs={{0,8},{4,12},{8,0},{12,4},{1,9},{5,13},{9,1},{13,5},{2,10},{6,14},... | collective-permute-start | bytes 405512 | tf_op jit(solution)/shard_map/ppermute | solution.py:441
  48.8 10.7 %collective-permute-start.14 = (f32[264,128]{1,0:T(8,128)S(1)}, f32[264,128]{1,0:T(8,128)S(1)}, u32[]{:S(2)}, u32[]{:S(2)}) collective-permute-start(f32[264,128]{1,0:T(8,128)S(1)} %get-tuple-element.89.refs_3_.refs_5_.refs_17_), channel_id=1, source_target_pairs={{0,4},{4,0},{8,12},{12,8},{1,5},{5,1},{9,13},{13,9},{2,6},{6,2},{1... | collective-permute-start | bytes 405512 | tf_op jit(solution)/shard_map/ppermute | solution.py:441
  61.6 7.0 %collective-permute-start.17 = (f32[392,128]{1,0:T(8,128)S(1)}, f32[392,128]{1,0:T(8,128)S(1)}, u32[]{:S(2)}, u32[]{:S(2)}) collective-permute-start(f32[392,128]{1,0:T(8,128)S(1)} %get-tuple-element.93.refs_3_), channel_id=1, source_target_pairs={{0,2},{1,3},{2,0},{3,1},{4,6},{5,7},{6,4},{7,5},{8,10},{9,11},{10,... | collective-permute-start | bytes 602120 | tf_op jit(solution)/shard_map/ppermute | solution.py:435
  70.7 10.5 %collective-permute-start.18 = (f32[264,128]{1,0:T(8,128)S(1)}, f32[264,128]{1,0:T(8,128)S(1)}, u32[]{:S(2)}, u32[]{:S(2)}) collective-permute-start(f32[264,128]{1,0:T(8,128)S(1)} %get-tuple-element.96), channel_id=1, source_target_pairs={{0,8},{4,12},{8,0},{12,4},{1,9},{5,13},{9,1},{13,5},{2,10},{6,14},... | collective-permute-start | bytes 405512 | tf_op jit(solution)/shard_map/ppermute | solution.py:441
  70.8 10.7 %collective-permute-start.19 = (f32[264,128]{1,0:T(8,128)S(1)}, f32[264,128]{1,0:T(8,128)S(1)}, u32[]{:S(2)}, u32[]{:S(2)}) collective-permute-start(f32[264,128]{1,0:T(8,128)S(1)} %get-tuple-element.97), channel_id=1, source_target_pairs={{0,4},{4,0},{8,12},{12,8},{1,5},{5,1},{9,13},{13,9},{2,6},{6,2},{1... | collective-permute-start | bytes 405512 | tf_op jit(solution)/shard_map/ppermute | solution.py:441
  72.5 9.0 %collective-permute-start.20 = (f32[264,128]{1,0:T(8,128)S(1)}, f32[264,128]{1,0:T(8,128)S(1)}, u32[]{:S(2)}, u32[]{:S(2)}) collective-permute-start(f32[264,128]{1,0:T(8,128)S(1)} %get-tuple-element.98), channel_id=1, source_target_pairs={{0,12},{4,8},{8,4},{12,0},{1,13},{5,9},{9,5},{13,1},{2,14},{6,10},... | collective-permute-start | bytes 405512 | tf_op jit(solution)/shard_map/ppermute | solution.py:441
  81.6 7.5 %collective-permute-start.23 = (f32[264,128]{1,0:T(8,128)S(1)}, f32[264,128]{1,0:T(8,128)S(1)}, u32[]{:S(2)}, u32[]{:S(2)}) collective-permute-start(f32[264,128]{1,0:T(8,128)S(1)} %get-tuple-element.102.refs_3_.refs_18_), channel_id=1, source_target_pairs={{0,12},{4,8},{8,4},{12,0},{1,13},{5,9},{9,5},{13,1},{2,14},{6,10},... | collective-permute-start | bytes 405512 | tf_op jit(solution)/shard_map/ppermute | solution.py:441
  83.8 12.4 %collective-permute-start.22 = (f32[264,128]{1,0:T(8,128)S(1)}, f32[264,128]{1,0:T(8,128)S(1)}, u32[]{:S(2)}, u32[]{:S(2)}) collective-permute-start(f32[264,128]{1,0:T(8,128)S(1)} %get-tuple-element.102.refs_3_.refs_18_), channel_id=1, source_target_pairs={{0,8},{4,12},{8,0},{12,4},{1,9},{5,13},{9,1},{13,5},{2,10},{6,14},... | collective-permute-start | bytes 405512 | tf_op jit(solution)/shard_map/ppermute | solution.py:441
  87.3 8.9 %collective-permute-start.21 = (f32[264,128]{1,0:T(8,128)S(1)}, f32[264,128]{1,0:T(8,128)S(1)}, u32[]{:S(2)}, u32[]{:S(2)}) collective-permute-start(f32[264,128]{1,0:T(8,128)S(1)} %get-tuple-element.102.refs_3_.refs_18_), channel_id=1, source_target_pairs={{0,4},{4,0},{8,12},{12,8},{1,5},{5,1},{9,13},{13,9},{2,6},{6,2},{1... | collective-permute-start | bytes 405512 | tf_op jit(solution)/shard_map/ppermute | solution.py:441
  98.3 5.9 %collective-permute-start.24 = (f32[392,128]{1,0:T(8,128)S(1)}, f32[392,128]{1,0:T(8,128)S(1)}, u32[]{:S(2)}, u32[]{:S(2)}) collective-permute-start(f32[392,128]{1,0:T(8,128)S(1)} %get-tuple-element.103.refs_0_), channel_id=1, source_target_pairs={{0,2},{1,3},{2,0},{3,1},{4,6},{5,7},{6,4},{7,5},{8,10},{9,11},{10,... | collective-permute-start | bytes 602120 | tf_op jit(solution)/shard_map/ppermute | solution.py:435
  104.4 5.4 %collective-permute-start.27 = (f32[8,128]{1,0:T(8,128)S(1)}, f32[8,128]{1,0:T(8,128)S(1)}, u32[]{:S(2)}, u32[]{:S(2)}) collective-permute-start(f32[8,128]{1,0:T(8,128)S(1)} %get-tuple-element.105.refs_3_), channel_id=1, source_target_pairs={{0,12},{4,8},{8,4},{12,0},{1,13},{5,9},{9,5},{13,1},{2,14},{6,10},... | collective-permute-start | bytes 12296 | tf_op jit(solution)/shard_map/ppermute | solution.py:441
  106.7 4.5 %collective-permute-start.26 = (f32[8,128]{1,0:T(8,128)S(1)}, f32[8,128]{1,0:T(8,128)S(1)}, u32[]{:S(2)}, u32[]{:S(2)}) collective-permute-start(f32[8,128]{1,0:T(8,128)S(1)} %get-tuple-element.105.refs_3_), channel_id=1, source_target_pairs={{0,8},{4,12},{8,0},{12,4},{1,9},{5,13},{9,1},{13,5},{2,10},{6,14},... | collective-permute-start | bytes 12296 | tf_op jit(solution)/shard_map/ppermute | solution.py:441
  106.7 4.5 %collective-permute-start.25 = (f32[8,128]{1,0:T(8,128)S(1)}, f32[8,128]{1,0:T(8,128)S(1)}, u32[]{:S(2)}, u32[]{:S(2)}) collective-permute-start(f32[8,128]{1,0:T(8,128)S(1)} %get-tuple-element.105.refs_3_), channel_id=1, source_target_pairs={{0,4},{4,0},{8,12},{12,8},{1,5},{5,1},{9,13},{13,9},{2,6},{6,2},{1... | collective-permute-start | bytes 12296 | tf_op jit(solution)/shard_map/ppermute | solution.py:441
  114.3 11.5 %collective-permute-start.28 = (f32[256,128]{1,0:T(8,128)S(1)}, f32[256,128]{1,0:T(8,128)S(1)}, u32[]{:S(2)}, u32[]{:S(2)}) collective-permute-start(f32[256,128]{1,0:T(8,128)S(1)} %get-tuple-element.114), channel_id=1, source_target_pairs={{0,8},{4,12},{8,0},{12,4},{1,9},{5,13},{9,1},{13,5},{2,10},{6,14},... | collective-permute-start | bytes 393224 | tf_op jit(solution)/shard_map/ppermute | solution.py:441
  116.3 9.5 %collective-permute-start.29 = (f32[256,128]{1,0:T(8,128)S(1)}, f32[256,128]{1,0:T(8,128)S(1)}, u32[]{:S(2)}, u32[]{:S(2)}) collective-permute-start(f32[256,128]{1,0:T(8,128)S(1)} %get-tuple-element.115), channel_id=1, source_target_pairs={{0,4},{4,0},{8,12},{12,8},{1,5},{5,1},{9,13},{13,9},{2,6},{6,2},{1... | collective-permute-start | bytes 393224 | tf_op jit(solution)/shard_map/ppermute | solution.py:441
  116.4 9.5 %collective-permute-start.30 = (f32[256,128]{1,0:T(8,128)S(1)}, f32[256,128]{1,0:T(8,128)S(1)}, u32[]{:S(2)}, u32[]{:S(2)}) collective-permute-start(f32[256,128]{1,0:T(8,128)S(1)} %get-tuple-element.116), channel_id=1, source_target_pairs={{0,12},{4,8},{8,4},{12,0},{1,13},{5,9},{9,5},{13,1},{2,14},{6,10},... | collective-permute-start | bytes 393224 | tf_op jit(solution)/shard_map/ppermute | solution.py:441
  126.5 7.6 %collective-permute-start.33 = (f32[264,128]{1,0:T(8,128)S(1)}, f32[264,128]{1,0:T(8,128)S(1)}, u32[]{:S(2)}, u32[]{:S(2)}) collective-permute-start(f32[264,128]{1,0:T(8,128)S(1)} %get-tuple-element.118.refs_3_.refs_5_.refs_14_), channel_id=1, source_target_pairs={{0,12},{4,8},{8,4},{12,0},{1,13},{5,9},{9,5},{13,1},{2,14},{6,10},... | collective-permute-start | bytes 405512 | tf_op jit(solution)/shard_map/ppermute | solution.py:441
  126.7 12.0 %collective-permute-start.32 = (f32[264,128]{1,0:T(8,128)S(1)}, f32[264,128]{1,0:T(8,128)S(1)}, u32[]{:S(2)}, u32[]{:S(2)}) collective-permute-start(f32[264,128]{1,0:T(8,128)S(1)} %get-tuple-element.118.refs_3_.refs_5_.refs_14_), channel_id=1, source_target_pairs={{0,8},{4,12},{8,0},{12,4},{1,9},{5,13},{9,1},{13,5},{2,10},{6,14},... | collective-permute-start | bytes 405512 | tf_op jit(solution)/shard_map/ppermute | solution.py:441
  130.0 8.8 %collective-permute-start.31 = (f32[264,128]{1,0:T(8,128)S(1)}, f32[264,128]{1,0:T(8,128)S(1)}, u32[]{:S(2)}, u32[]{:S(2)}) collective-permute-start(f32[264,128]{1,0:T(8,128)S(1)} %get-tuple-element.118.refs_3_.refs_5_.refs_14_), channel_id=1, source_target_pairs={{0,4},{4,0},{8,12},{12,8},{1,5},{5,1},{9,13},{13,9},{2,6},{6,2},{1... | collective-permute-start | bytes 405512 | tf_op jit(solution)/shard_map/ppermute | solution.py:441
  140.8 5.8 %collective-permute-start.34 = (f32[392,128]{1,0:T(8,128)S(1)}, f32[392,128]{1,0:T(8,128)S(1)}, u32[]{:S(2)}, u32[]{:S(2)}) collective-permute-start(f32[392,128]{1,0:T(8,128)S(1)} %get-tuple-element.119.refs_3_), channel_id=1, source_target_pairs={{0,2},{1,3},{2,0},{3,1},{4,6},{5,7},{6,4},{7,5},{8,10},{9,11},{10,... | collective-permute-start | bytes 602120 | tf_op jit(solution)/shard_map/ppermute | solution.py:435
  148.7 9.5 %collective-permute-start.35 = (f32[264,128]{1,0:T(8,128)S(1)}, f32[264,128]{1,0:T(8,128)S(1)}, u32[]{:S(2)}, u32[]{:S(2)}) collective-permute-start(f32[264,128]{1,0:T(8,128)S(1)} %get-tuple-element.122), channel_id=1, source_target_pairs={{0,8},{4,12},{8,0},{12,4},{1,9},{5,13},{9,1},{13,5},{2,10},{6,14},... | collective-permute-start | bytes 405512 | tf_op jit(solution)/shard_map/ppermute | solution.py:441
  148.8 9.4 %collective-permute-start.36 = (f32[264,128]{1,0:T(8,128)S(1)}, f32[264,128]{1,0:T(8,128)S(1)}, u32[]{:S(2)}, u32[]{:S(2)}) collective-permute-start(f32[264,128]{1,0:T(8,128)S(1)} %get-tuple-element.123), channel_id=1, source_target_pairs={{0,4},{4,0},{8,12},{12,8},{1,5},{5,1},{9,13},{13,9},{2,6},{6,2},{1... | collective-permute-start | bytes 405512 | tf_op jit(solution)/shard_map/ppermute | solution.py:441
  150.5 7.7 %collective-permute-start.37 = (f32[264,128]{1,0:T(8,128)S(1)}, f32[264,128]{1,0:T(8,128)S(1)}, u32[]{:S(2)}, u32[]{:S(2)}) collective-permute-start(f32[264,128]{1,0:T(8,128)S(1)} %get-tuple-element.124), channel_id=1, source_target_pairs={{0,12},{4,8},{8,4},{12,0},{1,13},{5,9},{9,5},{13,1},{2,14},{6,10},... | collective-permute-start | bytes 405512 | tf_op jit(solution)/shard_map/ppermute | solution.py:441
  158.3 7.6 %collective-permute-start.40 = (f32[264,128]{1,0:T(8,128)S(1)}, f32[264,128]{1,0:T(8,128)S(1)}, u32[]{:S(2)}, u32[]{:S(2)}) collective-permute-start(f32[264,128]{1,0:T(8,128)S(1)} %get-tuple-element.127.refs_3_.refs_15_), channel_id=1, source_target_pairs={{0,12},{4,8},{8,4},{12,0},{1,13},{5,9},{9,5},{13,1},{2,14},{6,10},... | collective-permute-start | bytes 405512 | tf_op jit(solution)/shard_map/ppermute | solution.py:441
  160.4 11.5 %collective-permute-start.39 = (f32[264,128]{1,0:T(8,128)S(1)}, f32[264,128]{1,0:T(8,128)S(1)}, u32[]{:S(2)}, u32[]{:S(2)}) collective-permute-start(f32[264,128]{1,0:T(8,128)S(1)} %get-tuple-element.127.refs_3_.refs_15_), channel_id=1, source_target_pairs={{0,8},{4,12},{8,0},{12,4},{1,9},{5,13},{9,1},{13,5},{2,10},{6,14},... | collective-permute-start | bytes 405512 | tf_op jit(solution)/shard_map/ppermute | solution.py:441
  165.9 6.0 %collective-permute-start.38 = (f32[264,128]{1,0:T(8,128)S(1)}, f32[264,128]{1,0:T(8,128)S(1)}, u32[]{:S(2)}, u32[]{:S(2)}) collective-permute-start(f32[264,128]{1,0:T(8,128)S(1)} %get-tuple-element.127.refs_3_.refs_15_), channel_id=1, source_target_pairs={{0,4},{4,0},{8,12},{12,8},{1,5},{5,1},{9,13},{13,9},{2,6},{6,2},{1... | collective-permute-start | bytes 405512 | tf_op jit(solution)/shard_map/ppermute | solution.py:441
  174.6 5.7 %collective-permute-start.41 = (f32[392,128]{1,0:T(8,128)S(1)}, f32[392,128]{1,0:T(8,128)S(1)}, u32[]{:S(2)}, u32[]{:S(2)}) collective-permute-start(f32[392,128]{1,0:T(8,128)S(1)} %get-tuple-element.128.refs_0_), channel_id=1, source_target_pairs={{0,2},{1,3},{2,0},{3,1},{4,6},{5,7},{6,4},{7,5},{8,10},{9,11},{10,... | collective-permute-start | bytes 602120 | tf_op jit(solution)/shard_map/ppermute | solution.py:435
  180.5 5.4 %collective-permute-start.44 = (f32[8,128]{1,0:T(8,128)S(1)}, f32[8,128]{1,0:T(8,128)S(1)}, u32[]{:S(2)}, u32[]{:S(2)}) collective-permute-start(f32[8,128]{1,0:T(8,128)S(1)} %get-tuple-element.130.refs_0_), channel_id=1, source_target_pairs={{0,12},{4,8},{8,4},{12,0},{1,13},{5,9},{9,5},{13,1},{2,14},{6,10},... | collective-permute-start | bytes 12296 | tf_op jit(solution)/shard_map/ppermute | solution.py:441
  182.2 4.5 %collective-permute-start.43 = (f32[8,128]{1,0:T(8,128)S(1)}, f32[8,128]{1,0:T(8,128)S(1)}, u32[]{:S(2)}, u32[]{:S(2)}) collective-permute-start(f32[8,128]{1,0:T(8,128)S(1)} %get-tuple-element.130.refs_0_), channel_id=1, source_target_pairs={{0,8},{4,12},{8,0},{12,4},{1,9},{5,13},{9,1},{13,5},{2,10},{6,14},... | collective-permute-start | bytes 12296 | tf_op jit(solution)/shard_map/ppermute | solution.py:441
  182.5 4.2 %collective-permute-start.42 = (f32[8,128]{1,0:T(8,128)S(1)}, f32[8,128]{1,0:T(8,128)S(1)}, u32[]{:S(2)}, u32[]{:S(2)}) collective-permute-start(f32[8,128]{1,0:T(8,128)S(1)} %get-tuple-element.130.refs_0_), channel_id=1, source_target_pairs={{0,4},{4,0},{8,12},{12,8},{1,5},{5,1},{9,13},{13,9},{2,6},{6,2},{1... | collective-permute-start | bytes 12296 | tf_op jit(solution)/shard_map/ppermute | solution.py:441
  186.9 2.0 %collective-permute-start.45 = (f32[1024,128]{1,0:T(8,128)S(1)}, f32[1024,128]{1,0:T(8,128)S(1)}, u32[]{:S(2)}, u32[]{:S(2)}) collective-permute-start(f32[1024,128]{1,0:T(8,128)S(1)} %shard_map.150.refs_1_), channel_id=1, source_target_pairs={{0,1},{1,0},{2,3},{3,2},{4,5},{5,4},{6,7},{7,6},{8,9},{9,8},{10,11... | collective-permute-start | bytes 1572872 | tf_op jit(solution)/shard_map/ppermute | solution.py:432

commit v10 on v8

--- a/solution.py
+++ b/solution.py
@@ -430,6 +430,7 @@
         return [v] + [lax.ppermute(v, "col", [(c, c ^ (2 * k)) for c in range(n_col)]) for k in range(1, nx)]
 
     ks = range(1, n)
+    scalar_ks = (1, 3, 2) if n == 4 else ks
 
     def over_row(v, k):
         return lax.ppermute(v, "row", [(i, i ^ k) for i in range(n)])
@@ -552,7 +553,7 @@
             [slab_shape, tile_shape, tile_shape],
             [*to_x(msg), scal, ad],
         )
-        shares = to_all_rows(share)
+        shares = [share] + [over_row(share, k) for k in scalar_ks]
         state = [*shares, keep, step, ax, ad, ad2, z, y, lower, upper, x, msg1, msg2]
         if outer + 1 < ADMM_ITERS:
             *pieces, x, z, y, ax, ppx = call(

time: 190 us -> 188 us (0.989)
  no operation moved by 1% of the time
where the time goes in v10:
time: 188 us
  waiting for transfers between devices  89.9 us (48%)
  starting transfers between devices  62.2 us (33%)
  Pallas kernels  30.3 us (16%)
  local copies, waits for them, and re-layouts  4.15 us (2%)
    ppermute x33, waiting for transfers between devices, over_row(): return lax.ppermute(v, 'row', [(i, i ^ k) for i in range(n)])  66 us
    ppermute x33, starting transfers between devices, over_row(): return lax.ppermute(v, 'row', [(i, i ^ k) for i in range(n)])  52.8 us
    pallas_call x22, Pallas kernels, call(): pl.pallas_call(run, out_shape=[jax.ShapeDtypeStruct(s, d) for s, d in out...  30.3 us
    ppermute x5, waiting for transfers between devices, to_x(): lax.ppermute(v, 'col', [(c, c ^ 2 * k) for c in range(n_col)])  19.4 us
    ppermute x5, starting transfers between devices, to_x(): lax.ppermute(v, 'col', [(c, c ^ 2 * k) for c in range(n_col)])  7.55 us
    ppermute x8, waiting for transfers between devices, to_core(): return lax.ppermute(v, 'col', [(c, c ^ 1) for c in range(n_col)])  4.49 us
    unnamed x23, local copies, waits for them, and re-layouts  3.82 us
  transfers between devices with their start and end apart: 46, of which 30 were waited for; matrix products, arithmetic and copies ran while one was open for 1% of the time, Pallas kernels for 3%

profile of v10, /device:TPU:0, one launch (start us, length us, event | category | flops | bytes accessed | tf_op | source)
XLA Modules:
  0.0 187.8 jit_solution(9066926418688752154)
XLA Ops:
  1.1 4.7 %collective-permute-start.3 = (f32[256,128]{1,0:T(8,128)}, f32[256,128]{1,0:T(8,128)S(1)}, u32[]{:S(2)}, u32[]{:S(2)}) collective-permute-start(f32[256,128]{1,0:T(8,128)} %refs_1_.3), channel_id=1, source_target_pairs={{0,12},{4,8},{8,4},{12,0},{1,13},{5,9},{9,5},{13,1},{2,14},{6,10},... | collective-permute-start | bytes 393224 | tf_op jit(solution)/shard_map/ppermute | solution.py:436
  7.3 1.4 copy-done
  10.3 1.5 shard_map.130
  11.9 5.8 %collective-permute-done.2.refs_5_ = f32[256,128]{1,0:T(8,128)S(1)} collective-permute-done((f32[256,128]{1,0:T(8,128)}, f32[256,128]{1,0:T(8,128)S(1)}, u32[]{:S(2)}, u32[]{:S(2)}) %collective-permute-start.2) | collective-permute-done | bytes 131104 | tf_op jit(solution)/shard_map/ppermute | solution.py:436
  17.8 1.4 shard_map.131
  19.7 1.1 collective-permute-done.4.refs_1_
  20.9 1.6 collective-permute-start.5
  22.6 1.3 shard_map.133
  24.1 1.4 shard_map.134
  25.5 2.4 %collective-permute-done.5.refs_3_ = f32[384,128]{1,0:T(8,128)S(1)} collective-permute-done((f32[384,128]{1,0:T(8,128)S(1)}, f32[384,128]{1,0:T(8,128)S(1)}, u32[]{:S(2)}, u32[]{:S(2)}) %collective-permute-start.5) | collective-permute-done | bytes 196640 | tf_op jit(solution)/shard_map/ppermute | solution.py:430
  27.9 2.5 %shard_map.135 = (f32[272,128]{1,0:T(8,128)S(1)}, f32[272,128]{1,0:T(8,128)S(1)}, f32[272,128]{1,0:T(8,128)S(1)}, f32[272,128]{1,0:T(8,128)S(1)}, f32[384,128]{1,0:T(8,128)S(1)}) custom-call(s32[2]{0:T(128)S(1)} %pad_add_fusion.refs_0_, s32[4]{0:T(128)S(1)} %pad_add_fusion.2.refs_1_, f32[384,128]{1,0:T(8,128)S(1)} %get-tuple-element.77.refs_0_.refs_2_, ...), custom_call_target="tpu_custom_call" | custom-call | flops 805306368 | bytes 7217152 | tf_op jit(solution)/shard_map/pallas_call | solution.py:34
  30.5 3.0 %collective-permute-start.9 = (f32[272,128]{1,0:T(8,128)S(1)}, f32[272,128]{1,0:T(8,128)S(1)}, u32[]{:S(2)}, u32[]{:S(2)}) collective-permute-start(f32[272,128]{1,0:T(8,128)S(1)} %get-tuple-element.89), channel_id=1, source_target_pairs={{0,8},{4,12},{8,0},{12,4},{1,9},{5,13},{9,1},{13,5},{2,10},{6,14},... | collective-permute-start | bytes 417800 | tf_op jit(solution)/shard_map/ppermute | solution.py:436
  33.6 1.3 collective-permute-start.10
  38.2 5.8 %collective-permute-done.9.refs_3_ = f32[272,128]{1,0:T(8,128)S(1)} collective-permute-done((f32[272,128]{1,0:T(8,128)S(1)}, f32[272,128]{1,0:T(8,128)S(1)}, u32[]{:S(2)}, u32[]{:S(2)}) %collective-permute-start.9) | collective-permute-done | bytes 139296 | tf_op jit(solution)/shard_map/ppermute | solution.py:436
  44.9 2.4 %collective-permute-start.16 = (f32[264,128]{1,0:T(8,128)S(1)}, f32[264,128]{1,0:T(8,128)S(1)}, u32[]{:S(2)}, u32[]{:S(2)}) collective-permute-start(f32[264,128]{1,0:T(8,128)S(1)} %get-tuple-element.93.refs_3_.refs_5_.refs_16_), channel_id=1, source_target_pairs={{0,12},{4,8},{8,4},{12,0},{1,13},{5,9},{9,5},{13,1},{2,14},{6,10},... | collective-permute-start | bytes 405512 | tf_op jit(solution)/shard_map/ppermute | solution.py:436
  47.3 2.2 %collective-permute-start.15 = (f32[264,128]{1,0:T(8,128)S(1)}, f32[264,128]{1,0:T(8,128)S(1)}, u32[]{:S(2)}, u32[]{:S(2)}) collective-permute-start(f32[264,128]{1,0:T(8,128)S(1)} %get-tuple-element.93.refs_3_.refs_5_.refs_16_), channel_id=1, source_target_pairs={{0,8},{4,12},{8,0},{12,4},{1,9},{5,13},{9,1},{13,5},{2,10},{6,14},... | collective-permute-start | bytes 405512 | tf_op jit(solution)/shard_map/ppermute | solution.py:436
  50.1 3.1 %collective-permute-done.16.refs_6_ = f32[264,128]{1,0:T(8,128)S(1)} collective-permute-done((f32[264,128]{1,0:T(8,128)S(1)}, f32[264,128]{1,0:T(8,128)S(1)}, u32[]{:S(2)}, u32[]{:S(2)}) %collective-permute-start.16) | collective-permute-done | bytes 135200 | tf_op jit(solution)/shard_map/ppermute | solution.py:436
  53.2 4.7 %collective-permute-done.15.refs_5_ = f32[264,128]{1,0:T(8,128)S(1)} collective-permute-done((f32[264,128]{1,0:T(8,128)S(1)}, f32[264,128]{1,0:T(8,128)S(1)}, u32[]{:S(2)}, u32[]{:S(2)}) %collective-permute-start.15) | collective-permute-done | bytes 135200 | tf_op jit(solution)/shard_map/ppermute | solution.py:436
  57.8 2.0 %shard_map.138 = (f32[392,128]{1,0:T(8,128)S(1)}, f32[256,128]{1,0:T(8,128)S(1)}) custom-call(s32[2]{0:T(128)S(1)} %pad_add_fusion.refs_0_, s32[4]{0:T(128)S(1)} %pad_add_fusion.2.refs_1_, s32[48]{0:T(128)S(1)} %pad_add_fusion.3.refs_2_, f32[264,128]{1,0:T(8,128)S(1)} %get-tuple-element.93.refs_3_.refs_5_.refs_16_, ...), custom_call_target="tpu_custom_call" | custom-call | flops 805306368 | bytes 4210688 | tf_op jit(solution)/shard_map/pallas_call | solution.py:34
  59.9 1.5 collective-permute-start.17
  61.4 4.2 %collective-permute-done.17.refs_3_ = f32[392,128]{1,0:T(8,128)S(1)} collective-permute-done((f32[392,128]{1,0:T(8,128)S(1)}, f32[392,128]{1,0:T(8,128)S(1)}, u32[]{:S(2)}, u32[]{:S(2)}) %collective-permute-start.17) | collective-permute-done | bytes 200736 | tf_op jit(solution)/shard_map/ppermute | solution.py:430
  65.6 2.5 %shard_map.139 = (f32[264,128]{1,0:T(8,128)S(1)}, f32[264,128]{1,0:T(8,128)S(1)}, f32[264,128]{1,0:T(8,128)S(1)}, f32[264,128]{1,0:T(8,128)S(1)}, f32[384,128]{1,0:T(8,128)S(1)}, /*index=5*/f32[8,128]{1,0:T(8,128)S(1)}) custom-call(s32[2]{0:T(128)S(1)} %pad_add_fusion.refs_0_, s32[4]{0:T(128)S(1)} %pad_add_fusion.2.refs_1_, ...), custom_call_target="tpu_custom_call" | custom-call | flops 805306368 | bytes 6823936 | tf_op jit(solution)/shard_map/pallas_call | solution.py:34
  68.3 3.0 %collective-permute-start.19 = (f32[264,128]{1,0:T(8,128)S(1)}, f32[264,128]{1,0:T(8,128)S(1)}, u32[]{:S(2)}, u32[]{:S(2)}) collective-permute-start(f32[264,128]{1,0:T(8,128)S(1)} %get-tuple-element.101), channel_id=1, source_target_pairs={{0,8},{4,12},{8,0},{12,4},{1,9},{5,13},{9,1},{13,5},{2,10},{6,14},... | collective-permute-start | bytes 405512 | tf_op jit(solution)/shard_map/ppermute | solution.py:436
  71.3 1.3 collective-permute-start.20
  72.6 2.6 %collective-permute-done.18.refs_1_ = f32[264,128]{1,0:T(8,128)S(1)} collective-permute-done((f32[264,128]{1,0:T(8,128)S(1)}, f32[264,128]{1,0:T(8,128)S(1)}, u32[]{:S(2)}, u32[]{:S(2)}) %collective-permute-start.18) | collective-permute-done | bytes 135200 | tf_op jit(solution)/shard_map/ppermute | solution.py:436
  75.3 3.7 %collective-permute-done.19.refs_2_ = f32[264,128]{1,0:T(8,128)S(1)} collective-permute-done((f32[264,128]{1,0:T(8,128)S(1)}, f32[264,128]{1,0:T(8,128)S(1)}, u32[]{:S(2)}, u32[]{:S(2)}) %collective-permute-start.19) | collective-permute-done | bytes 135200 | tf_op jit(solution)/shard_map/ppermute | solution.py:436
  79.1 4.0 %collective-permute-start.23 = (f32[264,128]{1,0:T(8,128)S(1)}, f32[264,128]{1,0:T(8,128)S(1)}, u32[]{:S(2)}, u32[]{:S(2)}) collective-permute-start(f32[264,128]{1,0:T(8,128)S(1)} %get-tuple-element.106.refs_3_.refs_17_), channel_id=1, source_target_pairs={{0,12},{4,8},{8,4},{12,0},{1,13},{5,9},{9,5},{13,1},{2,14},{6,10},... | collective-permute-start | bytes 405512 | tf_op jit(solution)/shard_map/ppermute | solution.py:436
  83.1 2.9 %collective-permute-start.22 = (f32[264,128]{1,0:T(8,128)S(1)}, f32[264,128]{1,0:T(8,128)S(1)}, u32[]{:S(2)}, u32[]{:S(2)}) collective-permute-start(f32[264,128]{1,0:T(8,128)S(1)} %get-tuple-element.106.refs_3_.refs_17_), channel_id=1, source_target_pairs={{0,8},{4,12},{8,0},{12,4},{1,9},{5,13},{9,1},{13,5},{2,10},{6,14},... | collective-permute-start | bytes 405512 | tf_op jit(solution)/shard_map/ppermute | solution.py:436
  86.4 1.2 collective-permute-done.23.refs_6_
  87.5 4.4 %collective-permute-done.22.refs_5_ = f32[264,128]{1,0:T(8,128)S(1)} collective-permute-done((f32[264,128]{1,0:T(8,128)S(1)}, f32[264,128]{1,0:T(8,128)S(1)}, u32[]{:S(2)}, u32[]{:S(2)}) %collective-permute-start.22) | collective-permute-done | bytes 135200 | tf_op jit(solution)/shard_map/ppermute | solution.py:436
  92.0 2.0 %shard_map.141 = (f32[392,128]{1,0:T(8,128)S(1)}, f32[256,128]{1,0:T(8,128)S(1)}) custom-call(s32[2]{0:T(128)S(1)} %pad_add_fusion.refs_0_, s32[4]{0:T(128)S(1)} %pad_add_fusion.2.refs_1_, s32[48]{0:T(128)S(1)} %pad_add_fusion.3.refs_2_, f32[264,128]{1,0:T(8,128)S(1)} %get-tuple-element.106.refs_3_.refs_17_, f32[264,128]{1,0:T(8,128)S(1)} %collective-permute-done.21.refs_4_, ...), custom_call_target="tpu_custom_call" | custom-call | flops 805306368 | bytes 4341760 | tf_op jit(solution)/shard_map/pallas_call | solution.py:34
  94.0 1.5 collective-permute-start.24
  95.5 4.2 %collective-permute-done.24.refs_1_ = f32[392,128]{1,0:T(8,128)S(1)} collective-permute-done((f32[392,128]{1,0:T(8,128)S(1)}, f32[392,128]{1,0:T(8,128)S(1)}, u32[]{:S(2)}, u32[]{:S(2)}) %collective-permute-start.24) | collective-permute-done | bytes 200736 | tf_op jit(solution)/shard_map/ppermute | solution.py:430
  100.0 1.8 collective-permute-start.27
  101.8 1.5 collective-permute-start.26
  104.5 2.9 %collective-permute-done.26.refs_4_ = f32[8,128]{1,0:T(8,128)S(1)} collective-permute-done((f32[8,128]{1,0:T(8,128)S(1)}, f32[8,128]{1,0:T(8,128)S(1)}, u32[]{:S(2)}, u32[]{:S(2)}) %collective-permute-start.26) | collective-permute-done | bytes 4128 | tf_op jit(solution)/shard_map/ppermute | solution.py:436
  107.3 3.4 %shard_map.143 = (f32[256,128]{1,0:T(8,128)S(1)}, f32[256,128]{1,0:T(8,128)S(1)}, f32[256,128]{1,0:T(8,128)S(1)}, f32[256,128]{1,0:T(8,128)S(1)}, f32[256,128]{1...) custom-call(s32[2]{0:T(128)S(1)} %pad_add_fusion.refs_0_, ...), custom_call_target="tpu_custom_call" | custom-call | flops 805306368 | bytes 8486912 | tf_op jit(solution)/shard_map/pallas_call | solution.py:34
  110.9 2.4 %collective-permute-start.29 = (f32[256,128]{1,0:T(8,128)S(1)}, f32[256,128]{1,0:T(8,128)S(1)}, u32[]{:S(2)}, u32[]{:S(2)}) collective-permute-start(f32[256,128]{1,0:T(8,128)S(1)} %get-tuple-element.119), channel_id=1, source_target_pairs={{0,8},{4,12},{8,0},{12,4},{1,9},{5,13},{9,1},{13,5},{2,10},{6,14},... | collective-permute-start | bytes 393224 | tf_op jit(solution)/shard_map/ppermute | solution.py:436
  113.2 2.0 %collective-permute-start.30 = (f32[256,128]{1,0:T(8,128)S(1)}, f32[256,128]{1,0:T(8,128)S(1)}, u32[]{:S(2)}, u32[]{:S(2)}) collective-permute-start(f32[256,128]{1,0:T(8,128)S(1)} %get-tuple-element.120), channel_id=1, source_target_pairs={{0,12},{4,8},{8,4},{12,0},{1,13},{5,9},{9,5},{13,1},{2,14},{6,10},... | collective-permute-start | bytes 393224 | tf_op jit(solution)/shard_map/ppermute | solution.py:436
  115.2 1.8 collective-permute-done.28.refs_2_
  117.0 6.5 %collective-permute-done.29.refs_3_ = f32[256,128]{1,0:T(8,128)S(1)} collective-permute-done((f32[256,128]{1,0:T(8,128)S(1)}, f32[256,128]{1,0:T(8,128)S(1)}, u32[]{:S(2)}, u32[]{:S(2)}) %collective-permute-start.29) | collective-permute-done | bytes 131104 | tf_op jit(solution)/shard_map/ppermute | solution.py:436
  124.2 3.2 %collective-permute-start.33 = (f32[264,128]{1,0:T(8,128)S(1)}, f32[264,128]{1,0:T(8,128)S(1)}, u32[]{:S(2)}, u32[]{:S(2)}) collective-permute-start(f32[264,128]{1,0:T(8,128)S(1)} %get-tuple-element.122.refs_3_.refs_5_.refs_14_), channel_id=1, source_target_pairs={{0,12},{4,8},{8,4},{12,0},{1,13},{5,9},{9,5},{13,1},{2,14},{6,10},... | collective-permute-start | bytes 405512 | tf_op jit(solution)/shard_map/ppermute | solution.py:436
  127.4 1.8 collective-permute-start.32
  129.7 1.4 collective-permute-done.33.refs_6_
  131.1 4.3 %collective-permute-done.32.refs_5_ = f32[264,128]{1,0:T(8,128)S(1)} collective-permute-done((f32[264,128]{1,0:T(8,128)S(1)}, f32[264,128]{1,0:T(8,128)S(1)}, u32[]{:S(2)}, u32[]{:S(2)}) %collective-permute-start.32) | collective-permute-done | bytes 135200 | tf_op jit(solution)/shard_map/ppermute | solution.py:436
  135.4 2.0 %shard_map.145 = (f32[392,128]{1,0:T(8,128)S(1)}, f32[256,128]{1,0:T(8,128)S(1)}) custom-call(s32[2]{0:T(128)S(1)} %pad_add_fusion.refs_0_, s32[4]{0:T(128)S(1)} %pad_add_fusion.2.refs_1_, s32[48]{0:T(128)S(1)} %pad_add_fusion.3.refs_2_, f32[264,128]{1,0:T(8,128)S(1)} %get-tuple-element.122.refs_3_.refs_5_.refs_14_, ...), custom_call_target="tpu_custom_call" | custom-call | flops 805306368 | bytes 4210688 | tf_op jit(solution)/shard_map/pallas_call | solution.py:34
  137.5 1.5 collective-permute-start.34
  138.9 4.3 %collective-permute-done.34.refs_3_ = f32[392,128]{1,0:T(8,128)S(1)} collective-permute-done((f32[392,128]{1,0:T(8,128)S(1)}, f32[392,128]{1,0:T(8,128)S(1)}, u32[]{:S(2)}, u32[]{:S(2)}) %collective-permute-start.34) | collective-permute-done | bytes 200736 | tf_op jit(solution)/shard_map/ppermute | solution.py:430
  143.2 2.5 %shard_map.146 = (f32[264,128]{1,0:T(8,128)S(1)}, f32[264,128]{1,0:T(8,128)S(1)}, f32[264,128]{1,0:T(8,128)S(1)}, f32[264,128]{1,0:T(8,128)S(1)}, f32[384,128]{1,0:T(8,128)S(1)}, /*index=5*/f32[8,128]{1,0:T(8,128)S(1)}) custom-call(s32[2]{0:T(128)S(1)} %pad_add_fusion.refs_0_, s32[4]{0:T(128)S(1)} %pad_add_fusion.2.refs_1_, ...), custom_call_target="tpu_custom_call" | custom-call | flops 805306368 | bytes 6823936 | tf_op jit(solution)/shard_map/pallas_call | solution.py:34
  146.2 3.4 %collective-permute-start.36 = (f32[264,128]{1,0:T(8,128)S(1)}, f32[264,128]{1,0:T(8,128)S(1)}, u32[]{:S(2)}, u32[]{:S(2)}) collective-permute-start(f32[264,128]{1,0:T(8,128)S(1)} %get-tuple-element.127), channel_id=1, source_target_pairs={{0,8},{4,12},{8,0},{12,4},{1,9},{5,13},{9,1},{13,5},{2,10},{6,14},... | collective-permute-start | bytes 405512 | tf_op jit(solution)/shard_map/ppermute | solution.py:436
  150.2 5.0 %collective-permute-done.35.refs_1_ = f32[264,128]{1,0:T(8,128)S(1)} collective-permute-done((f32[264,128]{1,0:T(8,128)S(1)}, f32[264,128]{1,0:T(8,128)S(1)}, u32[]{:S(2)}, u32[]{:S(2)}) %collective-permute-start.35) | collective-permute-done | bytes 135200 | tf_op jit(solution)/shard_map/ppermute | solution.py:436
  155.2 2.7 %collective-permute-done.36.refs_2_ = f32[264,128]{1,0:T(8,128)S(1)} collective-permute-done((f32[264,128]{1,0:T(8,128)S(1)}, f32[264,128]{1,0:T(8,128)S(1)}, u32[]{:S(2)}, u32[]{:S(2)}) %collective-permute-start.36) | collective-permute-done | bytes 135200 | tf_op jit(solution)/shard_map/ppermute | solution.py:436
  158.1 2.8 %collective-permute-start.40 = (f32[264,128]{1,0:T(8,128)S(1)}, f32[264,128]{1,0:T(8,128)S(1)}, u32[]{:S(2)}, u32[]{:S(2)}) collective-permute-start(f32[264,128]{1,0:T(8,128)S(1)} %get-tuple-element.131.refs_3_.refs_15_), channel_id=1, source_target_pairs={{0,12},{4,8},{8,4},{12,0},{1,13},{5,9},{9,5},{13,1},{2,14},{6,10},... | collective-permute-start | bytes 405512 | tf_op jit(solution)/shard_map/ppermute | solution.py:436
  160.9 1.0 collective-permute-start.39
  162.5 2.5 %collective-permute-done.40.refs_6_ = f32[264,128]{1,0:T(8,128)S(1)} collective-permute-done((f32[264,128]{1,0:T(8,128)S(1)}, f32[264,128]{1,0:T(8,128)S(1)}, u32[]{:S(2)}, u32[]{:S(2)}) %collective-permute-start.40) | collective-permute-done | bytes 135200 | tf_op jit(solution)/shard_map/ppermute | solution.py:436
  165.0 4.2 %collective-permute-done.39.refs_5_ = f32[264,128]{1,0:T(8,128)S(1)} collective-permute-done((f32[264,128]{1,0:T(8,128)S(1)}, f32[264,128]{1,0:T(8,128)S(1)}, u32[]{:S(2)}, u32[]{:S(2)}) %collective-permute-start.39) | collective-permute-done | bytes 135200 | tf_op jit(solution)/shard_map/ppermute | solution.py:436
  169.2 2.6 %shard_map.148 = (f32[392,128]{1,0:T(8,128)S(1)}, f32[256,128]{1,0:T(8,128)}) custom-call(s32[2]{0:T(128)S(1)} %pad_add_fusion.refs_0_, s32[4]{0:T(128)S(1)} %pad_add_fusion.2.refs_1_, s32[48]{0:T(128)S(1)} %pad_add_fusion.3.refs_2_, f32[264,128]{1,0:T(8,128)S(1)} %get-tuple-element.131.refs_3_.refs_15_, f32[264,128]{1,0:T(8,128)S(1)} %collective-permute-done.38.refs_4_, ...), custom_call_target="tpu_custom_call" | custom-call | flops 805306368 | bytes 4341760 | tf_op jit(solution)/shard_map/pallas_call | solution.py:34
  171.9 1.5 collective-permute-start.41
  173.4 4.2 %collective-permute-done.41.refs_1_ = f32[392,128]{1,0:T(8,128)S(1)} collective-permute-done((f32[392,128]{1,0:T(8,128)S(1)}, f32[392,128]{1,0:T(8,128)S(1)}, u32[]{:S(2)}, u32[]{:S(2)}) %collective-permute-start.41) | collective-permute-done | bytes 200736 | tf_op jit(solution)/shard_map/ppermute | solution.py:430
  177.9 2.4 %collective-permute-start.43 = (f32[8,128]{1,0:T(8,128)S(1)}, f32[8,128]{1,0:T(8,128)S(1)}, u32[]{:S(2)}, u32[]{:S(2)}) collective-permute-start(f32[8,128]{1,0:T(8,128)S(1)} %get-tuple-element.134.refs_0_), channel_id=1, source_target_pairs={{0,12},{4,8},{8,4},{12,0},{1,13},{5,9},{9,5},{13,1},{2,14},{6,10},... | collective-permute-start | bytes 12296 | tf_op jit(solution)/shard_map/ppermute | solution.py:436
  181.3 1.0 collective-permute-done.44.refs_3_
  182.3 1.0 collective-permute-done.43.refs_2_
  184.2 1.9 %collective-permute-done.45.refs_2_ = f32[1024,128]{1,0:T(8,128)S(1)} collective-permute-done((f32[1024,128]{1,0:T(8,128)S(1)}, f32[1024,128]{1,0:T(8,128)S(1)}, u32[]{:S(2)}, u32[]{:S(2)}) %collective-permute-start.45) | collective-permute-done | bytes 524320 | tf_op jit(solution)/shard_map/ppermute | solution.py:427
  186.1 1.7 shard_map.151
  (82 shorter events, 16.6 us)
Async XLA Ops:
  0.6 23.4 %collective-permute-start.6 = (f32[24,128,128]{2,1,0:T(8,128)}, f32[24,128,128]{2,1,0:T(8,128)S(1)}, u32[]{:S(2)}, u32[]{:S(2)}) collective-permute-start(f32[24,128,128]{2,1,0:T(8,128)} %bitcast.6), channel_id=1, source_target_pairs={{0,1},{1,0},{2,3},{3,2},{4,5},{5,4},{6,7},{7,6},{8,9},{9,8},{10,11... | collective-permute-start | bytes 4718600 | tf_op jit(solution)/shard_map/ppermute | solution.py:427
  1.1 10.7 %collective-permute-start.3 = (f32[256,128]{1,0:T(8,128)}, f32[256,128]{1,0:T(8,128)S(1)}, u32[]{:S(2)}, u32[]{:S(2)}) collective-permute-start(f32[256,128]{1,0:T(8,128)} %refs_1_.3), channel_id=1, source_target_pairs={{0,12},{4,8},{8,4},{12,0},{1,13},{5,9},{9,5},{13,1},{2,14},{6,10},... | collective-permute-start | bytes 393224 | tf_op jit(solution)/shard_map/ppermute | solution.py:436
  5.8 11.9 %collective-permute-start.2 = (f32[256,128]{1,0:T(8,128)}, f32[256,128]{1,0:T(8,128)S(1)}, u32[]{:S(2)}, u32[]{:S(2)}) collective-permute-start(f32[256,128]{1,0:T(8,128)} %refs_1_.3), channel_id=1, source_target_pairs={{0,8},{4,12},{8,0},{12,4},{1,9},{5,13},{9,1},{13,5},{2,10},{6,14},... | collective-permute-start | bytes 393224 | tf_op jit(solution)/shard_map/ppermute | solution.py:436
  5.8 11.9 %collective-permute-start.1 = (f32[256,128]{1,0:T(8,128)}, f32[256,128]{1,0:T(8,128)S(1)}, u32[]{:S(2)}, u32[]{:S(2)}) collective-permute-start(f32[256,128]{1,0:T(8,128)} %refs_1_.3), channel_id=1, source_target_pairs={{0,4},{4,0},{8,12},{12,8},{1,5},{5,1},{9,13},{13,9},{2,6},{6,2},{1... | collective-permute-start | bytes 393224 | tf_op jit(solution)/shard_map/ppermute | solution.py:436
  7.3 1.4 copy-start
  8.7 0.9 copy-start.5
  9.7 0.7 copy-start.8
  10.3 7.4 %copy-start.6 = (f32[256,128]{1,0:T(8,128)S(1)}, f32[256,128]{1,0:T(8,128)}, u32[]{:S(2)}) copy-start(f32[256,128]{1,0:T(8,128)} %refs_1_.3) | copy-start | bytes 393220
  17.7 4.7 %copy-start.9 = (s32[1,1,2]{2,1,0:T(1,128)S(1)}, s32[1,1,2]{2,1,0:T(1,128)}, u32[]{:S(2)}) copy-start(s32[1,1,2]{2,1,0:T(1,128)} %param.21) | copy-start | bytes 28
  17.7 4.8 %copy-start.1 = (f32[768,128]{1,0:T(8,128)S(1)}, f32[768,128]{1,0:T(8,128)}, u32[]{:S(2)}) copy-start(f32[768,128]{1,0:T(8,128)} %refs_1_.2) | copy-start | bytes 1179652
  17.7 4.8 %copy-start.2 = (f32[768,128]{1,0:T(8,128)S(1)}, f32[768,128]{1,0:T(8,128)}, u32[]{:S(2)}) copy-start(f32[768,128]{1,0:T(8,128)} %refs_2_.1) | copy-start | bytes 1179652
  17.8 4.8 %copy-start.3 = (f32[768,128]{1,0:T(8,128)S(1)}, f32[768,128]{1,0:T(8,128)}, u32[]{:S(2)}) copy-start(f32[768,128]{1,0:T(8,128)} %refs_3_.4) | copy-start | bytes 1179652
  17.8 4.8 %copy-start.4 = (f32[768,128]{1,0:T(8,128)S(1)}, f32[768,128]{1,0:T(8,128)}, u32[]{:S(2)}) copy-start(f32[768,128]{1,0:T(8,128)} %refs_4_.1) | copy-start | bytes 1179652
  19.2 1.7 collective-permute-start.4
  19.2 4.8 %collective-permute-start.7 = (f32[4,128,128]{2,1,0:T(8,128)S(1)}, f32[4,128,128]{2,1,0:T(8,128)S(1)}, u32[]{:S(2)}, u32[]{:S(2)}) collective-permute-start(f32[4,128,128]{2,1,0:T(8,128)S(1)} %bitcast.9), channel_id=1, source_target_pairs={{0,1},{1,0},{2,3},{3,2},{4,5},{5,4},{6,7},{7,6},{8,9},{9,8},{10,11... | collective-permute-start | bytes 786440 | tf_op jit(solution)/shard_map/ppermute | solution.py:427
  20.9 7.0 %collective-permute-start.5 = (f32[384,128]{1,0:T(8,128)S(1)}, f32[384,128]{1,0:T(8,128)S(1)}, u32[]{:S(2)}, u32[]{:S(2)}) collective-permute-start(f32[384,128]{1,0:T(8,128)S(1)} %get-tuple-element.77.refs_0_.refs_2_), channel_id=1, source_target_pairs={{0,2},{1,3},{2,0},{3,1},{4,6},{5,7},{6,4},{7,5},{8,10},{9,11},{10,... | collective-permute-start | bytes 589832 | tf_op jit(solution)/shard_map/ppermute | solution.py:430
  22.5 1.4 collective-permute-start
  27.9 7.0 %copy-start.10 = (f32[256]{0:T(256)S(1)}, f32[256]{0:T(256)}, u32[]{:S(2)}) copy-start(f32[256]{0:T(256)} %param.13) | copy-start | bytes 3076
  27.9 7.0 %copy-start.7 = (f32[256,128]{1,0:T(8,128)S(1)}, f32[256,128]{1,0:T(8,128)}, u32[]{:S(2)}) copy-start(f32[256,128]{1,0:T(8,128)} %refs_3_.5) | copy-start | bytes 393220
  30.5 7.7 %collective-permute-start.8 = (f32[272,128]{1,0:T(8,128)S(1)}, f32[272,128]{1,0:T(8,128)S(1)}, u32[]{:S(2)}, u32[]{:S(2)}) collective-permute-start(f32[272,128]{1,0:T(8,128)S(1)} %get-tuple-element.88), channel_id=1, source_target_pairs={{0,4},{4,0},{8,12},{12,8},{1,5},{5,1},{9,13},{13,9},{2,6},{6,2},{1... | collective-permute-start | bytes 417800 | tf_op jit(solution)/shard_map/ppermute | solution.py:436
  30.5 13.4 %collective-permute-start.9 = (f32[272,128]{1,0:T(8,128)S(1)}, f32[272,128]{1,0:T(8,128)S(1)}, u32[]{:S(2)}, u32[]{:S(2)}) collective-permute-start(f32[272,128]{1,0:T(8,128)S(1)} %get-tuple-element.89), channel_id=1, source_target_pairs={{0,8},{4,12},{8,0},{12,4},{1,9},{5,13},{9,1},{13,5},{2,10},{6,14},... | collective-permute-start | bytes 417800 | tf_op jit(solution)/shard_map/ppermute | solution.py:436
  33.6 10.4 %collective-permute-start.10 = (f32[272,128]{1,0:T(8,128)S(1)}, f32[272,128]{1,0:T(8,128)S(1)}, u32[]{:S(2)}, u32[]{:S(2)}) collective-permute-start(f32[272,128]{1,0:T(8,128)S(1)} %get-tuple-element.90), channel_id=1, source_target_pairs={{0,12},{4,8},{8,4},{12,0},{1,13},{5,9},{9,5},{13,1},{2,14},{6,10},... | collective-permute-start | bytes 417800 | tf_op jit(solution)/shard_map/ppermute | solution.py:436
  34.9 1.1 collective-permute-start.13
  34.9 1.6 collective-permute-start.12
  36.1 1.3 collective-permute-start.11
  44.9 8.3 %collective-permute-start.16 = (f32[264,128]{1,0:T(8,128)S(1)}, f32[264,128]{1,0:T(8,128)S(1)}, u32[]{:S(2)}, u32[]{:S(2)}) collective-permute-start(f32[264,128]{1,0:T(8,128)S(1)} %get-tuple-element.93.refs_3_.refs_5_.refs_16_), channel_id=1, source_target_pairs={{0,12},{4,8},{8,4},{12,0},{1,13},{5,9},{9,5},{13,1},{2,14},{6,10},... | collective-permute-start | bytes 405512 | tf_op jit(solution)/shard_map/ppermute | solution.py:436
  47.3 10.5 %collective-permute-start.15 = (f32[264,128]{1,0:T(8,128)S(1)}, f32[264,128]{1,0:T(8,128)S(1)}, u32[]{:S(2)}, u32[]{:S(2)}) collective-permute-start(f32[264,128]{1,0:T(8,128)S(1)} %get-tuple-element.93.refs_3_.refs_5_.refs_16_), channel_id=1, source_target_pairs={{0,8},{4,12},{8,0},{12,4},{1,9},{5,13},{9,1},{13,5},{2,10},{6,14},... | collective-permute-start | bytes 405512 | tf_op jit(solution)/shard_map/ppermute | solution.py:436
  49.5 8.3 %collective-permute-start.14 = (f32[264,128]{1,0:T(8,128)S(1)}, f32[264,128]{1,0:T(8,128)S(1)}, u32[]{:S(2)}, u32[]{:S(2)}) collective-permute-start(f32[264,128]{1,0:T(8,128)S(1)} %get-tuple-element.93.refs_3_.refs_5_.refs_16_), channel_id=1, source_target_pairs={{0,4},{4,0},{8,12},{12,8},{1,5},{5,1},{9,13},{13,9},{2,6},{6,2},{1... | collective-permute-start | bytes 405512 | tf_op jit(solution)/shard_map/ppermute | solution.py:436
  59.9 5.8 %collective-permute-start.17 = (f32[392,128]{1,0:T(8,128)S(1)}, f32[392,128]{1,0:T(8,128)S(1)}, u32[]{:S(2)}, u32[]{:S(2)}) collective-permute-start(f32[392,128]{1,0:T(8,128)S(1)} %get-tuple-element.97.refs_2_), channel_id=1, source_target_pairs={{0,2},{1,3},{2,0},{3,1},{4,6},{5,7},{6,4},{7,5},{8,10},{9,11},{10,... | collective-permute-start | bytes 602120 | tf_op jit(solution)/shard_map/ppermute | solution.py:430
  68.2 7.1 %collective-permute-start.18 = (f32[264,128]{1,0:T(8,128)S(1)}, f32[264,128]{1,0:T(8,128)S(1)}, u32[]{:S(2)}, u32[]{:S(2)}) collective-permute-start(f32[264,128]{1,0:T(8,128)S(1)} %get-tuple-element.100), channel_id=1, source_target_pairs={{0,4},{4,0},{8,12},{12,8},{1,5},{5,1},{9,13},{13,9},{2,6},{6,2},{1... | collective-permute-start | bytes 405512 | tf_op jit(solution)/shard_map/ppermute | solution.py:436
  68.3 10.7 %collective-permute-start.19 = (f32[264,128]{1,0:T(8,128)S(1)}, f32[264,128]{1,0:T(8,128)S(1)}, u32[]{:S(2)}, u32[]{:S(2)}) collective-permute-start(f32[264,128]{1,0:T(8,128)S(1)} %get-tuple-element.101), channel_id=1, source_target_pairs={{0,8},{4,12},{8,0},{12,4},{1,9},{5,13},{9,1},{13,5},{2,10},{6,14},... | collective-permute-start | bytes 405512 | tf_op jit(solution)/shard_map/ppermute | solution.py:436
  71.3 7.6 %collective-permute-start.20 = (f32[264,128]{1,0:T(8,128)S(1)}, f32[264,128]{1,0:T(8,128)S(1)}, u32[]{:S(2)}, u32[]{:S(2)}) collective-permute-start(f32[264,128]{1,0:T(8,128)S(1)} %get-tuple-element.102), channel_id=1, source_target_pairs={{0,12},{4,8},{8,4},{12,0},{1,13},{5,9},{9,5},{13,1},{2,14},{6,10},... | collective-permute-start | bytes 405512 | tf_op jit(solution)/shard_map/ppermute | solution.py:436
  79.1 8.5 %collective-permute-start.23 = (f32[264,128]{1,0:T(8,128)S(1)}, f32[264,128]{1,0:T(8,128)S(1)}, u32[]{:S(2)}, u32[]{:S(2)}) collective-permute-start(f32[264,128]{1,0:T(8,128)S(1)} %get-tuple-element.106.refs_3_.refs_17_), channel_id=1, source_target_pairs={{0,12},{4,8},{8,4},{12,0},{1,13},{5,9},{9,5},{13,1},{2,14},{6,10},... | collective-permute-start | bytes 405512 | tf_op jit(solution)/shard_map/ppermute | solution.py:436
  83.1 8.9 %collective-permute-start.22 = (f32[264,128]{1,0:T(8,128)S(1)}, f32[264,128]{1,0:T(8,128)S(1)}, u32[]{:S(2)}, u32[]{:S(2)}) collective-permute-start(f32[264,128]{1,0:T(8,128)S(1)} %get-tuple-element.106.refs_3_.refs_17_), channel_id=1, source_target_pairs={{0,8},{4,12},{8,0},{12,4},{1,9},{5,13},{9,1},{13,5},{2,10},{6,14},... | collective-permute-start | bytes 405512 | tf_op jit(solution)/shard_map/ppermute | solution.py:436
  85.9 6.1 %collective-permute-start.21 = (f32[264,128]{1,0:T(8,128)S(1)}, f32[264,128]{1,0:T(8,128)S(1)}, u32[]{:S(2)}, u32[]{:S(2)}) collective-permute-start(f32[264,128]{1,0:T(8,128)S(1)} %get-tuple-element.106.refs_3_.refs_17_), channel_id=1, source_target_pairs={{0,4},{4,0},{8,12},{12,8},{1,5},{5,1},{9,13},{13,9},{2,6},{6,2},{1... | collective-permute-start | bytes 405512 | tf_op jit(solution)/shard_map/ppermute | solution.py:436
  94.0 5.8 %collective-permute-start.24 = (f32[392,128]{1,0:T(8,128)S(1)}, f32[392,128]{1,0:T(8,128)S(1)}, u32[]{:S(2)}, u32[]{:S(2)}) collective-permute-start(f32[392,128]{1,0:T(8,128)S(1)} %get-tuple-element.107.refs_0_), channel_id=1, source_target_pairs={{0,2},{1,3},{2,0},{3,1},{4,6},{5,7},{6,4},{7,5},{8,10},{9,11},{10,... | collective-permute-start | bytes 602120 | tf_op jit(solution)/shard_map/ppermute | solution.py:430
  100.0 4.5 %collective-permute-start.27 = (f32[8,128]{1,0:T(8,128)S(1)}, f32[8,128]{1,0:T(8,128)S(1)}, u32[]{:S(2)}, u32[]{:S(2)}) collective-permute-start(f32[8,128]{1,0:T(8,128)S(1)} %get-tuple-element.109.refs_2_), channel_id=1, source_target_pairs={{0,8},{4,12},{8,0},{12,4},{1,9},{5,13},{9,1},{13,5},{2,10},{6,14},... | collective-permute-start | bytes 12296 | tf_op jit(solution)/shard_map/ppermute | solution.py:436
  101.8 5.6 %collective-permute-start.26 = (f32[8,128]{1,0:T(8,128)S(1)}, f32[8,128]{1,0:T(8,128)S(1)}, u32[]{:S(2)}, u32[]{:S(2)}) collective-permute-start(f32[8,128]{1,0:T(8,128)S(1)} %get-tuple-element.109.refs_2_), channel_id=1, source_target_pairs={{0,12},{4,8},{8,4},{12,0},{1,13},{5,9},{9,5},{13,1},{2,14},{6,10},... | collective-permute-start | bytes 12296 | tf_op jit(solution)/shard_map/ppermute | solution.py:436
  103.3 4.1 %collective-permute-start.25 = (f32[8,128]{1,0:T(8,128)S(1)}, f32[8,128]{1,0:T(8,128)S(1)}, u32[]{:S(2)}, u32[]{:S(2)}) collective-permute-start(f32[8,128]{1,0:T(8,128)S(1)} %get-tuple-element.109.refs_2_), channel_id=1, source_target_pairs={{0,4},{4,0},{8,12},{12,8},{1,5},{5,1},{9,13},{13,9},{2,6},{6,2},{1... | collective-permute-start | bytes 12296 | tf_op jit(solution)/shard_map/ppermute | solution.py:436
  110.8 6.2 %collective-permute-start.28 = (f32[256,128]{1,0:T(8,128)S(1)}, f32[256,128]{1,0:T(8,128)S(1)}, u32[]{:S(2)}, u32[]{:S(2)}) collective-permute-start(f32[256,128]{1,0:T(8,128)S(1)} %get-tuple-element.118), channel_id=1, source_target_pairs={{0,4},{4,0},{8,12},{12,8},{1,5},{5,1},{9,13},{13,9},{2,6},{6,2},{1... | collective-permute-start | bytes 393224 | tf_op jit(solution)/shard_map/ppermute | solution.py:436
  110.9 12.7 %collective-permute-start.29 = (f32[256,128]{1,0:T(8,128)S(1)}, f32[256,128]{1,0:T(8,128)S(1)}, u32[]{:S(2)}, u32[]{:S(2)}) collective-permute-start(f32[256,128]{1,0:T(8,128)S(1)} %get-tuple-element.119), channel_id=1, source_target_pairs={{0,8},{4,12},{8,0},{12,4},{1,9},{5,13},{9,1},{13,5},{2,10},{6,14},... | collective-permute-start | bytes 393224 | tf_op jit(solution)/shard_map/ppermute | solution.py:436
  113.2 10.3 %collective-permute-start.30 = (f32[256,128]{1,0:T(8,128)S(1)}, f32[256,128]{1,0:T(8,128)S(1)}, u32[]{:S(2)}, u32[]{:S(2)}) collective-permute-start(f32[256,128]{1,0:T(8,128)S(1)} %get-tuple-element.120), channel_id=1, source_target_pairs={{0,12},{4,8},{8,4},{12,0},{1,13},{5,9},{9,5},{13,1},{2,14},{6,10},... | collective-permute-start | bytes 393224 | tf_op jit(solution)/shard_map/ppermute | solution.py:436
  124.2 6.9 %collective-permute-start.33 = (f32[264,128]{1,0:T(8,128)S(1)}, f32[264,128]{1,0:T(8,128)S(1)}, u32[]{:S(2)}, u32[]{:S(2)}) collective-permute-start(f32[264,128]{1,0:T(8,128)S(1)} %get-tuple-element.122.refs_3_.refs_5_.refs_14_), channel_id=1, source_target_pairs={{0,12},{4,8},{8,4},{12,0},{1,13},{5,9},{9,5},{13,1},{2,14},{6,10},... | collective-permute-start | bytes 405512 | tf_op jit(solution)/shard_map/ppermute | solution.py:436
  127.4 8.0 %collective-permute-start.32 = (f32[264,128]{1,0:T(8,128)S(1)}, f32[264,128]{1,0:T(8,128)S(1)}, u32[]{:S(2)}, u32[]{:S(2)}) collective-permute-start(f32[264,128]{1,0:T(8,128)S(1)} %get-tuple-element.122.refs_3_.refs_5_.refs_14_), channel_id=1, source_target_pairs={{0,8},{4,12},{8,0},{12,4},{1,9},{5,13},{9,1},{13,5},{2,10},{6,14},... | collective-permute-start | bytes 405512 | tf_op jit(solution)/shard_map/ppermute | solution.py:436
  129.2 6.2 %collective-permute-start.31 = (f32[264,128]{1,0:T(8,128)S(1)}, f32[264,128]{1,0:T(8,128)S(1)}, u32[]{:S(2)}, u32[]{:S(2)}) collective-permute-start(f32[264,128]{1,0:T(8,128)S(1)} %get-tuple-element.122.refs_3_.refs_5_.refs_14_), channel_id=1, source_target_pairs={{0,4},{4,0},{8,12},{12,8},{1,5},{5,1},{9,13},{13,9},{2,6},{6,2},{1... | collective-permute-start | bytes 405512 | tf_op jit(solution)/shard_map/ppermute | solution.py:436
  137.5 5.8 %collective-permute-start.34 = (f32[392,128]{1,0:T(8,128)S(1)}, f32[392,128]{1,0:T(8,128)S(1)}, u32[]{:S(2)}, u32[]{:S(2)}) collective-permute-start(f32[392,128]{1,0:T(8,128)S(1)} %get-tuple-element.123.refs_2_), channel_id=1, source_target_pairs={{0,2},{1,3},{2,0},{3,1},{4,6},{5,7},{6,4},{7,5},{8,10},{9,11},{10,... | collective-permute-start | bytes 602120 | tf_op jit(solution)/shard_map/ppermute | solution.py:430
  145.8 9.5 %collective-permute-start.35 = (f32[264,128]{1,0:T(8,128)S(1)}, f32[264,128]{1,0:T(8,128)S(1)}, u32[]{:S(2)}, u32[]{:S(2)}) collective-permute-start(f32[264,128]{1,0:T(8,128)S(1)} %get-tuple-element.126), channel_id=1, source_target_pairs={{0,4},{4,0},{8,12},{12,8},{1,5},{5,1},{9,13},{13,9},{2,6},{6,2},{1... | collective-permute-start | bytes 405512 | tf_op jit(solution)/shard_map/ppermute | solution.py:436
  146.2 11.7 %collective-permute-start.36 = (f32[264,128]{1,0:T(8,128)S(1)}, f32[264,128]{1,0:T(8,128)S(1)}, u32[]{:S(2)}, u32[]{:S(2)}) collective-permute-start(f32[264,128]{1,0:T(8,128)S(1)} %get-tuple-element.127), channel_id=1, source_target_pairs={{0,8},{4,12},{8,0},{12,4},{1,9},{5,13},{9,1},{13,5},{2,10},{6,14},... | collective-permute-start | bytes 405512 | tf_op jit(solution)/shard_map/ppermute | solution.py:436
  149.6 8.4 %collective-permute-start.37 = (f32[264,128]{1,0:T(8,128)S(1)}, f32[264,128]{1,0:T(8,128)S(1)}, u32[]{:S(2)}, u32[]{:S(2)}) collective-permute-start(f32[264,128]{1,0:T(8,128)S(1)} %get-tuple-element.128), channel_id=1, source_target_pairs={{0,12},{4,8},{8,4},{12,0},{1,13},{5,9},{9,5},{13,1},{2,14},{6,10},... | collective-permute-start | bytes 405512 | tf_op jit(solution)/shard_map/ppermute | solution.py:436
  158.1 7.0 %collective-permute-start.40 = (f32[264,128]{1,0:T(8,128)S(1)}, f32[264,128]{1,0:T(8,128)S(1)}, u32[]{:S(2)}, u32[]{:S(2)}) collective-permute-start(f32[264,128]{1,0:T(8,128)S(1)} %get-tuple-element.131.refs_3_.refs_15_), channel_id=1, source_target_pairs={{0,12},{4,8},{8,4},{12,0},{1,13},{5,9},{9,5},{13,1},{2,14},{6,10},... | collective-permute-start | bytes 405512 | tf_op jit(solution)/shard_map/ppermute | solution.py:436
  160.9 8.4 %collective-permute-start.39 = (f32[264,128]{1,0:T(8,128)S(1)}, f32[264,128]{1,0:T(8,128)S(1)}, u32[]{:S(2)}, u32[]{:S(2)}) collective-permute-start(f32[264,128]{1,0:T(8,128)S(1)} %get-tuple-element.131.refs_3_.refs_15_), channel_id=1, source_target_pairs={{0,8},{4,12},{8,0},{12,4},{1,9},{5,13},{9,1},{13,5},{2,10},{6,14},... | collective-permute-start | bytes 405512 | tf_op jit(solution)/shard_map/ppermute | solution.py:436
  161.9 7.3 %collective-permute-start.38 = (f32[264,128]{1,0:T(8,128)S(1)}, f32[264,128]{1,0:T(8,128)S(1)}, u32[]{:S(2)}, u32[]{:S(2)}) collective-permute-start(f32[264,128]{1,0:T(8,128)S(1)} %get-tuple-element.131.refs_3_.refs_15_), channel_id=1, source_target_pairs={{0,4},{4,0},{8,12},{12,8},{1,5},{5,1},{9,13},{13,9},{2,6},{6,2},{1... | collective-permute-start | bytes 405512 | tf_op jit(solution)/shard_map/ppermute | solution.py:436
  171.9 5.7 %collective-permute-start.41 = (f32[392,128]{1,0:T(8,128)S(1)}, f32[392,128]{1,0:T(8,128)S(1)}, u32[]{:S(2)}, u32[]{:S(2)}) collective-permute-start(f32[392,128]{1,0:T(8,128)S(1)} %get-tuple-element.132.refs_0_), channel_id=1, source_target_pairs={{0,2},{1,3},{2,0},{3,1},{4,6},{5,7},{6,4},{7,5},{8,10},{9,11},{10,... | collective-permute-start | bytes 602120 | tf_op jit(solution)/shard_map/ppermute | solution.py:430
  177.8 4.5 %collective-permute-start.44 = (f32[8,128]{1,0:T(8,128)S(1)}, f32[8,128]{1,0:T(8,128)S(1)}, u32[]{:S(2)}, u32[]{:S(2)}) collective-permute-start(f32[8,128]{1,0:T(8,128)S(1)} %get-tuple-element.134.refs_0_), channel_id=1, source_target_pairs={{0,8},{4,12},{8,0},{12,4},{1,9},{5,13},{9,1},{13,5},{2,10},{6,14},... | collective-permute-start | bytes 12296 | tf_op jit(solution)/shard_map/ppermute | solution.py:436
  177.9 5.4 %collective-permute-start.43 = (f32[8,128]{1,0:T(8,128)S(1)}, f32[8,128]{1,0:T(8,128)S(1)}, u32[]{:S(2)}, u32[]{:S(2)}) collective-permute-start(f32[8,128]{1,0:T(8,128)S(1)} %get-tuple-element.134.refs_0_), channel_id=1, source_target_pairs={{0,12},{4,8},{8,4},{12,0},{1,13},{5,9},{9,5},{13,1},{2,14},{6,10},... | collective-permute-start | bytes 12296 | tf_op jit(solution)/shard_map/ppermute | solution.py:436
  180.3 3.6 %collective-permute-start.42 = (f32[8,128]{1,0:T(8,128)S(1)}, f32[8,128]{1,0:T(8,128)S(1)}, u32[]{:S(2)}, u32[]{:S(2)}) collective-permute-start(f32[8,128]{1,0:T(8,128)S(1)} %get-tuple-element.134.refs_0_), channel_id=1, source_target_pairs={{0,4},{4,0},{8,12},{12,8},{1,5},{5,1},{9,13},{13,9},{2,6},{6,2},{1... | collective-permute-start | bytes 12296 | tf_op jit(solution)/shard_map/ppermute | solution.py:436
  184.1 2.0 %collective-permute-start.45 = (f32[1024,128]{1,0:T(8,128)S(1)}, f32[1024,128]{1,0:T(8,128)S(1)}, u32[]{:S(2)}, u32[]{:S(2)}) collective-permute-start(f32[1024,128]{1,0:T(8,128)S(1)} %shard_map.150.refs_1_), channel_id=1, source_target_pairs={{0,1},{1,0},{2,3},{3,2},{4,5},{5,4},{6,7},{7,6},{8,9},{9,8},{10,11... | collective-permute-start | bytes 1572872 | tf_op jit(solution)/shard_map/ppermute | solution.py:427

commit v11 on v10

--- a/solution.py
+++ b/solution.py
@@ -293,12 +293,12 @@
         diag = pd[...] + SIGMA + full[pl.ds(at, own), :]
         dk[...] = diag
     else:
-        x, q, pd, dk, msg, res = rest
+        base, pd, dk, msg, res = rest
         diag = dk[...]
     total = msgs[0][0:own, :]
     for k in range(1, n):
         total = total + msgs[k][0:own, :]
-    r = -q[...] - pd[...] * x[...] - total
+    r = (-q[...] - pd[...] * x[...] if first else base[...]) - total
     s = r / diag
     res[...] = r
     msg[0:own, :] = s
@@ -306,6 +306,12 @@
     rz = jnp.sum(r * s, axis=0, keepdims=True)
     dd = jnp.sum(shift * s * s, axis=0, keepdims=True)
     msg[own : own + SC, :] = pack_rows(rz, dd)
+
+
+def base_kernel(x, q, pd, dk, base, pd_out, dk_out):
+    base[...] = -q[...] - pd[...] * x[...]
+    pd_out[...] = pd[...]
+    dk_out[...] = dk[...]
 
 
 def step_kernel(n, own, *refs):
@@ -527,10 +533,11 @@
                 total_scratch,
             )
         else:
+            base, pd, dk = call(base_kernel, [own_shape] * 3, [x, q, pd, dk], after=pieces[0])
             msg1, r = call(
                 functools.partial(residual_kernel, n, own, False),
                 [msg_shape, own_shape],
-                [*to_row(pieces), x, q, pd, dk],
+                [*to_row(pieces), base, pd, dk],
                 [place],
             )
         msg, pp1 = forward(to_all_rows(msg1), 1)

time: 188 us -> 188 us (level)
    pallas_call x22 -> x23, Pallas kernels: 30.3 us -> 30.3 us  [call(): pl.pallas_call(run, out_shape=[jax.ShapeDtypeStruct(s, d) for s, d in out...]
where the time goes in v11:
time: 188 us
  waiting for transfers between devices  89.8 us (48%)
  starting transfers between devices  62.2 us (33%)
  Pallas kernels  30.3 us (16%)
  local copies, waits for them, and re-layouts  4.15 us (2%)
    ppermute x33, waiting for transfers between devices, over_row(): return lax.ppermute(v, 'row', [(i, i ^ k) for i in range(n)])  66 us
    ppermute x33, starting transfers between devices, over_row(): return lax.ppermute(v, 'row', [(i, i ^ k) for i in range(n)])  52.7 us
    pallas_call x23, Pallas kernels, call(): pl.pallas_call(run, out_shape=[jax.ShapeDtypeStruct(s, d) for s, d in out...  30.3 us
    ppermute x5, waiting for transfers between devices, to_x(): lax.ppermute(v, 'col', [(c, c ^ 2 * k) for c in range(n_col)])  19.3 us
    ppermute x5, starting transfers between devices, to_x(): lax.ppermute(v, 'col', [(c, c ^ 2 * k) for c in range(n_col)])  7.59 us
    ppermute x8, waiting for transfers between devices, to_core(): return lax.ppermute(v, 'col', [(c, c ^ 1) for c in range(n_col)])  4.49 us
    unnamed x23, local copies, waits for them, and re-layouts  3.82 us
  transfers between devices with their start and end apart: 46, of which 30 were waited for; matrix products, arithmetic and copies ran while one was open for 1% of the time, Pallas kernels for 3%

profile of v11, /device:TPU:0, one launch (start us, length us, event | category | flops | bytes accessed | tf_op | source)
XLA Modules:
  0.0 187.8 jit_solution(17658637950073019871)
XLA Ops:
  1.1 4.7 %collective-permute-start.3 = (f32[256,128]{1,0:T(8,128)}, f32[256,128]{1,0:T(8,128)S(1)}, u32[]{:S(2)}, u32[]{:S(2)}) collective-permute-start(f32[256,128]{1,0:T(8,128)} %refs_1_.3), channel_id=1, source_target_pairs={{0,12},{4,8},{8,4},{12,0},{1,13},{5,9},{9,5},{13,1},{2,14},{6,10},... | collective-permute-start | bytes 393224 | tf_op jit(solution)/shard_map/ppermute | solution.py:442
  7.3 1.4 copy-done
  10.3 1.4 shard_map.130
  11.9 5.8 %collective-permute-done.2.refs_5_ = f32[256,128]{1,0:T(8,128)S(1)} collective-permute-done((f32[256,128]{1,0:T(8,128)}, f32[256,128]{1,0:T(8,128)S(1)}, u32[]{:S(2)}, u32[]{:S(2)}) %collective-permute-start.2) | collective-permute-done | bytes 131104 | tf_op jit(solution)/shard_map/ppermute | solution.py:442
  17.8 1.4 shard_map.131
  19.7 1.1 collective-permute-done.4.refs_1_
  20.9 1.6 collective-permute-start.5
  22.6 1.3 shard_map.133
  24.1 1.4 shard_map.134
  25.5 2.4 %collective-permute-done.5.refs_3_ = f32[384,128]{1,0:T(8,128)S(1)} collective-permute-done((f32[384,128]{1,0:T(8,128)S(1)}, f32[384,128]{1,0:T(8,128)S(1)}, u32[]{:S(2)}, u32[]{:S(2)}) %collective-permute-start.5) | collective-permute-done | bytes 196640 | tf_op jit(solution)/shard_map/ppermute | solution.py:436
  27.9 2.5 %shard_map.135 = (f32[272,128]{1,0:T(8,128)S(1)}, f32[272,128]{1,0:T(8,128)S(1)}, f32[272,128]{1,0:T(8,128)S(1)}, f32[272,128]{1,0:T(8,128)S(1)}, f32[384,128]{1,0:T(8,128)S(1)}) custom-call(s32[2]{0:T(128)S(1)} %pad_add_fusion.refs_0_, s32[4]{0:T(128)S(1)} %pad_add_fusion.2.refs_1_, f32[384,128]{1,0:T(8,128)S(1)} %get-tuple-element.80.refs_0_.refs_2_, ...), custom_call_target="tpu_custom_call" | custom-call | flops 805306368 | bytes 7217152 | tf_op jit(solution)/shard_map/pallas_call | solution.py:34
  30.5 3.0 %collective-permute-start.9 = (f32[272,128]{1,0:T(8,128)S(1)}, f32[272,128]{1,0:T(8,128)S(1)}, u32[]{:S(2)}, u32[]{:S(2)}) collective-permute-start(f32[272,128]{1,0:T(8,128)S(1)} %get-tuple-element.92), channel_id=1, source_target_pairs={{0,8},{4,12},{8,0},{12,4},{1,9},{5,13},{9,1},{13,5},{2,10},{6,14},... | collective-permute-start | bytes 417800 | tf_op jit(solution)/shard_map/ppermute | solution.py:442
  33.6 1.3 collective-permute-start.10
  38.2 5.8 %collective-permute-done.9.refs_3_ = f32[272,128]{1,0:T(8,128)S(1)} collective-permute-done((f32[272,128]{1,0:T(8,128)S(1)}, f32[272,128]{1,0:T(8,128)S(1)}, u32[]{:S(2)}, u32[]{:S(2)}) %collective-permute-start.9) | collective-permute-done | bytes 139296 | tf_op jit(solution)/shard_map/ppermute | solution.py:442
  44.9 2.4 %collective-permute-start.16 = (f32[264,128]{1,0:T(8,128)S(1)}, f32[264,128]{1,0:T(8,128)S(1)}, u32[]{:S(2)}, u32[]{:S(2)}) collective-permute-start(f32[264,128]{1,0:T(8,128)S(1)} %get-tuple-element.96.refs_3_.refs_5_.refs_16_), channel_id=1, source_target_pairs={{0,12},{4,8},{8,4},{12,0},{1,13},{5,9},{9,5},{13,1},{2,14},{6,10},... | collective-permute-start | bytes 405512 | tf_op jit(solution)/shard_map/ppermute | solution.py:442
  47.3 2.2 %collective-permute-start.15 = (f32[264,128]{1,0:T(8,128)S(1)}, f32[264,128]{1,0:T(8,128)S(1)}, u32[]{:S(2)}, u32[]{:S(2)}) collective-permute-start(f32[264,128]{1,0:T(8,128)S(1)} %get-tuple-element.96.refs_3_.refs_5_.refs_16_), channel_id=1, source_target_pairs={{0,8},{4,12},{8,0},{12,4},{1,9},{5,13},{9,1},{13,5},{2,10},{6,14},... | collective-permute-start | bytes 405512 | tf_op jit(solution)/shard_map/ppermute | solution.py:442
  50.1 3.1 %collective-permute-done.16.refs_6_ = f32[264,128]{1,0:T(8,128)S(1)} collective-permute-done((f32[264,128]{1,0:T(8,128)S(1)}, f32[264,128]{1,0:T(8,128)S(1)}, u32[]{:S(2)}, u32[]{:S(2)}) %collective-permute-start.16) | collective-permute-done | bytes 135200 | tf_op jit(solution)/shard_map/ppermute | solution.py:442
  53.2 4.7 %collective-permute-done.15.refs_5_ = f32[264,128]{1,0:T(8,128)S(1)} collective-permute-done((f32[264,128]{1,0:T(8,128)S(1)}, f32[264,128]{1,0:T(8,128)S(1)}, u32[]{:S(2)}, u32[]{:S(2)}) %collective-permute-start.15) | collective-permute-done | bytes 135200 | tf_op jit(solution)/shard_map/ppermute | solution.py:442
  57.9 2.0 %shard_map.138 = (f32[392,128]{1,0:T(8,128)S(1)}, f32[256,128]{1,0:T(8,128)S(1)}) custom-call(s32[2]{0:T(128)S(1)} %pad_add_fusion.refs_0_, s32[4]{0:T(128)S(1)} %pad_add_fusion.2.refs_1_, s32[48]{0:T(128)S(1)} %pad_add_fusion.3.refs_2_, f32[264,128]{1,0:T(8,128)S(1)} %get-tuple-element.96.refs_3_.refs_5_.refs_16_, ...), custom_call_target="tpu_custom_call" | custom-call | flops 805306368 | bytes 4210688 | tf_op jit(solution)/shard_map/pallas_call | solution.py:34
  59.9 1.5 collective-permute-start.17
  61.4 4.2 %collective-permute-done.17.refs_3_ = f32[392,128]{1,0:T(8,128)S(1)} collective-permute-done((f32[392,128]{1,0:T(8,128)S(1)}, f32[392,128]{1,0:T(8,128)S(1)}, u32[]{:S(2)}, u32[]{:S(2)}) %collective-permute-start.17) | collective-permute-done | bytes 200736 | tf_op jit(solution)/shard_map/ppermute | solution.py:436
  65.7 2.5 %shard_map.139 = (f32[264,128]{1,0:T(8,128)S(1)}, f32[264,128]{1,0:T(8,128)S(1)}, f32[264,128]{1,0:T(8,128)S(1)}, f32[264,128]{1,0:T(8,128)S(1)}, f32[384,128]{1,0:T(8,128)S(1)}, /*index=5*/f32[8,128]{1,0:T(8,128)S(1)}) custom-call(s32[2]{0:T(128)S(1)} %pad_add_fusion.refs_0_, s32[4]{0:T(128)S(1)} %pad_add_fusion.2.refs_1_, ...), custom_call_target="tpu_custom_call" | custom-call | flops 805306368 | bytes 6823936 | tf_op jit(solution)/shard_map/pallas_call | solution.py:34
  68.3 3.0 %collective-permute-start.19 = (f32[264,128]{1,0:T(8,128)S(1)}, f32[264,128]{1,0:T(8,128)S(1)}, u32[]{:S(2)}, u32[]{:S(2)}) collective-permute-start(f32[264,128]{1,0:T(8,128)S(1)} %get-tuple-element.104), channel_id=1, source_target_pairs={{0,8},{4,12},{8,0},{12,4},{1,9},{5,13},{9,1},{13,5},{2,10},{6,14},... | collective-permute-start | bytes 405512 | tf_op jit(solution)/shard_map/ppermute | solution.py:442
  71.3 1.3 collective-permute-start.20
  72.7 2.6 %collective-permute-done.18.refs_1_ = f32[264,128]{1,0:T(8,128)S(1)} collective-permute-done((f32[264,128]{1,0:T(8,128)S(1)}, f32[264,128]{1,0:T(8,128)S(1)}, u32[]{:S(2)}, u32[]{:S(2)}) %collective-permute-start.18) | collective-permute-done | bytes 135200 | tf_op jit(solution)/shard_map/ppermute | solution.py:442
  75.3 3.7 %collective-permute-done.19.refs_2_ = f32[264,128]{1,0:T(8,128)S(1)} collective-permute-done((f32[264,128]{1,0:T(8,128)S(1)}, f32[264,128]{1,0:T(8,128)S(1)}, u32[]{:S(2)}, u32[]{:S(2)}) %collective-permute-start.19) | collective-permute-done | bytes 135200 | tf_op jit(solution)/shard_map/ppermute | solution.py:442
  79.1 4.0 %collective-permute-start.23 = (f32[264,128]{1,0:T(8,128)S(1)}, f32[264,128]{1,0:T(8,128)S(1)}, u32[]{:S(2)}, u32[]{:S(2)}) collective-permute-start(f32[264,128]{1,0:T(8,128)S(1)} %get-tuple-element.109.refs_3_.refs_17_), channel_id=1, source_target_pairs={{0,12},{4,8},{8,4},{12,0},{1,13},{5,9},{9,5},{13,1},{2,14},{6,10},... | collective-permute-start | bytes 405512 | tf_op jit(solution)/shard_map/ppermute | solution.py:442
  83.1 2.8 %collective-permute-start.22 = (f32[264,128]{1,0:T(8,128)S(1)}, f32[264,128]{1,0:T(8,128)S(1)}, u32[]{:S(2)}, u32[]{:S(2)}) collective-permute-start(f32[264,128]{1,0:T(8,128)S(1)} %get-tuple-element.109.refs_3_.refs_17_), channel_id=1, source_target_pairs={{0,8},{4,12},{8,0},{12,4},{1,9},{5,13},{9,1},{13,5},{2,10},{6,14},... | collective-permute-start | bytes 405512 | tf_op jit(solution)/shard_map/ppermute | solution.py:442
  86.4 1.2 collective-permute-done.23.refs_6_
  87.6 4.4 %collective-permute-done.22.refs_5_ = f32[264,128]{1,0:T(8,128)S(1)} collective-permute-done((f32[264,128]{1,0:T(8,128)S(1)}, f32[264,128]{1,0:T(8,128)S(1)}, u32[]{:S(2)}, u32[]{:S(2)}) %collective-permute-start.22) | collective-permute-done | bytes 135200 | tf_op jit(solution)/shard_map/ppermute | solution.py:442
  92.0 2.0 %shard_map.141 = (f32[392,128]{1,0:T(8,128)S(1)}, f32[256,128]{1,0:T(8,128)S(1)}) custom-call(s32[2]{0:T(128)S(1)} %pad_add_fusion.refs_0_, s32[4]{0:T(128)S(1)} %pad_add_fusion.2.refs_1_, s32[48]{0:T(128)S(1)} %pad_add_fusion.3.refs_2_, f32[264,128]{1,0:T(8,128)S(1)} %get-tuple-element.109.refs_3_.refs_17_, f32[264,128]{1,0:T(8,128)S(1)} %collective-permute-done.21.refs_4_, ...), custom_call_target="tpu_custom_call" | custom-call | flops 805306368 | bytes 4341760 | tf_op jit(solution)/shard_map/pallas_call | solution.py:34
  94.0 1.5 collective-permute-start.24
  95.5 4.2 %collective-permute-done.24.refs_1_ = f32[392,128]{1,0:T(8,128)S(1)} collective-permute-done((f32[392,128]{1,0:T(8,128)S(1)}, f32[392,128]{1,0:T(8,128)S(1)}, u32[]{:S(2)}, u32[]{:S(2)}) %collective-permute-start.24) | collective-permute-done | bytes 200736 | tf_op jit(solution)/shard_map/ppermute | solution.py:436
  100.0 1.8 collective-permute-start.27
  101.8 1.5 collective-permute-start.26
  104.5 2.9 %collective-permute-done.26.refs_4_ = f32[8,128]{1,0:T(8,128)S(1)} collective-permute-done((f32[8,128]{1,0:T(8,128)S(1)}, f32[8,128]{1,0:T(8,128)S(1)}, u32[]{:S(2)}, u32[]{:S(2)}) %collective-permute-start.26) | collective-permute-done | bytes 4128 | tf_op jit(solution)/shard_map/ppermute | solution.py:442
  107.3 3.4 %shard_map.143 = (f32[256,128]{1,0:T(8,128)S(1)}, f32[256,128]{1,0:T(8,128)S(1)}, f32[256,128]{1,0:T(8,128)S(1)}, f32[256,128]{1,0:T(8,128)S(1)}, f32[256,128]{1...) custom-call(s32[2]{0:T(128)S(1)} %pad_add_fusion.refs_0_, ...), custom_call_target="tpu_custom_call" | custom-call | flops 805306368 | bytes 8486912 | tf_op jit(solution)/shard_map/pallas_call | solution.py:34
  110.8 2.4 %collective-permute-start.29 = (f32[256,128]{1,0:T(8,128)S(1)}, f32[256,128]{1,0:T(8,128)S(1)}, u32[]{:S(2)}, u32[]{:S(2)}) collective-permute-start(f32[256,128]{1,0:T(8,128)S(1)} %get-tuple-element.122), channel_id=1, source_target_pairs={{0,8},{4,12},{8,0},{12,4},{1,9},{5,13},{9,1},{13,5},{2,10},{6,14},... | collective-permute-start | bytes 393224 | tf_op jit(solution)/shard_map/ppermute | solution.py:442
  113.2 1.9 %collective-permute-start.30 = (f32[256,128]{1,0:T(8,128)S(1)}, f32[256,128]{1,0:T(8,128)S(1)}, u32[]{:S(2)}, u32[]{:S(2)}) collective-permute-start(f32[256,128]{1,0:T(8,128)S(1)} %get-tuple-element.123), channel_id=1, source_target_pairs={{0,12},{4,8},{8,4},{12,0},{1,13},{5,9},{9,5},{13,1},{2,14},{6,10},... | collective-permute-start | bytes 393224 | tf_op jit(solution)/shard_map/ppermute | solution.py:442
  115.2 1.8 collective-permute-done.28.refs_2_
  117.0 6.6 %collective-permute-done.29.refs_3_ = f32[256,128]{1,0:T(8,128)S(1)} collective-permute-done((f32[256,128]{1,0:T(8,128)S(1)}, f32[256,128]{1,0:T(8,128)S(1)}, u32[]{:S(2)}, u32[]{:S(2)}) %collective-permute-start.29) | collective-permute-done | bytes 131104 | tf_op jit(solution)/shard_map/ppermute | solution.py:442
  124.2 3.3 %collective-permute-start.33 = (f32[264,128]{1,0:T(8,128)S(1)}, f32[264,128]{1,0:T(8,128)S(1)}, u32[]{:S(2)}, u32[]{:S(2)}) collective-permute-start(f32[264,128]{1,0:T(8,128)S(1)} %get-tuple-element.128.refs_3_.refs_5_.refs_14_), channel_id=1, source_target_pairs={{0,12},{4,8},{8,4},{12,0},{1,13},{5,9},{9,5},{13,1},{2,14},{6,10},... | collective-permute-start | bytes 405512 | tf_op jit(solution)/shard_map/ppermute | solution.py:442
  127.4 1.8 collective-permute-start.32
  129.7 1.4 collective-permute-done.33.refs_6_
  131.1 4.3 %collective-permute-done.32.refs_5_ = f32[264,128]{1,0:T(8,128)S(1)} collective-permute-done((f32[264,128]{1,0:T(8,128)S(1)}, f32[264,128]{1,0:T(8,128)S(1)}, u32[]{:S(2)}, u32[]{:S(2)}) %collective-permute-start.32) | collective-permute-done | bytes 135200 | tf_op jit(solution)/shard_map/ppermute | solution.py:442
  135.4 2.0 %shard_map.146 = (f32[392,128]{1,0:T(8,128)S(1)}, f32[256,128]{1,0:T(8,128)S(1)}) custom-call(s32[2]{0:T(128)S(1)} %pad_add_fusion.refs_0_, s32[4]{0:T(128)S(1)} %pad_add_fusion.2.refs_1_, s32[48]{0:T(128)S(1)} %pad_add_fusion.3.refs_2_, f32[264,128]{1,0:T(8,128)S(1)} %get-tuple-element.128.refs_3_.refs_5_.refs_14_, ...), custom_call_target="tpu_custom_call" | custom-call | flops 805306368 | bytes 4210688 | tf_op jit(solution)/shard_map/pallas_call | solution.py:34
  137.4 1.5 collective-permute-start.34
  138.9 4.2 %collective-permute-done.34.refs_3_ = f32[392,128]{1,0:T(8,128)S(1)} collective-permute-done((f32[392,128]{1,0:T(8,128)S(1)}, f32[392,128]{1,0:T(8,128)S(1)}, u32[]{:S(2)}, u32[]{:S(2)}) %collective-permute-start.34) | collective-permute-done | bytes 200736 | tf_op jit(solution)/shard_map/ppermute | solution.py:436
  143.2 2.5 %shard_map.147 = (f32[264,128]{1,0:T(8,128)S(1)}, f32[264,128]{1,0:T(8,128)S(1)}, f32[264,128]{1,0:T(8,128)S(1)}, f32[264,128]{1,0:T(8,128)S(1)}, f32[384,128]{1,0:T(8,128)S(1)}, /*index=5*/f32[8,128]{1,0:T(8,128)S(1)}) custom-call(s32[2]{0:T(128)S(1)} %pad_add_fusion.refs_0_, s32[4]{0:T(128)S(1)} %pad_add_fusion.2.refs_1_, ...), custom_call_target="tpu_custom_call" | custom-call | flops 805306368 | bytes 6823936 | tf_op jit(solution)/shard_map/pallas_call | solution.py:34
  146.2 3.4 %collective-permute-start.36 = (f32[264,128]{1,0:T(8,128)S(1)}, f32[264,128]{1,0:T(8,128)S(1)}, u32[]{:S(2)}, u32[]{:S(2)}) collective-permute-start(f32[264,128]{1,0:T(8,128)S(1)} %get-tuple-element.133), channel_id=1, source_target_pairs={{0,8},{4,12},{8,0},{12,4},{1,9},{5,13},{9,1},{13,5},{2,10},{6,14},... | collective-permute-start | bytes 405512 | tf_op jit(solution)/shard_map/ppermute | solution.py:442
  150.2 4.9 %collective-permute-done.35.refs_1_ = f32[264,128]{1,0:T(8,128)S(1)} collective-permute-done((f32[264,128]{1,0:T(8,128)S(1)}, f32[264,128]{1,0:T(8,128)S(1)}, u32[]{:S(2)}, u32[]{:S(2)}) %collective-permute-start.35) | collective-permute-done | bytes 135200 | tf_op jit(solution)/shard_map/ppermute | solution.py:442
  155.1 2.8 %collective-permute-done.36.refs_2_ = f32[264,128]{1,0:T(8,128)S(1)} collective-permute-done((f32[264,128]{1,0:T(8,128)S(1)}, f32[264,128]{1,0:T(8,128)S(1)}, u32[]{:S(2)}, u32[]{:S(2)}) %collective-permute-start.36) | collective-permute-done | bytes 135200 | tf_op jit(solution)/shard_map/ppermute | solution.py:442
  158.0 2.8 %collective-permute-start.40 = (f32[264,128]{1,0:T(8,128)S(1)}, f32[264,128]{1,0:T(8,128)S(1)}, u32[]{:S(2)}, u32[]{:S(2)}) collective-permute-start(f32[264,128]{1,0:T(8,128)S(1)} %get-tuple-element.137.refs_3_.refs_15_), channel_id=1, source_target_pairs={{0,12},{4,8},{8,4},{12,0},{1,13},{5,9},{9,5},{13,1},{2,14},{6,10},... | collective-permute-start | bytes 405512 | tf_op jit(solution)/shard_map/ppermute | solution.py:442
  160.8 1.1 collective-permute-start.39
  162.5 2.5 %collective-permute-done.40.refs_6_ = f32[264,128]{1,0:T(8,128)S(1)} collective-permute-done((f32[264,128]{1,0:T(8,128)S(1)}, f32[264,128]{1,0:T(8,128)S(1)}, u32[]{:S(2)}, u32[]{:S(2)}) %collective-permute-start.40) | collective-permute-done | bytes 135200 | tf_op jit(solution)/shard_map/ppermute | solution.py:442
  165.0 4.2 %collective-permute-done.39.refs_5_ = f32[264,128]{1,0:T(8,128)S(1)} collective-permute-done((f32[264,128]{1,0:T(8,128)S(1)}, f32[264,128]{1,0:T(8,128)S(1)}, u32[]{:S(2)}, u32[]{:S(2)}) %collective-permute-start.39) | collective-permute-done | bytes 135200 | tf_op jit(solution)/shard_map/ppermute | solution.py:442
  169.2 2.6 %shard_map.149 = (f32[392,128]{1,0:T(8,128)S(1)}, f32[256,128]{1,0:T(8,128)}) custom-call(s32[2]{0:T(128)S(1)} %pad_add_fusion.refs_0_, s32[4]{0:T(128)S(1)} %pad_add_fusion.2.refs_1_, s32[48]{0:T(128)S(1)} %pad_add_fusion.3.refs_2_, f32[264,128]{1,0:T(8,128)S(1)} %get-tuple-element.137.refs_3_.refs_15_, f32[264,128]{1,0:T(8,128)S(1)} %collective-permute-done.38.refs_4_, ...), custom_call_target="tpu_custom_call" | custom-call | flops 805306368 | bytes 4341760 | tf_op jit(solution)/shard_map/pallas_call | solution.py:34
  171.9 1.5 collective-permute-start.41
  173.4 4.2 %collective-permute-done.41.refs_1_ = f32[392,128]{1,0:T(8,128)S(1)} collective-permute-done((f32[392,128]{1,0:T(8,128)S(1)}, f32[392,128]{1,0:T(8,128)S(1)}, u32[]{:S(2)}, u32[]{:S(2)}) %collective-permute-start.41) | collective-permute-done | bytes 200736 | tf_op jit(solution)/shard_map/ppermute | solution.py:436
  177.9 2.4 %collective-permute-start.43 = (f32[8,128]{1,0:T(8,128)S(1)}, f32[8,128]{1,0:T(8,128)S(1)}, u32[]{:S(2)}, u32[]{:S(2)}) collective-permute-start(f32[8,128]{1,0:T(8,128)S(1)} %get-tuple-element.140.refs_0_), channel_id=1, source_target_pairs={{0,12},{4,8},{8,4},{12,0},{1,13},{5,9},{9,5},{13,1},{2,14},{6,10},... | collective-permute-start | bytes 12296 | tf_op jit(solution)/shard_map/ppermute | solution.py:442
  181.2 1.0 collective-permute-done.44.refs_3_
  182.3 1.0 collective-permute-done.43.refs_2_
  184.2 1.9 %collective-permute-done.45.refs_2_ = f32[1024,128]{1,0:T(8,128)S(1)} collective-permute-done((f32[1024,128]{1,0:T(8,128)S(1)}, f32[1024,128]{1,0:T(8,128)S(1)}, u32[]{:S(2)}, u32[]{:S(2)}) %collective-permute-start.45) | collective-permute-done | bytes 524320 | tf_op jit(solution)/shard_map/ppermute | solution.py:433
  186.1 1.7 shard_map.152
  (83 shorter events, 16.6 us)
Async XLA Ops:
  0.6 23.4 %collective-permute-start.6 = (f32[24,128,128]{2,1,0:T(8,128)}, f32[24,128,128]{2,1,0:T(8,128)S(1)}, u32[]{:S(2)}, u32[]{:S(2)}) collective-permute-start(f32[24,128,128]{2,1,0:T(8,128)} %bitcast.6), channel_id=1, source_target_pairs={{0,1},{1,0},{2,3},{3,2},{4,5},{5,4},{6,7},{7,6},{8,9},{9,8},{10,11... | collective-permute-start | bytes 4718600 | tf_op jit(solution)/shard_map/ppermute | solution.py:433
  1.1 10.7 %collective-permute-start.3 = (f32[256,128]{1,0:T(8,128)}, f32[256,128]{1,0:T(8,128)S(1)}, u32[]{:S(2)}, u32[]{:S(2)}) collective-permute-start(f32[256,128]{1,0:T(8,128)} %refs_1_.3), channel_id=1, source_target_pairs={{0,12},{4,8},{8,4},{12,0},{1,13},{5,9},{9,5},{13,1},{2,14},{6,10},... | collective-permute-start | bytes 393224 | tf_op jit(solution)/shard_map/ppermute | solution.py:442
  5.8 11.9 %collective-permute-start.2 = (f32[256,128]{1,0:T(8,128)}, f32[256,128]{1,0:T(8,128)S(1)}, u32[]{:S(2)}, u32[]{:S(2)}) collective-permute-start(f32[256,128]{1,0:T(8,128)} %refs_1_.3), channel_id=1, source_target_pairs={{0,8},{4,12},{8,0},{12,4},{1,9},{5,13},{9,1},{13,5},{2,10},{6,14},... | collective-permute-start | bytes 393224 | tf_op jit(solution)/shard_map/ppermute | solution.py:442
  5.8 11.9 %collective-permute-start.1 = (f32[256,128]{1,0:T(8,128)}, f32[256,128]{1,0:T(8,128)S(1)}, u32[]{:S(2)}, u32[]{:S(2)}) collective-permute-start(f32[256,128]{1,0:T(8,128)} %refs_1_.3), channel_id=1, source_target_pairs={{0,4},{4,0},{8,12},{12,8},{1,5},{5,1},{9,13},{13,9},{2,6},{6,2},{1... | collective-permute-start | bytes 393224 | tf_op jit(solution)/shard_map/ppermute | solution.py:442
  7.3 1.4 copy-start
  8.7 0.9 copy-start.5
  9.7 0.7 copy-start.8
  10.3 7.4 %copy-start.6 = (f32[256,128]{1,0:T(8,128)S(1)}, f32[256,128]{1,0:T(8,128)}, u32[]{:S(2)}) copy-start(f32[256,128]{1,0:T(8,128)} %refs_1_.3) | copy-start | bytes 393220
  17.7 4.7 %copy-start.9 = (s32[1,1,2]{2,1,0:T(1,128)S(1)}, s32[1,1,2]{2,1,0:T(1,128)}, u32[]{:S(2)}) copy-start(s32[1,1,2]{2,1,0:T(1,128)} %param.21) | copy-start | bytes 28
  17.7 4.8 %copy-start.1 = (f32[768,128]{1,0:T(8,128)S(1)}, f32[768,128]{1,0:T(8,128)}, u32[]{:S(2)}) copy-start(f32[768,128]{1,0:T(8,128)} %refs_1_.2) | copy-start | bytes 1179652
  17.7 4.8 %copy-start.2 = (f32[768,128]{1,0:T(8,128)S(1)}, f32[768,128]{1,0:T(8,128)}, u32[]{:S(2)}) copy-start(f32[768,128]{1,0:T(8,128)} %refs_2_.1) | copy-start | bytes 1179652
  17.8 4.8 %copy-start.3 = (f32[768,128]{1,0:T(8,128)S(1)}, f32[768,128]{1,0:T(8,128)}, u32[]{:S(2)}) copy-start(f32[768,128]{1,0:T(8,128)} %refs_3_.4) | copy-start | bytes 1179652
  17.8 4.8 %copy-start.4 = (f32[768,128]{1,0:T(8,128)S(1)}, f32[768,128]{1,0:T(8,128)}, u32[]{:S(2)}) copy-start(f32[768,128]{1,0:T(8,128)} %refs_4_.1) | copy-start | bytes 1179652
  19.2 1.7 collective-permute-start.4
  19.2 4.8 %collective-permute-start.7 = (f32[4,128,128]{2,1,0:T(8,128)S(1)}, f32[4,128,128]{2,1,0:T(8,128)S(1)}, u32[]{:S(2)}, u32[]{:S(2)}) collective-permute-start(f32[4,128,128]{2,1,0:T(8,128)S(1)} %bitcast.9), channel_id=1, source_target_pairs={{0,1},{1,0},{2,3},{3,2},{4,5},{5,4},{6,7},{7,6},{8,9},{9,8},{10,11... | collective-permute-start | bytes 786440 | tf_op jit(solution)/shard_map/ppermute | solution.py:433
  20.9 7.0 %collective-permute-start.5 = (f32[384,128]{1,0:T(8,128)S(1)}, f32[384,128]{1,0:T(8,128)S(1)}, u32[]{:S(2)}, u32[]{:S(2)}) collective-permute-start(f32[384,128]{1,0:T(8,128)S(1)} %get-tuple-element.80.refs_0_.refs_2_), channel_id=1, source_target_pairs={{0,2},{1,3},{2,0},{3,1},{4,6},{5,7},{6,4},{7,5},{8,10},{9,11},{10,... | collective-permute-start | bytes 589832 | tf_op jit(solution)/shard_map/ppermute | solution.py:436
  22.5 1.4 collective-permute-start
  27.9 7.0 %copy-start.10 = (f32[256]{0:T(256)S(1)}, f32[256]{0:T(256)}, u32[]{:S(2)}) copy-start(f32[256]{0:T(256)} %param.13) | copy-start | bytes 3076
  27.9 7.0 %copy-start.7 = (f32[256,128]{1,0:T(8,128)S(1)}, f32[256,128]{1,0:T(8,128)}, u32[]{:S(2)}) copy-start(f32[256,128]{1,0:T(8,128)} %refs_3_.5) | copy-start | bytes 393220
  30.5 7.7 %collective-permute-start.8 = (f32[272,128]{1,0:T(8,128)S(1)}, f32[272,128]{1,0:T(8,128)S(1)}, u32[]{:S(2)}, u32[]{:S(2)}) collective-permute-start(f32[272,128]{1,0:T(8,128)S(1)} %get-tuple-element.91), channel_id=1, source_target_pairs={{0,4},{4,0},{8,12},{12,8},{1,5},{5,1},{9,13},{13,9},{2,6},{6,2},{1... | collective-permute-start | bytes 417800 | tf_op jit(solution)/shard_map/ppermute | solution.py:442
  30.5 13.4 %collective-permute-start.9 = (f32[272,128]{1,0:T(8,128)S(1)}, f32[272,128]{1,0:T(8,128)S(1)}, u32[]{:S(2)}, u32[]{:S(2)}) collective-permute-start(f32[272,128]{1,0:T(8,128)S(1)} %get-tuple-element.92), channel_id=1, source_target_pairs={{0,8},{4,12},{8,0},{12,4},{1,9},{5,13},{9,1},{13,5},{2,10},{6,14},... | collective-permute-start | bytes 417800 | tf_op jit(solution)/shard_map/ppermute | solution.py:442
  33.6 10.4 %collective-permute-start.10 = (f32[272,128]{1,0:T(8,128)S(1)}, f32[272,128]{1,0:T(8,128)S(1)}, u32[]{:S(2)}, u32[]{:S(2)}) collective-permute-start(f32[272,128]{1,0:T(8,128)S(1)} %get-tuple-element.93), channel_id=1, source_target_pairs={{0,12},{4,8},{8,4},{12,0},{1,13},{5,9},{9,5},{13,1},{2,14},{6,10},... | collective-permute-start | bytes 417800 | tf_op jit(solution)/shard_map/ppermute | solution.py:442
  34.9 1.1 collective-permute-start.13
  34.9 1.6 collective-permute-start.12
  36.1 1.3 collective-permute-start.11
  44.9 8.3 %collective-permute-start.16 = (f32[264,128]{1,0:T(8,128)S(1)}, f32[264,128]{1,0:T(8,128)S(1)}, u32[]{:S(2)}, u32[]{:S(2)}) collective-permute-start(f32[264,128]{1,0:T(8,128)S(1)} %get-tuple-element.96.refs_3_.refs_5_.refs_16_), channel_id=1, source_target_pairs={{0,12},{4,8},{8,4},{12,0},{1,13},{5,9},{9,5},{13,1},{2,14},{6,10},... | collective-permute-start | bytes 405512 | tf_op jit(solution)/shard_map/ppermute | solution.py:442
  47.3 10.5 %collective-permute-start.15 = (f32[264,128]{1,0:T(8,128)S(1)}, f32[264,128]{1,0:T(8,128)S(1)}, u32[]{:S(2)}, u32[]{:S(2)}) collective-permute-start(f32[264,128]{1,0:T(8,128)S(1)} %get-tuple-element.96.refs_3_.refs_5_.refs_16_), channel_id=1, source_target_pairs={{0,8},{4,12},{8,0},{12,4},{1,9},{5,13},{9,1},{13,5},{2,10},{6,14},... | collective-permute-start | bytes 405512 | tf_op jit(solution)/shard_map/ppermute | solution.py:442
  49.5 8.3 %collective-permute-start.14 = (f32[264,128]{1,0:T(8,128)S(1)}, f32[264,128]{1,0:T(8,128)S(1)}, u32[]{:S(2)}, u32[]{:S(2)}) collective-permute-start(f32[264,128]{1,0:T(8,128)S(1)} %get-tuple-element.96.refs_3_.refs_5_.refs_16_), channel_id=1, source_target_pairs={{0,4},{4,0},{8,12},{12,8},{1,5},{5,1},{9,13},{13,9},{2,6},{6,2},{1... | collective-permute-start | bytes 405512 | tf_op jit(solution)/shard_map/ppermute | solution.py:442
  59.9 5.8 %collective-permute-start.17 = (f32[392,128]{1,0:T(8,128)S(1)}, f32[392,128]{1,0:T(8,128)S(1)}, u32[]{:S(2)}, u32[]{:S(2)}) collective-permute-start(f32[392,128]{1,0:T(8,128)S(1)} %get-tuple-element.100.refs_2_), channel_id=1, source_target_pairs={{0,2},{1,3},{2,0},{3,1},{4,6},{5,7},{6,4},{7,5},{8,10},{9,11},{10,... | collective-permute-start | bytes 602120 | tf_op jit(solution)/shard_map/ppermute | solution.py:436
  68.2 7.1 %collective-permute-start.18 = (f32[264,128]{1,0:T(8,128)S(1)}, f32[264,128]{1,0:T(8,128)S(1)}, u32[]{:S(2)}, u32[]{:S(2)}) collective-permute-start(f32[264,128]{1,0:T(8,128)S(1)} %get-tuple-element.103), channel_id=1, source_target_pairs={{0,4},{4,0},{8,12},{12,8},{1,5},{5,1},{9,13},{13,9},{2,6},{6,2},{1... | collective-permute-start | bytes 405512 | tf_op jit(solution)/shard_map/ppermute | solution.py:442
  68.3 10.7 %collective-permute-start.19 = (f32[264,128]{1,0:T(8,128)S(1)}, f32[264,128]{1,0:T(8,128)S(1)}, u32[]{:S(2)}, u32[]{:S(2)}) collective-permute-start(f32[264,128]{1,0:T(8,128)S(1)} %get-tuple-element.104), channel_id=1, source_target_pairs={{0,8},{4,12},{8,0},{12,4},{1,9},{5,13},{9,1},{13,5},{2,10},{6,14},... | collective-permute-start | bytes 405512 | tf_op jit(solution)/shard_map/ppermute | solution.py:442
  71.3 7.6 %collective-permute-start.20 = (f32[264,128]{1,0:T(8,128)S(1)}, f32[264,128]{1,0:T(8,128)S(1)}, u32[]{:S(2)}, u32[]{:S(2)}) collective-permute-start(f32[264,128]{1,0:T(8,128)S(1)} %get-tuple-element.105), channel_id=1, source_target_pairs={{0,12},{4,8},{8,4},{12,0},{1,13},{5,9},{9,5},{13,1},{2,14},{6,10},... | collective-permute-start | bytes 405512 | tf_op jit(solution)/shard_map/ppermute | solution.py:442
  79.1 8.5 %collective-permute-start.23 = (f32[264,128]{1,0:T(8,128)S(1)}, f32[264,128]{1,0:T(8,128)S(1)}, u32[]{:S(2)}, u32[]{:S(2)}) collective-permute-start(f32[264,128]{1,0:T(8,128)S(1)} %get-tuple-element.109.refs_3_.refs_17_), channel_id=1, source_target_pairs={{0,12},{4,8},{8,4},{12,0},{1,13},{5,9},{9,5},{13,1},{2,14},{6,10},... | collective-permute-start | bytes 405512 | tf_op jit(solution)/shard_map/ppermute | solution.py:442
  83.1 8.9 %collective-permute-start.22 = (f32[264,128]{1,0:T(8,128)S(1)}, f32[264,128]{1,0:T(8,128)S(1)}, u32[]{:S(2)}, u32[]{:S(2)}) collective-permute-start(f32[264,128]{1,0:T(8,128)S(1)} %get-tuple-element.109.refs_3_.refs_17_), channel_id=1, source_target_pairs={{0,8},{4,12},{8,0},{12,4},{1,9},{5,13},{9,1},{13,5},{2,10},{6,14},... | collective-permute-start | bytes 405512 | tf_op jit(solution)/shard_map/ppermute | solution.py:442
  85.9 6.1 %collective-permute-start.21 = (f32[264,128]{1,0:T(8,128)S(1)}, f32[264,128]{1,0:T(8,128)S(1)}, u32[]{:S(2)}, u32[]{:S(2)}) collective-permute-start(f32[264,128]{1,0:T(8,128)S(1)} %get-tuple-element.109.refs_3_.refs_17_), channel_id=1, source_target_pairs={{0,4},{4,0},{8,12},{12,8},{1,5},{5,1},{9,13},{13,9},{2,6},{6,2},{1... | collective-permute-start | bytes 405512 | tf_op jit(solution)/shard_map/ppermute | solution.py:442
  94.0 5.8 %collective-permute-start.24 = (f32[392,128]{1,0:T(8,128)S(1)}, f32[392,128]{1,0:T(8,128)S(1)}, u32[]{:S(2)}, u32[]{:S(2)}) collective-permute-start(f32[392,128]{1,0:T(8,128)S(1)} %get-tuple-element.110.refs_0_), channel_id=1, source_target_pairs={{0,2},{1,3},{2,0},{3,1},{4,6},{5,7},{6,4},{7,5},{8,10},{9,11},{10,... | collective-permute-start | bytes 602120 | tf_op jit(solution)/shard_map/ppermute | solution.py:436
  100.0 4.5 %collective-permute-start.27 = (f32[8,128]{1,0:T(8,128)S(1)}, f32[8,128]{1,0:T(8,128)S(1)}, u32[]{:S(2)}, u32[]{:S(2)}) collective-permute-start(f32[8,128]{1,0:T(8,128)S(1)} %get-tuple-element.112.refs_2_), channel_id=1, source_target_pairs={{0,8},{4,12},{8,0},{12,4},{1,9},{5,13},{9,1},{13,5},{2,10},{6,14},... | collective-permute-start | bytes 12296 | tf_op jit(solution)/shard_map/ppermute | solution.py:442
  101.8 5.6 %collective-permute-start.26 = (f32[8,128]{1,0:T(8,128)S(1)}, f32[8,128]{1,0:T(8,128)S(1)}, u32[]{:S(2)}, u32[]{:S(2)}) collective-permute-start(f32[8,128]{1,0:T(8,128)S(1)} %get-tuple-element.112.refs_2_), channel_id=1, source_target_pairs={{0,12},{4,8},{8,4},{12,0},{1,13},{5,9},{9,5},{13,1},{2,14},{6,10},... | collective-permute-start | bytes 12296 | tf_op jit(solution)/shard_map/ppermute | solution.py:442
  103.3 4.1 %collective-permute-start.25 = (f32[8,128]{1,0:T(8,128)S(1)}, f32[8,128]{1,0:T(8,128)S(1)}, u32[]{:S(2)}, u32[]{:S(2)}) collective-permute-start(f32[8,128]{1,0:T(8,128)S(1)} %get-tuple-element.112.refs_2_), channel_id=1, source_target_pairs={{0,4},{4,0},{8,12},{12,8},{1,5},{5,1},{9,13},{13,9},{2,6},{6,2},{1... | collective-permute-start | bytes 12296 | tf_op jit(solution)/shard_map/ppermute | solution.py:442
  110.8 6.2 %collective-permute-start.28 = (f32[256,128]{1,0:T(8,128)S(1)}, f32[256,128]{1,0:T(8,128)S(1)}, u32[]{:S(2)}, u32[]{:S(2)}) collective-permute-start(f32[256,128]{1,0:T(8,128)S(1)} %get-tuple-element.121), channel_id=1, source_target_pairs={{0,4},{4,0},{8,12},{12,8},{1,5},{5,1},{9,13},{13,9},{2,6},{6,2},{1... | collective-permute-start | bytes 393224 | tf_op jit(solution)/shard_map/ppermute | solution.py:442
  110.8 12.7 %collective-permute-start.29 = (f32[256,128]{1,0:T(8,128)S(1)}, f32[256,128]{1,0:T(8,128)S(1)}, u32[]{:S(2)}, u32[]{:S(2)}) collective-permute-start(f32[256,128]{1,0:T(8,128)S(1)} %get-tuple-element.122), channel_id=1, source_target_pairs={{0,8},{4,12},{8,0},{12,4},{1,9},{5,13},{9,1},{13,5},{2,10},{6,14},... | collective-permute-start | bytes 393224 | tf_op jit(solution)/shard_map/ppermute | solution.py:442
  113.2 10.3 %collective-permute-start.30 = (f32[256,128]{1,0:T(8,128)S(1)}, f32[256,128]{1,0:T(8,128)S(1)}, u32[]{:S(2)}, u32[]{:S(2)}) collective-permute-start(f32[256,128]{1,0:T(8,128)S(1)} %get-tuple-element.123), channel_id=1, source_target_pairs={{0,12},{4,8},{8,4},{12,0},{1,13},{5,9},{9,5},{13,1},{2,14},{6,10},... | collective-permute-start | bytes 393224 | tf_op jit(solution)/shard_map/ppermute | solution.py:442
  124.2 6.9 %collective-permute-start.33 = (f32[264,128]{1,0:T(8,128)S(1)}, f32[264,128]{1,0:T(8,128)S(1)}, u32[]{:S(2)}, u32[]{:S(2)}) collective-permute-start(f32[264,128]{1,0:T(8,128)S(1)} %get-tuple-element.128.refs_3_.refs_5_.refs_14_), channel_id=1, source_target_pairs={{0,12},{4,8},{8,4},{12,0},{1,13},{5,9},{9,5},{13,1},{2,14},{6,10},... | collective-permute-start | bytes 405512 | tf_op jit(solution)/shard_map/ppermute | solution.py:442
  127.4 8.0 %collective-permute-start.32 = (f32[264,128]{1,0:T(8,128)S(1)}, f32[264,128]{1,0:T(8,128)S(1)}, u32[]{:S(2)}, u32[]{:S(2)}) collective-permute-start(f32[264,128]{1,0:T(8,128)S(1)} %get-tuple-element.128.refs_3_.refs_5_.refs_14_), channel_id=1, source_target_pairs={{0,8},{4,12},{8,0},{12,4},{1,9},{5,13},{9,1},{13,5},{2,10},{6,14},... | collective-permute-start | bytes 405512 | tf_op jit(solution)/shard_map/ppermute | solution.py:442
  129.2 6.2 %collective-permute-start.31 = (f32[264,128]{1,0:T(8,128)S(1)}, f32[264,128]{1,0:T(8,128)S(1)}, u32[]{:S(2)}, u32[]{:S(2)}) collective-permute-start(f32[264,128]{1,0:T(8,128)S(1)} %get-tuple-element.128.refs_3_.refs_5_.refs_14_), channel_id=1, source_target_pairs={{0,4},{4,0},{8,12},{12,8},{1,5},{5,1},{9,13},{13,9},{2,6},{6,2},{1... | collective-permute-start | bytes 405512 | tf_op jit(solution)/shard_map/ppermute | solution.py:442
  137.4 5.8 %collective-permute-start.34 = (f32[392,128]{1,0:T(8,128)S(1)}, f32[392,128]{1,0:T(8,128)S(1)}, u32[]{:S(2)}, u32[]{:S(2)}) collective-permute-start(f32[392,128]{1,0:T(8,128)S(1)} %get-tuple-element.129.refs_2_), channel_id=1, source_target_pairs={{0,2},{1,3},{2,0},{3,1},{4,6},{5,7},{6,4},{7,5},{8,10},{9,11},{10,... | collective-permute-start | bytes 602120 | tf_op jit(solution)/shard_map/ppermute | solution.py:436
  145.7 9.4 %collective-permute-start.35 = (f32[264,128]{1,0:T(8,128)S(1)}, f32[264,128]{1,0:T(8,128)S(1)}, u32[]{:S(2)}, u32[]{:S(2)}) collective-permute-start(f32[264,128]{1,0:T(8,128)S(1)} %get-tuple-element.132), channel_id=1, source_target_pairs={{0,4},{4,0},{8,12},{12,8},{1,5},{5,1},{9,13},{13,9},{2,6},{6,2},{1... | collective-permute-start | bytes 405512 | tf_op jit(solution)/shard_map/ppermute | solution.py:442
  146.2 11.7 %collective-permute-start.36 = (f32[264,128]{1,0:T(8,128)S(1)}, f32[264,128]{1,0:T(8,128)S(1)}, u32[]{:S(2)}, u32[]{:S(2)}) collective-permute-start(f32[264,128]{1,0:T(8,128)S(1)} %get-tuple-element.133), channel_id=1, source_target_pairs={{0,8},{4,12},{8,0},{12,4},{1,9},{5,13},{9,1},{13,5},{2,10},{6,14},... | collective-permute-start | bytes 405512 | tf_op jit(solution)/shard_map/ppermute | solution.py:442
  149.5 8.3 %collective-permute-start.37 = (f32[264,128]{1,0:T(8,128)S(1)}, f32[264,128]{1,0:T(8,128)S(1)}, u32[]{:S(2)}, u32[]{:S(2)}) collective-permute-start(f32[264,128]{1,0:T(8,128)S(1)} %get-tuple-element.134), channel_id=1, source_target_pairs={{0,12},{4,8},{8,4},{12,0},{1,13},{5,9},{9,5},{13,1},{2,14},{6,10},... | collective-permute-start | bytes 405512 | tf_op jit(solution)/shard_map/ppermute | solution.py:442
  158.0 7.0 %collective-permute-start.40 = (f32[264,128]{1,0:T(8,128)S(1)}, f32[264,128]{1,0:T(8,128)S(1)}, u32[]{:S(2)}, u32[]{:S(2)}) collective-permute-start(f32[264,128]{1,0:T(8,128)S(1)} %get-tuple-element.137.refs_3_.refs_15_), channel_id=1, source_target_pairs={{0,12},{4,8},{8,4},{12,0},{1,13},{5,9},{9,5},{13,1},{2,14},{6,10},... | collective-permute-start | bytes 405512 | tf_op jit(solution)/shard_map/ppermute | solution.py:442
  160.8 8.4 %collective-permute-start.39 = (f32[264,128]{1,0:T(8,128)S(1)}, f32[264,128]{1,0:T(8,128)S(1)}, u32[]{:S(2)}, u32[]{:S(2)}) collective-permute-start(f32[264,128]{1,0:T(8,128)S(1)} %get-tuple-element.137.refs_3_.refs_15_), channel_id=1, source_target_pairs={{0,8},{4,12},{8,0},{12,4},{1,9},{5,13},{9,1},{13,5},{2,10},{6,14},... | collective-permute-start | bytes 405512 | tf_op jit(solution)/shard_map/ppermute | solution.py:442
  161.9 7.3 %collective-permute-start.38 = (f32[264,128]{1,0:T(8,128)S(1)}, f32[264,128]{1,0:T(8,128)S(1)}, u32[]{:S(2)}, u32[]{:S(2)}) collective-permute-start(f32[264,128]{1,0:T(8,128)S(1)} %get-tuple-element.137.refs_3_.refs_15_), channel_id=1, source_target_pairs={{0,4},{4,0},{8,12},{12,8},{1,5},{5,1},{9,13},{13,9},{2,6},{6,2},{1... | collective-permute-start | bytes 405512 | tf_op jit(solution)/shard_map/ppermute | solution.py:442
  171.9 5.7 %collective-permute-start.41 = (f32[392,128]{1,0:T(8,128)S(1)}, f32[392,128]{1,0:T(8,128)S(1)}, u32[]{:S(2)}, u32[]{:S(2)}) collective-permute-start(f32[392,128]{1,0:T(8,128)S(1)} %get-tuple-element.138.refs_0_), channel_id=1, source_target_pairs={{0,2},{1,3},{2,0},{3,1},{4,6},{5,7},{6,4},{7,5},{8,10},{9,11},{10,... | collective-permute-start | bytes 602120 | tf_op jit(solution)/shard_map/ppermute | solution.py:436
  177.8 4.5 %collective-permute-start.44 = (f32[8,128]{1,0:T(8,128)S(1)}, f32[8,128]{1,0:T(8,128)S(1)}, u32[]{:S(2)}, u32[]{:S(2)}) collective-permute-start(f32[8,128]{1,0:T(8,128)S(1)} %get-tuple-element.140.refs_0_), channel_id=1, source_target_pairs={{0,8},{4,12},{8,0},{12,4},{1,9},{5,13},{9,1},{13,5},{2,10},{6,14},... | collective-permute-start | bytes 12296 | tf_op jit(solution)/shard_map/ppermute | solution.py:442
  177.9 5.4 %collective-permute-start.43 = (f32[8,128]{1,0:T(8,128)S(1)}, f32[8,128]{1,0:T(8,128)S(1)}, u32[]{:S(2)}, u32[]{:S(2)}) collective-permute-start(f32[8,128]{1,0:T(8,128)S(1)} %get-tuple-element.140.refs_0_), channel_id=1, source_target_pairs={{0,12},{4,8},{8,4},{12,0},{1,13},{5,9},{9,5},{13,1},{2,14},{6,10},... | collective-permute-start | bytes 12296 | tf_op jit(solution)/shard_map/ppermute | solution.py:442
  180.3 3.6 %collective-permute-start.42 = (f32[8,128]{1,0:T(8,128)S(1)}, f32[8,128]{1,0:T(8,128)S(1)}, u32[]{:S(2)}, u32[]{:S(2)}) collective-permute-start(f32[8,128]{1,0:T(8,128)S(1)} %get-tuple-element.140.refs_0_), channel_id=1, source_target_pairs={{0,4},{4,0},{8,12},{12,8},{1,5},{5,1},{9,13},{13,9},{2,6},{6,2},{1... | collective-permute-start | bytes 12296 | tf_op jit(solution)/shard_map/ppermute | solution.py:442
  184.1 2.0 %collective-permute-start.45 = (f32[1024,128]{1,0:T(8,128)S(1)}, f32[1024,128]{1,0:T(8,128)S(1)}, u32[]{:S(2)}, u32[]{:S(2)}) collective-permute-start(f32[1024,128]{1,0:T(8,128)S(1)} %shard_map.151.refs_1_), channel_id=1, source_target_pairs={{0,1},{1,0},{2,3},{3,2},{4,5},{5,4},{6,7},{7,6},{8,9},{9,8},{10,11... | collective-permute-start | bytes 1572872 | tf_op jit(solution)/shard_map/ppermute | solution.py:433
